TPU v7x, 512 devices: a whole 4x8x8 slice. The times are simulated.
512 devices in a mesh: dp: 4 (over z_hi), segment: 16 (over y, core), patch: 8 (over x, z_lo).
Axes of the slice: x: 4, y: 8, z: 8 (z_hi: 4, z_lo: 2; z = z_hi * 2 + z_lo), core: 2. Of those that a mesh axis runs over, the one named last changes fastest.
Arguments:
- hidden: bfloat16 [64, 1024, 1536], P(('dp', 'segment'), 'patch'), parts along dimension 0, may hold values from -6 to 6
- w_qkv: bfloat16 [16, 1536, 4608], P('segment', None, 'patch'), may hold values from -0.12552947 to 0.12552947
- norm_gain: float32 [16, 1536], P('segment'), may hold values from 0.5 to 1.5
- box_vec: float32 [16, 1536], P('segment'), may hold values from -4 to 4
- gate: float32 [64, 1536], P(('dp', 'segment')), parts along dimension 0, may hold values from 4 to 16
- box_mask: int32 [64, 1024], P(('dp', 'segment'), 'patch'), parts along dimension 0, may hold values 0 or 1
- stale_kv: bfloat16 [64, 2, 1024, 1536], P(('dp', 'segment'), None, 'patch'), parts along dimension 0, may hold values from -6 to 6
Outputs:
- hidden_out: bfloat16 [64, 1024, 1536], P(('dp', 'segment'), 'patch'), parts along dimension 0
- fresh_kv: bfloat16 [64, 2, 1024, 1536], P(('dp', 'segment'), None, 'patch'), parts along dimension 0
There are 4 independent parts, one for each index of `dp`. A program takes and returns all parts, laid end to end along the dimension named above; an argument that names none is the same for every part. Nothing has to cross between parts.
All inputs are finite; a program needn't handle non-finite values. No bound on the sum of `box_mask` on one device may be relied on, other than what follows from the above.
Results may differ from a plain program's by a relative error of at most 0.023.
Values may be sent and summed in bfloat16 or wider, within the bound.
No kernel may reach another device: no remote copies, remote signals or barrier semaphores. Data moves between devices by JAX's collectives and lax.ppermute only.
A program may use at most 64 MiB of HBM per device.

v0:
```python
import jax
import jax.numpy as jnp
from jax import lax
from jax.sharding import PartitionSpec as P

HEADS = 12
HEAD_DIM = 128


def from_behind(shard, axis, by):
    count = lax.axis_size(axis)
    return lax.ppermute(shard, axis, [(i, (i + by) % count) for i in range(count)])


def partial_attention(queries, keys, values):
    count = queries.shape[0]
    length = keys.shape[0]
    qh = queries.reshape(count, HEADS, HEAD_DIM)
    kh = keys.reshape(length, HEADS, HEAD_DIM)
    vh = values.reshape(length, HEADS, HEAD_DIM)
    scores = jnp.einsum("nhd,thd->nht", qh, kh, preferred_element_type=jnp.float32) * HEAD_DIM ** (
        -0.5
    )
    top = jnp.max(scores, axis=-1)
    weights = jnp.exp(scores - top[..., None])
    total = jnp.sum(weights, axis=-1)
    summed = jnp.einsum(
        "nht,thd->nhd", weights.astype(jnp.bfloat16), vh, preferred_element_type=jnp.float32
    )
    return (summed.reshape(count, HEADS * HEAD_DIM), top, total)


def local(hidden, w_qkv, norm_gain, box_vec, gate, box_mask, stale_kv):
    state = hidden[0].astype(jnp.float32)
    rows = state.shape[0]
    width = HEADS * HEAD_DIM
    inverse = lax.rsqrt(jnp.mean(state * state, axis=-1, keepdims=True) + 1e-06)
    normed = (
        state * inverse * norm_gain[0] + box_mask[0][:, None].astype(jnp.float32) * box_vec[0]
    ).astype(jnp.bfloat16)
    weight = w_qkv[0]
    columns = jnp.dot(
        lax.all_gather(normed, "patch", axis=0, tiled=True),
        weight,
        preferred_element_type=jnp.float32,
    ).astype(jnp.bfloat16)
    qkv = lax.all_to_all(columns, "patch", split_axis=0, concat_axis=1, tiled=True)
    queries = qkv[:, :width]
    keys_new = qkv[:, width : 2 * width]
    values_new = qkv[:, 2 * width :]
    fresh = jnp.stack([keys_new, values_new])
    own_start = lax.axis_index("patch") * rows
    whole = lax.all_gather(stale_kv[0], "patch", axis=1, tiled=True)
    whole = lax.dynamic_update_slice_in_dim(whole, fresh, own_start, 1)
    summed, top, total = partial_attention(queries, whole[0], whole[1])
    attended = (summed.reshape(rows, HEADS, HEAD_DIM) / total[..., None]).reshape(rows, width)
    updated = (state + gate[0] * attended).astype(jnp.bfloat16)
    passed = from_behind(updated[None], "segment", 1)
    return (passed, fresh[None])


def solution(mesh):
    placed = (
        P(("dp", "segment"), "patch", None),
        P("segment", None, "patch"),
        P("segment", None),
        P("segment", None),
        P(("dp", "segment"), None),
        P(("dp", "segment"), "patch"),
        P(("dp", "segment"), None, "patch", None),
    )
    return jax.shard_map(
        local,
        mesh=mesh,
        in_specs=placed,
        out_specs=(P(("dp", "segment"), "patch", None), P(("dp", "segment"), None, "patch", None)),
        check_vma=False,
    )
```

profile of v0, /device:TPU:1, one launch (start us, length us, event | category | flops | bytes accessed | tf_op | source)
XLA Modules:
  0.0 265.4 jit_solution(11302217391138647032)
XLA Ops:
  7.2 0.0 copy-start
  7.2 0.0 all-gather.4.cloned.1.call-start
  7.2 0.8 reduce.1
  8.1 0.7 reduce.2
  8.8 1.2 fusion.23
  9.9 0.7 convert_bitcast_fusion.1
  10.6 2.0 fusion.26
  12.6 0.0 all-gather.4.cloned.1.call-update
  12.6 0.0 all-gather.6.cloned.1.call-start
  12.7 2.3 copy.13
  15.0 0.0 all-gather.6.cloned.1.call-update
  15.0 80.0 %all-gather.4.cloned.1.call-done = bf16[1024,1536]{1,0:T(8,128)(2,1)} async-done(((bf16[128,1536]{1,0:T(8,128)(2,1)}), bf16[1024,1536]{1,0:T(8,128)(2,1)}) %all-gather.4.cloned.1.call-update) | async-done | bytes 3145744 | tf_op jit(solution)/shard_map/all_gather | solution.py:43
  94.9 0.0 copy-done
  94.9 3.9 %fusion.12 = bf16[72,8,8,128]{3,2,1,0:T(8,128)(2,1)S(1)} fusion(bf16[1024,1536]{1,0:T(8,128)(2,1)} %all-gather.4.cloned.1.call-done, bf16[1,1536,576]{1,2,0:T(8,128)(2,1)S(1)} %copy-done), kind=kOutput, calls=%fused_computation.11 | convolution fusion | flops 1812529152 | bytes 6094848 | tf_op jit(solution)/shard_map/dot_general | solution.py:42
  98.9 0.0 copy-start.2
  98.9 1.3 copy.25
  100.1 3.6 %all-to-all-start = ((bf16[8,128,576]{1,2,0:T(8,128)(2,1)}), bf16[8,128,576]{1,2,0:T(8,128)(2,1)S(1)}, u32[]{:S(2)}, u32[]{:S(2)}) async-start(bf16[8,128,576]{1,2,0:T(8,128)(2,1)} %bitcast.67), calls=%async_computation | async-start | bytes 2359296 | tf_op jit(solution)/shard_map/all_to_all | solution.py:47
  103.7 20.4 %all-to-all-done = bf16[8,128,576]{1,2,0:T(8,128)(2,1)S(1)} async-done(((bf16[8,128,576]{1,2,0:T(8,128)(2,1)}), bf16[8,128,576]{1,2,0:T(8,128)(2,1)S(1)}, u32[]{:S(2)}, u32[]{:S(2)}) %all-to-all-start) | async-done | bytes 1179680 | tf_op jit(solution)/shard_map/all_to_all | solution.py:47
  124.2 1.0 fusion.32
  125.2 112.2 %all-gather.6.cloned.1.call-done = bf16[1,2,1024,1536]{2,3,1,0:T(8,128)(2,1)} async-done(((bf16[1,2,128,1536]{2,3,1,0:T(8,128)(2,1)}), bf16[1,2,1024,1536]{2,3,1,0:T(8,128)(2,1)}) %all-gather.6.cloned.1.call-update) | async-done | bytes 6291472 | tf_op jit(solution)/shard_map/all_gather | solution.py:53
  237.4 2.3 fusion.28
  239.6 3.6 %fusion.31 = (bf16[1,1024,1536]{1,2,0:T(8,128)(2,1)S(1)}, bf16[1,1024,1536]{1,2,0:T(8,128)(2,1)S(1)}) fusion(bf16[2,1024,1536]{1,2,0:T(8,128)(2,1)} %get-tuple-element.10), kind=kLoop, calls=%fused_computation.32 | loop fusion | bytes 12582912 | tf_op jit(solution)/shard_map/slice | solution.py:55
  243.2 1.3 bitcast_reduce_fusion
  244.5 1.0 fusion.1
  245.5 0.0 copy-start.1
  245.5 2.6 fusion.20
  248.1 2.3 copy.18
  250.4 1.2 fusion.27
  251.6 1.6 collective-permute-start
  253.1 1.2 copy.19
  254.3 3.6 %collective-permute-done = bf16[1,128,1536]{2,1,0:T(8,128)(2,1)S(1)} collective-permute-done((bf16[1,128,1536]{2,1,0:T(8,128)(2,1)S(1)}, bf16[1,128,1536]{2,1,0:T(8,128)(2,1)S(1)}, u32[]{:S(2)}, u32[]{:S(2)}) %collective-permute-start) | collective-permute-done | bytes 393248 | tf_op jit(solution)/shard_map/ppermute | solution.py:12
  257.9 0.7 copy.28
  (4 shorter events, 0.0 us)
Async XLA Ops:
  7.2 87.8 %copy-start = (bf16[1,1536,576]{1,2,0:T(8,128)(2,1)S(1)}, bf16[1,1536,576]{1,2,0:T(8,128)(2,1)}, u32[]{:S(2)}) copy-start(bf16[1,1536,576]{1,2,0:T(8,128)(2,1)} %param.8) | copy-start | bytes 5308420
  7.2 87.8 %all-gather.4.cloned.1.call-start = ((), (), s32[]{:S(2)}) async-start(), calls=%async_computation.1 | async-start | bytes 3538944 | tf_op jit(solution)/shard_map/all_gather | solution.py:43
  12.6 224.7 %all-gather.6.cloned.1.call-start = ((), (), s32[]{:S(2)}) async-start(), calls=%async_computation.2 | async-start | bytes 7077888 | tf_op jit(solution)/shard_map/all_gather | solution.py:53
  98.9 4.8 %copy-start.2 = (f32[1,1536]{1,0:T(1,128)S(1)}, f32[1,1536]{1,0:T(1,128)}, u32[]{:S(2)}) copy-start(f32[1,1536]{1,0:T(1,128)} %param.11) | copy-start | bytes 18436
  100.1 24.1 %all-to-all-start = ((bf16[8,128,576]{1,2,0:T(8,128)(2,1)}), bf16[8,128,576]{1,2,0:T(8,128)(2,1)S(1)}, u32[]{:S(2)}, u32[]{:S(2)}) async-start(bf16[8,128,576]{1,2,0:T(8,128)(2,1)} %bitcast.67), calls=%async_computation | async-start | bytes 2359296 | tf_op jit(solution)/shard_map/all_to_all | solution.py:47
  245.5 4.9 %copy-start.1 = (bf16[1,128,1536]{2,1,0:T(8,128)(2,1)S(1)}, bf16[1,128,1536]{2,1,0:T(8,128)(2,1)}, u32[]{:S(2)}) copy-start(bf16[1,128,1536]{2,1,0:T(8,128)(2,1)} %param.7) | copy-start | bytes 1179652
  251.6 6.3 %collective-permute-start = (bf16[1,128,1536]{2,1,0:T(8,128)(2,1)S(1)}, bf16[1,128,1536]{2,1,0:T(8,128)(2,1)S(1)}, u32[]{:S(2)}, u32[]{:S(2)}) collective-permute-start(bf16[1,128,1536]{2,1,0:T(8,128)(2,1)S(1)} %fusion.27), channel_id=1, source_target_pairs={{0,8},{8,16},{16,24},{24,32},{32,40},{40,48},{48,56},{56,64},{64,7... | collective-permute-start | bytes 1179656 | tf_op jit(solution)/shard_map/ppermute | solution.py:12
Sparse Core Ops, SparseCore 0:
  12.7 82.1 all-gather.3
  97.5 139.7 all-gather.5
where the time goes:
time: 267 us; the launch traced here: 265 us
  waiting for transfers between devices  216 us (81%)
  between operations  14.1 us (5%)
  local copies, waits for them, and re-layouts  12.3 us (5%)
  other arithmetic  9.9 us (4%)
  matrix products  7.76 us (3%)
  starting transfers between devices  5.2 us (2%)
    all_gather x1, waiting for transfers between devices, local(): whole = lax.all_gather(stale_kv[0], 'patch', axis=1, tiled=True)  112 us
    all_gather x1, waiting for transfers between devices, local(): lax.all_gather(normed, 'patch', axis=0, tiled=True)  80 us
    all_to_all x1, waiting for transfers between devices, local(): lax.all_to_all(columns, 'patch', split_axis=0, concat_axis=1, tiled=True)  20.4 us
  transfers between devices with their start and end apart: 4, of which 4 were waited for; matrix products, arithmetic and copies ran while one was open for 4% of the time, Pallas kernels for 0%

commit v1 on v0

v1 whole, which is shorter than its diff:
```python
import jax
import jax.numpy as jnp
from jax import lax
from jax.experimental import pallas as pl
from jax.experimental.pallas import tpu as pltpu
from jax.sharding import PartitionSpec as P

HEAD_DIM = 128
ROWS = 128
D = 1536
UNIT = 384
HALF = 192
SCALE = HEAD_DIM ** (-0.5)
BF = jnp.bfloat16
F32 = jnp.float32
NT = (((1,), (1,)), ((), ()))
VM = pl.BlockSpec(memory_space=pltpu.VMEM)
PARAMS = pltpu.CompilerParams(vmem_limit_bytes=48 * 1024 * 1024)


def spot(x, z):
    return 2 * (x % 4) + z


def ahead(z):
    return 1 - 2 * z


def x_pairs(steps):
    return [(spot(x, z), spot(x + ahead(z) * steps, z)) for x in range(4) for z in range(2)]


def partner_pairs():
    return [(spot(x, z), spot(x, 1 - z)) for x in range(4) for z in range(2)]


def far_pairs(parts):
    pairs = []
    for dp in range(parts):
        for x in range(4):
            for z in range(2):
                there = (2 * dp + z - ahead(z)) % (2 * parts)
                pairs.append((dp * 8 + spot(x, z), (there // 2) * 8 + spot(x, there % 2)))
    return pairs


def where_am_i():
    p = lax.axis_index("patch")
    return p // 2, p % 2


def call(body, out, count, **more):
    return pl.pallas_call(
        body,
        out_shape=out,
        in_specs=[VM] * count,
        out_specs=jax.tree.map(lambda _: VM, out),
        compiler_params=PARAMS,
        **more,
    )


def norm_body(h_ref, g_ref, b_ref, m_ref, o_ref):
    h = h_ref[0].astype(F32)
    inverse = lax.rsqrt(jnp.mean(h * h, axis=-1, keepdims=True) + 1e-06)
    mask = jnp.broadcast_to(m_ref[...].astype(F32), (ROWS, ROWS)).T[:, :1]
    o_ref[...] = (h * inverse * g_ref[...] + mask * b_ref[...]).astype(BF)


def project(blocks, weight, o_ref):
    x, z = where_am_i()
    tokens = jnp.concatenate([b[...] for b in blocks], axis=0)
    got = lax.dot_general(tokens, weight, NT, preferred_element_type=F32).astype(BF)
    for j in range(4):
        o_ref[(x + (1 - 2 * z) * j + 4) % 4] = got[ROWS * j : ROWS * (j + 1)]


def front_body(t0, t1, t2, t3, w_ref, o_ref):
    _, z = where_am_i()
    project((t0, t1, t2, t3), w_ref[pl.ds(pl.multiple_of(HALF * z, HALF), UNIT), :], o_ref)


def back_body(t0, t1, t2, t3, w_ref, o_ref):
    project((t0, t1, t2, t3), w_ref[...], o_ref)


def mid_body(t0, t1, t2, t3, w_ref, u_ref, o_ref, both):
    _, z = where_am_i()
    mine = w_ref[pl.ds(pl.multiple_of(UNIT * (1 - z), HALF), HALF), :]
    both[pl.ds(pl.multiple_of(HALF * z, HALF), HALF), :] = mine
    both[pl.ds(pl.multiple_of(HALF * (1 - z), HALF), HALF), :] = u_ref[...]
    project((t0, t1, t2, t3), both[...], o_ref)


def pick(index, refs, at):
    a, b, c = (r[at] for r in refs)
    return jnp.where(index == 0, a, jnp.where(index == 1, b, c))


def roles(x, z):
    left = 1 + z
    right = 2 - z
    q = jnp.where(x == 0, 0, jnp.where(x == 3, right, left))
    k = jnp.where(x == 0, right, jnp.where(x == 3, left, 0))
    v = jnp.where(x == 0, left, jnp.where(x == 3, 0, right))
    return q, k, v


def attend_body(a_ref, b_ref, c_ref, s_ref, o_ref):
    x, z = where_am_i()
    refs = (a_ref, b_ref, c_ref)
    qi, ki, vi = roles(x, z)
    for j in range(4):
        o_ref[j, 1] = pick(ki, refs, j)
        o_ref[j, 2] = pick(vi, refs, j)
    for head in range(3):
        cols = slice(HEAD_DIM * head, HEAD_DIM * (head + 1))
        kept = [
            [s_ref[2 * j + side, kv, :, cols] for side in (z, 1 - z) for j in range(4)]
            for kv in range(2)
        ]
        for j in range(4):
            q = pick(qi, refs, (j, slice(None), cols))
            keys = list(kept[0])
            values = list(kept[1])
            keys[j] = o_ref[j, 1, :, cols]
            values[j] = o_ref[j, 2, :, cols]
            scores = lax.dot_general(
                q, jnp.concatenate(keys, axis=0), NT, preferred_element_type=F32
            ) * SCALE
            top = jnp.max(scores, axis=-1, keepdims=True)
            weights = jnp.exp(scores - top)
            total = jnp.sum(weights, axis=-1, keepdims=True)
            summed = jnp.dot(
                weights.astype(BF), jnp.concatenate(values, axis=0), preferred_element_type=F32
            )
            o_ref[j, 0, :, cols] = (summed / total).astype(BF)


def finish_body(r_ref, h_ref, g_ref, o_ref, f_ref):
    for group in range(4):
        cols = slice(UNIT * group, UNIT * (group + 1))
        r = r_ref.at[group ^ 1]
        o_ref[0, :, cols] = (
            h_ref[0, :, cols].astype(F32) + g_ref[:, cols] * r[0].astype(F32)
        ).astype(BF)
        f_ref[0, 0, :, cols] = r[1]
        f_ref[0, 1, :, cols] = r[2]


def local(hidden, w_qkv, norm_gain, box_vec, gate, box_mask, stale_kv):
    parts = lax.axis_size("dp")
    segments = lax.axis_size("segment")
    _, z = where_am_i()
    shape = jax.ShapeDtypeStruct
    unit = shape((4, ROWS, UNIT), BF)

    normed = call(norm_body, shape((ROWS, D), BF), 4)(hidden, norm_gain, box_vec, box_mask)
    weight = jnp.swapaxes(w_qkv[0], 0, 1)
    lead = lax.dynamic_slice_in_dim(weight, HALF * z, UNIT, 0)
    rest = lax.dynamic_slice_in_dim(weight, UNIT * (1 - z), HALF, 0)
    lead = lax.ppermute(lead, ("dp", "patch"), far_pairs(parts))
    rest = lax.ppermute(rest, "patch", partner_pairs())
    t1 = lax.ppermute(normed, "patch", x_pairs(3))
    t3 = lax.ppermute(normed, "patch", x_pairs(1))
    t2 = lax.ppermute(normed, "patch", x_pairs(2))
    tokens = (normed, t1, t2, t3)

    groups = [stale_kv[0, :, :, UNIT * (p // 2 ^ 1) : UNIT * (p // 2 ^ 1) + UNIT] for p in range(8)]
    kept = lax.all_to_all(jnp.stack(groups), "patch", 0, 0)

    front = call(front_body, unit, 5)(*tokens, weight)
    front = lax.ppermute(front, "patch", x_pairs(1))
    back = call(back_body, unit, 5)(*tokens, lead)
    back = lax.ppermute(back, "patch", x_pairs(3))
    mid = call(mid_body, unit, 6, scratch_shapes=[pltpu.VMEM((UNIT, D), BF)])(*tokens, weight, rest)

    mixed = call(attend_body, shape((4, 3, ROWS, UNIT), BF), 4)(mid, front, back, kept)
    mixed = lax.all_to_all(
        mixed, "patch", 0, 0, axis_index_groups=[[0, 2, 4, 6], [1, 3, 5, 7]]
    )
    updated, fresh = call(
        finish_body, (shape((1, ROWS, D), BF), shape((1, 2, ROWS, D), BF)), 3
    )(mixed, hidden, gate)
    passed = lax.ppermute(updated, "segment", [(i, (i + 1) % segments) for i in range(segments)])
    return (passed, fresh)


def solution(mesh):
    placed = (
        P(("dp", "segment"), "patch", None),
        P("segment", None, "patch"),
        P("segment", None),
        P("segment", None),
        P(("dp", "segment"), None),
        P(("dp", "segment"), "patch"),
        P(("dp", "segment"), None, "patch", None),
    )
    return jax.shard_map(
        local,
        mesh=mesh,
        in_specs=placed,
        out_specs=(P(("dp", "segment"), "patch", None), P(("dp", "segment"), None, "patch", None)),
        check_vma=False,
    )
```

time: 267 us -> 115 us (0.43)
  waiting for transfers between devices: 216 us -> 26.8 us
  starting transfers between devices: 5.2 us -> 38.2 us
  blocking collectives: 0 us -> 19.2 us
  between operations: 14.1 us -> 0.88 us
  Pallas kernels: 0 us -> 11.5 us
  other arithmetic: 9.9 us -> 0 us
  matrix products: 7.76 us -> 0 us
  local copies, waits for them, and re-layouts: 12.3 us -> 16.5 us
    all_gather x2 -> x0, waiting for transfers between devices: 192 us -> none  [the longest x1 112 us: local(): whole = lax.all_gather(stale_kv[0], 'patch', axis=1, tiled=True)]
    ppermute x1 -> x8, starting transfers between devices: 1.56 us -> 31.4 us  [the longest x1 10 us: local(): lead = lax.ppermute(lead, ('dp', 'patch'), far_pairs(parts))]
    ppermute x1 -> x8, waiting for transfers between devices: 3.56 us -> 26.8 us  [the longest x1 9.68 us: local(): t3 = lax.ppermute(normed, 'patch', x_pairs(1))]
    all_to_all x1, waiting for transfers between devices: 20.4 us -> 0.01 us  [local(): kept = lax.all_to_all(jnp.stack(groups), 'patch', 0, 0)]
    all_to_all x0 -> x1, blocking collectives: none -> 19.2 us  [local(): lax.all_to_all(mixed, 'patch', 0, 0, axis_index_groups=[[0, 2, 4, 6], [1,...]
    pallas_call x0 -> x6, Pallas kernels: none -> 11.5 us  [the longest x1 5.88 us: local(): call(attend_body, shape((4, 3, ROWS, UNIT), BF), 4)(mid, front, back, kept)]
    unnamed x9 -> x36, local copies, waits for them, and re-layouts: 4.22 us -> 14.7 us
    dot_general x3 -> x0, matrix products: 7.76 us -> none  [the longest x1 3.91 us: local(): jnp.dot(lax.all_gather(normed, 'patch', axis=0, tiled=True), weight, pref...]
  transfers between devices with their start and end apart: 4 -> 9, of which waited for: 4 -> 6; matrix products, arithmetic and copies ran while one was open for 4% -> 1% of each run, Pallas kernels for 0% -> 4%
where the time goes in v1:
time: 115 us; the launch traced here: 113 us
  starting transfers between devices  38.2 us (33%)
  waiting for transfers between devices  26.8 us (23%)
  blocking collectives  19.2 us (17%)
  local copies, waits for them, and re-layouts  16.5 us (14%)
  Pallas kernels  11.5 us (10%)
    all_to_all x1, blocking collectives, local(): lax.all_to_all(mixed, 'patch', 0, 0, axis_index_groups=[[0, 2, 4, 6], [1,...  19.2 us
    unnamed x36, local copies, waits for them, and re-layouts  14.7 us
    ppermute x1, starting transfers between devices, local(): lead = lax.ppermute(lead, ('dp', 'patch'), far_pairs(parts))  10 us
    ppermute x1, waiting for transfers between devices, local(): t3 = lax.ppermute(normed, 'patch', x_pairs(1))  9.68 us
    all_to_all x1, starting transfers between devices, local(): kept = lax.all_to_all(jnp.stack(groups), 'patch', 0, 0)  6.79 us
    pallas_call x1, Pallas kernels, local(): call(attend_body, shape((4, 3, ROWS, UNIT), BF), 4)(mid, front, back, kept)  5.88 us
    ppermute x1, waiting for transfers between devices, local(): lax.ppermute(updated, 'segment', [(i, (i + 1) % segments) for i in range(...  4.72 us
    ppermute x1, starting transfers between devices, local(): back = lax.ppermute(back, 'patch', x_pairs(3))  4.57 us
  transfers between devices with their start and end apart: 9, of which 6 were waited for; matrix products, arithmetic and copies ran while one was open for 1% of the time, Pallas kernels for 4%

profile of v1, /device:TPU:1, one launch (start us, length us, event | category | flops | bytes accessed | tf_op | source)
XLA Modules:
  0.0 113.1 jit_solution(7834532705691459920)
XLA Ops:
  0.6 1.7 %slice_dynamic-update-slice_fusion.6 = bf16[8,2,128,384]{3,2,1,0:T(8,128)(2,1)} fusion(bf16[1,2,128,1536]{3,2,1,0:T(8,128)(2,1)} %param.13), kind=kLoop, calls=%fused_computation.8 | loop fusion | bytes 393216
  2.3 1.6 %slice_dynamic-update-slice_fusion.7 = bf16[8,2,128,384]{3,2,1,0:T(8,128)(2,1)} fusion(bf16[8,2,128,384]{3,2,1,0:T(8,128)(2,1)} %slice_dynamic-update-slice_fusion.6, bf16[1,2,128,1536]{3,2,1,0:T(8,128)(2,1)} %param.13), kind=kLoop, calls=%fused_computation.9 | loop fusion | bytes 393216
  4.0 1.6 %slice_dynamic-update-slice_fusion.4 = bf16[8,2,128,384]{3,2,1,0:T(8,128)(2,1)} fusion(bf16[8,2,128,384]{3,2,1,0:T(8,128)(2,1)} %slice_dynamic-update-slice_fusion.7, bf16[1,2,128,1536]{3,2,1,0:T(8,128)(2,1)} %param.13), kind=kLoop, calls=%fused_computation.6 | loop fusion | bytes 393216
  5.6 1.6 %slice_dynamic-update-slice_fusion.5 = bf16[8,2,128,384]{3,2,1,0:T(8,128)(2,1)} fusion(bf16[8,2,128,384]{3,2,1,0:T(8,128)(2,1)} %slice_dynamic-update-slice_fusion.4, bf16[1,2,128,1536]{3,2,1,0:T(8,128)(2,1)} %param.13), kind=kLoop, calls=%fused_computation.7 | loop fusion | bytes 393216
  10.0 6.8 %all-to-all-start = ((bf16[8,2,128,384]{3,2,1,0:T(8,128)(2,1)}), bf16[8,2,128,384]{3,2,1,0:T(8,128)(2,1)}, u32[]{:S(2)}, u32[]{:S(2)}) async-start(bf16[8,2,128,384]{3,2,1,0:T(8,128)(2,1)} %slice_dynamic-update-slice_fusion.1), calls=%async_computation | async-start | bytes 3145728 | tf_op jit(solution)/shard_map/all_to_all | solution.py:170
  16.9 1.1 dynamic-slice_bitcast_fusion
  18.0 10.0 %collective-permute-start.5 = (bf16[384,1536]{1,0:T(8,128)(2,1)}, bf16[384,1536]{1,0:T(8,128)(2,1)}, u32[]{:S(2)}, u32[]{:S(2)}) collective-permute-start(bf16[384,1536]{1,0:T(8,128)(2,1)} %dynamic-slice_bitcast_fusion), channel_id=1, source_target_pairs={{0,385},{1,128},{2,387},{3,130},{4,389},{5,132},{6,391},{7,134},{1... | collective-permute-start | bytes 3538952 | tf_op jit(solution)/shard_map/ppermute | solution.py:162
  28.4 4.3 %collective-permute-start = (bf16[128,1536]{1,0:T(8,128)(2,1)S(1)}, bf16[128,1536]{1,0:T(8,128)(2,1)S(1)}, u32[]{:S(2)}, u32[]{:S(2)}) collective-permute-start(bf16[128,1536]{1,0:T(8,128)(2,1)S(1)} %shard_map.86.t0), channel_id=1, source_target_pairs={{0,6},{1,3},{2,0},{3,5},{4,2},{5,7},{6,4},{7,1},{8,14},{9,11},{10,... | collective-permute-start | bytes 1179656 | tf_op jit(solution)/shard_map/ppermute | solution.py:164
  32.7 2.5 %collective-permute-start.1 = (bf16[128,1536]{1,0:T(8,128)(2,1)S(1)}, bf16[128,1536]{1,0:T(8,128)(2,1)S(1)}, u32[]{:S(2)}, u32[]{:S(2)}) collective-permute-start(bf16[128,1536]{1,0:T(8,128)(2,1)S(1)} %shard_map.86.t0), channel_id=1, source_target_pairs={{0,4},{1,5},{2,6},{3,7},{4,0},{5,1},{6,2},{7,3},{8,12},{9,13},{10,... | collective-permute-start | bytes 1179656 | tf_op jit(solution)/shard_map/ppermute | solution.py:166
  35.2 2.5 %collective-permute-start.2 = (bf16[128,1536]{1,0:T(8,128)(2,1)S(1)}, bf16[128,1536]{1,0:T(8,128)(2,1)S(1)}, u32[]{:S(2)}, u32[]{:S(2)}) collective-permute-start(bf16[128,1536]{1,0:T(8,128)(2,1)S(1)} %shard_map.86.t0), channel_id=1, source_target_pairs={{0,2},{1,7},{2,4},{3,1},{4,6},{5,3},{6,0},{7,5},{8,10},{9,15},{10,... | collective-permute-start | bytes 1179656 | tf_op jit(solution)/shard_map/ppermute | solution.py:165
  37.7 1.9 %collective-permute-start.3 = (bf16[192,1536]{1,0:T(8,128)(2,1)S(1)}, bf16[192,1536]{1,0:T(8,128)(2,1)S(1)}, u32[]{:S(2)}, u32[]{:S(2)}) collective-permute-start(bf16[192,1536]{1,0:T(8,128)(2,1)S(1)} %dynamic-slice_bitcast_fusion.1), channel_id=1, source_target_pairs={{0,1},{1,0},{2,3},{3,2},{4,5},{5,4},{6,7},{7,6},{8,9},{9,8},{10,11... | collective-permute-start | bytes 1769480 | tf_op jit(solution)/shard_map/ppermute | solution.py:163
  39.7 4.5 %collective-permute-done.t1 = bf16[128,1536]{1,0:T(8,128)(2,1)S(1)} collective-permute-done((bf16[128,1536]{1,0:T(8,128)(2,1)S(1)}, bf16[128,1536]{1,0:T(8,128)(2,1)S(1)}, u32[]{:S(2)}, u32[]{:S(2)}) %collective-permute-start) | collective-permute-done | bytes 393248 | tf_op jit(solution)/shard_map/ppermute | solution.py:164
  44.1 2.8 %collective-permute-done.1.t2 = bf16[128,1536]{1,0:T(8,128)(2,1)S(1)} collective-permute-done((bf16[128,1536]{1,0:T(8,128)(2,1)S(1)}, bf16[128,1536]{1,0:T(8,128)(2,1)S(1)}, u32[]{:S(2)}, u32[]{:S(2)}) %collective-permute-start.1) | collective-permute-done | bytes 393248 | tf_op jit(solution)/shard_map/ppermute | solution.py:166
  46.9 9.7 %collective-permute-done.2.t3 = bf16[128,1536]{1,0:T(8,128)(2,1)S(1)} collective-permute-done((bf16[128,1536]{1,0:T(8,128)(2,1)S(1)}, bf16[128,1536]{1,0:T(8,128)(2,1)S(1)}, u32[]{:S(2)}, u32[]{:S(2)}) %collective-permute-start.2) | collective-permute-done | bytes 393248 | tf_op jit(solution)/shard_map/ppermute | solution.py:165
  56.6 1.0 shard_map.88
  57.6 1.9 %collective-permute-start.4 = (bf16[4,128,384]{2,1,0:T(8,128)(2,1)S(1)}, bf16[4,128,384]{2,1,0:T(8,128)(2,1)S(1)}, u32[]{:S(2)}, u32[]{:S(2)}) collective-permute-start(bf16[4,128,384]{2,1,0:T(8,128)(2,1)S(1)} %shard_map.88), channel_id=1, source_target_pairs={{0,2},{1,7},{2,4},{3,1},{4,6},{5,3},{6,0},{7,5},{8,10},{9,15},{10,... | collective-permute-start | bytes 1179656 | tf_op jit(solution)/shard_map/ppermute | solution.py:173
  59.5 2.3 %shard_map.89 = bf16[4,128,384]{2,1,0:T(8,128)(2,1)S(1)} custom-call(bf16[128,1536]{1,0:T(8,128)(2,1)S(1)} %shard_map.86.t0, bf16[128,1536]{1,0:T(8,128)(2,1)S(1)} %collective-permute-done.t1, bf16[128,1536]{1,0:T(8,128)(2,1)S(1)} %collective-permute-done.1.t2, bf16[128,1536]{1,0:T(8,128)(2,1)S(1)} %collective-permute-done.2.t3, ...), custom_call_target="tpu_custom_call" | custom-call | tf_op jit(solution)/shard_map/pallas_call | solution.py:174
  61.8 4.6 %collective-permute-start.6 = (bf16[4,128,384]{2,1,0:T(8,128)(2,1)S(1)}, bf16[4,128,384]{2,1,0:T(8,128)(2,1)S(1)}, u32[]{:S(2)}, u32[]{:S(2)}) collective-permute-start(bf16[4,128,384]{2,1,0:T(8,128)(2,1)S(1)} %shard_map.89), channel_id=1, source_target_pairs={{0,6},{1,3},{2,0},{3,5},{4,2},{5,7},{6,4},{7,1},{8,14},{9,11},{10,... | collective-permute-start | bytes 1179656 | tf_op jit(solution)/shard_map/ppermute | solution.py:175
  66.4 1.0 shard_map.87.a_ref
  68.2 2.7 %collective-permute-done.4.b_ref = bf16[4,128,384]{2,1,0:T(8,128)(2,1)S(1)} collective-permute-done((bf16[4,128,384]{2,1,0:T(8,128)(2,1)S(1)}, bf16[4,128,384]{2,1,0:T(8,128)(2,1)S(1)}, u32[]{:S(2)}, u32[]{:S(2)}) %collective-permute-start.4) | collective-permute-done | bytes 393248 | tf_op jit(solution)/shard_map/ppermute | solution.py:173
  70.9 0.7 copy-done.5
  71.7 2.4 %collective-permute-done.6.c_ref = bf16[4,128,384]{2,1,0:T(8,128)(2,1)S(1)} collective-permute-done((bf16[4,128,384]{2,1,0:T(8,128)(2,1)S(1)}, bf16[4,128,384]{2,1,0:T(8,128)(2,1)S(1)}, u32[]{:S(2)}, u32[]{:S(2)}) %collective-permute-start.6) | collective-permute-done | bytes 393248 | tf_op jit(solution)/shard_map/ppermute | solution.py:175
  74.1 0.7 copy-done.7
  74.8 1.0 copy-done.4
  75.8 1.0 copy-done.6
  76.8 1.0 copy-done.8
  77.8 5.9 %shard_map.90 = bf16[4,3,128,384]{3,2,1,0:T(8,128)(2,1)S(1)} custom-call(bf16[4,128,384]{2,1,0:T(8,128)(2,1)S(1)} %copy-done.4, bf16[4,128,384]{2,1,0:T(8,128)(2,1)S(1)} %copy-done.6, bf16[4,128,384]{2,1,0:T(8,128)(2,1)S(1)} %copy-done.8, bf16[8,2,128,384]{3,2,1,0:T(8,128)(2,1)} %all-to-all-done.s_ref), custom_call_target="tpu_custom_call" | custom-call | tf_op jit(solution)/shard_map/pallas_call | solution.py:178
  83.7 19.2 %all_to_all.10.r_ref = bf16[4,3,128,384]{3,2,1,0:T(8,128)(2,1)S(1)} all-to-all(bf16[4,3,128,384]{3,2,1,0:T(8,128)(2,1)S(1)} %shard_map.90), channel_id=1, replica_groups={{0,2,4,6},{1,3,5,7},{8,10,12,14},{9,11,13,15},{16,18,20,22},{17,19,21,2..., dimensions={0} | all-to-all | bytes 2359296 | tf_op jit(solution)/shard_map/all_to_all | solution.py:179
  103.0 1.0 shard_map.91
  104.0 3.7 %collective-permute-start.7 = (bf16[1,128,1536]{2,1,0:T(8,128)(2,1)S(1)}, bf16[1,128,1536]{2,1,0:T(8,128)(2,1)S(1)}, u32[]{:S(2)}, u32[]{:S(2)}) collective-permute-start(bf16[1,128,1536]{2,1,0:T(8,128)(2,1)S(1)} %get-tuple-element.4), channel_id=1, source_target_pairs={{0,8},{8,16},{16,24},{24,32},{32,40},{40,48},{48,56},{56,64},{64,7... | collective-permute-start | bytes 1179656 | tf_op jit(solution)/shard_map/ppermute | solution.py:185
  107.7 4.7 %collective-permute-done.7 = bf16[1,128,1536]{2,1,0:T(8,128)(2,1)S(1)} collective-permute-done((bf16[1,128,1536]{2,1,0:T(8,128)(2,1)S(1)}, bf16[1,128,1536]{2,1,0:T(8,128)(2,1)S(1)}, u32[]{:S(2)}, u32[]{:S(2)}) %collective-permute-start.7) | collective-permute-done | bytes 393248 | tf_op jit(solution)/shard_map/ppermute | solution.py:185
  112.4 0.7 copy.17
  (32 shorter events, 4.0 us)
Async XLA Ops:
  0.6 6.6 %copy-start.13 = (bf16[1,2,128,1536]{3,2,1,0:T(8,128)(2,1)S(1)}, bf16[1,2,128,1536]{3,2,1,0:T(8,128)(2,1)}, u32[]{:S(2)}) copy-start(bf16[1,2,128,1536]{3,2,1,0:T(8,128)(2,1)} %param.13) | copy-start | bytes 2359300
  10.0 6.9 %copy-start = (bf16[1,1536,576]{1,2,0:T(8,128)(2,1)S(1)}, bf16[1,1536,576]{1,2,0:T(8,128)(2,1)}, u32[]{:S(2)}) copy-start(bf16[1,1536,576]{1,2,0:T(8,128)(2,1)} %param.8) | copy-start | bytes 5308420
  10.0 64.8 %all-to-all-start = ((bf16[8,2,128,384]{3,2,1,0:T(8,128)(2,1)}), bf16[8,2,128,384]{3,2,1,0:T(8,128)(2,1)}, u32[]{:S(2)}, u32[]{:S(2)}) async-start(bf16[8,2,128,384]{3,2,1,0:T(8,128)(2,1)} %slice_dynamic-update-slice_fusion.1), calls=%async_computation | async-start | bytes 3145728 | tf_op jit(solution)/shard_map/all_to_all | solution.py:170
  16.8 11.2 %copy-start.1 = (bf16[1,128,1536]{2,1,0:T(8,128)(2,1)S(1)}, bf16[1,128,1536]{2,1,0:T(8,128)(2,1)}, u32[]{:S(2)}) copy-start(bf16[1,128,1536]{2,1,0:T(8,128)(2,1)} %h_ref.3) | copy-start | bytes 1179652
  16.8 11.2 %copy-start.9 = (f32[1,1536]{1,0:T(1,128)S(1)}, f32[1,1536]{1,0:T(1,128)}, u32[]{:S(2)}) copy-start(f32[1,1536]{1,0:T(1,128)} %g_ref.2) | copy-start | bytes 18436
  16.9 11.2 %copy-start.10 = (f32[1,1536]{1,0:T(1,128)S(1)}, f32[1,1536]{1,0:T(1,128)}, u32[]{:S(2)}) copy-start(f32[1,1536]{1,0:T(1,128)} %b_ref.1) | copy-start | bytes 18436
  16.9 11.2 %copy-start.12 = (s32[1,128]{1,0:T(1,128)S(1)}, s32[1,128]{1,0:T(1,128)}, u32[]{:S(2)}) copy-start(s32[1,128]{1,0:T(1,128)} %m_ref.1) | copy-start | bytes 1540
  18.0 41.5 %collective-permute-start.5 = (bf16[384,1536]{1,0:T(8,128)(2,1)}, bf16[384,1536]{1,0:T(8,128)(2,1)}, u32[]{:S(2)}, u32[]{:S(2)}) collective-permute-start(bf16[384,1536]{1,0:T(8,128)(2,1)} %dynamic-slice_bitcast_fusion), channel_id=1, source_target_pairs={{0,385},{1,128},{2,387},{3,130},{4,389},{5,132},{6,391},{7,134},{1... | collective-permute-start | bytes 3538952 | tf_op jit(solution)/shard_map/ppermute | solution.py:162
  28.4 15.8 %collective-permute-start = (bf16[128,1536]{1,0:T(8,128)(2,1)S(1)}, bf16[128,1536]{1,0:T(8,128)(2,1)S(1)}, u32[]{:S(2)}, u32[]{:S(2)}) collective-permute-start(bf16[128,1536]{1,0:T(8,128)(2,1)S(1)} %shard_map.86.t0), channel_id=1, source_target_pairs={{0,6},{1,3},{2,0},{3,5},{4,2},{5,7},{6,4},{7,1},{8,14},{9,11},{10,... | collective-permute-start | bytes 1179656 | tf_op jit(solution)/shard_map/ppermute | solution.py:164
  32.7 14.2 %collective-permute-start.1 = (bf16[128,1536]{1,0:T(8,128)(2,1)S(1)}, bf16[128,1536]{1,0:T(8,128)(2,1)S(1)}, u32[]{:S(2)}, u32[]{:S(2)}) collective-permute-start(bf16[128,1536]{1,0:T(8,128)(2,1)S(1)} %shard_map.86.t0), channel_id=1, source_target_pairs={{0,4},{1,5},{2,6},{3,7},{4,0},{5,1},{6,2},{7,3},{8,12},{9,13},{10,... | collective-permute-start | bytes 1179656 | tf_op jit(solution)/shard_map/ppermute | solution.py:166
  35.2 21.4 %collective-permute-start.2 = (bf16[128,1536]{1,0:T(8,128)(2,1)S(1)}, bf16[128,1536]{1,0:T(8,128)(2,1)S(1)}, u32[]{:S(2)}, u32[]{:S(2)}) collective-permute-start(bf16[128,1536]{1,0:T(8,128)(2,1)S(1)} %shard_map.86.t0), channel_id=1, source_target_pairs={{0,2},{1,7},{2,4},{3,1},{4,6},{5,3},{6,0},{7,5},{8,10},{9,15},{10,... | collective-permute-start | bytes 1179656 | tf_op jit(solution)/shard_map/ppermute | solution.py:165
  37.7 28.7 %collective-permute-start.3 = (bf16[192,1536]{1,0:T(8,128)(2,1)S(1)}, bf16[192,1536]{1,0:T(8,128)(2,1)S(1)}, u32[]{:S(2)}, u32[]{:S(2)}) collective-permute-start(bf16[192,1536]{1,0:T(8,128)(2,1)S(1)} %dynamic-slice_bitcast_fusion.1), channel_id=1, source_target_pairs={{0,1},{1,0},{2,3},{3,2},{4,5},{5,4},{6,7},{7,6},{8,9},{9,8},{10,11... | collective-permute-start | bytes 1769480 | tf_op jit(solution)/shard_map/ppermute | solution.py:163
  57.6 13.3 %collective-permute-start.4 = (bf16[4,128,384]{2,1,0:T(8,128)(2,1)S(1)}, bf16[4,128,384]{2,1,0:T(8,128)(2,1)S(1)}, u32[]{:S(2)}, u32[]{:S(2)}) collective-permute-start(bf16[4,128,384]{2,1,0:T(8,128)(2,1)S(1)} %shard_map.88), channel_id=1, source_target_pairs={{0,2},{1,7},{2,4},{3,1},{4,6},{5,3},{6,0},{7,5},{8,10},{9,15},{10,... | collective-permute-start | bytes 1179656 | tf_op jit(solution)/shard_map/ppermute | solution.py:173
  61.8 12.3 %collective-permute-start.6 = (bf16[4,128,384]{2,1,0:T(8,128)(2,1)S(1)}, bf16[4,128,384]{2,1,0:T(8,128)(2,1)S(1)}, u32[]{:S(2)}, u32[]{:S(2)}) collective-permute-start(bf16[4,128,384]{2,1,0:T(8,128)(2,1)S(1)} %shard_map.89), channel_id=1, source_target_pairs={{0,6},{1,3},{2,0},{3,5},{4,2},{5,7},{6,4},{7,1},{8,14},{9,11},{10,... | collective-permute-start | bytes 1179656 | tf_op jit(solution)/shard_map/ppermute | solution.py:175
  67.5 0.7 copy-start.3
  70.9 0.7 copy-start.5
  74.1 0.7 copy-start.7
  74.8 1.0 copy-start.4
  75.8 1.0 copy-start.6
  76.8 1.0 copy-start.8
  83.7 19.3 %copy-start.2 = (bf16[1,128,1536]{2,1,0:T(8,128)(2,1)S(1)}, bf16[1,128,1536]{2,1,0:T(8,128)(2,1)}, u32[]{:S(2)}) copy-start(bf16[1,128,1536]{2,1,0:T(8,128)(2,1)} %h_ref.3) | copy-start | bytes 1179652
  83.7 19.3 %copy-start.11 = (f32[1,1536]{1,0:T(1,128)S(1)}, f32[1,1536]{1,0:T(1,128)}, u32[]{:S(2)}) copy-start(f32[1,1536]{1,0:T(1,128)} %g_ref.3) | copy-start | bytes 18436
  104.0 8.4 %collective-permute-start.7 = (bf16[1,128,1536]{2,1,0:T(8,128)(2,1)S(1)}, bf16[1,128,1536]{2,1,0:T(8,128)(2,1)S(1)}, u32[]{:S(2)}, u32[]{:S(2)}) collective-permute-start(bf16[1,128,1536]{2,1,0:T(8,128)(2,1)S(1)} %get-tuple-element.4), channel_id=1, source_target_pairs={{0,8},{8,16},{16,24},{24,32},{32,40},{40,48},{48,56},{56,64},{64,7... | collective-permute-start | bytes 1179656 | tf_op jit(solution)/shard_map/ppermute | solution.py:185

commit v2 on v1

--- a/solution.py
+++ b/solution.py
@@ -15,7 +15,7 @@
 F32 = jnp.float32
 NT = (((1,), (1,)), ((), ()))
 VM = pl.BlockSpec(memory_space=pltpu.VMEM)
-PARAMS = pltpu.CompilerParams(vmem_limit_bytes=48 * 1024 * 1024)
+PARAMS = pltpu.CompilerParams(vmem_limit_bytes=16 * 1024 * 1024)
 
 
 def spot(x, z):
@@ -67,6 +67,13 @@
     o_ref[...] = (h * inverse * g_ref[...] + mask * b_ref[...]).astype(BF)
 
 
+def spread_body(s_ref, n_ref, o_ref):
+    del n_ref
+    for x in range(4):
+        for z in range(2):
+            o_ref[spot(x, z)] = s_ref[0, :, :, UNIT * (x ^ 1) : UNIT * ((x ^ 1) + 1)]
+
+
 def project(blocks, weight, o_ref):
     x, z = where_am_i()
     tokens = jnp.concatenate([b[...] for b in blocks], axis=0)
@@ -75,7 +82,8 @@
         o_ref[(x + (1 - 2 * z) * j + 4) % 4] = got[ROWS * j : ROWS * (j + 1)]
 
 
-def front_body(t0, t1, t2, t3, w_ref, o_ref):
+def front_body(t0, t1, t2, t3, w_ref, early_ref, o_ref):
+    del early_ref
     _, z = where_am_i()
     project((t0, t1, t2, t3), w_ref[pl.ds(pl.multiple_of(HALF * z, HALF), UNIT), :], o_ref)
 
@@ -106,13 +114,18 @@
     return q, k, v
 
 
-def attend_body(a_ref, b_ref, c_ref, s_ref, o_ref):
+def sort_body(a_ref, b_ref, c_ref, q_ref, kv_ref):
+    refs = (a_ref, b_ref, c_ref)
+    qi, ki, vi = roles(*where_am_i())
+    for j in range(4):
+        q_ref[j] = pick(qi, refs, j)
+        kv_ref[j, 0] = pick(ki, refs, j)
+        kv_ref[j, 1] = pick(vi, refs, j)
+
+
+def attend_body(q_ref, kv_ref, s_ref, g_ref, *o_refs):
     x, z = where_am_i()
-    refs = (a_ref, b_ref, c_ref)
-    qi, ki, vi = roles(x, z)
-    for j in range(4):
-        o_ref[j, 1] = pick(ki, refs, j)
-        o_ref[j, 2] = pick(vi, refs, j)
+    gates = g_ref[x ^ 1]
     for head in range(3):
         cols = slice(HEAD_DIM * head, HEAD_DIM * (head + 1))
         kept = [
@@ -120,11 +133,11 @@
             for kv in range(2)
         ]
         for j in range(4):
-            q = pick(qi, refs, (j, slice(None), cols))
+            q = q_ref[j, :, cols]
             keys = list(kept[0])
             values = list(kept[1])
-            keys[j] = o_ref[j, 1, :, cols]
-            values[j] = o_ref[j, 2, :, cols]
+            keys[j] = kv_ref[j, 0, :, cols]
+            values[j] = kv_ref[j, 1, :, cols]
             scores = lax.dot_general(
                 q, jnp.concatenate(keys, axis=0), NT, preferred_element_type=F32
             ) * SCALE
@@ -134,18 +147,20 @@
             summed = jnp.dot(
                 weights.astype(BF), jnp.concatenate(values, axis=0), preferred_element_type=F32
             )
-            o_ref[j, 0, :, cols] = (summed / total).astype(BF)
-
-
-def finish_body(r_ref, h_ref, g_ref, o_ref, f_ref):
+            o_refs[0][j, :, cols] = (gates[:, cols] * (summed / total)).astype(BF)
+
+
+def finish_body(a0, a1, a2, a3, h_ref, o_ref):
+    x, z = where_am_i()
+    for j, ref in enumerate((a0, a1, a2, a3)):
+        group = ((x + (1 - 2 * z) * j + 4) % 4) ^ 1
+        cols = pl.ds(pl.multiple_of(UNIT * group, UNIT), UNIT)
+        o_ref[0, :, cols] = (h_ref[0, :, cols].astype(F32) + ref[...].astype(F32)).astype(BF)
+
+
+def fresh_body(r_ref, f_ref):
     for group in range(4):
-        cols = slice(UNIT * group, UNIT * (group + 1))
-        r = r_ref.at[group ^ 1]
-        o_ref[0, :, cols] = (
-            h_ref[0, :, cols].astype(F32) + g_ref[:, cols] * r[0].astype(F32)
-        ).astype(BF)
-        f_ref[0, 0, :, cols] = r[1]
-        f_ref[0, 1, :, cols] = r[2]
+        f_ref[0, :, :, UNIT * group : UNIT * (group + 1)] = r_ref[group ^ 1]
 
 
 def local(hidden, w_qkv, norm_gain, box_vec, gate, box_mask, stale_kv):
@@ -166,23 +181,37 @@
     t2 = lax.ppermute(normed, "patch", x_pairs(2))
     tokens = (normed, t1, t2, t3)
 
-    groups = [stale_kv[0, :, :, UNIT * (p // 2 ^ 1) : UNIT * (p // 2 ^ 1) + UNIT] for p in range(8)]
-    kept = lax.all_to_all(jnp.stack(groups), "patch", 0, 0)
-
-    front = call(front_body, unit, 5)(*tokens, weight)
+    spread = call(spread_body, shape((8, 2, ROWS, UNIT), BF), 2)(stale_kv, t1)
+    kept = lax.all_to_all(spread, "patch", 0, 0)
+
+    before = lax.ppermute(hidden, "segment", [(i, (i + 1) % segments) for i in range(segments)])
+    front = call(front_body, unit, 6)(*tokens, weight, before)
     front = lax.ppermute(front, "patch", x_pairs(1))
     back = call(back_body, unit, 5)(*tokens, lead)
     back = lax.ppermute(back, "patch", x_pairs(3))
     mid = call(mid_body, unit, 6, scratch_shapes=[pltpu.VMEM((UNIT, D), BF)])(*tokens, weight, rest)
 
-    mixed = call(attend_body, shape((4, 3, ROWS, UNIT), BF), 4)(mid, front, back, kept)
-    mixed = lax.all_to_all(
-        mixed, "patch", 0, 0, axis_index_groups=[[0, 2, 4, 6], [1, 3, 5, 7]]
-    )
-    updated, fresh = call(
-        finish_body, (shape((1, ROWS, D), BF), shape((1, 2, ROWS, D), BF)), 3
-    )(mixed, hidden, gate)
-    passed = lax.ppermute(updated, "segment", [(i, (i + 1) % segments) for i in range(segments)])
+    queries, own_kv = call(sort_body, (unit, shape((4, 2, ROWS, UNIT), BF)), 3)(mid, front, back)
+    fresh = lax.all_to_all(
+        own_kv, "patch", 0, 0, axis_index_groups=[[0, 2, 4, 6], [1, 3, 5, 7]]
+    )
+    fresh = call(fresh_body, shape((1, 2, ROWS, D), BF), 1)(fresh)
+    mixed = call(attend_body, (unit,), 4)(queries, own_kv, kept, gate.reshape(4, 1, UNIT))[0]
+
+    x, _ = where_am_i()
+    came = []
+    for j in range(4):
+        there = lax.rem(x + (1 - 2 * z) * j + 4, 4)
+        piece = lax.dynamic_index_in_dim(mixed, there, 0, keepdims=False)
+        pairs = [
+            (s * 8 + src, (s + 1) % segments * 8 + dst)
+            for s in range(segments)
+            for src, dst in x_pairs(j)
+        ]
+        came.append(lax.ppermute(piece, ("segment", "patch"), pairs))
+    passed = call(finish_body, shape((1, ROWS, D), BF), 5)(
+        came[0], came[3], came[2], came[1], before
+    )
     return (passed, fresh)
 
 

time: 115 us -> 119 us (1.035)
  starting transfers between devices: 38.2 us -> 63.3 us
  blocking collectives: 19.2 us -> 0 us
  local copies, waits for them, and re-layouts: 16.5 us -> 7.3 us
  Pallas kernels: 11.5 us -> 18.9 us
    all_to_all x1 -> x0, blocking collectives: 19.2 us -> none  [local(): lax.all_to_all(mixed, 'patch', 0, 0, axis_index_groups=[[0, 2, 4, 6], [1,...]
    ppermute x1 -> x5, starting transfers between devices: 3.68 us -> 19.9 us  [the longest x4 15.8 us: local(): came.append(lax.ppermute(piece, ('segment', 'patch'), pairs))]
    unnamed x36 -> x20, local copies, waits for them, and re-layouts: 14.7 us -> 6.09 us
    all_to_all x1 -> x2, starting transfers between devices: 6.79 us -> 12.9 us  [the longest x1 8.25 us: local(): kept = lax.all_to_all(spread, 'patch', 0, 0)]
    pallas_call x3 -> x6, Pallas kernels: 7.87 us -> 12 us  [the longest x1 5.54 us: local(): call(attend_body, (unit,), 4)]
    ppermute x1 -> x5, waiting for transfers between devices: 4.72 us -> 1.98 us  [the longest x4 1.97 us: local(): came.append(lax.ppermute(piece, ('segment', 'patch'), pairs))]
    ppermute x1, starting transfers between devices: 2.48 us -> 4.6 us  [local(): t2 = lax.ppermute(normed, 'patch', x_pairs(2))]
    ppermute x1, waiting for transfers between devices: 2.79 us -> 4.73 us  [local(): t2 = lax.ppermute(normed, 'patch', x_pairs(2))]
  transfers between devices with their start and end apart: 9 -> 14, of which waited for: 6 -> 6; matrix products, arithmetic and copies ran while one was open for 1% -> 1% of each run, Pallas kernels for 4% -> 13%
where the time goes in v2:
time: 119 us; the launch traced here: 117 us
  starting transfers between devices  63.3 us (53%)
  waiting for transfers between devices  26.9 us (23%)
  Pallas kernels  18.9 us (16%)
  local copies, waits for them, and re-layouts  7.3 us (6%)
    ppermute x4, starting transfers between devices, local(): came.append(lax.ppermute(piece, ('segment', 'patch'), pairs))  15.8 us
    ppermute x1, starting transfers between devices, local(): lead = lax.ppermute(lead, ('dp', 'patch'), far_pairs(parts))  10.1 us
    ppermute x1, waiting for transfers between devices, local(): t3 = lax.ppermute(normed, 'patch', x_pairs(1))  9.34 us
    all_to_all x1, starting transfers between devices, local(): kept = lax.all_to_all(spread, 'patch', 0, 0)  8.25 us
    unnamed x20, local copies, waits for them, and re-layouts  6.09 us
    pallas_call x1, Pallas kernels, local(): call(attend_body, (unit,), 4)  5.54 us
    ppermute x1, waiting for transfers between devices, local(): t1 = lax.ppermute(normed, 'patch', x_pairs(3))  5.4 us
    ppermute x1, starting transfers between devices, local(): t1 = lax.ppermute(normed, 'patch', x_pairs(3))  5.2 us
  transfers between devices with their start and end apart: 14, of which 6 were waited for; matrix products, arithmetic and copies ran while one was open for 1% of the time, Pallas kernels for 13%

profile of v2, /device:TPU:1, one launch (start us, length us, event | category | flops | bytes accessed | tf_op | source)
XLA Modules:
  0.0 117.2 jit_solution(15285174055591026597)
XLA Ops:
  2.7 2.0 %shard_map.86.t0 = bf16[128,1536]{1,0:T(8,128)(2,1)} custom-call(bf16[1,128,1536]{2,1,0:T(8,128)(2,1)} %h_ref.1, f32[1,1536]{1,0:T(1,128)S(1)} %copy-done.6, f32[1,1536]{1,0:T(1,128)S(1)} %copy-done.7, s32[1,128]{1,0:T(1,128)S(1)} %copy-done.9), custom_call_target="tpu_custom_call" | custom-call | tf_op jit(solution)/shard_map/pallas_call | solution.py:173
  4.7 5.2 %collective-permute-start = (bf16[128,1536]{1,0:T(8,128)(2,1)}, bf16[128,1536]{1,0:T(8,128)(2,1)S(1)}, u32[]{:S(2)}, u32[]{:S(2)}) collective-permute-start(bf16[128,1536]{1,0:T(8,128)(2,1)} %shard_map.86.t0), channel_id=1, source_target_pairs={{0,6},{1,3},{2,0},{3,5},{4,2},{5,7},{6,4},{7,1},{8,14},{9,11},{10,... | collective-permute-start | bytes 1179656 | tf_op jit(solution)/shard_map/ppermute | solution.py:179
  9.9 5.4 %collective-permute-done.t1.n_ref = bf16[128,1536]{1,0:T(8,128)(2,1)S(1)} collective-permute-done((bf16[128,1536]{1,0:T(8,128)(2,1)}, bf16[128,1536]{1,0:T(8,128)(2,1)S(1)}, u32[]{:S(2)}, u32[]{:S(2)}) %collective-permute-start) | collective-permute-done | bytes 393248 | tf_op jit(solution)/shard_map/ppermute | solution.py:179
  15.3 1.1 copy-done.5
  16.6 1.2 copy-done.1
  18.5 8.3 %all-to-all-start = ((bf16[8,2,128,384]{3,2,1,0:T(8,128)(2,1)}), bf16[8,2,128,384]{3,2,1,0:T(8,128)(2,1)S(1)}, u32[]{:S(2)}, u32[]{:S(2)}) async-start(bf16[8,2,128,384]{3,2,1,0:T(8,128)(2,1)} %copy-done.1), calls=%async_computation | async-start | bytes 3145728 | tf_op jit(solution)/shard_map/all_to_all | solution.py:185
  26.8 1.1 dynamic-slice_bitcast_fusion
  27.9 10.1 %collective-permute-start.6 = (bf16[384,1536]{1,0:T(8,128)(2,1)}, bf16[384,1536]{1,0:T(8,128)(2,1)}, u32[]{:S(2)}, u32[]{:S(2)}) collective-permute-start(bf16[384,1536]{1,0:T(8,128)(2,1)} %dynamic-slice_bitcast_fusion), channel_id=1, source_target_pairs={{0,385},{1,128},{2,387},{3,130},{4,389},{5,132},{6,391},{7,134},{1... | collective-permute-start | bytes 3538952 | tf_op jit(solution)/shard_map/ppermute | solution.py:177
  38.0 4.6 %collective-permute-start.1 = (bf16[128,1536]{1,0:T(8,128)(2,1)}, bf16[128,1536]{1,0:T(8,128)(2,1)}, u32[]{:S(2)}, u32[]{:S(2)}) collective-permute-start(bf16[128,1536]{1,0:T(8,128)(2,1)} %shard_map.86.t0), channel_id=1, source_target_pairs={{0,4},{1,5},{2,6},{3,7},{4,0},{5,1},{6,2},{7,3},{8,12},{9,13},{10,... | collective-permute-start | bytes 1179656 | tf_op jit(solution)/shard_map/ppermute | solution.py:181
  42.6 2.2 %collective-permute-start.2 = (bf16[128,1536]{1,0:T(8,128)(2,1)}, bf16[128,1536]{1,0:T(8,128)(2,1)}, u32[]{:S(2)}, u32[]{:S(2)}) collective-permute-start(bf16[128,1536]{1,0:T(8,128)(2,1)} %shard_map.86.t0), channel_id=1, source_target_pairs={{0,2},{1,7},{2,4},{3,1},{4,6},{5,3},{6,0},{7,5},{8,10},{9,15},{10,... | collective-permute-start | bytes 1179656 | tf_op jit(solution)/shard_map/ppermute | solution.py:180
  44.8 4.1 %collective-permute-start.4 = (bf16[1,128,1536]{2,1,0:T(8,128)(2,1)}, bf16[1,128,1536]{2,1,0:T(8,128)(2,1)}, u32[]{:S(2)}, u32[]{:S(2)}) collective-permute-start(bf16[1,128,1536]{2,1,0:T(8,128)(2,1)} %h_ref.1), channel_id=1, source_target_pairs={{0,8},{8,16},{16,24},{24,32},{32,40},{40,48},{48,56},{56,64},{64,7... | collective-permute-start | bytes 1179656 | tf_op jit(solution)/shard_map/ppermute | solution.py:187
  49.0 1.9 %collective-permute-start.3 = (bf16[192,1536]{1,0:T(8,128)(2,1)S(1)}, bf16[192,1536]{1,0:T(8,128)(2,1)S(1)}, u32[]{:S(2)}, u32[]{:S(2)}) collective-permute-start(bf16[192,1536]{1,0:T(8,128)(2,1)S(1)} %dynamic-slice_bitcast_fusion.1), channel_id=1, source_target_pairs={{0,1},{1,0},{2,3},{3,2},{4,5},{5,4},{6,7},{7,6},{8,9},{9,8},{10,11... | collective-permute-start | bytes 1769480 | tf_op jit(solution)/shard_map/ppermute | solution.py:178
  50.9 4.7 %collective-permute-done.1.t2 = bf16[128,1536]{1,0:T(8,128)(2,1)} collective-permute-done((bf16[128,1536]{1,0:T(8,128)(2,1)}, bf16[128,1536]{1,0:T(8,128)(2,1)}, u32[]{:S(2)}, u32[]{:S(2)}) %collective-permute-start.1) | collective-permute-done | bytes 393248 | tf_op jit(solution)/shard_map/ppermute | solution.py:181
  55.6 9.3 %collective-permute-done.2.t3 = bf16[128,1536]{1,0:T(8,128)(2,1)} collective-permute-done((bf16[128,1536]{1,0:T(8,128)(2,1)}, bf16[128,1536]{1,0:T(8,128)(2,1)}, u32[]{:S(2)}, u32[]{:S(2)}) %collective-permute-start.2) | collective-permute-done | bytes 393248 | tf_op jit(solution)/shard_map/ppermute | solution.py:180
  65.0 1.0 copy-done.3
  66.0 2.4 %shard_map.88 = bf16[4,128,384]{2,1,0:T(8,128)(2,1)S(1)} custom-call(bf16[128,1536]{1,0:T(8,128)(2,1)} %shard_map.86.t0, bf16[128,1536]{1,0:T(8,128)(2,1)S(1)} %copy-done.3, bf16[128,1536]{1,0:T(8,128)(2,1)} %collective-permute-done.1.t2, bf16[128,1536]{1,0:T(8,128)(2,1)} %collective-permute-done.2.t3, bf16[576,1536]{1,0:T(8,128)(2,1)S(1)} %bitcast.20, ...), custom_call_target="tpu_custom_call" | custom-call | tf_op jit(solution)/shard_map/pallas_call | solution.py:188
  68.4 1.9 %collective-permute-start.5 = (bf16[4,128,384]{2,1,0:T(8,128)(2,1)S(1)}, bf16[4,128,384]{2,1,0:T(8,128)(2,1)S(1)}, u32[]{:S(2)}, u32[]{:S(2)}) collective-permute-start(bf16[4,128,384]{2,1,0:T(8,128)(2,1)S(1)} %shard_map.88), channel_id=1, source_target_pairs={{0,2},{1,7},{2,4},{3,1},{4,6},{5,3},{6,0},{7,5},{8,10},{9,15},{10,... | collective-permute-start | bytes 1179656 | tf_op jit(solution)/shard_map/ppermute | solution.py:189
  70.3 2.6 %shard_map.89 = bf16[4,128,384]{2,1,0:T(8,128)(2,1)S(1)} custom-call(bf16[128,1536]{1,0:T(8,128)(2,1)} %shard_map.86.t0, bf16[128,1536]{1,0:T(8,128)(2,1)S(1)} %copy-done.4, bf16[128,1536]{1,0:T(8,128)(2,1)} %collective-permute-done.1.t2, bf16[128,1536]{1,0:T(8,128)(2,1)} %collective-permute-done.2.t3, bf16[384,1536]{1,0:T(8,128)(2,1)} %collective-permute-done.6.w_ref), custom_call_target="tpu_custom_call" | custom-call | tf_op jit(solution)/shard_map/pallas_call | solution.py:190
  72.9 4.6 %collective-permute-start.7 = (bf16[4,128,384]{2,1,0:T(8,128)(2,1)S(1)}, bf16[4,128,384]{2,1,0:T(8,128)(2,1)S(1)}, u32[]{:S(2)}, u32[]{:S(2)}) collective-permute-start(bf16[4,128,384]{2,1,0:T(8,128)(2,1)S(1)} %shard_map.89), channel_id=1, source_target_pairs={{0,6},{1,3},{2,0},{3,5},{4,2},{5,7},{6,4},{7,1},{8,14},{9,11},{10,... | collective-permute-start | bytes 1179656 | tf_op jit(solution)/shard_map/ppermute | solution.py:191
  77.5 2.3 %shard_map.87.a_ref = bf16[4,128,384]{2,1,0:T(8,128)(2,1)S(1)} custom-call(bf16[128,1536]{1,0:T(8,128)(2,1)} %shard_map.86.t0, bf16[128,1536]{1,0:T(8,128)(2,1)S(1)} %copy-done.4, bf16[128,1536]{1,0:T(8,128)(2,1)} %collective-permute-done.1.t2, bf16[128,1536]{1,0:T(8,128)(2,1)} %collective-permute-done.2.t3, bf16[576,1536]{1,0:T(8,128)(2,1)S(1)} %bitcast.21, ...), custom_call_target="tpu_custom_call" | custom-call | tf_op jit(solution)/shard_map/pallas_call | solution.py:192
  79.8 1.9 %collective-permute-done.5.b_ref = bf16[4,128,384]{2,1,0:T(8,128)(2,1)S(1)} collective-permute-done((bf16[4,128,384]{2,1,0:T(8,128)(2,1)S(1)}, bf16[4,128,384]{2,1,0:T(8,128)(2,1)S(1)}, u32[]{:S(2)}, u32[]{:S(2)}) %collective-permute-start.5) | collective-permute-done | bytes 393248 | tf_op jit(solution)/shard_map/ppermute | solution.py:189
  81.7 3.5 %collective-permute-done.7.c_ref = bf16[4,128,384]{2,1,0:T(8,128)(2,1)S(1)} collective-permute-done((bf16[4,128,384]{2,1,0:T(8,128)(2,1)S(1)}, bf16[4,128,384]{2,1,0:T(8,128)(2,1)S(1)}, u32[]{:S(2)}, u32[]{:S(2)}) %collective-permute-start.7) | collective-permute-done | bytes 393248 | tf_op jit(solution)/shard_map/ppermute | solution.py:191
  85.2 1.1 shard_map.90
  86.3 4.7 %all-to-all-start.1 = ((bf16[4,2,128,384]{3,2,1,0:T(8,128)(2,1)}), bf16[4,2,128,384]{3,2,1,0:T(8,128)(2,1)S(1)}, u32[]{:S(2)}, u32[]{:S(2)}) async-start(bf16[4,2,128,384]{3,2,1,0:T(8,128)(2,1)} %get-tuple-element.5.kv_ref), calls=%async_computation.1 | async-start | bytes 1572864 | tf_op jit(solution)/shard_map/all_to_all | solution.py:195
  91.0 5.5 %shard_map.92 = bf16[4,128,384]{2,1,0:T(8,128)(2,1)S(1)} custom-call(bf16[4,128,384]{2,1,0:T(8,128)(2,1)S(1)} %get-tuple-element.4.q_ref, bf16[4,2,128,384]{3,2,1,0:T(8,128)(2,1)} %get-tuple-element.5.kv_ref, bf16[8,2,128,384]{3,2,1,0:T(8,128)(2,1)S(1)} %all-to-all-done.s_ref, f32[4,1,384]{2,1,0:T(1,128)S(1)} %bitcast.22), custom_call_target="tpu_custom_call" | custom-call | tf_op jit(solution)/shard_map/pallas_call | solution.py:199
  96.6 7.9 %collective-permute-start.10 = (bf16[128,384]{1,0:T(8,128)(2,1)S(1)}, bf16[128,384]{1,0:T(8,128)(2,1)S(1)}, u32[]{:S(2)}, u32[]{:S(2)}) collective-permute-start(bf16[128,384]{1,0:T(8,128)(2,1)S(1)} %get-tuple-element.7), channel_id=1, source_target_pairs={{0,12},{1,13},{2,14},{3,15},{4,8},{5,9},{6,10},{7,11},{8,20},{9,21... | collective-permute-start | bytes 294920 | tf_op jit(solution)/shard_map/ppermute | solution.py:211
  104.6 1.9 %collective-permute-start.11 = (bf16[128,384]{1,0:T(8,128)(2,1)S(1)}, bf16[128,384]{1,0:T(8,128)(2,1)S(1)}, u32[]{:S(2)}, u32[]{:S(2)}) collective-permute-start(bf16[128,384]{1,0:T(8,128)(2,1)S(1)} %get-tuple-element.6), channel_id=1, source_target_pairs={{0,10},{1,15},{2,12},{3,9},{4,14},{5,11},{6,8},{7,13},{8,18},{9,23... | collective-permute-start | bytes 294920 | tf_op jit(solution)/shard_map/ppermute | solution.py:211
  106.5 1.9 %collective-permute-start.8 = (bf16[128,384]{1,0:T(8,128)(2,1)S(1)}, bf16[128,384]{1,0:T(8,128)(2,1)S(1)}, u32[]{:S(2)}, u32[]{:S(2)}) collective-permute-start(bf16[128,384]{1,0:T(8,128)(2,1)S(1)} %get-tuple-element.9), channel_id=1, source_target_pairs={{0,8},{1,9},{2,10},{3,11},{4,12},{5,13},{6,14},{7,15},{8,16},{9,17... | collective-permute-start | bytes 294920 | tf_op jit(solution)/shard_map/ppermute | solution.py:211
  108.4 4.0 %collective-permute-start.9 = (bf16[128,384]{1,0:T(8,128)(2,1)S(1)}, bf16[128,384]{1,0:T(8,128)(2,1)S(1)}, u32[]{:S(2)}, u32[]{:S(2)}) collective-permute-start(bf16[128,384]{1,0:T(8,128)(2,1)S(1)} %get-tuple-element.8), channel_id=1, source_target_pairs={{0,14},{1,11},{2,8},{3,13},{4,10},{5,15},{6,12},{7,9},{8,22},{9,19... | collective-permute-start | bytes 294920 | tf_op jit(solution)/shard_map/ppermute | solution.py:211
  112.4 0.9 shard_map.94
  113.4 2.0 %collective-permute-done.9.a1 = bf16[128,384]{1,0:T(8,128)(2,1)S(1)} collective-permute-done((bf16[128,384]{1,0:T(8,128)(2,1)S(1)}, bf16[128,384]{1,0:T(8,128)(2,1)S(1)}, u32[]{:S(2)}, u32[]{:S(2)}) %collective-permute-start.9) | collective-permute-done | bytes 98336 | tf_op jit(solution)/shard_map/ppermute | solution.py:211
  115.3 1.9 %shard_map.93 = bf16[1,128,1536]{2,1,0:T(8,128)(2,1)} custom-call(bf16[128,384]{1,0:T(8,128)(2,1)S(1)} %collective-permute-done.8.a0, bf16[128,384]{1,0:T(8,128)(2,1)S(1)} %collective-permute-done.9.a1, bf16[128,384]{1,0:T(8,128)(2,1)S(1)} %collective-permute-done.10.a2, bf16[128,384]{1,0:T(8,128)(2,1)S(1)} %collective-permute-done.11.a3, ...), custom_call_target="tpu_custom_call" | custom-call | tf_op jit(solution)/shard_map/pallas_call | solution.py:212
  (28 shorter events, 3.0 us)
Async XLA Ops:
  0.6 0.7 copy-start.6
  1.3 0.7 copy-start.7
  2.0 0.7 copy-start.9
  4.7 10.6 %collective-permute-start = (bf16[128,1536]{1,0:T(8,128)(2,1)}, bf16[128,1536]{1,0:T(8,128)(2,1)S(1)}, u32[]{:S(2)}, u32[]{:S(2)}) collective-permute-start(bf16[128,1536]{1,0:T(8,128)(2,1)} %shard_map.86.t0), channel_id=1, source_target_pairs={{0,6},{1,3},{2,0},{3,5},{4,2},{5,7},{6,4},{7,1},{8,14},{9,11},{10,... | collective-permute-start | bytes 1179656 | tf_op jit(solution)/shard_map/ppermute | solution.py:179
  15.3 1.1 copy-start.5
  16.6 1.2 %copy-start.1 = (bf16[8,2,128,384]{3,2,1,0:T(8,128)(2,1)}, bf16[8,2,128,384]{3,2,1,0:T(8,128)(2,1)S(1)}, u32[]{:S(2)}) copy-start(bf16[8,2,128,384]{3,2,1,0:T(8,128)(2,1)S(1)} %shard_map.91) | copy-start | bytes 4718596
  17.8 0.7 copy-start.2
  18.5 8.3 %copy-start = (bf16[1,1536,576]{1,2,0:T(8,128)(2,1)S(1)}, bf16[1,1536,576]{1,2,0:T(8,128)(2,1)}, u32[]{:S(2)}) copy-start(bf16[1,1536,576]{1,2,0:T(8,128)(2,1)} %param.8) | copy-start | bytes 5308420
  18.5 67.8 %all-to-all-start = ((bf16[8,2,128,384]{3,2,1,0:T(8,128)(2,1)}), bf16[8,2,128,384]{3,2,1,0:T(8,128)(2,1)S(1)}, u32[]{:S(2)}, u32[]{:S(2)}) async-start(bf16[8,2,128,384]{3,2,1,0:T(8,128)(2,1)} %copy-done.1), calls=%async_computation | async-start | bytes 3145728 | tf_op jit(solution)/shard_map/all_to_all | solution.py:185
  27.9 42.4 %collective-permute-start.6 = (bf16[384,1536]{1,0:T(8,128)(2,1)}, bf16[384,1536]{1,0:T(8,128)(2,1)}, u32[]{:S(2)}, u32[]{:S(2)}) collective-permute-start(bf16[384,1536]{1,0:T(8,128)(2,1)} %dynamic-slice_bitcast_fusion), channel_id=1, source_target_pairs={{0,385},{1,128},{2,387},{3,130},{4,389},{5,132},{6,391},{7,134},{1... | collective-permute-start | bytes 3538952 | tf_op jit(solution)/shard_map/ppermute | solution.py:177
  38.0 17.6 %collective-permute-start.1 = (bf16[128,1536]{1,0:T(8,128)(2,1)}, bf16[128,1536]{1,0:T(8,128)(2,1)}, u32[]{:S(2)}, u32[]{:S(2)}) collective-permute-start(bf16[128,1536]{1,0:T(8,128)(2,1)} %shard_map.86.t0), channel_id=1, source_target_pairs={{0,4},{1,5},{2,6},{3,7},{4,0},{5,1},{6,2},{7,3},{8,12},{9,13},{10,... | collective-permute-start | bytes 1179656 | tf_op jit(solution)/shard_map/ppermute | solution.py:181
  42.6 22.4 %collective-permute-start.2 = (bf16[128,1536]{1,0:T(8,128)(2,1)}, bf16[128,1536]{1,0:T(8,128)(2,1)}, u32[]{:S(2)}, u32[]{:S(2)}) collective-permute-start(bf16[128,1536]{1,0:T(8,128)(2,1)} %shard_map.86.t0), channel_id=1, source_target_pairs={{0,2},{1,7},{2,4},{3,1},{4,6},{5,3},{6,0},{7,5},{8,10},{9,15},{10,... | collective-permute-start | bytes 1179656 | tf_op jit(solution)/shard_map/ppermute | solution.py:180
  44.8 20.2 %collective-permute-start.4 = (bf16[1,128,1536]{2,1,0:T(8,128)(2,1)}, bf16[1,128,1536]{2,1,0:T(8,128)(2,1)}, u32[]{:S(2)}, u32[]{:S(2)}) collective-permute-start(bf16[1,128,1536]{2,1,0:T(8,128)(2,1)} %h_ref.1), channel_id=1, source_target_pairs={{0,8},{8,16},{16,24},{24,32},{32,40},{40,48},{48,56},{56,64},{64,7... | collective-permute-start | bytes 1179656 | tf_op jit(solution)/shard_map/ppermute | solution.py:187
  49.0 28.6 %collective-permute-start.3 = (bf16[192,1536]{1,0:T(8,128)(2,1)S(1)}, bf16[192,1536]{1,0:T(8,128)(2,1)S(1)}, u32[]{:S(2)}, u32[]{:S(2)}) collective-permute-start(bf16[192,1536]{1,0:T(8,128)(2,1)S(1)} %dynamic-slice_bitcast_fusion.1), channel_id=1, source_target_pairs={{0,1},{1,0},{2,3},{3,2},{4,5},{5,4},{6,7},{7,6},{8,9},{9,8},{10,11... | collective-permute-start | bytes 1769480 | tf_op jit(solution)/shard_map/ppermute | solution.py:178
  65.0 1.0 copy-start.3
  65.9 4.3 %copy-start.4 = (bf16[128,1536]{1,0:T(8,128)(2,1)S(1)}, bf16[128,1536]{1,0:T(8,128)(2,1)}, u32[]{:S(2)}) copy-start(bf16[128,1536]{1,0:T(8,128)(2,1)} %copy-done.2) | copy-start | bytes 1179652
  68.4 13.3 %collective-permute-start.5 = (bf16[4,128,384]{2,1,0:T(8,128)(2,1)S(1)}, bf16[4,128,384]{2,1,0:T(8,128)(2,1)S(1)}, u32[]{:S(2)}, u32[]{:S(2)}) collective-permute-start(bf16[4,128,384]{2,1,0:T(8,128)(2,1)S(1)} %shard_map.88), channel_id=1, source_target_pairs={{0,2},{1,7},{2,4},{3,1},{4,6},{5,3},{6,0},{7,5},{8,10},{9,15},{10,... | collective-permute-start | bytes 1179656 | tf_op jit(solution)/shard_map/ppermute | solution.py:189
  72.9 12.3 %collective-permute-start.7 = (bf16[4,128,384]{2,1,0:T(8,128)(2,1)S(1)}, bf16[4,128,384]{2,1,0:T(8,128)(2,1)S(1)}, u32[]{:S(2)}, u32[]{:S(2)}) collective-permute-start(bf16[4,128,384]{2,1,0:T(8,128)(2,1)S(1)} %shard_map.89), channel_id=1, source_target_pairs={{0,6},{1,3},{2,0},{3,5},{4,2},{5,7},{6,4},{7,1},{8,14},{9,11},{10,... | collective-permute-start | bytes 1179656 | tf_op jit(solution)/shard_map/ppermute | solution.py:191
  79.8 11.2 %copy-start.8 = (f32[1,1536]{1,0:T(1,128)S(1)}, f32[1,1536]{1,0:T(1,128)}, u32[]{:S(2)}) copy-start(f32[1,1536]{1,0:T(1,128)} %param.11) | copy-start | bytes 18436
  86.3 26.1 %all-to-all-start.1 = ((bf16[4,2,128,384]{3,2,1,0:T(8,128)(2,1)}), bf16[4,2,128,384]{3,2,1,0:T(8,128)(2,1)S(1)}, u32[]{:S(2)}, u32[]{:S(2)}) async-start(bf16[4,2,128,384]{3,2,1,0:T(8,128)(2,1)} %get-tuple-element.5.kv_ref), calls=%async_computation.1 | async-start | bytes 1572864 | tf_op jit(solution)/shard_map/all_to_all | solution.py:195
  96.6 16.7 %collective-permute-start.10 = (bf16[128,384]{1,0:T(8,128)(2,1)S(1)}, bf16[128,384]{1,0:T(8,128)(2,1)S(1)}, u32[]{:S(2)}, u32[]{:S(2)}) collective-permute-start(bf16[128,384]{1,0:T(8,128)(2,1)S(1)} %get-tuple-element.7), channel_id=1, source_target_pairs={{0,12},{1,13},{2,14},{3,15},{4,8},{5,9},{6,10},{7,11},{8,20},{9,21... | collective-permute-start | bytes 294920 | tf_op jit(solution)/shard_map/ppermute | solution.py:211
  104.6 8.8 %collective-permute-start.11 = (bf16[128,384]{1,0:T(8,128)(2,1)S(1)}, bf16[128,384]{1,0:T(8,128)(2,1)S(1)}, u32[]{:S(2)}, u32[]{:S(2)}) collective-permute-start(bf16[128,384]{1,0:T(8,128)(2,1)S(1)} %get-tuple-element.6), channel_id=1, source_target_pairs={{0,10},{1,15},{2,12},{3,9},{4,14},{5,11},{6,8},{7,13},{8,18},{9,23... | collective-permute-start | bytes 294920 | tf_op jit(solution)/shard_map/ppermute | solution.py:211
  106.5 6.9 %collective-permute-start.8 = (bf16[128,384]{1,0:T(8,128)(2,1)S(1)}, bf16[128,384]{1,0:T(8,128)(2,1)S(1)}, u32[]{:S(2)}, u32[]{:S(2)}) collective-permute-start(bf16[128,384]{1,0:T(8,128)(2,1)S(1)} %get-tuple-element.9), channel_id=1, source_target_pairs={{0,8},{1,9},{2,10},{3,11},{4,12},{5,13},{6,14},{7,15},{8,16},{9,17... | collective-permute-start | bytes 294920 | tf_op jit(solution)/shard_map/ppermute | solution.py:211
  108.4 7.0 %collective-permute-start.9 = (bf16[128,384]{1,0:T(8,128)(2,1)S(1)}, bf16[128,384]{1,0:T(8,128)(2,1)S(1)}, u32[]{:S(2)}, u32[]{:S(2)}) collective-permute-start(bf16[128,384]{1,0:T(8,128)(2,1)S(1)} %get-tuple-element.8), channel_id=1, source_target_pairs={{0,14},{1,11},{2,8},{3,13},{4,10},{5,15},{6,12},{7,9},{8,22},{9,19... | collective-permute-start | bytes 294920 | tf_op jit(solution)/shard_map/ppermute | solution.py:211

commit v3 on v2

v3 whole, which is shorter than its diff:
```python
import jax
import jax.numpy as jnp
from jax import lax
from jax.experimental import pallas as pl
from jax.experimental.pallas import tpu as pltpu
from jax.sharding import PartitionSpec as P

HEAD_DIM = 128
ROWS = 128
D = 1536
UNIT = 384
HALF = 192
SCALE = HEAD_DIM ** (-0.5)
BF = jnp.bfloat16
F32 = jnp.float32
NT = (((1,), (1,)), ((), ()))
VM = pl.BlockSpec(memory_space=pltpu.VMEM)
PARAMS = pltpu.CompilerParams(vmem_limit_bytes=16 * 1024 * 1024)


def spot(x, z):
    return 2 * (x % 4) + z


def ahead(z):
    return 1 - 2 * z


def x_pairs(steps):
    return [(spot(x, z), spot(x + ahead(z) * steps, z)) for x in range(4) for z in range(2)]


def partner_pairs():
    return [(spot(x, z), spot(x, 1 - z)) for x in range(4) for z in range(2)]


def far_pairs(parts):
    pairs = []
    for dp in range(parts):
        for x in range(4):
            for z in range(2):
                there = (2 * dp + z - ahead(z)) % (2 * parts)
                pairs.append((dp * 8 + spot(x, z), (there // 2) * 8 + spot(x, there % 2)))
    return pairs


def where_am_i():
    p = lax.axis_index("patch")
    return p // 2, p % 2


def call(body, out, count, **more):
    return pl.pallas_call(
        body,
        out_shape=out,
        in_specs=[VM] * count,
        out_specs=jax.tree.map(lambda _: VM, out),
        compiler_params=PARAMS,
        **more,
    )


def norm_body(h_ref, g_ref, b_ref, m_ref, s_ref, w_ref, own, b1, b2, b3, lead, rest):
    x, z = where_am_i()
    h = h_ref[0].astype(F32)
    inverse = lax.rsqrt(jnp.mean(h * h, axis=-1, keepdims=True) + 1e-06)
    mask = jnp.broadcast_to(m_ref[...].astype(F32), (ROWS, ROWS)).T[:, :1]
    normed = (h * inverse * g_ref[...] + mask * b_ref[...]).astype(BF)
    for j, bundle in enumerate((own, b1, b2, b3)):
        for g in range(4):
            bundle[g] = normed[:, UNIT * g : UNIT * (g + 1)]
        group = ((x + (1 - 2 * z) * j + 4) % 4) ^ 1
        cols = pl.ds(pl.multiple_of(UNIT * group, UNIT), UNIT)
        bundle[4] = s_ref[0, 0, :, cols]
        bundle[5] = s_ref[0, 1, :, cols]
    lead[...] = w_ref[pl.ds(pl.multiple_of(HALF * z, HALF), UNIT), :]
    rest[...] = w_ref[pl.ds(pl.multiple_of(UNIT * (1 - z), HALF), HALF), :]


def near_body(t0, t1, t3, o_ref):
    for i, ref in enumerate((t0, t1, t3)):
        o_ref[i] = ref[4:6]


def far_body(t2, o_ref):
    o_ref[...] = t2[4:6]


def project_body(t0, t1, t2, t3, w_ref, v_ref, u_ref, early, front_o, back_o, opp_o, keep_o, both):
    del early
    _, z = where_am_i()
    mine = w_ref[pl.ds(pl.multiple_of(UNIT * (1 - z), HALF), HALF), :]
    both[pl.ds(pl.multiple_of(HALF * z, HALF), HALF), :] = mine
    both[pl.ds(pl.multiple_of(HALF * (1 - z), HALF), HALF), :] = u_ref[...]
    tokens = jnp.concatenate(
        [jnp.concatenate([b[g] for g in range(4)], axis=1) for b in (t0, t1, t2, t3)], axis=0
    )

    def product(weight):
        got = lax.dot_general(tokens, weight, NT, preferred_element_type=F32).astype(BF)
        return [got[ROWS * j : ROWS * (j + 1)] for j in range(4)]

    front = product(w_ref[pl.ds(pl.multiple_of(HALF * z, HALF), UNIT), :])
    mid = product(both[...])
    back = product(v_ref[...])
    for j in range(4):
        front_o[j] = front[j]
        back_o[j] = back[j]
        keep_o[j] = mid[j]
    front_o[4] = mid[1]
    front_o[5] = back[1]
    back_o[4] = mid[3]
    back_o[5] = front[3]
    opp_o[0] = front[2]
    opp_o[1] = mid[2]
    opp_o[2] = back[2]
    keep_o[4] = front[0]
    keep_o[5] = back[0]


def roles(x, z):
    left = 1 + z
    right = 2 - z
    q = jnp.where(x == 0, 0, jnp.where(x == 3, right, left))
    k = jnp.where(x == 0, right, jnp.where(x == 3, left, 0))
    v = jnp.where(x == 0, left, jnp.where(x == 3, 0, right))
    return q, k, v


def attend_body(m_ref, a_ref, b_ref, t0, t1, t2, t3, pn_ref, pf_ref, g_ref, *o_refs):
    x, z = where_am_i()
    gates = g_ref[pl.ds(x ^ 1, 1), :]
    roled = roles(x, z)
    for head in range(3):
        cols = slice(HEAD_DIM * head, HEAD_DIM * (head + 1))

        def part(index, j):
            own = m_ref[j, :, cols]
            behind = a_ref[(j + 1) % 4, :, cols]
            ahead = b_ref[(j + 3) % 4, :, cols]
            return jnp.where(index == 0, own, jnp.where(index == 1, behind, ahead))

        kept = [
            [t[4 + kv, :, cols] for t in (t0, t1, t2, t3)]
            + [pn_ref[i, kv, :, cols] for i in range(3)]
            + [pf_ref[kv, :, cols]]
            for kv in range(2)
        ]
        for j in range(4):
            q, k, v = (part(index, j) for index in roled)
            keys = list(kept[0])
            values = list(kept[1])
            keys[j] = k
            values[j] = v
            scores = lax.dot_general(
                q, jnp.concatenate(keys, axis=0), NT, preferred_element_type=F32
            ) * SCALE
            top = jnp.max(scores, axis=-1, keepdims=True)
            weights = jnp.exp(scores - top)
            total = jnp.sum(weights, axis=-1, keepdims=True)
            summed = jnp.dot(
                weights.astype(BF), jnp.concatenate(values, axis=0), preferred_element_type=F32
            )
            o_refs[j][:, cols] = (gates[:, cols] * (summed / total)).astype(BF)


def fresh_body(k_ref, a_ref, b_ref, p_ref, f_ref):
    x, z = where_am_i()
    rows = (
        (0, (k_ref.at[4], k_ref.at[0], k_ref.at[5])),
        (1, (b_ref.at[5], b_ref.at[4], b_ref.at[3])),
        (2, (p_ref.at[0], p_ref.at[1], p_ref.at[2])),
        (3, (a_ref.at[1], a_ref.at[4], a_ref.at[5])),
    )
    for j, refs in rows:
        source = (x + (1 - 2 * z) * j + 4) % 4
        for unit, ref in zip((2 * z, 1, 2 - 2 * z), refs):
            g = 3 * source + unit

            @pl.when(g >= 4)
            def _():
                cols = pl.ds(pl.multiple_of(UNIT * (g % 4), UNIT), UNIT)
                f_ref[0, g // 4 - 1, :, cols] = ref[...]


def finish_body(a0, a1, a2, a3, h_ref, o_ref):
    x, z = where_am_i()
    for j, ref in enumerate((a0, a1, a2, a3)):
        group = ((x + (1 - 2 * z) * j + 4) % 4) ^ 1
        cols = pl.ds(pl.multiple_of(UNIT * group, UNIT), UNIT)
        o_ref[0, :, cols] = (h_ref[0, :, cols].astype(F32) + ref[...].astype(F32)).astype(BF)


def local(hidden, w_qkv, norm_gain, box_vec, gate, box_mask, stale_kv):
    parts = lax.axis_size("dp")
    segments = lax.axis_size("segment")

    def blocks(*lead):
        return jax.ShapeDtypeStruct((*lead, ROWS, UNIT), BF)

    def rows(count):
        return jax.ShapeDtypeStruct((count, D), BF)

    weight = jnp.swapaxes(w_qkv[0], 0, 1)
    t0, b1, b2, b3, lead, rest = call(
        norm_body, (blocks(6), blocks(6), blocks(6), blocks(6), rows(UNIT), rows(HALF)), 6
    )(hidden, norm_gain, box_vec, box_mask, stale_kv, weight)
    lead = lax.ppermute(lead, ("dp", "patch"), far_pairs(parts))
    t3 = lax.ppermute(b1, "patch", x_pairs(1))
    t1 = lax.ppermute(b3, "patch", x_pairs(3))
    t2 = lax.ppermute(b2, "patch", x_pairs(2))
    rest = lax.ppermute(rest, "patch", partner_pairs())
    before = lax.ppermute(hidden, "segment", [(i, (i + 1) % segments) for i in range(segments)])

    near = call(near_body, blocks(3, 2), 3)(t0, t1, t3)
    near = lax.ppermute(near, "patch", partner_pairs())
    far = call(far_body, blocks(2), 1)(t2)
    far = lax.ppermute(far, "patch", partner_pairs())

    front, back, opposite, keep = call(
        project_body,
        (blocks(6), blocks(6), blocks(3), blocks(6)),
        8,
        scratch_shapes=[pltpu.VMEM((UNIT, D), BF)],
    )(t0, t1, t2, t3, weight, lead, rest, before)
    front = lax.ppermute(front, "patch", x_pairs(1))
    back = lax.ppermute(back, "patch", x_pairs(3))
    opposite = lax.ppermute(opposite, "patch", x_pairs(2))

    out = call(attend_body, (blocks(),) * 4, 10)(
        keep, front, back, t0, t1, t2, t3, near, far, gate.reshape(4, UNIT)
    )
    fresh = call(fresh_body, jax.ShapeDtypeStruct((1, 2, ROWS, D), BF), 4)(
        keep, front, back, opposite
    )

    came = []
    for j in range(4):
        pairs = [
            (s * 8 + src, (s + 1) % segments * 8 + dst)
            for s in range(segments)
            for src, dst in x_pairs(j)
        ]
        came.append(lax.ppermute(out[j], ("segment", "patch"), pairs))
    passed = call(finish_body, jax.ShapeDtypeStruct((1, ROWS, D), BF), 5)(
        came[0], came[3], came[2], came[1], before
    )
    return (passed, fresh)


def solution(mesh):
    placed = (
        P(("dp", "segment"), "patch", None),
        P("segment", None, "patch"),
        P("segment", None),
        P("segment", None),
        P(("dp", "segment"), None),
        P(("dp", "segment"), "patch"),
        P(("dp", "segment"), None, "patch", None),
    )
    return jax.shard_map(
        local,
        mesh=mesh,
        in_specs=placed,
        out_specs=(P(("dp", "segment"), "patch", None), P(("dp", "segment"), None, "patch", None)),
        check_vma=False,
    )
```

time: 119 us -> 110 us (0.924); the launches traced: 117 us -> 110 us
  waiting for transfers between devices: 26.9 us -> 15.6 us
  starting transfers between devices: 63.3 us -> 72.9 us
  Pallas kernels: 18.9 us -> 14.6 us
  local copies, waits for them, and re-layouts: 7.3 us -> 5.67 us
    all_to_all x2 -> x0, starting transfers between devices: 12.9 us -> none  [the longest x1 8.25 us: local(): kept = lax.all_to_all(spread, 'patch', 0, 0)]
    ppermute x7 -> x10, waiting for transfers between devices: 21.4 us -> 9.45 us  [the longest x1 4.96 us: local(): t1 = lax.ppermute(b3, 'patch', x_pairs(3))]
    ppermute x1, starting transfers between devices: 4.14 us -> 14.9 us  [local(): lax.ppermute(hidden, 'segment', [(i, (i + 1) % segments) for i in range(s...]
    ppermute x7 -> x10, starting transfers between devices: 27.8 us -> 37.4 us  [the longest x4 20.4 us: local(): came.append(lax.ppermute(out[j], ('segment', 'patch'), pairs))]
    pallas_call x9 -> x7, Pallas kernels: 18.9 us -> 14.6 us  [the longest x1 5.73 us: local(): call(attend_body, (blocks(),) * 4, 10)]
    ppermute x1, waiting for transfers between devices: 0.01 us -> 1.78 us  [local(): lax.ppermute(hidden, 'segment', [(i, (i + 1) % segments) for i in range(s...]
    ppermute x1, starting transfers between devices: 10.1 us -> 11.5 us  [local(): lead = lax.ppermute(lead, ('dp', 'patch'), far_pairs(parts))]
    unnamed x20 -> x22, local copies, waits for them, and re-layouts: 6.09 us -> 5.66 us
  transfers between devices with their start and end apart: 14 -> 15, of which waited for: 6 -> 6; matrix products, arithmetic and copies ran while one was open for 1% -> 0% of each run, Pallas kernels for 13% -> 12%
where the time goes in v3:
time: 110 us
  starting transfers between devices  72.9 us (66%)
  waiting for transfers between devices  15.6 us (14%)
  Pallas kernels  14.6 us (13%)
  local copies, waits for them, and re-layouts  5.67 us (5%)
    ppermute x4, starting transfers between devices, local(): came.append(lax.ppermute(out[j], ('segment', 'patch'), pairs))  20.4 us
    ppermute x1, starting transfers between devices, local(): lax.ppermute(hidden, 'segment', [(i, (i + 1) % segments) for i in range(s...  14.9 us
    ppermute x1, starting transfers between devices, local(): lead = lax.ppermute(lead, ('dp', 'patch'), far_pairs(parts))  11.5 us
    pallas_call x1, Pallas kernels, local(): call(attend_body, (blocks(),) * 4, 10)  5.73 us
    unnamed x22, local copies, waits for them, and re-layouts  5.66 us
    ppermute x1, starting transfers between devices, local(): back = lax.ppermute(back, 'patch', x_pairs(3))  5.29 us
    ppermute x1, waiting for transfers between devices, local(): t1 = lax.ppermute(b3, 'patch', x_pairs(3))  4.96 us
    ppermute x1, starting transfers between devices, local(): t1 = lax.ppermute(b3, 'patch', x_pairs(3))  4.39 us
  transfers between devices with their start and end apart: 15, of which 6 were waited for; matrix products, arithmetic and copies ran while one was open for 0% of the time, Pallas kernels for 12%

profile of v3, /device:TPU:1, one launch (start us, length us, event | category | flops | bytes accessed | tf_op | source)
XLA Modules:
  0.0 109.6 jit_solution(12840117254715816382)
XLA Ops:
  0.6 1.5 %copy-done = bf16[1,1536,576]{1,2,0:T(8,128)(2,1)S(1)} copy-done((bf16[1,1536,576]{1,2,0:T(8,128)(2,1)S(1)}, bf16[1,1536,576]{1,2,0:T(8,128)(2,1)}, u32[]{:S(2)}) %copy-start) | copy-done | bytes 1769496
  2.1 1.1 %copy-done.4 = bf16[1,2,128,1536]{3,2,1,0:T(8,128)(2,1)S(1)} copy-done((bf16[1,2,128,1536]{3,2,1,0:T(8,128)(2,1)S(1)}, bf16[1,2,128,1536]{3,2,1,0:T(8,128)(2,1)}, u32[]{:S(2)}) %copy-start.4) | copy-done | bytes 786456
  3.2 1.0 copy-done.5
  4.2 0.7 copy-done.7
  4.9 0.7 copy-done.8
  6.9 11.5 %collective-permute-start.3 = (bf16[384,1536]{1,0:T(8,128)(2,1)S(1)}, bf16[384,1536]{1,0:T(8,128)(2,1)S(1)}, u32[]{:S(2)}, u32[]{:S(2)}) collective-permute-start(bf16[384,1536]{1,0:T(8,128)(2,1)S(1)} %get-tuple-element.20), channel_id=1, source_target_pairs={{0,385},{1,128},{2,387},{3,130},{4,389},{5,132},{6,391},{7,134},{1... | collective-permute-start | bytes 3538952 | tf_op jit(solution)/shard_map/ppermute | solution.py:208
  18.4 4.4 %collective-permute-start = (bf16[6,128,384]{2,1,0:T(8,128)(2,1)S(1)}, bf16[6,128,384]{2,1,0:T(8,128)(2,1)S(1)}, u32[]{:S(2)}, u32[]{:S(2)}) collective-permute-start(bf16[6,128,384]{2,1,0:T(8,128)(2,1)S(1)} %get-tuple-element.17), channel_id=1, source_target_pairs={{0,6},{1,3},{2,0},{3,5},{4,2},{5,7},{6,4},{7,1},{8,14},{9,11},{10,... | collective-permute-start | bytes 1769480 | tf_op jit(solution)/shard_map/ppermute | solution.py:210
  22.8 1.9 %collective-permute-start.2 = (bf16[6,128,384]{2,1,0:T(8,128)(2,1)S(1)}, bf16[6,128,384]{2,1,0:T(8,128)(2,1)S(1)}, u32[]{:S(2)}, u32[]{:S(2)}) collective-permute-start(bf16[6,128,384]{2,1,0:T(8,128)(2,1)S(1)} %get-tuple-element.19), channel_id=1, source_target_pairs={{0,2},{1,7},{2,4},{3,1},{4,6},{5,3},{6,0},{7,5},{8,10},{9,15},{10,... | collective-permute-start | bytes 1769480 | tf_op jit(solution)/shard_map/ppermute | solution.py:209
  24.7 3.6 %collective-permute-start.1 = (bf16[6,128,384]{2,1,0:T(8,128)(2,1)S(1)}, bf16[6,128,384]{2,1,0:T(8,128)(2,1)S(1)}, u32[]{:S(2)}, u32[]{:S(2)}) collective-permute-start(bf16[6,128,384]{2,1,0:T(8,128)(2,1)S(1)} %get-tuple-element.18), channel_id=1, source_target_pairs={{0,4},{1,5},{2,6},{3,7},{4,0},{5,1},{6,2},{7,3},{8,12},{9,13},{10,... | collective-permute-start | bytes 1769480 | tf_op jit(solution)/shard_map/ppermute | solution.py:211
  28.3 1.9 %collective-permute-start.4 = (bf16[192,1536]{1,0:T(8,128)(2,1)S(1)}, bf16[192,1536]{1,0:T(8,128)(2,1)S(1)}, u32[]{:S(2)}, u32[]{:S(2)}) collective-permute-start(bf16[192,1536]{1,0:T(8,128)(2,1)S(1)} %get-tuple-element.21), channel_id=1, source_target_pairs={{0,1},{1,0},{2,3},{3,2},{4,5},{5,4},{6,7},{7,6},{8,9},{9,8},{10,11... | collective-permute-start | bytes 1769480 | tf_op jit(solution)/shard_map/ppermute | solution.py:212
  30.2 5.0 %collective-permute-done.t1 = bf16[6,128,384]{2,1,0:T(8,128)(2,1)S(1)} collective-permute-done((bf16[6,128,384]{2,1,0:T(8,128)(2,1)S(1)}, bf16[6,128,384]{2,1,0:T(8,128)(2,1)S(1)}, u32[]{:S(2)}, u32[]{:S(2)}) %collective-permute-start) | collective-permute-done | bytes 589856 | tf_op jit(solution)/shard_map/ppermute | solution.py:210
  35.2 14.9 %collective-permute-start.5 = (bf16[1,128,1536]{2,1,0:T(8,128)(2,1)S(1)}, bf16[1,128,1536]{2,1,0:T(8,128)(2,1)S(1)}, u32[]{:S(2)}, u32[]{:S(2)}) collective-permute-start(bf16[1,128,1536]{2,1,0:T(8,128)(2,1)S(1)} %copy-done.6), channel_id=1, source_target_pairs={{0,8},{8,16},{16,24},{24,32},{32,40},{40,48},{48,56},{56,64},{64,7... | collective-permute-start | bytes 1179656 | tf_op jit(solution)/shard_map/ppermute | solution.py:213
  50.1 0.9 shard_map.88
  51.0 2.0 %collective-permute-start.8 = (bf16[3,2,128,384]{3,2,1,0:T(8,128)(2,1)}, bf16[3,2,128,384]{3,2,1,0:T(8,128)(2,1)}, u32[]{:S(2)}, u32[]{:S(2)}) collective-permute-start(bf16[3,2,128,384]{3,2,1,0:T(8,128)(2,1)} %shard_map.88), channel_id=1, source_target_pairs={{0,1},{1,0},{2,3},{3,2},{4,5},{5,4},{6,7},{7,6},{8,9},{9,8},{10,11... | collective-permute-start | bytes 1769480 | tf_op jit(solution)/shard_map/ppermute | solution.py:216
  53.1 1.8 %collective-permute-done.5.early.h_ref = bf16[1,128,1536]{2,1,0:T(8,128)(2,1)S(1)} collective-permute-done((bf16[1,128,1536]{2,1,0:T(8,128)(2,1)S(1)}, bf16[1,128,1536]{2,1,0:T(8,128)(2,1)S(1)}, u32[]{:S(2)}, u32[]{:S(2)}) %collective-permute-start.5) | collective-permute-done | bytes 393248 | tf_op jit(solution)/shard_map/ppermute | solution.py:213
  54.9 3.7 %shard_map.87 = (bf16[6,128,384]{2,1,0:T(8,128)(2,1)}, bf16[6,128,384]{2,1,0:T(8,128)(2,1)}, bf16[3,128,384]{2,1,0:T(8,128)(2,1)}, bf16[6,128,384]{2,1,0:T(8,128)(2,1)S(1)}) custom-call(bf16[6,128,384]{2,1,0:T(8,128)(2,1)S(1)} %get-tuple-element.16.t0, bf16[6,128,384]{2,1,0:T(8,128)(2,1)S(1)} %collective-permute-done.t1, ...), custom_call_target="tpu_custom_call" | custom-call | tf_op jit(solution)/shard_map/pallas_call | solution.py:220
  58.6 1.9 %collective-permute-start.6 = (bf16[6,128,384]{2,1,0:T(8,128)(2,1)}, bf16[6,128,384]{2,1,0:T(8,128)(2,1)S(1)}, u32[]{:S(2)}, u32[]{:S(2)}) collective-permute-start(bf16[6,128,384]{2,1,0:T(8,128)(2,1)} %get-tuple-element.23), channel_id=1, source_target_pairs={{0,2},{1,7},{2,4},{3,1},{4,6},{5,3},{6,0},{7,5},{8,10},{9,15},{10,... | collective-permute-start | bytes 1769480 | tf_op jit(solution)/shard_map/ppermute | solution.py:226
  60.5 5.3 %collective-permute-start.7 = (bf16[6,128,384]{2,1,0:T(8,128)(2,1)}, bf16[6,128,384]{2,1,0:T(8,128)(2,1)}, u32[]{:S(2)}, u32[]{:S(2)}) collective-permute-start(bf16[6,128,384]{2,1,0:T(8,128)(2,1)} %get-tuple-element.24), channel_id=1, source_target_pairs={{0,6},{1,3},{2,0},{3,5},{4,2},{5,7},{6,4},{7,1},{8,14},{9,11},{10,... | collective-permute-start | bytes 1769480 | tf_op jit(solution)/shard_map/ppermute | solution.py:227
  65.8 0.7 shard_map.89
  66.4 1.9 %collective-permute-start.9 = (bf16[2,128,384]{2,1,0:T(8,128)(2,1)}, bf16[2,128,384]{2,1,0:T(8,128)(2,1)}, u32[]{:S(2)}, u32[]{:S(2)}) collective-permute-start(bf16[2,128,384]{2,1,0:T(8,128)(2,1)} %shard_map.89), channel_id=1, source_target_pairs={{0,1},{1,0},{2,3},{3,2},{4,5},{5,4},{6,7},{7,6},{8,9},{9,8},{10,11... | collective-permute-start | bytes 589832 | tf_op jit(solution)/shard_map/ppermute | solution.py:218
  68.4 3.1 %collective-permute-start.14 = (bf16[3,128,384]{2,1,0:T(8,128)(2,1)}, bf16[3,128,384]{2,1,0:T(8,128)(2,1)}, u32[]{:S(2)}, u32[]{:S(2)}) collective-permute-start(bf16[3,128,384]{2,1,0:T(8,128)(2,1)} %get-tuple-element.29), channel_id=1, source_target_pairs={{0,4},{1,5},{2,6},{3,7},{4,0},{5,1},{6,2},{7,3},{8,12},{9,13},{10,... | collective-permute-start | bytes 884744 | tf_op jit(solution)/shard_map/ppermute | solution.py:228
  71.5 1.9 %collective-permute-done.9.pf_ref = bf16[2,128,384]{2,1,0:T(8,128)(2,1)} collective-permute-done((bf16[2,128,384]{2,1,0:T(8,128)(2,1)}, bf16[2,128,384]{2,1,0:T(8,128)(2,1)}, u32[]{:S(2)}, u32[]{:S(2)}) %collective-permute-start.9) | collective-permute-done | bytes 196640 | tf_op jit(solution)/shard_map/ppermute | solution.py:218
  73.5 1.7 %collective-permute-done.6.a_ref = bf16[6,128,384]{2,1,0:T(8,128)(2,1)S(1)} collective-permute-done((bf16[6,128,384]{2,1,0:T(8,128)(2,1)}, bf16[6,128,384]{2,1,0:T(8,128)(2,1)S(1)}, u32[]{:S(2)}, u32[]{:S(2)}) %collective-permute-start.6) | collective-permute-done | bytes 589856 | tf_op jit(solution)/shard_map/ppermute | solution.py:226
  75.2 2.7 %collective-permute-done.7.b_ref = bf16[6,128,384]{2,1,0:T(8,128)(2,1)} collective-permute-done((bf16[6,128,384]{2,1,0:T(8,128)(2,1)}, bf16[6,128,384]{2,1,0:T(8,128)(2,1)}, u32[]{:S(2)}, u32[]{:S(2)}) %collective-permute-start.7) | collective-permute-done | bytes 589856 | tf_op jit(solution)/shard_map/ppermute | solution.py:227
  77.8 5.7 %shard_map.90 = (bf16[128,384]{1,0:T(8,128)(2,1)S(1)}, bf16[128,384]{1,0:T(8,128)(2,1)S(1)}, bf16[128,384]{1,0:T(8,128)(2,1)S(1)}, bf16[128,384]{1,0:T(8,128)(2,1)S(1)}) custom-call(bf16[6,128,384]{2,1,0:T(8,128)(2,1)S(1)} %get-tuple-element.22.m_ref.k_ref, bf16[6,128,384]{2,1,0:T(8,128)(2,1)S(1)} %collective-permute-done.6.a_ref, ...), custom_call_target="tpu_custom_call" | custom-call | tf_op jit(solution)/shard_map/pallas_call | solution.py:230
  83.6 9.3 %collective-permute-start.10 = (bf16[128,384]{1,0:T(8,128)(2,1)S(1)}, bf16[128,384]{1,0:T(8,128)(2,1)S(1)}, u32[]{:S(2)}, u32[]{:S(2)}) collective-permute-start(bf16[128,384]{1,0:T(8,128)(2,1)S(1)} %get-tuple-element.25), channel_id=1, source_target_pairs={{0,8},{1,9},{2,10},{3,11},{4,12},{5,13},{6,14},{7,15},{8,16},{9,17... | collective-permute-start | bytes 294920 | tf_op jit(solution)/shard_map/ppermute | solution.py:244
  92.9 5.1 %collective-permute-start.11 = (bf16[128,384]{1,0:T(8,128)(2,1)S(1)}, bf16[128,384]{1,0:T(8,128)(2,1)S(1)}, u32[]{:S(2)}, u32[]{:S(2)}) collective-permute-start(bf16[128,384]{1,0:T(8,128)(2,1)S(1)} %get-tuple-element.26), channel_id=1, source_target_pairs={{0,14},{1,11},{2,8},{3,13},{4,10},{5,15},{6,12},{7,9},{8,22},{9,19... | collective-permute-start | bytes 294920 | tf_op jit(solution)/shard_map/ppermute | solution.py:244
  97.9 1.9 %collective-permute-start.12 = (bf16[128,384]{1,0:T(8,128)(2,1)S(1)}, bf16[128,384]{1,0:T(8,128)(2,1)S(1)}, u32[]{:S(2)}, u32[]{:S(2)}) collective-permute-start(bf16[128,384]{1,0:T(8,128)(2,1)S(1)} %get-tuple-element.27), channel_id=1, source_target_pairs={{0,12},{1,13},{2,14},{3,15},{4,8},{5,9},{6,10},{7,11},{8,20},{9,21... | collective-permute-start | bytes 294920 | tf_op jit(solution)/shard_map/ppermute | solution.py:244
  99.9 4.2 %collective-permute-start.13 = (bf16[128,384]{1,0:T(8,128)(2,1)S(1)}, bf16[128,384]{1,0:T(8,128)(2,1)S(1)}, u32[]{:S(2)}, u32[]{:S(2)}) collective-permute-start(bf16[128,384]{1,0:T(8,128)(2,1)S(1)} %get-tuple-element.28), channel_id=1, source_target_pairs={{0,10},{1,15},{2,12},{3,9},{4,14},{5,11},{6,8},{7,13},{8,18},{9,23... | collective-permute-start | bytes 294920 | tf_op jit(solution)/shard_map/ppermute | solution.py:244
  104.0 2.2 %shard_map.92 = bf16[1,2,128,1536]{3,2,1,0:T(8,128)(2,1)} custom-call(bf16[6,128,384]{2,1,0:T(8,128)(2,1)S(1)} %get-tuple-element.22.m_ref.k_ref, bf16[6,128,384]{2,1,0:T(8,128)(2,1)S(1)} %collective-permute-done.6.a_ref, bf16[6,128,384]{2,1,0:T(8,128)(2,1)} %collective-permute-done.7.b_ref, bf16[3,128,384]{2,1,0:T(8,128)(2,1)} %collective-permute-done.14.p_ref), custom_call_target="tpu_custom_call" | custom-call | tf_op jit(solution)/shard_map/pallas_call | solution.py:233
  106.2 2.5 %collective-permute-done.13.a3 = bf16[128,384]{1,0:T(8,128)(2,1)S(1)} collective-permute-done((bf16[128,384]{1,0:T(8,128)(2,1)S(1)}, bf16[128,384]{1,0:T(8,128)(2,1)S(1)}, u32[]{:S(2)}, u32[]{:S(2)}) %collective-permute-start.13) | collective-permute-done | bytes 98336 | tf_op jit(solution)/shard_map/ppermute | solution.py:244
  108.8 0.9 shard_map.91
  (29 shorter events, 1.3 us)
Async XLA Ops:
  0.6 1.5 %copy-start = (bf16[1,1536,576]{1,2,0:T(8,128)(2,1)S(1)}, bf16[1,1536,576]{1,2,0:T(8,128)(2,1)}, u32[]{:S(2)}) copy-start(bf16[1,1536,576]{1,2,0:T(8,128)(2,1)} %param.8) | copy-start | bytes 5308420
  2.1 1.1 %copy-start.4 = (bf16[1,2,128,1536]{3,2,1,0:T(8,128)(2,1)S(1)}, bf16[1,2,128,1536]{3,2,1,0:T(8,128)(2,1)}, u32[]{:S(2)}) copy-start(bf16[1,2,128,1536]{3,2,1,0:T(8,128)(2,1)} %s_ref.1) | copy-start | bytes 2359300
  3.2 1.0 copy-start.5
  4.2 0.7 copy-start.7
  4.9 0.7 copy-start.8
  5.6 0.7 copy-start.9
  6.3 28.9 %copy-start.6 = (bf16[1,128,1536]{2,1,0:T(8,128)(2,1)S(1)}, bf16[1,128,1536]{2,1,0:T(8,128)(2,1)}, u32[]{:S(2)}) copy-start(bf16[1,128,1536]{2,1,0:T(8,128)(2,1)} %h_ref.1) | copy-start | bytes 1179652
  6.9 48.0 %collective-permute-start.3 = (bf16[384,1536]{1,0:T(8,128)(2,1)S(1)}, bf16[384,1536]{1,0:T(8,128)(2,1)S(1)}, u32[]{:S(2)}, u32[]{:S(2)}) collective-permute-start(bf16[384,1536]{1,0:T(8,128)(2,1)S(1)} %get-tuple-element.20), channel_id=1, source_target_pairs={{0,385},{1,128},{2,387},{3,130},{4,389},{5,132},{6,391},{7,134},{1... | collective-permute-start | bytes 3538952 | tf_op jit(solution)/shard_map/ppermute | solution.py:208
  18.4 16.8 %collective-permute-start = (bf16[6,128,384]{2,1,0:T(8,128)(2,1)S(1)}, bf16[6,128,384]{2,1,0:T(8,128)(2,1)S(1)}, u32[]{:S(2)}, u32[]{:S(2)}) collective-permute-start(bf16[6,128,384]{2,1,0:T(8,128)(2,1)S(1)} %get-tuple-element.17), channel_id=1, source_target_pairs={{0,6},{1,3},{2,0},{3,5},{4,2},{5,7},{6,4},{7,1},{8,14},{9,11},{10,... | collective-permute-start | bytes 1769480 | tf_op jit(solution)/shard_map/ppermute | solution.py:210
  22.8 27.4 %collective-permute-start.2 = (bf16[6,128,384]{2,1,0:T(8,128)(2,1)S(1)}, bf16[6,128,384]{2,1,0:T(8,128)(2,1)S(1)}, u32[]{:S(2)}, u32[]{:S(2)}) collective-permute-start(bf16[6,128,384]{2,1,0:T(8,128)(2,1)S(1)} %get-tuple-element.19), channel_id=1, source_target_pairs={{0,2},{1,7},{2,4},{3,1},{4,6},{5,3},{6,0},{7,5},{8,10},{9,15},{10,... | collective-permute-start | bytes 1769480 | tf_op jit(solution)/shard_map/ppermute | solution.py:209
  24.7 30.2 %collective-permute-start.1 = (bf16[6,128,384]{2,1,0:T(8,128)(2,1)S(1)}, bf16[6,128,384]{2,1,0:T(8,128)(2,1)S(1)}, u32[]{:S(2)}, u32[]{:S(2)}) collective-permute-start(bf16[6,128,384]{2,1,0:T(8,128)(2,1)S(1)} %get-tuple-element.18), channel_id=1, source_target_pairs={{0,4},{1,5},{2,6},{3,7},{4,0},{5,1},{6,2},{7,3},{8,12},{9,13},{10,... | collective-permute-start | bytes 1769480 | tf_op jit(solution)/shard_map/ppermute | solution.py:211
  28.3 26.5 %collective-permute-start.4 = (bf16[192,1536]{1,0:T(8,128)(2,1)S(1)}, bf16[192,1536]{1,0:T(8,128)(2,1)S(1)}, u32[]{:S(2)}, u32[]{:S(2)}) collective-permute-start(bf16[192,1536]{1,0:T(8,128)(2,1)S(1)} %get-tuple-element.21), channel_id=1, source_target_pairs={{0,1},{1,0},{2,3},{3,2},{4,5},{5,4},{6,7},{7,6},{8,9},{9,8},{10,11... | collective-permute-start | bytes 1769480 | tf_op jit(solution)/shard_map/ppermute | solution.py:212
  35.2 19.6 %collective-permute-start.5 = (bf16[1,128,1536]{2,1,0:T(8,128)(2,1)S(1)}, bf16[1,128,1536]{2,1,0:T(8,128)(2,1)S(1)}, u32[]{:S(2)}, u32[]{:S(2)}) collective-permute-start(bf16[1,128,1536]{2,1,0:T(8,128)(2,1)S(1)} %copy-done.6), channel_id=1, source_target_pairs={{0,8},{8,16},{16,24},{24,32},{32,40},{40,48},{48,56},{56,64},{64,7... | collective-permute-start | bytes 1179656 | tf_op jit(solution)/shard_map/ppermute | solution.py:213
  50.1 4.7 %copy-start.1 = (bf16[1,1536,576]{1,2,0:T(8,128)(2,1)S(1)}, bf16[1,1536,576]{1,2,0:T(8,128)(2,1)}, u32[]{:S(2)}) copy-start(bf16[1,1536,576]{1,2,0:T(8,128)(2,1)} %param.8) | copy-start | bytes 5308420
  51.0 20.4 %copy-start.10 = (f32[1,1536]{1,0:T(1,128)S(1)}, f32[1,1536]{1,0:T(1,128)}, u32[]{:S(2)}) copy-start(f32[1,1536]{1,0:T(1,128)} %param.11) | copy-start | bytes 18436
  51.0 22.4 %collective-permute-start.8 = (bf16[3,2,128,384]{3,2,1,0:T(8,128)(2,1)}, bf16[3,2,128,384]{3,2,1,0:T(8,128)(2,1)}, u32[]{:S(2)}, u32[]{:S(2)}) collective-permute-start(bf16[3,2,128,384]{3,2,1,0:T(8,128)(2,1)} %shard_map.88), channel_id=1, source_target_pairs={{0,1},{1,0},{2,3},{3,2},{4,5},{5,4},{6,7},{7,6},{8,9},{9,8},{10,11... | collective-permute-start | bytes 1769480 | tf_op jit(solution)/shard_map/ppermute | solution.py:216
  54.9 3.7 %copy-start.2 = (bf16[1,128,1536]{2,1,0:T(8,128)(2,1)}, bf16[1,128,1536]{2,1,0:T(8,128)(2,1)S(1)}, u32[]{:S(2)}) copy-start(bf16[1,128,1536]{2,1,0:T(8,128)(2,1)S(1)} %collective-permute-done.5.early.h_ref) | copy-start | bytes 1179652
  58.6 16.6 %collective-permute-start.6 = (bf16[6,128,384]{2,1,0:T(8,128)(2,1)}, bf16[6,128,384]{2,1,0:T(8,128)(2,1)S(1)}, u32[]{:S(2)}, u32[]{:S(2)}) collective-permute-start(bf16[6,128,384]{2,1,0:T(8,128)(2,1)} %get-tuple-element.23), channel_id=1, source_target_pairs={{0,2},{1,7},{2,4},{3,1},{4,6},{5,3},{6,0},{7,5},{8,10},{9,15},{10,... | collective-permute-start | bytes 1769480 | tf_op jit(solution)/shard_map/ppermute | solution.py:226
  60.5 17.4 %collective-permute-start.7 = (bf16[6,128,384]{2,1,0:T(8,128)(2,1)}, bf16[6,128,384]{2,1,0:T(8,128)(2,1)}, u32[]{:S(2)}, u32[]{:S(2)}) collective-permute-start(bf16[6,128,384]{2,1,0:T(8,128)(2,1)} %get-tuple-element.24), channel_id=1, source_target_pairs={{0,6},{1,3},{2,0},{3,5},{4,2},{5,7},{6,4},{7,1},{8,14},{9,11},{10,... | collective-permute-start | bytes 1769480 | tf_op jit(solution)/shard_map/ppermute | solution.py:227
  66.4 7.0 %collective-permute-start.9 = (bf16[2,128,384]{2,1,0:T(8,128)(2,1)}, bf16[2,128,384]{2,1,0:T(8,128)(2,1)}, u32[]{:S(2)}, u32[]{:S(2)}) collective-permute-start(bf16[2,128,384]{2,1,0:T(8,128)(2,1)} %shard_map.89), channel_id=1, source_target_pairs={{0,1},{1,0},{2,3},{3,2},{4,5},{5,4},{6,7},{7,6},{8,9},{9,8},{10,11... | collective-permute-start | bytes 589832 | tf_op jit(solution)/shard_map/ppermute | solution.py:218
  68.4 35.7 %collective-permute-start.14 = (bf16[3,128,384]{2,1,0:T(8,128)(2,1)}, bf16[3,128,384]{2,1,0:T(8,128)(2,1)}, u32[]{:S(2)}, u32[]{:S(2)}) collective-permute-start(bf16[3,128,384]{2,1,0:T(8,128)(2,1)} %get-tuple-element.29), channel_id=1, source_target_pairs={{0,4},{1,5},{2,6},{3,7},{4,0},{5,1},{6,2},{7,3},{8,12},{9,13},{10,... | collective-permute-start | bytes 884744 | tf_op jit(solution)/shard_map/ppermute | solution.py:228
  83.6 22.7 %collective-permute-start.10 = (bf16[128,384]{1,0:T(8,128)(2,1)S(1)}, bf16[128,384]{1,0:T(8,128)(2,1)S(1)}, u32[]{:S(2)}, u32[]{:S(2)}) collective-permute-start(bf16[128,384]{1,0:T(8,128)(2,1)S(1)} %get-tuple-element.25), channel_id=1, source_target_pairs={{0,8},{1,9},{2,10},{3,11},{4,12},{5,13},{6,14},{7,15},{8,16},{9,17... | collective-permute-start | bytes 294920 | tf_op jit(solution)/shard_map/ppermute | solution.py:244
  92.9 13.4 %collective-permute-start.11 = (bf16[128,384]{1,0:T(8,128)(2,1)S(1)}, bf16[128,384]{1,0:T(8,128)(2,1)S(1)}, u32[]{:S(2)}, u32[]{:S(2)}) collective-permute-start(bf16[128,384]{1,0:T(8,128)(2,1)S(1)} %get-tuple-element.26), channel_id=1, source_target_pairs={{0,14},{1,11},{2,8},{3,13},{4,10},{5,15},{6,12},{7,9},{8,22},{9,19... | collective-permute-start | bytes 294920 | tf_op jit(solution)/shard_map/ppermute | solution.py:244
  97.9 8.3 %collective-permute-start.12 = (bf16[128,384]{1,0:T(8,128)(2,1)S(1)}, bf16[128,384]{1,0:T(8,128)(2,1)S(1)}, u32[]{:S(2)}, u32[]{:S(2)}) collective-permute-start(bf16[128,384]{1,0:T(8,128)(2,1)S(1)} %get-tuple-element.27), channel_id=1, source_target_pairs={{0,12},{1,13},{2,14},{3,15},{4,8},{5,9},{6,10},{7,11},{8,20},{9,21... | collective-permute-start | bytes 294920 | tf_op jit(solution)/shard_map/ppermute | solution.py:244
  99.8 8.9 %copy-start.3 = (bf16[1,128,1536]{2,1,0:T(8,128)(2,1)S(1)}, bf16[1,128,1536]{2,1,0:T(8,128)(2,1)}, u32[]{:S(2)}) copy-start(bf16[1,128,1536]{2,1,0:T(8,128)(2,1)} %copy-done.2) | copy-start | bytes 1179652
  99.9 8.9 %collective-permute-start.13 = (bf16[128,384]{1,0:T(8,128)(2,1)S(1)}, bf16[128,384]{1,0:T(8,128)(2,1)S(1)}, u32[]{:S(2)}, u32[]{:S(2)}) collective-permute-start(bf16[128,384]{1,0:T(8,128)(2,1)S(1)} %get-tuple-element.28), channel_id=1, source_target_pairs={{0,10},{1,15},{2,12},{3,9},{4,14},{5,11},{6,8},{7,13},{8,18},{9,23... | collective-permute-start | bytes 294920 | tf_op jit(solution)/shard_map/ppermute | solution.py:244

commit v4 on v3

--- a/solution.py
+++ b/solution.py
@@ -60,21 +60,59 @@
     )
 
 
-def norm_body(h_ref, g_ref, b_ref, m_ref, s_ref, w_ref, own, b1, b2, b3, lead, rest):
+def norm_body(h_hbm, g_hbm, b_hbm, m_hbm, s_hbm, w_hbm, own, b1, b2, lead, rest, *scratch):
+    h_ref, g_ref, b_ref, m_ref, s_ref, l_sem, r_sem, *sems = scratch
     x, z = where_am_i()
+    copies = [
+        pltpu.make_async_copy(src, dst, sem)
+        for src, dst, sem in zip(
+            (h_hbm, g_hbm, b_hbm, m_hbm, s_hbm), (h_ref, g_ref, b_ref, m_ref, s_ref), sems
+        )
+    ]
+    copies.append(
+        pltpu.make_async_copy(
+            w_hbm.at[pl.ds(pl.multiple_of(HALF * z, HALF), UNIT), :], lead, l_sem
+        )
+    )
+    copies.append(
+        pltpu.make_async_copy(
+            w_hbm.at[pl.ds(pl.multiple_of(UNIT * (1 - z), HALF), HALF), :], rest, r_sem
+        )
+    )
+    for copy in copies:
+        copy.start()
+    for copy in copies[:4]:
+        copy.wait()
     h = h_ref[0].astype(F32)
     inverse = lax.rsqrt(jnp.mean(h * h, axis=-1, keepdims=True) + 1e-06)
     mask = jnp.broadcast_to(m_ref[...].astype(F32), (ROWS, ROWS)).T[:, :1]
     normed = (h * inverse * g_ref[...] + mask * b_ref[...]).astype(BF)
-    for j, bundle in enumerate((own, b1, b2, b3)):
+    for bundle in (own, b1, b2):
         for g in range(4):
             bundle[g] = normed[:, UNIT * g : UNIT * (g + 1)]
+    copies[4].wait()
+
+    def stale(j, kv):
         group = ((x + (1 - 2 * z) * j + 4) % 4) ^ 1
-        cols = pl.ds(pl.multiple_of(UNIT * group, UNIT), UNIT)
-        bundle[4] = s_ref[0, 0, :, cols]
-        bundle[5] = s_ref[0, 1, :, cols]
-    lead[...] = w_ref[pl.ds(pl.multiple_of(HALF * z, HALF), UNIT), :]
-    rest[...] = w_ref[pl.ds(pl.multiple_of(UNIT * (1 - z), HALF), HALF), :]
+        return s_ref[0, kv, :, pl.ds(pl.multiple_of(UNIT * group, UNIT), UNIT)]
+
+    for kv in range(2):
+        own[4 + kv] = stale(0, kv)
+        b1[4 + kv] = stale(1, kv)
+        b2[4 + kv] = stale(3, kv)
+    b1[6] = stale(2, 0)
+    b2[6] = stale(2, 1)
+    copies[5].wait()
+    copies[6].wait()
+
+
+def pass_body(t1, t3, from1, from3):
+    from1[0] = t1[0]
+    from1[1] = t1[1]
+    from1[2] = t1[6]
+    from3[0] = t3[2]
+    from3[1] = t3[3]
+    from3[2] = t3[6]
 
 
 def near_body(t0, t1, t3, o_ref):
@@ -82,19 +120,22 @@
         o_ref[i] = ref[4:6]
 
 
-def far_body(t2, o_ref):
-    o_ref[...] = t2[4:6]
-
-
-def project_body(t0, t1, t2, t3, w_ref, v_ref, u_ref, early, front_o, back_o, opp_o, keep_o, both):
+def far_body(c_ref, d_ref, after, o_ref):
+    del after
+    o_ref[0] = d_ref[2]
+    o_ref[1] = c_ref[2]
+
+
+def project_body(t0, t1, c_ref, d_ref, t3, w_ref, v_ref, u_ref, early, *outs):
     del early
+    front_o, back_o, opp_o, keep_o, both = outs
     _, z = where_am_i()
     mine = w_ref[pl.ds(pl.multiple_of(UNIT * (1 - z), HALF), HALF), :]
     both[pl.ds(pl.multiple_of(HALF * z, HALF), HALF), :] = mine
     both[pl.ds(pl.multiple_of(HALF * (1 - z), HALF), HALF), :] = u_ref[...]
-    tokens = jnp.concatenate(
-        [jnp.concatenate([b[g] for g in range(4)], axis=1) for b in (t0, t1, t2, t3)], axis=0
-    )
+    placed = [[t[g] for g in range(4)] for t in (t0, t1, t3)]
+    placed.insert(2, [c_ref[0], c_ref[1], d_ref[0], d_ref[1]])
+    tokens = jnp.concatenate([jnp.concatenate(b, axis=1) for b in placed], axis=0)
 
     def product(weight):
         got = lax.dot_general(tokens, weight, NT, preferred_element_type=F32).astype(BF)
@@ -127,9 +168,9 @@
     return q, k, v
 
 
-def attend_body(m_ref, a_ref, b_ref, t0, t1, t2, t3, pn_ref, pf_ref, g_ref, *o_refs):
+def attend_body(m_ref, a_ref, b_ref, t0, t1, c_ref, d_ref, t3, pn_ref, pf_ref, g_ref, *o_refs):
     x, z = where_am_i()
-    gates = g_ref[pl.ds(x ^ 1, 1), :]
+    gates = g_ref[:, pl.ds(pl.multiple_of(UNIT * (x ^ 1), UNIT), UNIT)]
     roled = roles(x, z)
     for head in range(3):
         cols = slice(HEAD_DIM * head, HEAD_DIM * (head + 1))
@@ -141,7 +182,8 @@
             return jnp.where(index == 0, own, jnp.where(index == 1, behind, ahead))
 
         kept = [
-            [t[4 + kv, :, cols] for t in (t0, t1, t2, t3)]
+            [t0[4 + kv, :, cols], t1[4 + kv, :, cols]]
+            + [(d_ref, c_ref)[kv][2, :, cols], t3[4 + kv, :, cols]]
             + [pn_ref[i, kv, :, cols] for i in range(3)]
             + [pf_ref[kv, :, cols]]
             for kv in range(2)
@@ -164,7 +206,8 @@
             o_refs[j][:, cols] = (gates[:, cols] * (summed / total)).astype(BF)
 
 
-def fresh_body(k_ref, a_ref, b_ref, p_ref, f_ref):
+def fresh_body(k_ref, a_ref, b_ref, p_ref, after, f_ref):
+    del after
     x, z = where_am_i()
     rows = (
         (0, (k_ref.at[4], k_ref.at[0], k_ref.at[5])),
@@ -202,36 +245,51 @@
         return jax.ShapeDtypeStruct((count, D), BF)
 
     weight = jnp.swapaxes(w_qkv[0], 0, 1)
-    t0, b1, b2, b3, lead, rest = call(
-        norm_body, (blocks(6), blocks(6), blocks(6), blocks(6), rows(UNIT), rows(HALF)), 6
+    t0, t3, t1, lead, rest = pl.pallas_call(
+        norm_body,
+        out_shape=(blocks(6), blocks(7), blocks(7), rows(UNIT), rows(HALF)),
+        in_specs=[pl.BlockSpec(memory_space=pltpu.HBM)] * 6,
+        out_specs=(VM,) * 5,
+        scratch_shapes=[
+            pltpu.VMEM((1, ROWS, D), BF),
+            pltpu.VMEM((1, D), F32),
+            pltpu.VMEM((1, D), F32),
+            pltpu.VMEM((1, ROWS), jnp.int32),
+            pltpu.VMEM((1, 2, ROWS, D), BF),
+        ]
+        + [pltpu.SemaphoreType.DMA] * 7,
+        compiler_params=pltpu.CompilerParams(vmem_limit_bytes=60 * 1024 * 1024),
     )(hidden, norm_gain, box_vec, box_mask, stale_kv, weight)
     lead = lax.ppermute(lead, ("dp", "patch"), far_pairs(parts))
-    t3 = lax.ppermute(b1, "patch", x_pairs(1))
-    t1 = lax.ppermute(b3, "patch", x_pairs(3))
-    t2 = lax.ppermute(b2, "patch", x_pairs(2))
+    t3 = lax.ppermute(t3, "patch", x_pairs(1))
+    t1 = lax.ppermute(t1, "patch", x_pairs(3))
     rest = lax.ppermute(rest, "patch", partner_pairs())
     before = lax.ppermute(hidden, "segment", [(i, (i + 1) % segments) for i in range(segments)])
 
+    t2a, t2b = call(pass_body, (blocks(3), blocks(3)), 2)(t1, t3)
+    t2a = lax.ppermute(t2a, "patch", x_pairs(3))
+    t2b = lax.ppermute(t2b, "patch", x_pairs(1))
     near = call(near_body, blocks(3, 2), 3)(t0, t1, t3)
     near = lax.ppermute(near, "patch", partner_pairs())
-    far = call(far_body, blocks(2), 1)(t2)
+    far = call(far_body, blocks(2), 3)(t2a, t2b, near)
     far = lax.ppermute(far, "patch", partner_pairs())
 
     front, back, opposite, keep = call(
         project_body,
         (blocks(6), blocks(6), blocks(3), blocks(6)),
-        8,
+        9,
         scratch_shapes=[pltpu.VMEM((UNIT, D), BF)],
-    )(t0, t1, t2, t3, weight, lead, rest, before)
+    )(t0, t1, t2a, t2b, t3, weight, lead, rest, before)
     front = lax.ppermute(front, "patch", x_pairs(1))
     back = lax.ppermute(back, "patch", x_pairs(3))
+    opposite, mark = lax.optimization_barrier((opposite, back[0, :16, :128]))
     opposite = lax.ppermute(opposite, "patch", x_pairs(2))
 
-    out = call(attend_body, (blocks(),) * 4, 10)(
-        keep, front, back, t0, t1, t2, t3, near, far, gate.reshape(4, UNIT)
-    )
-    fresh = call(fresh_body, jax.ShapeDtypeStruct((1, 2, ROWS, D), BF), 4)(
-        keep, front, back, opposite
+    out = call(attend_body, (blocks(),) * 4, 11)(
+        keep, front, back, t0, t1, t2a, t2b, t3, near, far, gate
+    )
+    fresh = call(fresh_body, jax.ShapeDtypeStruct((1, 2, ROWS, D), BF), 5)(
+        keep, front, back, opposite, mark
     )
 
     came = []

time: 110 us -> 99.6 us (0.905); the launches traced: 110 us -> 98 us
  starting transfers between devices: 72.9 us -> 56.4 us
  waiting for transfers between devices: 15.6 us -> 27.8 us
  local copies, waits for them, and re-layouts: 5.67 us -> 0.02 us
  Pallas kernels: 14.6 us -> 12.9 us
    ppermute x1, starting transfers between devices: 14.9 us -> 2.43 us  [local(): lax.ppermute(hidden, 'segment', [(i, (i + 1) % segments) for i in range(s...]
    ppermute x3 -> x4, waiting for transfers between devices: 4.96 us -> 16.6 us  [the longest x1 7.78 us: local(): t1 = lax.ppermute(t1, 'patch', x_pairs(3))]
    unnamed x22 -> x8, local copies, waits for them, and re-layouts: 5.66 us -> 0.02 us
    ppermute x4, starting transfers between devices: 20.4 us -> 16.8 us  [local(): came.append(lax.ppermute(out[j], ('segment', 'patch'), pairs))]
    ppermute x1, starting transfers between devices: 5.29 us -> 1.92 us  [local(): back = lax.ppermute(back, 'patch', x_pairs(3))]
    ppermute x1, waiting for transfers between devices: 2.68 us -> 5.89 us  [local(): back = lax.ppermute(back, 'patch', x_pairs(3))]
    ppermute x1, waiting for transfers between devices: 1.94 us -> 0.01 us  [local(): far = lax.ppermute(far, 'patch', partner_pairs())]
    ppermute x4, waiting for transfers between devices: 2.54 us -> 4.37 us  [local(): came.append(lax.ppermute(out[j], ('segment', 'patch'), pairs))]
  transfers between devices with their start and end apart: 15 -> 16, of which waited for: 6 -> 9; matrix products, arithmetic and copies ran while one was open for 0% -> 0% of each run, Pallas kernels for 12% -> 8%
where the time goes in v4:
time: 99.6 us; the launch traced here: 98 us
  starting transfers between devices  56.4 us (57%)
  waiting for transfers between devices  27.8 us (28%)
  Pallas kernels  12.9 us (13%)
    ppermute x4, starting transfers between devices, local(): came.append(lax.ppermute(out[j], ('segment', 'patch'), pairs))  16.8 us
    ppermute x1, starting transfers between devices, local(): lead = lax.ppermute(lead, ('dp', 'patch'), far_pairs(parts))  11.6 us
    ppermute x1, waiting for transfers between devices, local(): t1 = lax.ppermute(t1, 'patch', x_pairs(3))  7.78 us
    ppermute x1, waiting for transfers between devices, local(): back = lax.ppermute(back, 'patch', x_pairs(3))  5.89 us
    ppermute x1, waiting for transfers between devices, local(): t3 = lax.ppermute(t3, 'patch', x_pairs(1))  4.92 us
    pallas_call x1, Pallas kernels, local(): call(attend_body, (blocks(),) * 4, 11)  4.45 us
    ppermute x1, starting transfers between devices, local(): t1 = lax.ppermute(t1, 'patch', x_pairs(3))  4.39 us
    ppermute x4, waiting for transfers between devices, local(): came.append(lax.ppermute(out[j], ('segment', 'patch'), pairs))  4.37 us
  transfers between devices with their start and end apart: 16, of which 9 were waited for; matrix products, arithmetic and copies ran while one was open for 0% of the time, Pallas kernels for 8%

profile of v4, /device:TPU:1, one launch (start us, length us, event | category | flops | bytes accessed | tf_op | source)
XLA Modules:
  0.0 98.0 jit_solution(768305973470486067)
XLA Ops:
  0.6 3.8 %shard_map.86 = (bf16[6,128,384]{2,1,0:T(8,128)(2,1)}, bf16[7,128,384]{2,1,0:T(8,128)(2,1)}, bf16[7,128,384]{2,1,0:T(8,128)(2,1)}, bf16[384,1536]{1,0:T(8,128)(2,1)}, bf16[192,1536]{1,0:T(8,128)(2,1)}) custom-call(bf16[1,128,1536]{2,1,0:T(8,128)(2,1)} %h_hbm.1, f32[1,1536]{1,0:T(1,128)} %g_hbm.1, f32[1,1536]{1,0:T(1,128)} %b_hbm.1, s32[1,128]{1,0:T(1,128)} %m_hbm.1, ...), custom_call_target="tpu_custom_call" | custom-call | tf_op jit(solution)/shard_map/pallas_call | solution.py:248
  4.5 11.6 %collective-permute-start.4 = (bf16[384,1536]{1,0:T(8,128)(2,1)}, bf16[384,1536]{1,0:T(8,128)(2,1)S(1)}, u32[]{:S(2)}, u32[]{:S(2)}) collective-permute-start(bf16[384,1536]{1,0:T(8,128)(2,1)} %get-tuple-element.24), channel_id=1, source_target_pairs={{0,385},{1,128},{2,387},{3,130},{4,389},{5,132},{6,391},{7,134},{1... | collective-permute-start | bytes 3538952 | tf_op jit(solution)/shard_map/ppermute | solution.py:263
  16.1 4.4 %collective-permute-start = (bf16[7,128,384]{2,1,0:T(8,128)(2,1)}, bf16[7,128,384]{2,1,0:T(8,128)(2,1)S(1)}, u32[]{:S(2)}, u32[]{:S(2)}) collective-permute-start(bf16[7,128,384]{2,1,0:T(8,128)(2,1)} %get-tuple-element.20), channel_id=1, source_target_pairs={{0,6},{1,3},{2,0},{3,5},{4,2},{5,7},{6,4},{7,1},{8,14},{9,11},{10,... | collective-permute-start | bytes 2064392 | tf_op jit(solution)/shard_map/ppermute | solution.py:265
  20.5 1.9 %collective-permute-start.1 = (bf16[7,128,384]{2,1,0:T(8,128)(2,1)}, bf16[7,128,384]{2,1,0:T(8,128)(2,1)S(1)}, u32[]{:S(2)}, u32[]{:S(2)}) collective-permute-start(bf16[7,128,384]{2,1,0:T(8,128)(2,1)} %get-tuple-element.21), channel_id=1, source_target_pairs={{0,2},{1,7},{2,4},{3,1},{4,6},{5,3},{6,0},{7,5},{8,10},{9,15},{10,... | collective-permute-start | bytes 2064392 | tf_op jit(solution)/shard_map/ppermute | solution.py:264
  22.4 1.9 %collective-permute-start.5 = (bf16[192,1536]{1,0:T(8,128)(2,1)}, bf16[192,1536]{1,0:T(8,128)(2,1)S(1)}, u32[]{:S(2)}, u32[]{:S(2)}) collective-permute-start(bf16[192,1536]{1,0:T(8,128)(2,1)} %get-tuple-element.25), channel_id=1, source_target_pairs={{0,1},{1,0},{2,3},{3,2},{4,5},{5,4},{6,7},{7,6},{8,9},{9,8},{10,11... | collective-permute-start | bytes 1769480 | tf_op jit(solution)/shard_map/ppermute | solution.py:266
  24.3 2.4 %collective-permute-start.6 = (bf16[1,128,1536]{2,1,0:T(8,128)(2,1)S(1)}, bf16[1,128,1536]{2,1,0:T(8,128)(2,1)S(1)}, u32[]{:S(2)}, u32[]{:S(2)}) collective-permute-start(bf16[1,128,1536]{2,1,0:T(8,128)(2,1)S(1)} %copy-done.3), channel_id=1, source_target_pairs={{0,8},{8,16},{16,24},{24,32},{32,40},{40,48},{48,56},{56,64},{64,7... | collective-permute-start | bytes 1179656 | tf_op jit(solution)/shard_map/ppermute | solution.py:267
  26.8 7.8 %collective-permute-done.t1 = bf16[7,128,384]{2,1,0:T(8,128)(2,1)S(1)} collective-permute-done((bf16[7,128,384]{2,1,0:T(8,128)(2,1)}, bf16[7,128,384]{2,1,0:T(8,128)(2,1)S(1)}, u32[]{:S(2)}, u32[]{:S(2)}) %collective-permute-start) | collective-permute-done | bytes 688160 | tf_op jit(solution)/shard_map/ppermute | solution.py:265
  34.6 4.9 %collective-permute-done.1.t3 = bf16[7,128,384]{2,1,0:T(8,128)(2,1)S(1)} collective-permute-done((bf16[7,128,384]{2,1,0:T(8,128)(2,1)}, bf16[7,128,384]{2,1,0:T(8,128)(2,1)S(1)}, u32[]{:S(2)}, u32[]{:S(2)}) %collective-permute-start.1) | collective-permute-done | bytes 688160 | tf_op jit(solution)/shard_map/ppermute | solution.py:264
  39.5 0.1 shard_map.87
  39.5 1.9 %collective-permute-start.2 = (bf16[3,128,384]{2,1,0:T(8,128)(2,1)S(1)}, bf16[3,128,384]{2,1,0:T(8,128)(2,1)S(1)}, u32[]{:S(2)}, u32[]{:S(2)}) collective-permute-start(bf16[3,128,384]{2,1,0:T(8,128)(2,1)S(1)} %get-tuple-element.22), channel_id=1, source_target_pairs={{0,6},{1,3},{2,0},{3,5},{4,2},{5,7},{6,4},{7,1},{8,14},{9,11},{10,... | collective-permute-start | bytes 884744 | tf_op jit(solution)/shard_map/ppermute | solution.py:270
  41.5 3.4 %collective-permute-start.3 = (bf16[3,128,384]{2,1,0:T(8,128)(2,1)S(1)}, bf16[3,128,384]{2,1,0:T(8,128)(2,1)S(1)}, u32[]{:S(2)}, u32[]{:S(2)}) collective-permute-start(bf16[3,128,384]{2,1,0:T(8,128)(2,1)S(1)} %get-tuple-element.23), channel_id=1, source_target_pairs={{0,2},{1,7},{2,4},{3,1},{4,6},{5,3},{6,0},{7,5},{8,10},{9,15},{10,... | collective-permute-start | bytes 884744 | tf_op jit(solution)/shard_map/ppermute | solution.py:271
  44.9 0.1 shard_map.89
  44.9 2.1 %collective-permute-start.9 = (bf16[3,2,128,384]{3,2,1,0:T(8,128)(2,1)S(1)}, bf16[3,2,128,384]{3,2,1,0:T(8,128)(2,1)S(1)}, u32[]{:S(2)}, u32[]{:S(2)}) collective-permute-start(bf16[3,2,128,384]{3,2,1,0:T(8,128)(2,1)S(1)} %shard_map.89), channel_id=1, source_target_pairs={{0,1},{1,0},{2,3},{3,2},{4,5},{5,4},{6,7},{7,6},{8,9},{9,8},{10,11... | collective-permute-start | bytes 1769480 | tf_op jit(solution)/shard_map/ppermute | solution.py:273
  47.0 0.8 collective-permute-done.2.c_ref
  47.8 3.1 %collective-permute-done.3.d_ref = bf16[3,128,384]{2,1,0:T(8,128)(2,1)S(1)} collective-permute-done((bf16[3,128,384]{2,1,0:T(8,128)(2,1)S(1)}, bf16[3,128,384]{2,1,0:T(8,128)(2,1)S(1)}, u32[]{:S(2)}, u32[]{:S(2)}) %collective-permute-start.3) | collective-permute-done | bytes 294944 | tf_op jit(solution)/shard_map/ppermute | solution.py:271
  50.9 2.6 %shard_map.88 = (bf16[6,128,384]{2,1,0:T(8,128)(2,1)S(1)}, bf16[6,128,384]{2,1,0:T(8,128)(2,1)S(1)}, bf16[3,128,384]{2,1,0:T(8,128)(2,1)S(1)}, bf16[6,128,384]{2,1,0:T(8,128)(2,1)S(1)}) custom-call(bf16[6,128,384]{2,1,0:T(8,128)(2,1)S(1)} %copy-done.1, bf16[7,128,384]{2,1,0:T(8,128)(2,1)S(1)} %collective-permute-done.t1, ...), custom_call_target="tpu_custom_call" | custom-call | tf_op jit(solution)/shard_map/pallas_call | solution.py:277
  53.5 1.9 %collective-permute-start.8 = (bf16[6,128,384]{2,1,0:T(8,128)(2,1)S(1)}, bf16[6,128,384]{2,1,0:T(8,128)(2,1)S(1)}, u32[]{:S(2)}, u32[]{:S(2)}) collective-permute-start(bf16[6,128,384]{2,1,0:T(8,128)(2,1)S(1)} %get-tuple-element.28), channel_id=1, source_target_pairs={{0,6},{1,3},{2,0},{3,5},{4,2},{5,7},{6,4},{7,1},{8,14},{9,11},{10,... | collective-permute-start | bytes 1769480 | tf_op jit(solution)/shard_map/ppermute | solution.py:284
  55.5 3.4 %collective-permute-start.7 = (bf16[6,128,384]{2,1,0:T(8,128)(2,1)S(1)}, bf16[6,128,384]{2,1,0:T(8,128)(2,1)S(1)}, u32[]{:S(2)}, u32[]{:S(2)}) collective-permute-start(bf16[6,128,384]{2,1,0:T(8,128)(2,1)S(1)} %get-tuple-element.27), channel_id=1, source_target_pairs={{0,2},{1,7},{2,4},{3,1},{4,6},{5,3},{6,0},{7,5},{8,10},{9,15},{10,... | collective-permute-start | bytes 1769480 | tf_op jit(solution)/shard_map/ppermute | solution.py:283
  58.8 0.2 collective-permute-done.9.after.pn_ref
  59.1 2.2 %collective-permute-start.10 = (bf16[2,128,384]{2,1,0:T(8,128)(2,1)S(1)}, bf16[2,128,384]{2,1,0:T(8,128)(2,1)S(1)}, u32[]{:S(2)}, u32[]{:S(2)}) collective-permute-start(bf16[2,128,384]{2,1,0:T(8,128)(2,1)S(1)} %shard_map.90), channel_id=1, source_target_pairs={{0,1},{1,0},{2,3},{3,2},{4,5},{5,4},{6,7},{7,6},{8,9},{9,8},{10,11... | collective-permute-start | bytes 589832 | tf_op jit(solution)/shard_map/ppermute | solution.py:275
  61.3 5.9 %collective-permute-done.8.b_ref = bf16[6,128,384]{2,1,0:T(8,128)(2,1)S(1)} collective-permute-done((bf16[6,128,384]{2,1,0:T(8,128)(2,1)S(1)}, bf16[6,128,384]{2,1,0:T(8,128)(2,1)S(1)}, u32[]{:S(2)}, u32[]{:S(2)}) %collective-permute-start.8) | collective-permute-done | bytes 589856 | tf_op jit(solution)/shard_map/ppermute | solution.py:284
  67.2 2.5 %collective-permute-start.15 = (bf16[3,128,384]{2,1,0:T(8,128)(2,1)S(1)}, bf16[3,128,384]{2,1,0:T(8,128)(2,1)S(1)}, u32[]{:S(2)}, u32[]{:S(2)}) collective-permute-start(bf16[3,128,384]{2,1,0:T(8,128)(2,1)S(1)} %get-tuple-element.34), channel_id=1, source_target_pairs={{0,4},{1,5},{2,6},{3,7},{4,0},{5,1},{6,2},{7,3},{8,12},{9,13},{10,... | collective-permute-start | bytes 884744 | tf_op jit(solution)/shard_map/ppermute | solution.py:286
  69.7 0.7 collective-permute-done.7.a_ref
  70.3 4.4 %shard_map.91 = (bf16[128,384]{1,0:T(8,128)(2,1)S(1)}, bf16[128,384]{1,0:T(8,128)(2,1)S(1)}, bf16[128,384]{1,0:T(8,128)(2,1)S(1)}, bf16[128,384]{1,0:T(8,128)(2,1)S(1)}) custom-call(bf16[6,128,384]{2,1,0:T(8,128)(2,1)S(1)} %get-tuple-element.26.m_ref.k_ref, bf16[6,128,384]{2,1,0:T(8,128)(2,1)S(1)} %collective-permute-done.7.a_ref, ...), custom_call_target="tpu_custom_call" | custom-call | tf_op jit(solution)/shard_map/pallas_call | solution.py:288
  74.8 8.4 %collective-permute-start.11 = (bf16[128,384]{1,0:T(8,128)(2,1)S(1)}, bf16[128,384]{1,0:T(8,128)(2,1)S(1)}, u32[]{:S(2)}, u32[]{:S(2)}) collective-permute-start(bf16[128,384]{1,0:T(8,128)(2,1)S(1)} %get-tuple-element.29), channel_id=1, source_target_pairs={{0,8},{1,9},{2,10},{3,11},{4,12},{5,13},{6,14},{7,15},{8,16},{9,17... | collective-permute-start | bytes 294920 | tf_op jit(solution)/shard_map/ppermute | solution.py:302
  83.1 1.9 %collective-permute-start.12 = (bf16[128,384]{1,0:T(8,128)(2,1)S(1)}, bf16[128,384]{1,0:T(8,128)(2,1)S(1)}, u32[]{:S(2)}, u32[]{:S(2)}) collective-permute-start(bf16[128,384]{1,0:T(8,128)(2,1)S(1)} %get-tuple-element.30), channel_id=1, source_target_pairs={{0,14},{1,11},{2,8},{3,13},{4,10},{5,15},{6,12},{7,9},{8,22},{9,19... | collective-permute-start | bytes 294920 | tf_op jit(solution)/shard_map/ppermute | solution.py:302
  85.1 3.8 %collective-permute-start.13 = (bf16[128,384]{1,0:T(8,128)(2,1)S(1)}, bf16[128,384]{1,0:T(8,128)(2,1)S(1)}, u32[]{:S(2)}, u32[]{:S(2)}) collective-permute-start(bf16[128,384]{1,0:T(8,128)(2,1)S(1)} %get-tuple-element.31), channel_id=1, source_target_pairs={{0,12},{1,13},{2,14},{3,15},{4,8},{5,9},{6,10},{7,11},{8,20},{9,21... | collective-permute-start | bytes 294920 | tf_op jit(solution)/shard_map/ppermute | solution.py:302
  88.9 2.8 %collective-permute-start.14 = (bf16[128,384]{1,0:T(8,128)(2,1)S(1)}, bf16[128,384]{1,0:T(8,128)(2,1)S(1)}, u32[]{:S(2)}, u32[]{:S(2)}) collective-permute-start(bf16[128,384]{1,0:T(8,128)(2,1)S(1)} %get-tuple-element.32), channel_id=1, source_target_pairs={{0,10},{1,15},{2,12},{3,9},{4,14},{5,11},{6,8},{7,13},{8,18},{9,23... | collective-permute-start | bytes 294920 | tf_op jit(solution)/shard_map/ppermute | solution.py:302
  91.7 0.8 collective-permute-done.13.a2
  92.5 3.5 %collective-permute-done.14.a3 = bf16[128,384]{1,0:T(8,128)(2,1)S(1)} collective-permute-done((bf16[128,384]{1,0:T(8,128)(2,1)S(1)}, bf16[128,384]{1,0:T(8,128)(2,1)S(1)}, u32[]{:S(2)}, u32[]{:S(2)}) %collective-permute-start.14) | collective-permute-done | bytes 98336 | tf_op jit(solution)/shard_map/ppermute | solution.py:302
  96.0 0.9 shard_map.92
  96.9 1.1 %shard_map.93 = bf16[1,2,128,1536]{3,2,1,0:T(8,128)(2,1)} custom-call(bf16[6,128,384]{2,1,0:T(8,128)(2,1)S(1)} %get-tuple-element.26.m_ref.k_ref, bf16[6,128,384]{2,1,0:T(8,128)(2,1)S(1)} %collective-permute-done.7.a_ref, bf16[6,128,384]{2,1,0:T(8,128)(2,1)S(1)} %collective-permute-done.8.b_ref, bf16[3,128,384]{2,1,0:T(8,128)(2,1)S(1)} %collective-permute-done.15.p_ref, ...), custom_call_target="tpu_custom_call" | custom-call | tf_op jit(solution)/shard_map/pallas_call | solution.py:291
  (17 shorter events, 0.1 us)
Async XLA Ops:
  0.6 23.7 %copy-start.3 = (bf16[1,128,1536]{2,1,0:T(8,128)(2,1)S(1)}, bf16[1,128,1536]{2,1,0:T(8,128)(2,1)}, u32[]{:S(2)}) copy-start(bf16[1,128,1536]{2,1,0:T(8,128)(2,1)} %h_hbm.1) | copy-start | bytes 1179652
  4.4 40.4 %copy-start.1 = (bf16[6,128,384]{2,1,0:T(8,128)(2,1)S(1)}, bf16[6,128,384]{2,1,0:T(8,128)(2,1)}, u32[]{:S(2)}) copy-start(bf16[6,128,384]{2,1,0:T(8,128)(2,1)} %get-tuple-element.19.t0) | copy-start | bytes 1769476
  4.5 46.5 %collective-permute-start.4 = (bf16[384,1536]{1,0:T(8,128)(2,1)}, bf16[384,1536]{1,0:T(8,128)(2,1)S(1)}, u32[]{:S(2)}, u32[]{:S(2)}) collective-permute-start(bf16[384,1536]{1,0:T(8,128)(2,1)} %get-tuple-element.24), channel_id=1, source_target_pairs={{0,385},{1,128},{2,387},{3,130},{4,389},{5,132},{6,391},{7,134},{1... | collective-permute-start | bytes 3538952 | tf_op jit(solution)/shard_map/ppermute | solution.py:263
  16.1 18.5 %collective-permute-start = (bf16[7,128,384]{2,1,0:T(8,128)(2,1)}, bf16[7,128,384]{2,1,0:T(8,128)(2,1)S(1)}, u32[]{:S(2)}, u32[]{:S(2)}) collective-permute-start(bf16[7,128,384]{2,1,0:T(8,128)(2,1)} %get-tuple-element.20), channel_id=1, source_target_pairs={{0,6},{1,3},{2,0},{3,5},{4,2},{5,7},{6,4},{7,1},{8,14},{9,11},{10,... | collective-permute-start | bytes 2064392 | tf_op jit(solution)/shard_map/ppermute | solution.py:265
  20.5 19.0 %collective-permute-start.1 = (bf16[7,128,384]{2,1,0:T(8,128)(2,1)}, bf16[7,128,384]{2,1,0:T(8,128)(2,1)S(1)}, u32[]{:S(2)}, u32[]{:S(2)}) collective-permute-start(bf16[7,128,384]{2,1,0:T(8,128)(2,1)} %get-tuple-element.21), channel_id=1, source_target_pairs={{0,2},{1,7},{2,4},{3,1},{4,6},{5,3},{6,0},{7,5},{8,10},{9,15},{10,... | collective-permute-start | bytes 2064392 | tf_op jit(solution)/shard_map/ppermute | solution.py:264
  22.4 24.6 %collective-permute-start.5 = (bf16[192,1536]{1,0:T(8,128)(2,1)}, bf16[192,1536]{1,0:T(8,128)(2,1)S(1)}, u32[]{:S(2)}, u32[]{:S(2)}) collective-permute-start(bf16[192,1536]{1,0:T(8,128)(2,1)} %get-tuple-element.25), channel_id=1, source_target_pairs={{0,1},{1,0},{2,3},{3,2},{4,5},{5,4},{6,7},{7,6},{8,9},{9,8},{10,11... | collective-permute-start | bytes 1769480 | tf_op jit(solution)/shard_map/ppermute | solution.py:266
  24.3 20.6 %collective-permute-start.6 = (bf16[1,128,1536]{2,1,0:T(8,128)(2,1)S(1)}, bf16[1,128,1536]{2,1,0:T(8,128)(2,1)S(1)}, u32[]{:S(2)}, u32[]{:S(2)}) collective-permute-start(bf16[1,128,1536]{2,1,0:T(8,128)(2,1)S(1)} %copy-done.3), channel_id=1, source_target_pairs={{0,8},{8,16},{16,24},{24,32},{32,40},{40,48},{48,56},{56,64},{64,7... | collective-permute-start | bytes 1179656 | tf_op jit(solution)/shard_map/ppermute | solution.py:267
  39.5 8.2 %collective-permute-start.2 = (bf16[3,128,384]{2,1,0:T(8,128)(2,1)S(1)}, bf16[3,128,384]{2,1,0:T(8,128)(2,1)S(1)}, u32[]{:S(2)}, u32[]{:S(2)}) collective-permute-start(bf16[3,128,384]{2,1,0:T(8,128)(2,1)S(1)} %get-tuple-element.22), channel_id=1, source_target_pairs={{0,6},{1,3},{2,0},{3,5},{4,2},{5,7},{6,4},{7,1},{8,14},{9,11},{10,... | collective-permute-start | bytes 884744 | tf_op jit(solution)/shard_map/ppermute | solution.py:270
  41.5 9.4 %collective-permute-start.3 = (bf16[3,128,384]{2,1,0:T(8,128)(2,1)S(1)}, bf16[3,128,384]{2,1,0:T(8,128)(2,1)S(1)}, u32[]{:S(2)}, u32[]{:S(2)}) collective-permute-start(bf16[3,128,384]{2,1,0:T(8,128)(2,1)S(1)} %get-tuple-element.23), channel_id=1, source_target_pairs={{0,2},{1,7},{2,4},{3,1},{4,6},{5,3},{6,0},{7,5},{8,10},{9,15},{10,... | collective-permute-start | bytes 884744 | tf_op jit(solution)/shard_map/ppermute | solution.py:271
  44.8 6.1 %copy-start = (bf16[1,1536,576]{1,2,0:T(8,128)(2,1)S(1)}, bf16[1,1536,576]{1,2,0:T(8,128)(2,1)}, u32[]{:S(2)}) copy-start(bf16[1,1536,576]{1,2,0:T(8,128)(2,1)} %param.8) | copy-start | bytes 5308420
  44.9 14.1 %collective-permute-start.9 = (bf16[3,2,128,384]{3,2,1,0:T(8,128)(2,1)S(1)}, bf16[3,2,128,384]{3,2,1,0:T(8,128)(2,1)S(1)}, u32[]{:S(2)}, u32[]{:S(2)}) collective-permute-start(bf16[3,2,128,384]{3,2,1,0:T(8,128)(2,1)S(1)} %shard_map.89), channel_id=1, source_target_pairs={{0,1},{1,0},{2,3},{3,2},{4,5},{5,4},{6,7},{7,6},{8,9},{9,8},{10,11... | collective-permute-start | bytes 1769480 | tf_op jit(solution)/shard_map/ppermute | solution.py:273
  53.5 16.8 %copy-start.2 = (f32[1,1536]{1,0:T(1,128)S(1)}, f32[1,1536]{1,0:T(1,128)}, u32[]{:S(2)}) copy-start(f32[1,1536]{1,0:T(1,128)} %g_ref.1) | copy-start | bytes 18436
  53.5 13.6 %collective-permute-start.8 = (bf16[6,128,384]{2,1,0:T(8,128)(2,1)S(1)}, bf16[6,128,384]{2,1,0:T(8,128)(2,1)S(1)}, u32[]{:S(2)}, u32[]{:S(2)}) collective-permute-start(bf16[6,128,384]{2,1,0:T(8,128)(2,1)S(1)} %get-tuple-element.28), channel_id=1, source_target_pairs={{0,6},{1,3},{2,0},{3,5},{4,2},{5,7},{6,4},{7,1},{8,14},{9,11},{10,... | collective-permute-start | bytes 1769480 | tf_op jit(solution)/shard_map/ppermute | solution.py:284
  55.5 14.8 %collective-permute-start.7 = (bf16[6,128,384]{2,1,0:T(8,128)(2,1)S(1)}, bf16[6,128,384]{2,1,0:T(8,128)(2,1)S(1)}, u32[]{:S(2)}, u32[]{:S(2)}) collective-permute-start(bf16[6,128,384]{2,1,0:T(8,128)(2,1)S(1)} %get-tuple-element.27), channel_id=1, source_target_pairs={{0,2},{1,7},{2,4},{3,1},{4,6},{5,3},{6,0},{7,5},{8,10},{9,15},{10,... | collective-permute-start | bytes 1769480 | tf_op jit(solution)/shard_map/ppermute | solution.py:283
  59.1 10.6 %collective-permute-start.10 = (bf16[2,128,384]{2,1,0:T(8,128)(2,1)S(1)}, bf16[2,128,384]{2,1,0:T(8,128)(2,1)S(1)}, u32[]{:S(2)}, u32[]{:S(2)}) collective-permute-start(bf16[2,128,384]{2,1,0:T(8,128)(2,1)S(1)} %shard_map.90), channel_id=1, source_target_pairs={{0,1},{1,0},{2,3},{3,2},{4,5},{5,4},{6,7},{7,6},{8,9},{9,8},{10,11... | collective-permute-start | bytes 589832 | tf_op jit(solution)/shard_map/ppermute | solution.py:275
  67.2 29.7 %collective-permute-start.15 = (bf16[3,128,384]{2,1,0:T(8,128)(2,1)S(1)}, bf16[3,128,384]{2,1,0:T(8,128)(2,1)S(1)}, u32[]{:S(2)}, u32[]{:S(2)}) collective-permute-start(bf16[3,128,384]{2,1,0:T(8,128)(2,1)S(1)} %get-tuple-element.34), channel_id=1, source_target_pairs={{0,4},{1,5},{2,6},{3,7},{4,0},{5,1},{6,2},{7,3},{8,12},{9,13},{10,... | collective-permute-start | bytes 884744 | tf_op jit(solution)/shard_map/ppermute | solution.py:286
  74.8 16.9 %collective-permute-start.11 = (bf16[128,384]{1,0:T(8,128)(2,1)S(1)}, bf16[128,384]{1,0:T(8,128)(2,1)S(1)}, u32[]{:S(2)}, u32[]{:S(2)}) collective-permute-start(bf16[128,384]{1,0:T(8,128)(2,1)S(1)} %get-tuple-element.29), channel_id=1, source_target_pairs={{0,8},{1,9},{2,10},{3,11},{4,12},{5,13},{6,14},{7,15},{8,16},{9,17... | collective-permute-start | bytes 294920 | tf_op jit(solution)/shard_map/ppermute | solution.py:302
  83.1 8.5 %collective-permute-start.12 = (bf16[128,384]{1,0:T(8,128)(2,1)S(1)}, bf16[128,384]{1,0:T(8,128)(2,1)S(1)}, u32[]{:S(2)}, u32[]{:S(2)}) collective-permute-start(bf16[128,384]{1,0:T(8,128)(2,1)S(1)} %get-tuple-element.30), channel_id=1, source_target_pairs={{0,14},{1,11},{2,8},{3,13},{4,10},{5,15},{6,12},{7,9},{8,22},{9,19... | collective-permute-start | bytes 294920 | tf_op jit(solution)/shard_map/ppermute | solution.py:302
  85.1 7.4 %collective-permute-start.13 = (bf16[128,384]{1,0:T(8,128)(2,1)S(1)}, bf16[128,384]{1,0:T(8,128)(2,1)S(1)}, u32[]{:S(2)}, u32[]{:S(2)}) collective-permute-start(bf16[128,384]{1,0:T(8,128)(2,1)S(1)} %get-tuple-element.31), channel_id=1, source_target_pairs={{0,12},{1,13},{2,14},{3,15},{4,8},{5,9},{6,10},{7,11},{8,20},{9,21... | collective-permute-start | bytes 294920 | tf_op jit(solution)/shard_map/ppermute | solution.py:302
  88.9 7.1 %collective-permute-start.14 = (bf16[128,384]{1,0:T(8,128)(2,1)S(1)}, bf16[128,384]{1,0:T(8,128)(2,1)S(1)}, u32[]{:S(2)}, u32[]{:S(2)}) collective-permute-start(bf16[128,384]{1,0:T(8,128)(2,1)S(1)} %get-tuple-element.32), channel_id=1, source_target_pairs={{0,10},{1,15},{2,12},{3,9},{4,14},{5,11},{6,8},{7,13},{8,18},{9,23... | collective-permute-start | bytes 294920 | tf_op jit(solution)/shard_map/ppermute | solution.py:302

commit v5 on v3

--- a/solution.py
+++ b/solution.py
@@ -60,40 +60,56 @@
     )
 
 
-def norm_body(h_ref, g_ref, b_ref, m_ref, s_ref, w_ref, own, b1, b2, b3, lead, rest):
-    x, z = where_am_i()
+def slot(x, z, j):
+    return (x + (1 - 2 * z) * j + 4) % 4
+
+
+def norm_body(h_hbm, g_hbm, b_hbm, m_hbm, s_hbm, o_ref, *scratch):
+    h_ref, g_ref, b_ref, m_ref, s_ref, *sems = scratch
+    copies = [
+        pltpu.make_async_copy(src, dst, sem)
+        for src, dst, sem in zip(
+            (h_hbm, g_hbm, b_hbm, m_hbm, s_hbm), (h_ref, g_ref, b_ref, m_ref, s_ref), sems
+        )
+    ]
+    for copy in copies:
+        copy.start()
+    for copy in copies[:4]:
+        copy.wait()
     h = h_ref[0].astype(F32)
     inverse = lax.rsqrt(jnp.mean(h * h, axis=-1, keepdims=True) + 1e-06)
     mask = jnp.broadcast_to(m_ref[...].astype(F32), (ROWS, ROWS)).T[:, :1]
     normed = (h * inverse * g_ref[...] + mask * b_ref[...]).astype(BF)
-    for j, bundle in enumerate((own, b1, b2, b3)):
+    for x in range(4):
         for g in range(4):
-            bundle[g] = normed[:, UNIT * g : UNIT * (g + 1)]
-        group = ((x + (1 - 2 * z) * j + 4) % 4) ^ 1
-        cols = pl.ds(pl.multiple_of(UNIT * group, UNIT), UNIT)
-        bundle[4] = s_ref[0, 0, :, cols]
-        bundle[5] = s_ref[0, 1, :, cols]
-    lead[...] = w_ref[pl.ds(pl.multiple_of(HALF * z, HALF), UNIT), :]
-    rest[...] = w_ref[pl.ds(pl.multiple_of(UNIT * (1 - z), HALF), HALF), :]
-
-
-def near_body(t0, t1, t3, o_ref):
-    for i, ref in enumerate((t0, t1, t3)):
-        o_ref[i] = ref[4:6]
-
-
-def far_body(t2, o_ref):
-    o_ref[...] = t2[4:6]
-
-
-def project_body(t0, t1, t2, t3, w_ref, v_ref, u_ref, early, front_o, back_o, opp_o, keep_o, both):
+            o_ref[x, g] = normed[:, UNIT * g : UNIT * (g + 1)]
+    copies[4].wait()
+    for x in range(4):
+        for kv in range(2):
+            o_ref[x, 4 + kv] = s_ref[0, kv, :, UNIT * (x ^ 1) : UNIT * ((x ^ 1) + 1)]
+
+
+def kept_body(t_ref, o_ref):
+    for x in range(4):
+        o_ref[x] = t_ref[x, 4:6]
+
+
+def project_body(t_ref, w_ref, n_ref, p_ref, early, front_o, back_o, opp_o, keep_o, other, both):
     del early
-    _, z = where_am_i()
+    x, z = where_am_i()
+    other[: D * 3 // 16] = n_ref[...]
+    other[D * 3 // 16 :] = p_ref[...]
     mine = w_ref[pl.ds(pl.multiple_of(UNIT * (1 - z), HALF), HALF), :]
     both[pl.ds(pl.multiple_of(HALF * z, HALF), HALF), :] = mine
-    both[pl.ds(pl.multiple_of(HALF * (1 - z), HALF), HALF), :] = u_ref[...]
+    both[pl.ds(pl.multiple_of(HALF * (1 - z), HALF), HALF), :] = other[
+        pl.ds(pl.multiple_of(UNIT * z, HALF), HALF), :
+    ]
     tokens = jnp.concatenate(
-        [jnp.concatenate([b[g] for g in range(4)], axis=1) for b in (t0, t1, t2, t3)], axis=0
+        [
+            jnp.concatenate([t_ref[slot(x, z, j), g] for g in range(4)], axis=1)
+            for j in range(4)
+        ],
+        axis=0,
     )
 
     def product(weight):
@@ -102,7 +118,7 @@
 
     front = product(w_ref[pl.ds(pl.multiple_of(HALF * z, HALF), UNIT), :])
     mid = product(both[...])
-    back = product(v_ref[...])
+    back = product(other[pl.ds(pl.multiple_of(HALF * (1 - z), HALF), UNIT), :])
     for j in range(4):
         front_o[j] = front[j]
         back_o[j] = back[j]
@@ -127,9 +143,9 @@
     return q, k, v
 
 
-def attend_body(m_ref, a_ref, b_ref, t0, t1, t2, t3, pn_ref, pf_ref, g_ref, *o_refs):
-    x, z = where_am_i()
-    gates = g_ref[pl.ds(x ^ 1, 1), :]
+def attend_body(m_ref, a_ref, b_ref, t_ref, p_ref, g_ref, *o_refs):
+    x, z = where_am_i()
+    gates = g_ref[:, pl.ds(pl.multiple_of(UNIT * (x ^ 1), UNIT), UNIT)]
     roled = roles(x, z)
     for head in range(3):
         cols = slice(HEAD_DIM * head, HEAD_DIM * (head + 1))
@@ -141,9 +157,8 @@
             return jnp.where(index == 0, own, jnp.where(index == 1, behind, ahead))
 
         kept = [
-            [t[4 + kv, :, cols] for t in (t0, t1, t2, t3)]
-            + [pn_ref[i, kv, :, cols] for i in range(3)]
-            + [pf_ref[kv, :, cols]]
+            [t_ref[slot(x, z, j), 4 + kv, :, cols] for j in range(4)]
+            + [p_ref[j, kv, :, cols] for j in range(4)]
             for kv in range(2)
         ]
         for j in range(4):
@@ -164,7 +179,8 @@
             o_refs[j][:, cols] = (gates[:, cols] * (summed / total)).astype(BF)
 
 
-def fresh_body(k_ref, a_ref, b_ref, p_ref, f_ref):
+def fresh_body(k_ref, a_ref, b_ref, p_ref, after, f_ref):
+    del after
     x, z = where_am_i()
     rows = (
         (0, (k_ref.at[4], k_ref.at[0], k_ref.at[5])),
@@ -173,7 +189,7 @@
         (3, (a_ref.at[1], a_ref.at[4], a_ref.at[5])),
     )
     for j, refs in rows:
-        source = (x + (1 - 2 * z) * j + 4) % 4
+        source = slot(x, z, j)
         for unit, ref in zip((2 * z, 1, 2 - 2 * z), refs):
             g = 3 * source + unit
 
@@ -186,7 +202,7 @@
 def finish_body(a0, a1, a2, a3, h_ref, o_ref):
     x, z = where_am_i()
     for j, ref in enumerate((a0, a1, a2, a3)):
-        group = ((x + (1 - 2 * z) * j + 4) % 4) ^ 1
+        group = (slot(x, z, j)) ^ 1
         cols = pl.ds(pl.multiple_of(UNIT * group, UNIT), UNIT)
         o_ref[0, :, cols] = (h_ref[0, :, cols].astype(F32) + ref[...].astype(F32)).astype(BF)
 
@@ -198,40 +214,46 @@
     def blocks(*lead):
         return jax.ShapeDtypeStruct((*lead, ROWS, UNIT), BF)
 
-    def rows(count):
-        return jax.ShapeDtypeStruct((count, D), BF)
-
     weight = jnp.swapaxes(w_qkv[0], 0, 1)
-    t0, b1, b2, b3, lead, rest = call(
-        norm_body, (blocks(6), blocks(6), blocks(6), blocks(6), rows(UNIT), rows(HALF)), 6
-    )(hidden, norm_gain, box_vec, box_mask, stale_kv, weight)
-    lead = lax.ppermute(lead, ("dp", "patch"), far_pairs(parts))
-    t3 = lax.ppermute(b1, "patch", x_pairs(1))
-    t1 = lax.ppermute(b3, "patch", x_pairs(3))
-    t2 = lax.ppermute(b2, "patch", x_pairs(2))
-    rest = lax.ppermute(rest, "patch", partner_pairs())
+    packed = pl.pallas_call(
+        norm_body,
+        out_shape=blocks(4, 6),
+        in_specs=[pl.BlockSpec(memory_space=pltpu.HBM)] * 5,
+        out_specs=VM,
+        scratch_shapes=[
+            pltpu.VMEM((1, ROWS, D), BF),
+            pltpu.VMEM((1, D), F32),
+            pltpu.VMEM((1, D), F32),
+            pltpu.VMEM((1, ROWS), jnp.int32),
+            pltpu.VMEM((1, 2, ROWS, D), BF),
+        ]
+        + [pltpu.SemaphoreType.DMA] * 5,
+        compiler_params=pltpu.CompilerParams(vmem_limit_bytes=60 * 1024 * 1024),
+    )(hidden, norm_gain, box_vec, box_mask, stale_kv)
+    came = lax.all_to_all(
+        packed, "patch", 0, 0, axis_index_groups=[[0, 2, 4, 6], [1, 3, 5, 7]]
+    )
+    half = weight.shape[0] // 2
+    first = lax.ppermute(weight[:half], ("dp", "patch"), far_pairs(parts))
+    second = lax.ppermute(weight[half:], "patch", partner_pairs())
     before = lax.ppermute(hidden, "segment", [(i, (i + 1) % segments) for i in range(segments)])
-
-    near = call(near_body, blocks(3, 2), 3)(t0, t1, t3)
-    near = lax.ppermute(near, "patch", partner_pairs())
-    far = call(far_body, blocks(2), 1)(t2)
-    far = lax.ppermute(far, "patch", partner_pairs())
+    kept = call(kept_body, blocks(4, 2), 1)(came)
+    kept = lax.ppermute(kept, "patch", partner_pairs())
 
     front, back, opposite, keep = call(
         project_body,
         (blocks(6), blocks(6), blocks(3), blocks(6)),
-        8,
-        scratch_shapes=[pltpu.VMEM((UNIT, D), BF)],
-    )(t0, t1, t2, t3, weight, lead, rest, before)
+        5,
+        scratch_shapes=[pltpu.VMEM((2 * half, D), BF), pltpu.VMEM((UNIT, D), BF)],
+    )(came, weight, first, second, before)
     front = lax.ppermute(front, "patch", x_pairs(1))
     back = lax.ppermute(back, "patch", x_pairs(3))
+    opposite, mark = lax.optimization_barrier((opposite, back[0, :16, :128]))
     opposite = lax.ppermute(opposite, "patch", x_pairs(2))
 
-    out = call(attend_body, (blocks(),) * 4, 10)(
-        keep, front, back, t0, t1, t2, t3, near, far, gate.reshape(4, UNIT)
-    )
-    fresh = call(fresh_body, jax.ShapeDtypeStruct((1, 2, ROWS, D), BF), 4)(
-        keep, front, back, opposite
+    out = call(attend_body, (blocks(),) * 4, 6)(keep, front, back, came, kept, gate)
+    fresh = call(fresh_body, jax.ShapeDtypeStruct((1, 2, ROWS, D), BF), 5)(
+        keep, front, back, opposite, mark
     )
 
     came = []

time: 110 us -> 102 us (0.927)
  the two profiles are of different devices: /device:TPU:1 before, /device:TPU:25 now
where the time goes in v5:
time: 102 us; the launch traced here: 101 us
  starting transfers between devices  51.9 us (51%)
  waiting for transfers between devices  29.4 us (29%)
  Pallas kernels  12.2 us (12%)
  local copies, waits for them, and re-layouts  7.27 us (7%)
    ppermute x4, starting transfers between devices, local(): came.append(lax.ppermute(out[j], ('segment', 'patch'), pairs))  18.9 us
    ppermute x1, starting transfers between devices, local(): first = lax.ppermute(weight[:half], ('dp', 'patch'), far_pairs(parts))  10.7 us
    ppermute x1, waiting for transfers between devices, local(): first = lax.ppermute(weight[:half], ('dp', 'patch'), far_pairs(parts))  8.74 us
    ppermute x1, waiting for transfers between devices, local(): back = lax.ppermute(back, 'patch', x_pairs(3))  6.02 us
    unnamed x14, local copies, waits for them, and re-layouts  5.67 us
    ppermute x1, waiting for transfers between devices, local(): lax.ppermute(hidden, 'segment', [(i, (i + 1) % segments) for i in range(s...  4.72 us
    pallas_call x1, Pallas kernels, local(): call(attend_body, (blocks(),) * 4, 6)(keep, front, back, came, kept, gate)  4.5 us
    ppermute x4, waiting for transfers between devices, local(): came.append(lax.ppermute(out[j], ('segment', 'patch'), pairs))  4.38 us
  transfers between devices with their start and end apart: 12, of which 8 were waited for; matrix products, arithmetic and copies ran while one was open for 2% of the time, Pallas kernels for 6%

profile of v5, /device:TPU:25, one launch (start us, length us, event | category | flops | bytes accessed | tf_op | source)
XLA Modules:
  0.0 101.5 jit_solution(5445289967949470507)
XLA Ops:
  0.6 2.9 %shard_map.86 = bf16[4,6,128,384]{3,2,1,0:T(8,128)(2,1)} custom-call(bf16[1,128,1536]{2,1,0:T(8,128)(2,1)} %h_hbm.1, f32[1,1536]{1,0:T(1,128)} %g_hbm.1, f32[1,1536]{1,0:T(1,128)} %b_hbm.1, s32[1,128]{1,0:T(1,128)} %m_hbm.1, bf16[1,2,128,1536]{3,2,1,0:T(8,128)(2,1)} %s_hbm.1), custom_call_target="tpu_custom_call" | custom-call | tf_op jit(solution)/shard_map/pallas_call | solution.py:218
  3.6 4.0 %all-to-all-start = ((bf16[4,6,128,384]{3,2,1,0:T(8,128)(2,1)}), bf16[4,6,128,384]{3,2,1,0:T(8,128)(2,1)S(1)}, u32[]{:S(2)}, u32[]{:S(2)}) async-start(bf16[4,6,128,384]{3,2,1,0:T(8,128)(2,1)} %shard_map.86), calls=%async_computation | async-start | bytes 4718592 | tf_op jit(solution)/shard_map/all_to_all | solution.py:233
  7.6 1.6 %fusion = (bf16[288,1536]{1,0:T(8,128)(2,1)S(1)}, bf16[288,1536]{1,0:T(8,128)(2,1)S(1)}) fusion(bf16[576,1536]{1,0:T(8,128)(2,1)} %bitcast.5), kind=kLoop, calls=%fused_computation.1 | loop fusion | bytes 3538944 | tf_op jit(solution)/shard_map/slice | solution.py:238
  9.2 10.7 %collective-permute-start = (bf16[288,1536]{1,0:T(8,128)(2,1)S(1)}, bf16[288,1536]{1,0:T(8,128)(2,1)S(1)}, u32[]{:S(2)}, u32[]{:S(2)}) collective-permute-start(bf16[288,1536]{1,0:T(8,128)(2,1)S(1)} %get-tuple-element.23), channel_id=1, source_target_pairs={{0,385},{1,128},{2,387},{3,130},{4,389},{5,132},{6,391},{7,134},{1... | collective-permute-start | bytes 2654216 | tf_op jit(solution)/shard_map/ppermute | solution.py:237
  19.9 1.9 %collective-permute-start.1 = (bf16[288,1536]{1,0:T(8,128)(2,1)S(1)}, bf16[288,1536]{1,0:T(8,128)(2,1)S(1)}, u32[]{:S(2)}, u32[]{:S(2)}) collective-permute-start(bf16[288,1536]{1,0:T(8,128)(2,1)S(1)} %get-tuple-element.22), channel_id=1, source_target_pairs={{0,1},{1,0},{2,3},{3,2},{4,5},{5,4},{6,7},{7,6},{8,9},{9,8},{10,11... | collective-permute-start | bytes 2654216 | tf_op jit(solution)/shard_map/ppermute | solution.py:238
  21.8 3.6 %collective-permute-start.2 = (bf16[1,128,1536]{2,1,0:T(8,128)(2,1)S(1)}, bf16[1,128,1536]{2,1,0:T(8,128)(2,1)S(1)}, u32[]{:S(2)}, u32[]{:S(2)}) collective-permute-start(bf16[1,128,1536]{2,1,0:T(8,128)(2,1)S(1)} %copy-done.6), channel_id=1, source_target_pairs={{0,8},{8,16},{16,24},{24,32},{32,40},{40,48},{48,56},{56,64},{64,7... | collective-permute-start | bytes 1179656 | tf_op jit(solution)/shard_map/ppermute | solution.py:239
  25.5 4.7 %collective-permute-done.2.early.h_ref = bf16[1,128,1536]{2,1,0:T(8,128)(2,1)S(1)} collective-permute-done((bf16[1,128,1536]{2,1,0:T(8,128)(2,1)S(1)}, bf16[1,128,1536]{2,1,0:T(8,128)(2,1)S(1)}, u32[]{:S(2)}, u32[]{:S(2)}) %collective-permute-start.2) | collective-permute-done | bytes 393248 | tf_op jit(solution)/shard_map/ppermute | solution.py:239
  30.2 8.7 %collective-permute-done.n_ref = bf16[288,1536]{1,0:T(8,128)(2,1)S(1)} collective-permute-done((bf16[288,1536]{1,0:T(8,128)(2,1)S(1)}, bf16[288,1536]{1,0:T(8,128)(2,1)S(1)}, u32[]{:S(2)}, u32[]{:S(2)}) %collective-permute-start) | collective-permute-done | bytes 884768 | tf_op jit(solution)/shard_map/ppermute | solution.py:237
  38.9 0.9 copy-done.1
  39.9 1.8 %collective-permute-done.1.p_ref = bf16[288,1536]{1,0:T(8,128)(2,1)S(1)} collective-permute-done((bf16[288,1536]{1,0:T(8,128)(2,1)S(1)}, bf16[288,1536]{1,0:T(8,128)(2,1)S(1)}, u32[]{:S(2)}, u32[]{:S(2)}) %collective-permute-start.1) | collective-permute-done | bytes 884768 | tf_op jit(solution)/shard_map/ppermute | solution.py:238
  41.7 0.9 copy-done.3
  42.6 1.5 %copy-done = bf16[1,1536,576]{1,2,0:T(8,128)(2,1)S(1)} copy-done((bf16[1,1536,576]{1,2,0:T(8,128)(2,1)S(1)}, bf16[1,1536,576]{1,2,0:T(8,128)(2,1)}, u32[]{:S(2)}) %copy-start) | copy-done | bytes 1769496
  44.1 1.2 %copy-done.2 = bf16[288,1536]{1,0:T(8,128)(2,1)S(1)} copy-done((bf16[288,1536]{1,0:T(8,128)(2,1)S(1)}, bf16[288,1536]{1,0:T(8,128)(2,1)}, u32[]{:S(2)}) %copy-start.2) | copy-done | bytes 884760
  45.3 1.2 %copy-done.4 = bf16[288,1536]{1,0:T(8,128)(2,1)S(1)} copy-done((bf16[288,1536]{1,0:T(8,128)(2,1)S(1)}, bf16[288,1536]{1,0:T(8,128)(2,1)}, u32[]{:S(2)}) %copy-start.4) | copy-done | bytes 884760
  46.4 2.7 %shard_map.87 = (bf16[6,128,384]{2,1,0:T(8,128)(2,1)S(1)}, bf16[6,128,384]{2,1,0:T(8,128)(2,1)S(1)}, bf16[3,128,384]{2,1,0:T(8,128)(2,1)S(1)}, bf16[6,128,384]{2,1,0:T(8,128)(2,1)S(1)}) custom-call(bf16[4,6,128,384]{3,2,1,0:T(8,128)(2,1)S(1)} %all-to-all-done.t_ref, bf16[576,1536]{1,0:T(8,128)(2,1)S(1)} %bitcast.6, bf16[288,1536]{1,0:T(8,128)(2,1)S(1)} %copy-done.2, ...), custom_call_target="tpu_custom_call" | custom-call | tf_op jit(solution)/shard_map/pallas_call | solution.py:243
  49.1 4.3 %collective-permute-start.4 = (bf16[6,128,384]{2,1,0:T(8,128)(2,1)S(1)}, bf16[6,128,384]{2,1,0:T(8,128)(2,1)S(1)}, u32[]{:S(2)}, u32[]{:S(2)}) collective-permute-start(bf16[6,128,384]{2,1,0:T(8,128)(2,1)S(1)} %get-tuple-element.14), channel_id=1, source_target_pairs={{0,6},{1,3},{2,0},{3,5},{4,2},{5,7},{6,4},{7,1},{8,14},{9,11},{10,... | collective-permute-start | bytes 1769480 | tf_op jit(solution)/shard_map/ppermute | solution.py:250
  53.4 0.1 shard_map.88
  53.5 1.9 %collective-permute-start.5 = (bf16[4,2,128,384]{3,2,1,0:T(8,128)(2,1)S(1)}, bf16[4,2,128,384]{3,2,1,0:T(8,128)(2,1)S(1)}, u32[]{:S(2)}, u32[]{:S(2)}) collective-permute-start(bf16[4,2,128,384]{3,2,1,0:T(8,128)(2,1)S(1)} %shard_map.88), channel_id=1, source_target_pairs={{0,1},{1,0},{2,3},{3,2},{4,5},{5,4},{6,7},{7,6},{8,9},{9,8},{10,11... | collective-permute-start | bytes 2359304 | tf_op jit(solution)/shard_map/ppermute | solution.py:241
  55.4 2.2 %collective-permute-start.3 = (bf16[6,128,384]{2,1,0:T(8,128)(2,1)S(1)}, bf16[6,128,384]{2,1,0:T(8,128)(2,1)S(1)}, u32[]{:S(2)}, u32[]{:S(2)}) collective-permute-start(bf16[6,128,384]{2,1,0:T(8,128)(2,1)S(1)} %get-tuple-element.13), channel_id=1, source_target_pairs={{0,2},{1,7},{2,4},{3,1},{4,6},{5,3},{6,0},{7,5},{8,10},{9,15},{10,... | collective-permute-start | bytes 1769480 | tf_op jit(solution)/shard_map/ppermute | solution.py:249
  57.6 6.0 %collective-permute-done.4.b_ref = bf16[6,128,384]{2,1,0:T(8,128)(2,1)S(1)} collective-permute-done((bf16[6,128,384]{2,1,0:T(8,128)(2,1)S(1)}, bf16[6,128,384]{2,1,0:T(8,128)(2,1)S(1)}, u32[]{:S(2)}, u32[]{:S(2)}) %collective-permute-start.4) | collective-permute-done | bytes 589856 | tf_op jit(solution)/shard_map/ppermute | solution.py:250
  63.7 4.3 %collective-permute-start.10 = (bf16[3,128,384]{2,1,0:T(8,128)(2,1)S(1)}, bf16[3,128,384]{2,1,0:T(8,128)(2,1)S(1)}, u32[]{:S(2)}, u32[]{:S(2)}) collective-permute-start(bf16[3,128,384]{2,1,0:T(8,128)(2,1)S(1)} %get-tuple-element.20), channel_id=1, source_target_pairs={{0,4},{1,5},{2,6},{3,7},{4,0},{5,1},{6,2},{7,3},{8,12},{9,13},{10,... | collective-permute-start | bytes 884744 | tf_op jit(solution)/shard_map/ppermute | solution.py:252
  68.0 3.5 %collective-permute-done.3.a_ref = bf16[6,128,384]{2,1,0:T(8,128)(2,1)S(1)} collective-permute-done((bf16[6,128,384]{2,1,0:T(8,128)(2,1)S(1)}, bf16[6,128,384]{2,1,0:T(8,128)(2,1)S(1)}, u32[]{:S(2)}, u32[]{:S(2)}) %collective-permute-start.3) | collective-permute-done | bytes 589856 | tf_op jit(solution)/shard_map/ppermute | solution.py:249
  71.4 0.3 collective-permute-done.5.p_ref
  71.7 4.5 %shard_map.89 = (bf16[128,384]{1,0:T(8,128)(2,1)S(1)}, bf16[128,384]{1,0:T(8,128)(2,1)S(1)}, bf16[128,384]{1,0:T(8,128)(2,1)S(1)}, bf16[128,384]{1,0:T(8,128)(2,1)S(1)}) custom-call(bf16[6,128,384]{2,1,0:T(8,128)(2,1)S(1)} %get-tuple-element.12.m_ref.k_ref, bf16[6,128,384]{2,1,0:T(8,128)(2,1)S(1)} %collective-permute-done.3.a_ref, ...), custom_call_target="tpu_custom_call" | custom-call | tf_op jit(solution)/shard_map/pallas_call | solution.py:254
  76.2 11.3 %collective-permute-start.6 = (bf16[128,384]{1,0:T(8,128)(2,1)S(1)}, bf16[128,384]{1,0:T(8,128)(2,1)S(1)}, u32[]{:S(2)}, u32[]{:S(2)}) collective-permute-start(bf16[128,384]{1,0:T(8,128)(2,1)S(1)} %get-tuple-element.15), channel_id=1, source_target_pairs={{0,8},{1,9},{2,10},{3,11},{4,12},{5,13},{6,14},{7,15},{8,16},{9,17... | collective-permute-start | bytes 294920 | tf_op jit(solution)/shard_map/ppermute | solution.py:266
  87.5 1.9 %collective-permute-start.7 = (bf16[128,384]{1,0:T(8,128)(2,1)S(1)}, bf16[128,384]{1,0:T(8,128)(2,1)S(1)}, u32[]{:S(2)}, u32[]{:S(2)}) collective-permute-start(bf16[128,384]{1,0:T(8,128)(2,1)S(1)} %get-tuple-element.16), channel_id=1, source_target_pairs={{0,14},{1,11},{2,8},{3,13},{4,10},{5,15},{6,12},{7,9},{8,22},{9,19... | collective-permute-start | bytes 294920 | tf_op jit(solution)/shard_map/ppermute | solution.py:266
  89.4 1.9 %collective-permute-start.8 = (bf16[128,384]{1,0:T(8,128)(2,1)S(1)}, bf16[128,384]{1,0:T(8,128)(2,1)S(1)}, u32[]{:S(2)}, u32[]{:S(2)}) collective-permute-start(bf16[128,384]{1,0:T(8,128)(2,1)S(1)} %get-tuple-element.17), channel_id=1, source_target_pairs={{0,12},{1,13},{2,14},{3,15},{4,8},{5,9},{6,10},{7,11},{8,20},{9,21... | collective-permute-start | bytes 294920 | tf_op jit(solution)/shard_map/ppermute | solution.py:266
  91.4 3.8 %collective-permute-start.9 = (bf16[128,384]{1,0:T(8,128)(2,1)S(1)}, bf16[128,384]{1,0:T(8,128)(2,1)S(1)}, u32[]{:S(2)}, u32[]{:S(2)}) collective-permute-start(bf16[128,384]{1,0:T(8,128)(2,1)S(1)} %get-tuple-element.18), channel_id=1, source_target_pairs={{0,10},{1,15},{2,12},{3,9},{4,14},{5,11},{6,8},{7,13},{8,18},{9,23... | collective-permute-start | bytes 294920 | tf_op jit(solution)/shard_map/ppermute | solution.py:266
  95.1 1.1 %shard_map.91 = bf16[1,2,128,1536]{3,2,1,0:T(8,128)(2,1)} custom-call(bf16[6,128,384]{2,1,0:T(8,128)(2,1)S(1)} %get-tuple-element.12.m_ref.k_ref, bf16[6,128,384]{2,1,0:T(8,128)(2,1)S(1)} %collective-permute-done.3.a_ref, bf16[6,128,384]{2,1,0:T(8,128)(2,1)S(1)} %collective-permute-done.4.b_ref, bf16[3,128,384]{2,1,0:T(8,128)(2,1)S(1)} %collective-permute-done.10.p_ref, ...), custom_call_target="tpu_custom_call" | custom-call | tf_op jit(solution)/shard_map/pallas_call | solution.py:255
  96.2 1.6 %collective-permute-done.8.a2 = bf16[128,384]{1,0:T(8,128)(2,1)S(1)} collective-permute-done((bf16[128,384]{1,0:T(8,128)(2,1)S(1)}, bf16[128,384]{1,0:T(8,128)(2,1)S(1)}, u32[]{:S(2)}, u32[]{:S(2)}) %collective-permute-start.8) | collective-permute-done | bytes 98336 | tf_op jit(solution)/shard_map/ppermute | solution.py:266
  97.8 2.8 %collective-permute-done.9.a3 = bf16[128,384]{1,0:T(8,128)(2,1)S(1)} collective-permute-done((bf16[128,384]{1,0:T(8,128)(2,1)S(1)}, bf16[128,384]{1,0:T(8,128)(2,1)S(1)}, u32[]{:S(2)}, u32[]{:S(2)}) %collective-permute-start.9) | collective-permute-done | bytes 98336 | tf_op jit(solution)/shard_map/ppermute | solution.py:266
  100.6 0.9 shard_map.90
  (14 shorter events, 0.0 us)
Async XLA Ops:
  3.6 39.0 %all-to-all-start = ((bf16[4,6,128,384]{3,2,1,0:T(8,128)(2,1)}), bf16[4,6,128,384]{3,2,1,0:T(8,128)(2,1)S(1)}, u32[]{:S(2)}, u32[]{:S(2)}) async-start(bf16[4,6,128,384]{3,2,1,0:T(8,128)(2,1)} %shard_map.86), calls=%async_computation | async-start | bytes 4718592 | tf_op jit(solution)/shard_map/all_to_all | solution.py:233
  7.6 14.2 %copy-start.6 = (bf16[1,128,1536]{2,1,0:T(8,128)(2,1)S(1)}, bf16[1,128,1536]{2,1,0:T(8,128)(2,1)}, u32[]{:S(2)}) copy-start(bf16[1,128,1536]{2,1,0:T(8,128)(2,1)} %h_hbm.1) | copy-start | bytes 1179652
  9.2 29.7 %collective-permute-start = (bf16[288,1536]{1,0:T(8,128)(2,1)S(1)}, bf16[288,1536]{1,0:T(8,128)(2,1)S(1)}, u32[]{:S(2)}, u32[]{:S(2)}) collective-permute-start(bf16[288,1536]{1,0:T(8,128)(2,1)S(1)} %get-tuple-element.23), channel_id=1, source_target_pairs={{0,385},{1,128},{2,387},{3,130},{4,389},{5,132},{6,391},{7,134},{1... | collective-permute-start | bytes 2654216 | tf_op jit(solution)/shard_map/ppermute | solution.py:237
  19.9 21.8 %collective-permute-start.1 = (bf16[288,1536]{1,0:T(8,128)(2,1)S(1)}, bf16[288,1536]{1,0:T(8,128)(2,1)S(1)}, u32[]{:S(2)}, u32[]{:S(2)}) collective-permute-start(bf16[288,1536]{1,0:T(8,128)(2,1)S(1)} %get-tuple-element.22), channel_id=1, source_target_pairs={{0,1},{1,0},{2,3},{3,2},{4,5},{5,4},{6,7},{7,6},{8,9},{9,8},{10,11... | collective-permute-start | bytes 2654216 | tf_op jit(solution)/shard_map/ppermute | solution.py:238
  21.8 8.4 %collective-permute-start.2 = (bf16[1,128,1536]{2,1,0:T(8,128)(2,1)S(1)}, bf16[1,128,1536]{2,1,0:T(8,128)(2,1)S(1)}, u32[]{:S(2)}, u32[]{:S(2)}) collective-permute-start(bf16[1,128,1536]{2,1,0:T(8,128)(2,1)S(1)} %copy-done.6), channel_id=1, source_target_pairs={{0,8},{8,16},{16,24},{24,32},{32,40},{40,48},{48,56},{56,64},{64,7... | collective-permute-start | bytes 1179656 | tf_op jit(solution)/shard_map/ppermute | solution.py:239
  38.9 0.9 copy-start.1
  41.7 0.9 copy-start.3
  42.6 1.5 %copy-start = (bf16[1,1536,576]{1,2,0:T(8,128)(2,1)S(1)}, bf16[1,1536,576]{1,2,0:T(8,128)(2,1)}, u32[]{:S(2)}) copy-start(bf16[1,1536,576]{1,2,0:T(8,128)(2,1)} %param.8) | copy-start | bytes 5308420
  44.1 1.2 %copy-start.2 = (bf16[288,1536]{1,0:T(8,128)(2,1)S(1)}, bf16[288,1536]{1,0:T(8,128)(2,1)}, u32[]{:S(2)}) copy-start(bf16[288,1536]{1,0:T(8,128)(2,1)} %copy-done.1) | copy-start | bytes 2654212
  45.3 1.2 %copy-start.4 = (bf16[288,1536]{1,0:T(8,128)(2,1)S(1)}, bf16[288,1536]{1,0:T(8,128)(2,1)}, u32[]{:S(2)}) copy-start(bf16[288,1536]{1,0:T(8,128)(2,1)} %copy-done.3) | copy-start | bytes 2654212
  49.1 22.6 %copy-start.5 = (f32[1,1536]{1,0:T(1,128)S(1)}, f32[1,1536]{1,0:T(1,128)}, u32[]{:S(2)}) copy-start(f32[1,1536]{1,0:T(1,128)} %g_ref.1) | copy-start | bytes 18436
  49.1 14.6 %collective-permute-start.4 = (bf16[6,128,384]{2,1,0:T(8,128)(2,1)S(1)}, bf16[6,128,384]{2,1,0:T(8,128)(2,1)S(1)}, u32[]{:S(2)}, u32[]{:S(2)}) collective-permute-start(bf16[6,128,384]{2,1,0:T(8,128)(2,1)S(1)} %get-tuple-element.14), channel_id=1, source_target_pairs={{0,6},{1,3},{2,0},{3,5},{4,2},{5,7},{6,4},{7,1},{8,14},{9,11},{10,... | collective-permute-start | bytes 1769480 | tf_op jit(solution)/shard_map/ppermute | solution.py:250
  53.5 18.2 %collective-permute-start.5 = (bf16[4,2,128,384]{3,2,1,0:T(8,128)(2,1)S(1)}, bf16[4,2,128,384]{3,2,1,0:T(8,128)(2,1)S(1)}, u32[]{:S(2)}, u32[]{:S(2)}) collective-permute-start(bf16[4,2,128,384]{3,2,1,0:T(8,128)(2,1)S(1)} %shard_map.88), channel_id=1, source_target_pairs={{0,1},{1,0},{2,3},{3,2},{4,5},{5,4},{6,7},{7,6},{8,9},{9,8},{10,11... | collective-permute-start | bytes 2359304 | tf_op jit(solution)/shard_map/ppermute | solution.py:241
  55.4 16.0 %collective-permute-start.3 = (bf16[6,128,384]{2,1,0:T(8,128)(2,1)S(1)}, bf16[6,128,384]{2,1,0:T(8,128)(2,1)S(1)}, u32[]{:S(2)}, u32[]{:S(2)}) collective-permute-start(bf16[6,128,384]{2,1,0:T(8,128)(2,1)S(1)} %get-tuple-element.13), channel_id=1, source_target_pairs={{0,2},{1,7},{2,4},{3,1},{4,6},{5,3},{6,0},{7,5},{8,10},{9,15},{10,... | collective-permute-start | bytes 1769480 | tf_op jit(solution)/shard_map/ppermute | solution.py:249
  63.7 31.5 %collective-permute-start.10 = (bf16[3,128,384]{2,1,0:T(8,128)(2,1)S(1)}, bf16[3,128,384]{2,1,0:T(8,128)(2,1)S(1)}, u32[]{:S(2)}, u32[]{:S(2)}) collective-permute-start(bf16[3,128,384]{2,1,0:T(8,128)(2,1)S(1)} %get-tuple-element.20), channel_id=1, source_target_pairs={{0,4},{1,5},{2,6},{3,7},{4,0},{5,1},{6,2},{7,3},{8,12},{9,13},{10,... | collective-permute-start | bytes 884744 | tf_op jit(solution)/shard_map/ppermute | solution.py:252
  76.2 20.0 %collective-permute-start.6 = (bf16[128,384]{1,0:T(8,128)(2,1)S(1)}, bf16[128,384]{1,0:T(8,128)(2,1)S(1)}, u32[]{:S(2)}, u32[]{:S(2)}) collective-permute-start(bf16[128,384]{1,0:T(8,128)(2,1)S(1)} %get-tuple-element.15), channel_id=1, source_target_pairs={{0,8},{1,9},{2,10},{3,11},{4,12},{5,13},{6,14},{7,15},{8,16},{9,17... | collective-permute-start | bytes 294920 | tf_op jit(solution)/shard_map/ppermute | solution.py:266
  87.5 8.7 %collective-permute-start.7 = (bf16[128,384]{1,0:T(8,128)(2,1)S(1)}, bf16[128,384]{1,0:T(8,128)(2,1)S(1)}, u32[]{:S(2)}, u32[]{:S(2)}) collective-permute-start(bf16[128,384]{1,0:T(8,128)(2,1)S(1)} %get-tuple-element.16), channel_id=1, source_target_pairs={{0,14},{1,11},{2,8},{3,13},{4,10},{5,15},{6,12},{7,9},{8,22},{9,19... | collective-permute-start | bytes 294920 | tf_op jit(solution)/shard_map/ppermute | solution.py:266
  89.4 8.4 %collective-permute-start.8 = (bf16[128,384]{1,0:T(8,128)(2,1)S(1)}, bf16[128,384]{1,0:T(8,128)(2,1)S(1)}, u32[]{:S(2)}, u32[]{:S(2)}) collective-permute-start(bf16[128,384]{1,0:T(8,128)(2,1)S(1)} %get-tuple-element.17), channel_id=1, source_target_pairs={{0,12},{1,13},{2,14},{3,15},{4,8},{5,9},{6,10},{7,11},{8,20},{9,21... | collective-permute-start | bytes 294920 | tf_op jit(solution)/shard_map/ppermute | solution.py:266
  91.4 9.3 %collective-permute-start.9 = (bf16[128,384]{1,0:T(8,128)(2,1)S(1)}, bf16[128,384]{1,0:T(8,128)(2,1)S(1)}, u32[]{:S(2)}, u32[]{:S(2)}) collective-permute-start(bf16[128,384]{1,0:T(8,128)(2,1)S(1)} %get-tuple-element.18), channel_id=1, source_target_pairs={{0,10},{1,15},{2,12},{3,9},{4,14},{5,11},{6,8},{7,13},{8,18},{9,23... | collective-permute-start | bytes 294920 | tf_op jit(solution)/shard_map/ppermute | solution.py:266

commit v6 on v5

--- a/solution.py
+++ b/solution.py
@@ -15,7 +15,11 @@
 F32 = jnp.float32
 NT = (((1,), (1,)), ((), ()))
 VM = pl.BlockSpec(memory_space=pltpu.VMEM)
-PARAMS = pltpu.CompilerParams(vmem_limit_bytes=16 * 1024 * 1024)
+HBM = pl.BlockSpec(memory_space=pltpu.HBM)
+ANY = pl.BlockSpec(memory_space=pl.ANY)
+MIB = 1024 * 1024
+PROJECT_ROOM = 50
+PLANES = [[0, 2, 4, 6], [1, 3, 5, 7]]
 
 
 def spot(x, z):
@@ -49,61 +53,74 @@
     return p // 2, p % 2
 
 
-def call(body, out, count, **more):
+def call(body, out, count, spec=VM, room=16, **more):
     return pl.pallas_call(
         body,
         out_shape=out,
-        in_specs=[VM] * count,
-        out_specs=jax.tree.map(lambda _: VM, out),
-        compiler_params=PARAMS,
+        in_specs=[spec] * count,
+        out_specs=jax.tree.map(lambda _: spec, out),
+        compiler_params=pltpu.CompilerParams(vmem_limit_bytes=room * MIB),
         **more,
     )
+
+
+class Copies:
+    def __init__(self, sems):
+        self.sems = sems
+        self.count = 0
+
+    def start(self, source, target):
+        copy = pltpu.make_async_copy(source, target, self.sems.at[self.count])
+        self.count += 1
+        copy.start()
+        return copy
+
+
+def wait_all(copies):
+    for copy in copies:
+        copy.wait()
 
 
 def slot(x, z, j):
     return (x + (1 - 2 * z) * j + 4) % 4
 
 
-def norm_body(h_hbm, g_hbm, b_hbm, m_hbm, s_hbm, o_ref, *scratch):
-    h_ref, g_ref, b_ref, m_ref, s_ref, *sems = scratch
-    copies = [
-        pltpu.make_async_copy(src, dst, sem)
-        for src, dst, sem in zip(
-            (h_hbm, g_hbm, b_hbm, m_hbm, s_hbm), (h_ref, g_ref, b_ref, m_ref, s_ref), sems
+def norm_body(h_hbm, g_hbm, b_hbm, m_hbm, s_hbm, w_hbm, o_hbm, v_hbm, u_hbm, *scratch):
+    h_ref, g_ref, b_ref, m_ref, n_ref, sems = scratch
+    copies = Copies(sems)
+    mine = [
+        copies.start(src, dst)
+        for src, dst in ((h_hbm, h_ref), (g_hbm, g_ref), (b_hbm, b_ref), (m_hbm, m_ref))
+    ]
+    rest = [
+        copies.start(
+            s_hbm.at[0, kv, :, UNIT * (x ^ 1) : UNIT * ((x ^ 1) + 1)], o_hbm.at[x, 4 + kv]
         )
+        for x in range(4)
+        for kv in range(2)
     ]
-    for copy in copies:
-        copy.start()
-    for copy in copies[:4]:
-        copy.wait()
+    rest.append(copies.start(w_hbm.at[:HALF], v_hbm))
+    rest.append(copies.start(w_hbm.at[HALF:], u_hbm))
+    wait_all(mine)
     h = h_ref[0].astype(F32)
     inverse = lax.rsqrt(jnp.mean(h * h, axis=-1, keepdims=True) + 1e-06)
     mask = jnp.broadcast_to(m_ref[...].astype(F32), (ROWS, ROWS)).T[:, :1]
     normed = (h * inverse * g_ref[...] + mask * b_ref[...]).astype(BF)
-    for x in range(4):
-        for g in range(4):
-            o_ref[x, g] = normed[:, UNIT * g : UNIT * (g + 1)]
-    copies[4].wait()
-    for x in range(4):
-        for kv in range(2):
-            o_ref[x, 4 + kv] = s_ref[0, kv, :, UNIT * (x ^ 1) : UNIT * ((x ^ 1) + 1)]
-
-
-def kept_body(t_ref, o_ref):
-    for x in range(4):
-        o_ref[x] = t_ref[x, 4:6]
-
-
-def project_body(t_ref, w_ref, n_ref, p_ref, early, front_o, back_o, opp_o, keep_o, other, both):
+    for g in range(4):
+        n_ref[g] = normed[:, UNIT * g : UNIT * (g + 1)]
+    wait_all([copies.start(n_ref, o_hbm.at[x, :4]) for x in range(4)])
+    wait_all(rest)
+
+
+def project_body(t_hbm, w_hbm, v_hbm, u_hbm, early, f_ref, b_ref, o_ref, k_ref, s_out, *scratch):
     del early
+    t_ref, w_ref, other, both, sems = scratch
     x, z = where_am_i()
-    other[: D * 3 // 16] = n_ref[...]
-    other[D * 3 // 16 :] = p_ref[...]
-    mine = w_ref[pl.ds(pl.multiple_of(UNIT * (1 - z), HALF), HALF), :]
-    both[pl.ds(pl.multiple_of(HALF * z, HALF), HALF), :] = mine
-    both[pl.ds(pl.multiple_of(HALF * (1 - z), HALF), HALF), :] = other[
-        pl.ds(pl.multiple_of(UNIT * z, HALF), HALF), :
-    ]
+    copies = Copies(sems)
+    first = [copies.start(t_hbm.at[:, :4], t_ref), copies.start(w_hbm, w_ref)]
+    second = [copies.start(v_hbm, other.at[:HALF]), copies.start(u_hbm, other.at[HALF:])]
+    last = [copies.start(t_hbm.at[:, 4:], s_out)]
+    wait_all(first)
     tokens = jnp.concatenate(
         [
             jnp.concatenate([t_ref[slot(x, z, j), g] for g in range(4)], axis=1)
@@ -117,21 +134,31 @@
         return [got[ROWS * j : ROWS * (j + 1)] for j in range(4)]
 
     front = product(w_ref[pl.ds(pl.multiple_of(HALF * z, HALF), UNIT), :])
-    mid = product(both[...])
+    for j in range(4):
+        f_ref[j] = front[j]
+    k_ref[4] = front[0]
+    b_ref[5] = front[3]
+    o_ref[0] = front[2]
+    wait_all(second)
     back = product(other[pl.ds(pl.multiple_of(HALF * (1 - z), HALF), UNIT), :])
     for j in range(4):
-        front_o[j] = front[j]
-        back_o[j] = back[j]
-        keep_o[j] = mid[j]
-    front_o[4] = mid[1]
-    front_o[5] = back[1]
-    back_o[4] = mid[3]
-    back_o[5] = front[3]
-    opp_o[0] = front[2]
-    opp_o[1] = mid[2]
-    opp_o[2] = back[2]
-    keep_o[4] = front[0]
-    keep_o[5] = back[0]
+        b_ref[j] = back[j]
+    k_ref[5] = back[0]
+    f_ref[5] = back[1]
+    o_ref[2] = back[2]
+    both[pl.ds(pl.multiple_of(HALF * z, HALF), HALF), :] = w_ref[
+        pl.ds(pl.multiple_of(UNIT * (1 - z), HALF), HALF), :
+    ]
+    both[pl.ds(pl.multiple_of(HALF * (1 - z), HALF), HALF), :] = other[
+        pl.ds(pl.multiple_of(UNIT * z, HALF), HALF), :
+    ]
+    mid = product(both[...])
+    for j in range(4):
+        k_ref[j] = mid[j]
+    f_ref[4] = mid[1]
+    b_ref[4] = mid[3]
+    o_ref[1] = mid[2]
+    wait_all(last)
 
 
 def roles(x, z):
@@ -143,7 +170,7 @@
     return q, k, v
 
 
-def attend_body(m_ref, a_ref, b_ref, t_ref, p_ref, g_ref, *o_refs):
+def attend_body(m_ref, a_ref, b_ref, s_ref, p_ref, g_ref, *o_refs):
     x, z = where_am_i()
     gates = g_ref[:, pl.ds(pl.multiple_of(UNIT * (x ^ 1), UNIT), UNIT)]
     roled = roles(x, z)
@@ -157,7 +184,7 @@
             return jnp.where(index == 0, own, jnp.where(index == 1, behind, ahead))
 
         kept = [
-            [t_ref[slot(x, z, j), 4 + kv, :, cols] for j in range(4)]
+            [s_ref[slot(x, z, j), kv, :, cols] for j in range(4)]
             + [p_ref[j, kv, :, cols] for j in range(4)]
             for kv in range(2)
         ]
@@ -214,46 +241,53 @@
     def blocks(*lead):
         return jax.ShapeDtypeStruct((*lead, ROWS, UNIT), BF)
 
+    def rows(count):
+        return jax.ShapeDtypeStruct((count, D), BF)
+
     weight = jnp.swapaxes(w_qkv[0], 0, 1)
-    packed = pl.pallas_call(
+    packed, small, large = call(
         norm_body,
-        out_shape=blocks(4, 6),
-        in_specs=[pl.BlockSpec(memory_space=pltpu.HBM)] * 5,
-        out_specs=VM,
+        (blocks(4, 6), rows(HALF), rows(UNIT)),
+        6,
+        HBM,
+        60,
         scratch_shapes=[
             pltpu.VMEM((1, ROWS, D), BF),
             pltpu.VMEM((1, D), F32),
             pltpu.VMEM((1, D), F32),
             pltpu.VMEM((1, ROWS), jnp.int32),
-            pltpu.VMEM((1, 2, ROWS, D), BF),
-        ]
-        + [pltpu.SemaphoreType.DMA] * 5,
-        compiler_params=pltpu.CompilerParams(vmem_limit_bytes=60 * 1024 * 1024),
-    )(hidden, norm_gain, box_vec, box_mask, stale_kv)
-    came = lax.all_to_all(
-        packed, "patch", 0, 0, axis_index_groups=[[0, 2, 4, 6], [1, 3, 5, 7]]
-    )
-    half = weight.shape[0] // 2
-    first = lax.ppermute(weight[:half], ("dp", "patch"), far_pairs(parts))
-    second = lax.ppermute(weight[half:], "patch", partner_pairs())
+            pltpu.VMEM((4, ROWS, UNIT), BF),
+            pltpu.SemaphoreType.DMA((18,)),
+        ],
+    )(hidden, norm_gain, box_vec, box_mask, stale_kv, weight)
+    came = lax.all_to_all(packed, "patch", 0, 0, axis_index_groups=PLANES)
+    large = lax.ppermute(large, "patch", partner_pairs())
+    small = lax.ppermute(small, ("dp", "patch"), far_pairs(parts))
     before = lax.ppermute(hidden, "segment", [(i, (i + 1) % segments) for i in range(segments)])
-    kept = call(kept_body, blocks(4, 2), 1)(came)
-    kept = lax.ppermute(kept, "patch", partner_pairs())
-
-    front, back, opposite, keep = call(
+
+    front, back, opposite, mid, own = pl.pallas_call(
         project_body,
-        (blocks(6), blocks(6), blocks(3), blocks(6)),
-        5,
-        scratch_shapes=[pltpu.VMEM((2 * half, D), BF), pltpu.VMEM((UNIT, D), BF)],
-    )(came, weight, first, second, before)
+        out_shape=(blocks(6), blocks(6), blocks(3), blocks(6), blocks(4, 2)),
+        in_specs=[ANY] * 5,
+        out_specs=(VM, VM, VM, VM, ANY),
+        scratch_shapes=[
+            pltpu.VMEM((4, 4, ROWS, UNIT), BF),
+            pltpu.VMEM((UNIT + HALF, D), BF),
+            pltpu.VMEM((UNIT + HALF, D), BF),
+            pltpu.VMEM((UNIT, D), BF),
+            pltpu.SemaphoreType.DMA((5,)),
+        ],
+        compiler_params=pltpu.CompilerParams(vmem_limit_bytes=PROJECT_ROOM * MIB),
+    )(came, weight, small, large, before)
+    other = lax.ppermute(own, "patch", partner_pairs())
     front = lax.ppermute(front, "patch", x_pairs(1))
     back = lax.ppermute(back, "patch", x_pairs(3))
     opposite, mark = lax.optimization_barrier((opposite, back[0, :16, :128]))
     opposite = lax.ppermute(opposite, "patch", x_pairs(2))
 
-    out = call(attend_body, (blocks(),) * 4, 6)(keep, front, back, came, kept, gate)
+    out = call(attend_body, (blocks(),) * 4, 6)(mid, front, back, own, other, gate)
     fresh = call(fresh_body, jax.ShapeDtypeStruct((1, 2, ROWS, D), BF), 5)(
-        keep, front, back, opposite, mark
+        mid, front, back, opposite, mark
     )
 
     came = []

time: 102 us -> 170 us (1.67)
  the two profiles are of different devices: /device:TPU:25 before, /device:TPU:1 now
where the time goes in v6:
time: 170 us; the launch traced here: 169 us
  Pallas kernels  90 us (53%)
  starting transfers between devices  54.2 us (32%)
  waiting for transfers between devices  22.7 us (13%)
    pallas_call x1, Pallas kernels, local(): call(norm_body, (blocks(4, 6), rows(HALF), rows(UNIT)), 6, HBM, 60, scrat...  78.7 us
    ppermute x4, starting transfers between devices, local(): came.append(lax.ppermute(out[j], ('segment', 'patch'), pairs))  19.1 us
    ppermute x1, starting transfers between devices, local(): small = lax.ppermute(small, ('dp', 'patch'), far_pairs(parts))  8.85 us
    ppermute x1, waiting for transfers between devices, local(): front = lax.ppermute(front, 'patch', x_pairs(1))  5.89 us
    ppermute x1, waiting for transfers between devices, local(): lax.ppermute(hidden, 'segment', [(i, (i + 1) % segments) for i in range(s...  5.04 us
    ppermute x1, waiting for transfers between devices, local(): small = lax.ppermute(small, ('dp', 'patch'), far_pairs(parts))  4.87 us
    all_to_all x1, starting transfers between devices, local(): came = lax.all_to_all(packed, 'patch', 0, 0, axis_index_groups=PLANES)  4.85 us
    pallas_call x1, Pallas kernels, local(): pl.pallas_call(project_body, out_shape=(blocks(6), blocks(6), blocks(3),...  4.85 us
  transfers between devices with their start and end apart: 12, of which 6 were waited for; matrix products, arithmetic and copies ran while one was open for 0% of the time, Pallas kernels for 3%

profile of v6, /device:TPU:1, one launch (start us, length us, event | category | flops | bytes accessed | tf_op | source)
XLA Modules:
  0.0 169.2 jit_solution(6281122293636231521)
XLA Ops:
  0.6 78.7 %shard_map.86 = (bf16[4,6,128,384]{3,2,1,0:T(8,128)(2,1)}, bf16[192,1536]{1,0:T(8,128)(2,1)}, bf16[384,1536]{1,0:T(8,128)(2,1)}) custom-call(bf16[1,128,1536]{2,1,0:T(8,128)(2,1)} %h_hbm.1, f32[1,1536]{1,0:T(1,128)} %g_hbm.1, f32[1,1536]{1,0:T(1,128)} %b_hbm.1, s32[1,128]{1,0:T(1,128)} %m_hbm.1, bf16[1,2,128,1536]{3,2,1,0:T(8,128)(2,1)} %s_hbm.1, ...), custom_call_target="tpu_custom_call" | custom-call | tf_op jit(solution)/shard_map/pallas_call | solution.py:248
  79.3 4.9 %all-to-all-start = ((bf16[4,6,128,384]{3,2,1,0:T(8,128)(2,1)}), bf16[4,6,128,384]{3,2,1,0:T(8,128)(2,1)S(1)}, u32[]{:S(2)}, u32[]{:S(2)}) async-start(bf16[4,6,128,384]{3,2,1,0:T(8,128)(2,1)} %get-tuple-element.16), calls=%async_computation | async-start | bytes 4718592 | tf_op jit(solution)/shard_map/all_to_all | solution.py:263
  84.2 4.0 %collective-permute-start.1 = (bf16[384,1536]{1,0:T(8,128)(2,1)}, bf16[384,1536]{1,0:T(8,128)(2,1)}, u32[]{:S(2)}, u32[]{:S(2)}) collective-permute-start(bf16[384,1536]{1,0:T(8,128)(2,1)} %get-tuple-element.18), channel_id=1, source_target_pairs={{0,1},{1,0},{2,3},{3,2},{4,5},{5,4},{6,7},{7,6},{8,9},{9,8},{10,11... | collective-permute-start | bytes 3538952 | tf_op jit(solution)/shard_map/ppermute | solution.py:264
  88.2 0.0 copy-start
  88.2 8.8 %collective-permute-start = (bf16[192,1536]{1,0:T(8,128)(2,1)}, bf16[192,1536]{1,0:T(8,128)(2,1)S(1)}, u32[]{:S(2)}, u32[]{:S(2)}) collective-permute-start(bf16[192,1536]{1,0:T(8,128)(2,1)} %get-tuple-element.17), channel_id=1, source_target_pairs={{0,385},{1,128},{2,387},{3,130},{4,389},{5,132},{6,391},{7,134},{1... | collective-permute-start | bytes 1769480 | tf_op jit(solution)/shard_map/ppermute | solution.py:265
  97.1 2.7 %collective-permute-start.2 = (bf16[1,128,1536]{2,1,0:T(8,128)(2,1)}, bf16[1,128,1536]{2,1,0:T(8,128)(2,1)S(1)}, u32[]{:S(2)}, u32[]{:S(2)}) collective-permute-start(bf16[1,128,1536]{2,1,0:T(8,128)(2,1)} %h_hbm.1), channel_id=1, source_target_pairs={{0,8},{8,16},{16,24},{24,32},{32,40},{40,48},{48,56},{56,64},{64,7... | collective-permute-start | bytes 1179656 | tf_op jit(solution)/shard_map/ppermute | solution.py:266
  99.8 5.0 %collective-permute-done.2.early.h_ref = bf16[1,128,1536]{2,1,0:T(8,128)(2,1)S(1)} collective-permute-done((bf16[1,128,1536]{2,1,0:T(8,128)(2,1)}, bf16[1,128,1536]{2,1,0:T(8,128)(2,1)S(1)}, u32[]{:S(2)}, u32[]{:S(2)}) %collective-permute-start.2) | collective-permute-done | bytes 393248 | tf_op jit(solution)/shard_map/ppermute | solution.py:266
  104.8 4.9 %collective-permute-done.v_hbm = bf16[192,1536]{1,0:T(8,128)(2,1)S(1)} collective-permute-done((bf16[192,1536]{1,0:T(8,128)(2,1)}, bf16[192,1536]{1,0:T(8,128)(2,1)S(1)}, u32[]{:S(2)}, u32[]{:S(2)}) %collective-permute-start) | collective-permute-done | bytes 589856 | tf_op jit(solution)/shard_map/ppermute | solution.py:265
  109.7 0.7 collective-permute-done.1.u_hbm
  110.4 0.0 all-to-all-done.t_hbm
  110.4 1.4 copy-done.1
  111.8 4.8 %shard_map.87 = (bf16[6,128,384]{2,1,0:T(8,128)(2,1)S(1)}, bf16[6,128,384]{2,1,0:T(8,128)(2,1)S(1)}, bf16[3,128,384]{2,1,0:T(8,128)(2,1)S(1)}, bf16[6,128,384]{2...) custom-call(bf16[4,6,128,384]{3,2,1,0:T(8,128)(2,1)} %copy-done.1, bf16[576,1536]{1,0:T(8,128)(2,1)} %bitcast.6, ...), custom_call_target="tpu_custom_call" | custom-call | tf_op jit(solution)/shard_map/pallas_call | solution.py:268
  116.7 4.4 %collective-permute-start.4 = (bf16[6,128,384]{2,1,0:T(8,128)(2,1)S(1)}, bf16[6,128,384]{2,1,0:T(8,128)(2,1)S(1)}, u32[]{:S(2)}, u32[]{:S(2)}) collective-permute-start(bf16[6,128,384]{2,1,0:T(8,128)(2,1)S(1)} %get-tuple-element.21), channel_id=1, source_target_pairs={{0,6},{1,3},{2,0},{3,5},{4,2},{5,7},{6,4},{7,1},{8,14},{9,11},{10,... | collective-permute-start | bytes 1769480 | tf_op jit(solution)/shard_map/ppermute | solution.py:284
  121.1 3.8 %collective-permute-start.5 = (bf16[4,2,128,384]{3,2,1,0:T(8,128)(2,1)S(1)}, bf16[4,2,128,384]{3,2,1,0:T(8,128)(2,1)S(1)}, u32[]{:S(2)}, u32[]{:S(2)}) collective-permute-start(bf16[4,2,128,384]{3,2,1,0:T(8,128)(2,1)S(1)} %get-tuple-element.22.s_ref), channel_id=1, source_target_pairs={{0,1},{1,0},{2,3},{3,2},{4,5},{5,4},{6,7},{7,6},{8,9},{9,8},{10,11... | collective-permute-start | bytes 2359304 | tf_op jit(solution)/shard_map/ppermute | solution.py:282
  124.9 2.2 %collective-permute-start.3 = (bf16[6,128,384]{2,1,0:T(8,128)(2,1)S(1)}, bf16[6,128,384]{2,1,0:T(8,128)(2,1)S(1)}, u32[]{:S(2)}, u32[]{:S(2)}) collective-permute-start(bf16[6,128,384]{2,1,0:T(8,128)(2,1)S(1)} %get-tuple-element.20), channel_id=1, source_target_pairs={{0,2},{1,7},{2,4},{3,1},{4,6},{5,3},{6,0},{7,5},{8,10},{9,15},{10,... | collective-permute-start | bytes 1769480 | tf_op jit(solution)/shard_map/ppermute | solution.py:283
  127.1 1.4 collective-permute-done.4.b_ref
  128.4 4.4 %collective-permute-start.10 = (bf16[3,128,384]{2,1,0:T(8,128)(2,1)S(1)}, bf16[3,128,384]{2,1,0:T(8,128)(2,1)S(1)}, u32[]{:S(2)}, u32[]{:S(2)}) collective-permute-start(bf16[3,128,384]{2,1,0:T(8,128)(2,1)S(1)} %get-tuple-element.28), channel_id=1, source_target_pairs={{0,4},{1,5},{2,6},{3,7},{4,0},{5,1},{6,2},{7,3},{8,12},{9,13},{10,... | collective-permute-start | bytes 884744 | tf_op jit(solution)/shard_map/ppermute | solution.py:286
  132.8 5.9 %collective-permute-done.3.a_ref = bf16[6,128,384]{2,1,0:T(8,128)(2,1)S(1)} collective-permute-done((bf16[6,128,384]{2,1,0:T(8,128)(2,1)S(1)}, bf16[6,128,384]{2,1,0:T(8,128)(2,1)S(1)}, u32[]{:S(2)}, u32[]{:S(2)}) %collective-permute-start.3) | collective-permute-done | bytes 589856 | tf_op jit(solution)/shard_map/ppermute | solution.py:283
  138.7 0.0 collective-permute-done.5.p_ref
  138.7 0.0 copy-done
  138.7 4.5 %shard_map.88 = (bf16[128,384]{1,0:T(8,128)(2,1)S(1)}, bf16[128,384]{1,0:T(8,128)(2,1)S(1)}, bf16[128,384]{1,0:T(8,128)(2,1)S(1)}, bf16[128,384]{1,0:T(8,128)(2,1)S(1)}) custom-call(bf16[6,128,384]{2,1,0:T(8,128)(2,1)S(1)} %get-tuple-element.19.m_ref.k_ref, bf16[6,128,384]{2,1,0:T(8,128)(2,1)S(1)} %collective-permute-done.3.a_ref, ...), custom_call_target="tpu_custom_call" | custom-call | tf_op jit(solution)/shard_map/pallas_call | solution.py:288
  143.3 10.6 %collective-permute-start.6 = (bf16[128,384]{1,0:T(8,128)(2,1)S(1)}, bf16[128,384]{1,0:T(8,128)(2,1)S(1)}, u32[]{:S(2)}, u32[]{:S(2)}) collective-permute-start(bf16[128,384]{1,0:T(8,128)(2,1)S(1)} %get-tuple-element.23), channel_id=1, source_target_pairs={{0,8},{1,9},{2,10},{3,11},{4,12},{5,13},{6,14},{7,15},{8,16},{9,17... | collective-permute-start | bytes 294920 | tf_op jit(solution)/shard_map/ppermute | solution.py:300
  153.9 1.9 %collective-permute-start.7 = (bf16[128,384]{1,0:T(8,128)(2,1)S(1)}, bf16[128,384]{1,0:T(8,128)(2,1)S(1)}, u32[]{:S(2)}, u32[]{:S(2)}) collective-permute-start(bf16[128,384]{1,0:T(8,128)(2,1)S(1)} %get-tuple-element.24), channel_id=1, source_target_pairs={{0,14},{1,11},{2,8},{3,13},{4,10},{5,15},{6,12},{7,9},{8,22},{9,19... | collective-permute-start | bytes 294920 | tf_op jit(solution)/shard_map/ppermute | solution.py:300
  155.8 4.3 %collective-permute-start.8 = (bf16[128,384]{1,0:T(8,128)(2,1)S(1)}, bf16[128,384]{1,0:T(8,128)(2,1)S(1)}, u32[]{:S(2)}, u32[]{:S(2)}) collective-permute-start(bf16[128,384]{1,0:T(8,128)(2,1)S(1)} %get-tuple-element.25), channel_id=1, source_target_pairs={{0,12},{1,13},{2,14},{3,15},{4,8},{5,9},{6,10},{7,11},{8,20},{9,21... | collective-permute-start | bytes 294920 | tf_op jit(solution)/shard_map/ppermute | solution.py:300
  160.1 2.3 %collective-permute-start.9 = (bf16[128,384]{1,0:T(8,128)(2,1)S(1)}, bf16[128,384]{1,0:T(8,128)(2,1)S(1)}, u32[]{:S(2)}, u32[]{:S(2)}) collective-permute-start(bf16[128,384]{1,0:T(8,128)(2,1)S(1)} %get-tuple-element.26), channel_id=1, source_target_pairs={{0,10},{1,15},{2,12},{3,9},{4,14},{5,11},{6,8},{7,13},{8,18},{9,23... | collective-permute-start | bytes 294920 | tf_op jit(solution)/shard_map/ppermute | solution.py:300
  162.4 0.0 collective-permute-done.10.p_ref
  162.4 1.1 shard_map.90
  163.5 0.0 collective-permute-done.6.a0
  163.5 0.0 collective-permute-done.7.a1
  163.5 0.0 collective-permute-done.8.a2
  163.5 4.8 %collective-permute-done.9.a3 = bf16[128,384]{1,0:T(8,128)(2,1)S(1)} collective-permute-done((bf16[128,384]{1,0:T(8,128)(2,1)S(1)}, bf16[128,384]{1,0:T(8,128)(2,1)S(1)}, u32[]{:S(2)}, u32[]{:S(2)}) %collective-permute-start.9) | collective-permute-done | bytes 98336 | tf_op jit(solution)/shard_map/ppermute | solution.py:300
  168.3 0.9 shard_map.89
  (2 shorter events, 0.0 us)
Async XLA Ops:
  79.3 31.1 %all-to-all-start = ((bf16[4,6,128,384]{3,2,1,0:T(8,128)(2,1)}), bf16[4,6,128,384]{3,2,1,0:T(8,128)(2,1)S(1)}, u32[]{:S(2)}, u32[]{:S(2)}) async-start(bf16[4,6,128,384]{3,2,1,0:T(8,128)(2,1)} %get-tuple-element.16), calls=%async_computation | async-start | bytes 4718592 | tf_op jit(solution)/shard_map/all_to_all | solution.py:263
  84.2 26.2 %collective-permute-start.1 = (bf16[384,1536]{1,0:T(8,128)(2,1)}, bf16[384,1536]{1,0:T(8,128)(2,1)}, u32[]{:S(2)}, u32[]{:S(2)}) collective-permute-start(bf16[384,1536]{1,0:T(8,128)(2,1)} %get-tuple-element.18), channel_id=1, source_target_pairs={{0,1},{1,0},{2,3},{3,2},{4,5},{5,4},{6,7},{7,6},{8,9},{9,8},{10,11... | collective-permute-start | bytes 3538952 | tf_op jit(solution)/shard_map/ppermute | solution.py:264
  88.2 50.5 %copy-start = (f32[1,1536]{1,0:T(1,128)S(1)}, f32[1,1536]{1,0:T(1,128)}, u32[]{:S(2)}) copy-start(f32[1,1536]{1,0:T(1,128)} %g_ref.1) | copy-start | bytes 18436
  88.2 21.5 %collective-permute-start = (bf16[192,1536]{1,0:T(8,128)(2,1)}, bf16[192,1536]{1,0:T(8,128)(2,1)S(1)}, u32[]{:S(2)}, u32[]{:S(2)}) collective-permute-start(bf16[192,1536]{1,0:T(8,128)(2,1)} %get-tuple-element.17), channel_id=1, source_target_pairs={{0,385},{1,128},{2,387},{3,130},{4,389},{5,132},{6,391},{7,134},{1... | collective-permute-start | bytes 1769480 | tf_op jit(solution)/shard_map/ppermute | solution.py:265
  97.1 7.7 %collective-permute-start.2 = (bf16[1,128,1536]{2,1,0:T(8,128)(2,1)}, bf16[1,128,1536]{2,1,0:T(8,128)(2,1)S(1)}, u32[]{:S(2)}, u32[]{:S(2)}) collective-permute-start(bf16[1,128,1536]{2,1,0:T(8,128)(2,1)} %h_hbm.1), channel_id=1, source_target_pairs={{0,8},{8,16},{16,24},{24,32},{32,40},{40,48},{48,56},{56,64},{64,7... | collective-permute-start | bytes 1179656 | tf_op jit(solution)/shard_map/ppermute | solution.py:266
  110.4 1.4 copy-start.1
  116.7 11.7 %collective-permute-start.4 = (bf16[6,128,384]{2,1,0:T(8,128)(2,1)S(1)}, bf16[6,128,384]{2,1,0:T(8,128)(2,1)S(1)}, u32[]{:S(2)}, u32[]{:S(2)}) collective-permute-start(bf16[6,128,384]{2,1,0:T(8,128)(2,1)S(1)} %get-tuple-element.21), channel_id=1, source_target_pairs={{0,6},{1,3},{2,0},{3,5},{4,2},{5,7},{6,4},{7,1},{8,14},{9,11},{10,... | collective-permute-start | bytes 1769480 | tf_op jit(solution)/shard_map/ppermute | solution.py:284
  121.1 17.7 %collective-permute-start.5 = (bf16[4,2,128,384]{3,2,1,0:T(8,128)(2,1)S(1)}, bf16[4,2,128,384]{3,2,1,0:T(8,128)(2,1)S(1)}, u32[]{:S(2)}, u32[]{:S(2)}) collective-permute-start(bf16[4,2,128,384]{3,2,1,0:T(8,128)(2,1)S(1)} %get-tuple-element.22.s_ref), channel_id=1, source_target_pairs={{0,1},{1,0},{2,3},{3,2},{4,5},{5,4},{6,7},{7,6},{8,9},{9,8},{10,11... | collective-permute-start | bytes 2359304 | tf_op jit(solution)/shard_map/ppermute | solution.py:282
  124.9 13.8 %collective-permute-start.3 = (bf16[6,128,384]{2,1,0:T(8,128)(2,1)S(1)}, bf16[6,128,384]{2,1,0:T(8,128)(2,1)S(1)}, u32[]{:S(2)}, u32[]{:S(2)}) collective-permute-start(bf16[6,128,384]{2,1,0:T(8,128)(2,1)S(1)} %get-tuple-element.20), channel_id=1, source_target_pairs={{0,2},{1,7},{2,4},{3,1},{4,6},{5,3},{6,0},{7,5},{8,10},{9,15},{10,... | collective-permute-start | bytes 1769480 | tf_op jit(solution)/shard_map/ppermute | solution.py:283
  128.4 34.0 %collective-permute-start.10 = (bf16[3,128,384]{2,1,0:T(8,128)(2,1)S(1)}, bf16[3,128,384]{2,1,0:T(8,128)(2,1)S(1)}, u32[]{:S(2)}, u32[]{:S(2)}) collective-permute-start(bf16[3,128,384]{2,1,0:T(8,128)(2,1)S(1)} %get-tuple-element.28), channel_id=1, source_target_pairs={{0,4},{1,5},{2,6},{3,7},{4,0},{5,1},{6,2},{7,3},{8,12},{9,13},{10,... | collective-permute-start | bytes 884744 | tf_op jit(solution)/shard_map/ppermute | solution.py:286
  143.3 20.3 %collective-permute-start.6 = (bf16[128,384]{1,0:T(8,128)(2,1)S(1)}, bf16[128,384]{1,0:T(8,128)(2,1)S(1)}, u32[]{:S(2)}, u32[]{:S(2)}) collective-permute-start(bf16[128,384]{1,0:T(8,128)(2,1)S(1)} %get-tuple-element.23), channel_id=1, source_target_pairs={{0,8},{1,9},{2,10},{3,11},{4,12},{5,13},{6,14},{7,15},{8,16},{9,17... | collective-permute-start | bytes 294920 | tf_op jit(solution)/shard_map/ppermute | solution.py:300
  153.9 9.6 %collective-permute-start.7 = (bf16[128,384]{1,0:T(8,128)(2,1)S(1)}, bf16[128,384]{1,0:T(8,128)(2,1)S(1)}, u32[]{:S(2)}, u32[]{:S(2)}) collective-permute-start(bf16[128,384]{1,0:T(8,128)(2,1)S(1)} %get-tuple-element.24), channel_id=1, source_target_pairs={{0,14},{1,11},{2,8},{3,13},{4,10},{5,15},{6,12},{7,9},{8,22},{9,19... | collective-permute-start | bytes 294920 | tf_op jit(solution)/shard_map/ppermute | solution.py:300
  155.8 7.7 %collective-permute-start.8 = (bf16[128,384]{1,0:T(8,128)(2,1)S(1)}, bf16[128,384]{1,0:T(8,128)(2,1)S(1)}, u32[]{:S(2)}, u32[]{:S(2)}) collective-permute-start(bf16[128,384]{1,0:T(8,128)(2,1)S(1)} %get-tuple-element.25), channel_id=1, source_target_pairs={{0,12},{1,13},{2,14},{3,15},{4,8},{5,9},{6,10},{7,11},{8,20},{9,21... | collective-permute-start | bytes 294920 | tf_op jit(solution)/shard_map/ppermute | solution.py:300
  160.1 8.2 %collective-permute-start.9 = (bf16[128,384]{1,0:T(8,128)(2,1)S(1)}, bf16[128,384]{1,0:T(8,128)(2,1)S(1)}, u32[]{:S(2)}, u32[]{:S(2)}) collective-permute-start(bf16[128,384]{1,0:T(8,128)(2,1)S(1)} %get-tuple-element.26), channel_id=1, source_target_pairs={{0,10},{1,15},{2,12},{3,9},{4,14},{5,11},{6,8},{7,13},{8,18},{9,23... | collective-permute-start | bytes 294920 | tf_op jit(solution)/shard_map/ppermute | solution.py:300

commit v7 on v6

--- a/solution.py
+++ b/solution.py
@@ -85,22 +85,15 @@
     return (x + (1 - 2 * z) * j + 4) % 4
 
 
-def norm_body(h_hbm, g_hbm, b_hbm, m_hbm, s_hbm, w_hbm, o_hbm, v_hbm, u_hbm, *scratch):
-    h_ref, g_ref, b_ref, m_ref, n_ref, sems = scratch
+def norm_body(h_hbm, g_hbm, b_hbm, m_hbm, s_hbm, o_hbm, k0, k1, k2, k3, *scratch):
+    h_ref, g_ref, b_ref, m_ref, s_ref, n_ref, sems = scratch
+    x, z = where_am_i()
     copies = Copies(sems)
     mine = [
         copies.start(src, dst)
         for src, dst in ((h_hbm, h_ref), (g_hbm, g_ref), (b_hbm, b_ref), (m_hbm, m_ref))
     ]
-    rest = [
-        copies.start(
-            s_hbm.at[0, kv, :, UNIT * (x ^ 1) : UNIT * ((x ^ 1) + 1)], o_hbm.at[x, 4 + kv]
-        )
-        for x in range(4)
-        for kv in range(2)
-    ]
-    rest.append(copies.start(w_hbm.at[:HALF], v_hbm))
-    rest.append(copies.start(w_hbm.at[HALF:], u_hbm))
+    stale = copies.start(s_hbm, s_ref)
     wait_all(mine)
     h = h_ref[0].astype(F32)
     inverse = lax.rsqrt(jnp.mean(h * h, axis=-1, keepdims=True) + 1e-06)
@@ -108,18 +101,27 @@
     normed = (h * inverse * g_ref[...] + mask * b_ref[...]).astype(BF)
     for g in range(4):
         n_ref[g] = normed[:, UNIT * g : UNIT * (g + 1)]
-    wait_all([copies.start(n_ref, o_hbm.at[x, :4]) for x in range(4)])
-    wait_all(rest)
-
-
-def project_body(t_hbm, w_hbm, v_hbm, u_hbm, early, f_ref, b_ref, o_ref, k_ref, s_out, *scratch):
+    out = [copies.start(n_ref, o_hbm.at[i]) for i in range(4)]
+    stale.wait()
+    for j, target in enumerate((k0, k1, k2, k3)):
+        cols = pl.ds(pl.multiple_of(UNIT * (slot(x, z, j) ^ 1), UNIT), UNIT)
+        out.append(copies.start(s_ref.at[0, :, :, cols], target))
+    wait_all(out)
+
+
+def pack_body(k0, k1, k2, k3, early, o_ref):
+    del early
+    for j, ref in enumerate((k0, k1, k2, k3)):
+        o_ref[j] = ref[...]
+
+
+def project_body(t_hbm, w_hbm, v_hbm, u_hbm, early, f_ref, b_ref, o_ref, k_ref, *scratch):
     del early
     t_ref, w_ref, other, both, sems = scratch
     x, z = where_am_i()
     copies = Copies(sems)
-    first = [copies.start(t_hbm.at[:, :4], t_ref), copies.start(w_hbm, w_ref)]
+    first = [copies.start(t_hbm, t_ref), copies.start(w_hbm, w_ref)]
     second = [copies.start(v_hbm, other.at[:HALF]), copies.start(u_hbm, other.at[HALF:])]
-    last = [copies.start(t_hbm.at[:, 4:], s_out)]
     wait_all(first)
     tokens = jnp.concatenate(
         [
@@ -158,7 +160,6 @@
     f_ref[4] = mid[1]
     b_ref[4] = mid[3]
     o_ref[1] = mid[2]
-    wait_all(last)
 
 
 def roles(x, z):
@@ -184,7 +185,7 @@
             return jnp.where(index == 0, own, jnp.where(index == 1, behind, ahead))
 
         kept = [
-            [s_ref[slot(x, z, j), kv, :, cols] for j in range(4)]
+            [s_ref[j, kv, :, cols] for j in range(4)]
             + [p_ref[j, kv, :, cols] for j in range(4)]
             for kv in range(2)
         ]
@@ -241,45 +242,46 @@
     def blocks(*lead):
         return jax.ShapeDtypeStruct((*lead, ROWS, UNIT), BF)
 
-    def rows(count):
-        return jax.ShapeDtypeStruct((count, D), BF)
-
     weight = jnp.swapaxes(w_qkv[0], 0, 1)
-    packed, small, large = call(
+    packed, k0, k1, k2, k3 = pl.pallas_call(
         norm_body,
-        (blocks(4, 6), rows(HALF), rows(UNIT)),
-        6,
-        HBM,
-        60,
+        out_shape=(blocks(4, 4),) + (blocks(2),) * 4,
+        in_specs=[HBM] * 5,
+        out_specs=(HBM,) * 5,
         scratch_shapes=[
             pltpu.VMEM((1, ROWS, D), BF),
             pltpu.VMEM((1, D), F32),
             pltpu.VMEM((1, D), F32),
             pltpu.VMEM((1, ROWS), jnp.int32),
+            pltpu.VMEM((1, 2, ROWS, D), BF),
             pltpu.VMEM((4, ROWS, UNIT), BF),
-            pltpu.SemaphoreType.DMA((18,)),
+            pltpu.SemaphoreType.DMA((13,)),
         ],
-    )(hidden, norm_gain, box_vec, box_mask, stale_kv, weight)
+        compiler_params=pltpu.CompilerParams(vmem_limit_bytes=60 * MIB),
+    )(hidden, norm_gain, box_vec, box_mask, stale_kv)
     came = lax.all_to_all(packed, "patch", 0, 0, axis_index_groups=PLANES)
-    large = lax.ppermute(large, "patch", partner_pairs())
-    small = lax.ppermute(small, ("dp", "patch"), far_pairs(parts))
+    large = lax.ppermute(weight[HALF:], "patch", partner_pairs())
+    small = lax.ppermute(weight[:HALF], ("dp", "patch"), far_pairs(parts))
+    k1, k3 = lax.ppermute(k3, "patch", x_pairs(3)), lax.ppermute(k1, "patch", x_pairs(1))
+    k2 = lax.ppermute(k2, "patch", x_pairs(2))
     before = lax.ppermute(hidden, "segment", [(i, (i + 1) % segments) for i in range(segments)])
-
-    front, back, opposite, mid, own = pl.pallas_call(
+    own = call(pack_body, blocks(4, 2), 5)(k0, k1, k2, k3, before)
+    other = lax.ppermute(own, "patch", partner_pairs())
+
+    front, back, opposite, mid = pl.pallas_call(
         project_body,
-        out_shape=(blocks(6), blocks(6), blocks(3), blocks(6), blocks(4, 2)),
+        out_shape=(blocks(6), blocks(6), blocks(3), blocks(6)),
         in_specs=[ANY] * 5,
-        out_specs=(VM, VM, VM, VM, ANY),
+        out_specs=(VM,) * 4,
         scratch_shapes=[
             pltpu.VMEM((4, 4, ROWS, UNIT), BF),
             pltpu.VMEM((UNIT + HALF, D), BF),
             pltpu.VMEM((UNIT + HALF, D), BF),
             pltpu.VMEM((UNIT, D), BF),
-            pltpu.SemaphoreType.DMA((5,)),
+            pltpu.SemaphoreType.DMA((4,)),
         ],
         compiler_params=pltpu.CompilerParams(vmem_limit_bytes=PROJECT_ROOM * MIB),
-    )(came, weight, small, large, before)
-    other = lax.ppermute(own, "patch", partner_pairs())
+    )(came, weight, small, large, own)
     front = lax.ppermute(front, "patch", x_pairs(1))
     back = lax.ppermute(back, "patch", x_pairs(3))
     opposite, mark = lax.optimization_barrier((opposite, back[0, :16, :128]))

time: 170 us -> 108 us (0.64)
  the two profiles are of different devices: /device:TPU:1 before, /device:TPU:25 now
where the time goes in v7:
time: 108 us; the launch traced here: 107 us
  starting transfers between devices  65.8 us (61%)
  waiting for transfers between devices  21.8 us (20%)
  Pallas kernels  14 us (13%)
  local copies, waits for them, and re-layouts  4.65 us (4%)
    ppermute x4, starting transfers between devices, local(): came.append(lax.ppermute(out[j], ('segment', 'patch'), pairs))  17.9 us
    ppermute x1, starting transfers between devices, local(): small = lax.ppermute(weight[:HALF], ('dp', 'patch'), far_pairs(parts))  8.85 us
    ppermute x1, starting transfers between devices, local(): lax.ppermute(k1, 'patch', x_pairs(1))  6.5 us
    ppermute x1, waiting for transfers between devices, local(): back = lax.ppermute(back, 'patch', x_pairs(3))  6.02 us
    ppermute x4, waiting for transfers between devices, local(): came.append(lax.ppermute(out[j], ('segment', 'patch'), pairs))  5.48 us
    pallas_call x1, Pallas kernels, local(): pl.pallas_call(project_body, out_shape=(blocks(6), blocks(6), blocks(3),...  4.84 us
    ppermute x1, waiting for transfers between devices, local(): other = lax.ppermute(own, 'patch', partner_pairs())  4.71 us
    ppermute x1, starting transfers between devices, local(): lax.ppermute(k3, 'patch', x_pairs(3))  4.58 us
  transfers between devices with their start and end apart: 15, of which 7 were waited for; matrix products, arithmetic and copies ran while one was open for 1% of the time, Pallas kernels for 8%

profile of v7, /device:TPU:25, one launch (start us, length us, event | category | flops | bytes accessed | tf_op | source)
XLA Modules:
  0.0 107.2 jit_solution(10062241879256326497)
XLA Ops:
  0.6 2.4 %slice.13 = bf16[384,1536]{1,0:T(8,128)(2,1)} slice(bf16[576,1536]{1,0:T(8,128)(2,1)} %bitcast.5), slice={[192:576], [0:1536]} | slice | bytes 2359296 | tf_op jit(solution)/shard_map/slice | solution.py:263
  3.0 4.0 %collective-permute-start.1 = (bf16[384,1536]{1,0:T(8,128)(2,1)}, bf16[384,1536]{1,0:T(8,128)(2,1)}, u32[]{:S(2)}, u32[]{:S(2)}) collective-permute-start(bf16[384,1536]{1,0:T(8,128)(2,1)} %slice.13), channel_id=1, source_target_pairs={{0,1},{1,0},{2,3},{3,2},{4,5},{5,4},{6,7},{7,6},{8,9},{9,8},{10,11... | collective-permute-start | bytes 3538952 | tf_op jit(solution)/shard_map/ppermute | solution.py:263
  7.0 2.8 %shard_map.86 = (bf16[4,4,128,384]{3,2,1,0:T(8,128)(2,1)}, bf16[2,128,384]{2,1,0:T(8,128)(2,1)}, bf16[2,128,384]{2,1,0:T(8,128)(2,1)}, bf16[2,128,384]{2,1,0:T(8,128)(2,1)}, bf16[2,128,384]{2,1,0:T(8,128)(2,1)}) custom-call(bf16[1,128,1536]{2,1,0:T(8,128)(2,1)} %h_hbm.1, f32[1,1536]{1,0:T(1,128)} %g_hbm.1, f32[1,1536]{1,0:T(1,128)} %b_hbm.1, ...), custom_call_target="tpu_custom_call" | custom-call | tf_op jit(solution)/shard_map/pallas_call | solution.py:246
  9.8 0.0 copy-start
  9.8 4.2 %all-to-all-start = ((bf16[4,4,128,384]{3,2,1,0:T(8,128)(2,1)}), bf16[4,4,128,384]{3,2,1,0:T(8,128)(2,1)S(1)}, u32[]{:S(2)}, u32[]{:S(2)}) async-start(bf16[4,4,128,384]{3,2,1,0:T(8,128)(2,1)} %get-tuple-element.17), calls=%async_computation | async-start | bytes 3145728 | tf_op jit(solution)/shard_map/all_to_all | solution.py:262
  14.0 1.1 %slice.12 = bf16[192,1536]{1,0:T(8,128)(2,1)S(1)} slice(bf16[576,1536]{1,0:T(8,128)(2,1)} %bitcast.6), slice={[0:192], [0:1536]} | slice | bytes 1179648 | tf_op jit(solution)/shard_map/slice | solution.py:264
  15.1 8.8 %collective-permute-start = (bf16[192,1536]{1,0:T(8,128)(2,1)S(1)}, bf16[192,1536]{1,0:T(8,128)(2,1)S(1)}, u32[]{:S(2)}, u32[]{:S(2)}) collective-permute-start(bf16[192,1536]{1,0:T(8,128)(2,1)S(1)} %slice.12), channel_id=1, source_target_pairs={{0,385},{1,128},{2,387},{3,130},{4,389},{5,132},{6,391},{7,134},{1... | collective-permute-start | bytes 1769480 | tf_op jit(solution)/shard_map/ppermute | solution.py:264
  23.9 4.6 %collective-permute-start.2 = (bf16[2,128,384]{2,1,0:T(8,128)(2,1)}, bf16[2,128,384]{2,1,0:T(8,128)(2,1)S(1)}, u32[]{:S(2)}, u32[]{:S(2)}) collective-permute-start(bf16[2,128,384]{2,1,0:T(8,128)(2,1)} %get-tuple-element.19), channel_id=1, source_target_pairs={{0,6},{1,3},{2,0},{3,5},{4,2},{5,7},{6,4},{7,1},{8,14},{9,11},{10,... | collective-permute-start | bytes 589832 | tf_op jit(solution)/shard_map/ppermute | solution.py:265
  28.5 4.5 %collective-permute-start.5 = (bf16[1,128,1536]{2,1,0:T(8,128)(2,1)S(1)}, bf16[1,128,1536]{2,1,0:T(8,128)(2,1)S(1)}, u32[]{:S(2)}, u32[]{:S(2)}) collective-permute-start(bf16[1,128,1536]{2,1,0:T(8,128)(2,1)S(1)} %copy-done.3), channel_id=1, source_target_pairs={{0,8},{8,16},{16,24},{24,32},{32,40},{40,48},{48,56},{56,64},{64,7... | collective-permute-start | bytes 1179656 | tf_op jit(solution)/shard_map/ppermute | solution.py:267
  33.0 2.5 %collective-permute-start.3 = (bf16[2,128,384]{2,1,0:T(8,128)(2,1)S(1)}, bf16[2,128,384]{2,1,0:T(8,128)(2,1)S(1)}, u32[]{:S(2)}, u32[]{:S(2)}) collective-permute-start(bf16[2,128,384]{2,1,0:T(8,128)(2,1)S(1)} %copy-done.5), channel_id=1, source_target_pairs={{0,4},{1,5},{2,6},{3,7},{4,0},{5,1},{6,2},{7,3},{8,12},{9,13},{10,... | collective-permute-start | bytes 589832 | tf_op jit(solution)/shard_map/ppermute | solution.py:266
  35.5 1.2 %collective-permute-done.2.k1 = bf16[2,128,384]{2,1,0:T(8,128)(2,1)S(1)} collective-permute-done((bf16[2,128,384]{2,1,0:T(8,128)(2,1)}, bf16[2,128,384]{2,1,0:T(8,128)(2,1)S(1)}, u32[]{:S(2)}, u32[]{:S(2)}) %collective-permute-start.2) | collective-permute-done | bytes 196640 | tf_op jit(solution)/shard_map/ppermute | solution.py:265
  36.7 6.5 %collective-permute-start.4 = (bf16[2,128,384]{2,1,0:T(8,128)(2,1)S(1)}, bf16[2,128,384]{2,1,0:T(8,128)(2,1)S(1)}, u32[]{:S(2)}, u32[]{:S(2)}) collective-permute-start(bf16[2,128,384]{2,1,0:T(8,128)(2,1)S(1)} %copy-done.4), channel_id=1, source_target_pairs={{0,2},{1,7},{2,4},{3,1},{4,6},{5,3},{6,0},{7,5},{8,10},{9,15},{10,... | collective-permute-start | bytes 589832 | tf_op jit(solution)/shard_map/ppermute | solution.py:265
  43.2 3.6 %collective-permute-done.4.k3 = bf16[2,128,384]{2,1,0:T(8,128)(2,1)S(1)} collective-permute-done((bf16[2,128,384]{2,1,0:T(8,128)(2,1)S(1)}, bf16[2,128,384]{2,1,0:T(8,128)(2,1)S(1)}, u32[]{:S(2)}, u32[]{:S(2)}) %collective-permute-start.4) | collective-permute-done | bytes 196640 | tf_op jit(solution)/shard_map/ppermute | solution.py:265
  46.8 0.1 shard_map.87.early.s_ref
  47.0 1.1 %copy-done.2 = bf16[4,4,128,384]{3,2,1,0:T(8,128)(2,1)} copy-done((bf16[4,4,128,384]{3,2,1,0:T(8,128)(2,1)}, bf16[4,4,128,384]{3,2,1,0:T(8,128)(2,1)S(1)}, u32[]{:S(2)}) %copy-start.2) | copy-done | bytes 1572888
  48.1 4.8 %shard_map.88 = (bf16[6,128,384]{2,1,0:T(8,128)(2,1)S(1)}, bf16[6,128,384]{2,1,0:T(8,128)(2,1)S(1)}, bf16[3,128,384]{2,1,0:T(8,128)(2,1)S(1)}, bf16[6,128,384]{2,1,0:T(8,128)(2,1)S(1)}) custom-call(bf16[4,4,128,384]{3,2,1,0:T(8,128)(2,1)} %copy-done.2, bf16[576,1536]{1,0:T(8,128)(2,1)} %bitcast.7, bf16[192,1536]{1,0:T(8,128)(2,1)S(1)} %collective-permute-done.v_hbm, ...), custom_call_target="tpu_custom_call" | custom-call | tf_op jit(solution)/shard_map/pallas_call | solution.py:271
  53.0 2.8 %collective-permute-start.7 = (bf16[6,128,384]{2,1,0:T(8,128)(2,1)S(1)}, bf16[6,128,384]{2,1,0:T(8,128)(2,1)S(1)}, u32[]{:S(2)}, u32[]{:S(2)}) collective-permute-start(bf16[6,128,384]{2,1,0:T(8,128)(2,1)S(1)} %get-tuple-element.24), channel_id=1, source_target_pairs={{0,6},{1,3},{2,0},{3,5},{4,2},{5,7},{6,4},{7,1},{8,14},{9,11},{10,... | collective-permute-start | bytes 1769480 | tf_op jit(solution)/shard_map/ppermute | solution.py:286
  55.8 4.4 %collective-permute-start.8 = (bf16[4,2,128,384]{3,2,1,0:T(8,128)(2,1)S(1)}, bf16[4,2,128,384]{3,2,1,0:T(8,128)(2,1)S(1)}, u32[]{:S(2)}, u32[]{:S(2)}) collective-permute-start(bf16[4,2,128,384]{3,2,1,0:T(8,128)(2,1)S(1)} %shard_map.87.early.s_ref), channel_id=1, source_target_pairs={{0,1},{1,0},{2,3},{3,2},{4,5},{5,4},{6,7},{7,6},{8,9},{9,8},{10,11... | collective-permute-start | bytes 2359304 | tf_op jit(solution)/shard_map/ppermute | solution.py:269
  60.2 3.0 %collective-permute-start.6 = (bf16[6,128,384]{2,1,0:T(8,128)(2,1)S(1)}, bf16[6,128,384]{2,1,0:T(8,128)(2,1)S(1)}, u32[]{:S(2)}, u32[]{:S(2)}) collective-permute-start(bf16[6,128,384]{2,1,0:T(8,128)(2,1)S(1)} %get-tuple-element.23), channel_id=1, source_target_pairs={{0,2},{1,7},{2,4},{3,1},{4,6},{5,3},{6,0},{7,5},{8,10},{9,15},{10,... | collective-permute-start | bytes 1769480 | tf_op jit(solution)/shard_map/ppermute | solution.py:285
  63.2 6.0 %collective-permute-done.7.b_ref = bf16[6,128,384]{2,1,0:T(8,128)(2,1)S(1)} collective-permute-done((bf16[6,128,384]{2,1,0:T(8,128)(2,1)S(1)}, bf16[6,128,384]{2,1,0:T(8,128)(2,1)S(1)}, u32[]{:S(2)}, u32[]{:S(2)}) %collective-permute-start.7) | collective-permute-done | bytes 589856 | tf_op jit(solution)/shard_map/ppermute | solution.py:286
  69.2 2.7 %collective-permute-start.13 = (bf16[3,128,384]{2,1,0:T(8,128)(2,1)S(1)}, bf16[3,128,384]{2,1,0:T(8,128)(2,1)S(1)}, u32[]{:S(2)}, u32[]{:S(2)}) collective-permute-start(bf16[3,128,384]{2,1,0:T(8,128)(2,1)S(1)} %get-tuple-element.30), channel_id=1, source_target_pairs={{0,4},{1,5},{2,6},{3,7},{4,0},{5,1},{6,2},{7,3},{8,12},{9,13},{10,... | collective-permute-start | bytes 884744 | tf_op jit(solution)/shard_map/ppermute | solution.py:288
  71.9 4.7 %collective-permute-done.8.p_ref = bf16[4,2,128,384]{3,2,1,0:T(8,128)(2,1)S(1)} collective-permute-done((bf16[4,2,128,384]{3,2,1,0:T(8,128)(2,1)S(1)}, bf16[4,2,128,384]{3,2,1,0:T(8,128)(2,1)S(1)}, u32[]{:S(2)}, u32[]{:S(2)}) %collective-permute-start.8) | collective-permute-done | bytes 786464 | tf_op jit(solution)/shard_map/ppermute | solution.py:269
  76.6 0.8 collective-permute-done.6.a_ref
  77.5 4.4 %shard_map.89 = (bf16[128,384]{1,0:T(8,128)(2,1)S(1)}, bf16[128,384]{1,0:T(8,128)(2,1)S(1)}, bf16[128,384]{1,0:T(8,128)(2,1)S(1)}, bf16[128,384]{1,0:T(8,128)(2,1)S(1)}) custom-call(bf16[6,128,384]{2,1,0:T(8,128)(2,1)S(1)} %get-tuple-element.22.m_ref.k_ref, bf16[6,128,384]{2,1,0:T(8,128)(2,1)S(1)} %collective-permute-done.6.a_ref, ...), custom_call_target="tpu_custom_call" | custom-call | tf_op jit(solution)/shard_map/pallas_call | solution.py:290
  81.9 10.3 %collective-permute-start.9 = (bf16[128,384]{1,0:T(8,128)(2,1)S(1)}, bf16[128,384]{1,0:T(8,128)(2,1)S(1)}, u32[]{:S(2)}, u32[]{:S(2)}) collective-permute-start(bf16[128,384]{1,0:T(8,128)(2,1)S(1)} %get-tuple-element.25), channel_id=1, source_target_pairs={{0,8},{1,9},{2,10},{3,11},{4,12},{5,13},{6,14},{7,15},{8,16},{9,17... | collective-permute-start | bytes 294920 | tf_op jit(solution)/shard_map/ppermute | solution.py:302
  92.2 1.9 %collective-permute-start.10 = (bf16[128,384]{1,0:T(8,128)(2,1)S(1)}, bf16[128,384]{1,0:T(8,128)(2,1)S(1)}, u32[]{:S(2)}, u32[]{:S(2)}) collective-permute-start(bf16[128,384]{1,0:T(8,128)(2,1)S(1)} %get-tuple-element.26), channel_id=1, source_target_pairs={{0,14},{1,11},{2,8},{3,13},{4,10},{5,15},{6,12},{7,9},{8,22},{9,19... | collective-permute-start | bytes 294920 | tf_op jit(solution)/shard_map/ppermute | solution.py:302
  94.1 1.9 %collective-permute-start.11 = (bf16[128,384]{1,0:T(8,128)(2,1)S(1)}, bf16[128,384]{1,0:T(8,128)(2,1)S(1)}, u32[]{:S(2)}, u32[]{:S(2)}) collective-permute-start(bf16[128,384]{1,0:T(8,128)(2,1)S(1)} %get-tuple-element.27), channel_id=1, source_target_pairs={{0,12},{1,13},{2,14},{3,15},{4,8},{5,9},{6,10},{7,11},{8,20},{9,21... | collective-permute-start | bytes 294920 | tf_op jit(solution)/shard_map/ppermute | solution.py:302
  96.0 3.8 %collective-permute-start.12 = (bf16[128,384]{1,0:T(8,128)(2,1)S(1)}, bf16[128,384]{1,0:T(8,128)(2,1)S(1)}, u32[]{:S(2)}, u32[]{:S(2)}) collective-permute-start(bf16[128,384]{1,0:T(8,128)(2,1)S(1)} %get-tuple-element.28), channel_id=1, source_target_pairs={{0,10},{1,15},{2,12},{3,9},{4,14},{5,11},{6,8},{7,13},{8,18},{9,23... | collective-permute-start | bytes 294920 | tf_op jit(solution)/shard_map/ppermute | solution.py:302
  99.8 2.7 %collective-permute-done.11.a2 = bf16[128,384]{1,0:T(8,128)(2,1)S(1)} collective-permute-done((bf16[128,384]{1,0:T(8,128)(2,1)S(1)}, bf16[128,384]{1,0:T(8,128)(2,1)S(1)}, u32[]{:S(2)}, u32[]{:S(2)}) %collective-permute-start.11) | collective-permute-done | bytes 98336 | tf_op jit(solution)/shard_map/ppermute | solution.py:302
  102.5 2.8 %collective-permute-done.12.a3 = bf16[128,384]{1,0:T(8,128)(2,1)S(1)} collective-permute-done((bf16[128,384]{1,0:T(8,128)(2,1)S(1)}, bf16[128,384]{1,0:T(8,128)(2,1)S(1)}, u32[]{:S(2)}, u32[]{:S(2)}) %collective-permute-start.12) | collective-permute-done | bytes 98336 | tf_op jit(solution)/shard_map/ppermute | solution.py:302
  105.3 0.9 shard_map.90
  106.2 1.1 shard_map.91
  (19 shorter events, 0.0 us)
Async XLA Ops:
  3.0 43.9 %collective-permute-start.1 = (bf16[384,1536]{1,0:T(8,128)(2,1)}, bf16[384,1536]{1,0:T(8,128)(2,1)}, u32[]{:S(2)}, u32[]{:S(2)}) collective-permute-start(bf16[384,1536]{1,0:T(8,128)(2,1)} %slice.13), channel_id=1, source_target_pairs={{0,1},{1,0},{2,3},{3,2},{4,5},{5,4},{6,7},{7,6},{8,9},{9,8},{10,11... | collective-permute-start | bytes 3538952 | tf_op jit(solution)/shard_map/ppermute | solution.py:263
  9.8 18.8 %copy-start.3 = (bf16[1,128,1536]{2,1,0:T(8,128)(2,1)S(1)}, bf16[1,128,1536]{2,1,0:T(8,128)(2,1)}, u32[]{:S(2)}) copy-start(bf16[1,128,1536]{2,1,0:T(8,128)(2,1)} %h_hbm.1) | copy-start | bytes 1179652
  9.8 23.2 %copy-start.5 = (bf16[2,128,384]{2,1,0:T(8,128)(2,1)S(1)}, bf16[2,128,384]{2,1,0:T(8,128)(2,1)}, u32[]{:S(2)}) copy-start(bf16[2,128,384]{2,1,0:T(8,128)(2,1)} %get-tuple-element.20) | copy-start | bytes 589828
  9.8 26.9 %copy-start.4 = (bf16[2,128,384]{2,1,0:T(8,128)(2,1)S(1)}, bf16[2,128,384]{2,1,0:T(8,128)(2,1)}, u32[]{:S(2)}) copy-start(bf16[2,128,384]{2,1,0:T(8,128)(2,1)} %get-tuple-element.21) | copy-start | bytes 589828
  9.8 37.0 %copy-start = (bf16[2,128,384]{2,1,0:T(8,128)(2,1)S(1)}, bf16[2,128,384]{2,1,0:T(8,128)(2,1)}, u32[]{:S(2)}) copy-start(bf16[2,128,384]{2,1,0:T(8,128)(2,1)} %get-tuple-element.18.k0) | copy-start | bytes 589828
  9.8 37.1 %all-to-all-start = ((bf16[4,4,128,384]{3,2,1,0:T(8,128)(2,1)}), bf16[4,4,128,384]{3,2,1,0:T(8,128)(2,1)S(1)}, u32[]{:S(2)}, u32[]{:S(2)}) async-start(bf16[4,4,128,384]{3,2,1,0:T(8,128)(2,1)} %get-tuple-element.17), calls=%async_computation | async-start | bytes 3145728 | tf_op jit(solution)/shard_map/all_to_all | solution.py:262
  15.1 31.8 %collective-permute-start = (bf16[192,1536]{1,0:T(8,128)(2,1)S(1)}, bf16[192,1536]{1,0:T(8,128)(2,1)S(1)}, u32[]{:S(2)}, u32[]{:S(2)}) collective-permute-start(bf16[192,1536]{1,0:T(8,128)(2,1)S(1)} %slice.12), channel_id=1, source_target_pairs={{0,385},{1,128},{2,387},{3,130},{4,389},{5,132},{6,391},{7,134},{1... | collective-permute-start | bytes 1769480 | tf_op jit(solution)/shard_map/ppermute | solution.py:264
  23.9 12.7 %collective-permute-start.2 = (bf16[2,128,384]{2,1,0:T(8,128)(2,1)}, bf16[2,128,384]{2,1,0:T(8,128)(2,1)S(1)}, u32[]{:S(2)}, u32[]{:S(2)}) collective-permute-start(bf16[2,128,384]{2,1,0:T(8,128)(2,1)} %get-tuple-element.19), channel_id=1, source_target_pairs={{0,6},{1,3},{2,0},{3,5},{4,2},{5,7},{6,4},{7,1},{8,14},{9,11},{10,... | collective-permute-start | bytes 589832 | tf_op jit(solution)/shard_map/ppermute | solution.py:265
  28.5 18.3 %collective-permute-start.5 = (bf16[1,128,1536]{2,1,0:T(8,128)(2,1)S(1)}, bf16[1,128,1536]{2,1,0:T(8,128)(2,1)S(1)}, u32[]{:S(2)}, u32[]{:S(2)}) collective-permute-start(bf16[1,128,1536]{2,1,0:T(8,128)(2,1)S(1)} %copy-done.3), channel_id=1, source_target_pairs={{0,8},{8,16},{16,24},{24,32},{32,40},{40,48},{48,56},{56,64},{64,7... | collective-permute-start | bytes 1179656 | tf_op jit(solution)/shard_map/ppermute | solution.py:267
  33.0 10.2 %collective-permute-start.3 = (bf16[2,128,384]{2,1,0:T(8,128)(2,1)S(1)}, bf16[2,128,384]{2,1,0:T(8,128)(2,1)S(1)}, u32[]{:S(2)}, u32[]{:S(2)}) collective-permute-start(bf16[2,128,384]{2,1,0:T(8,128)(2,1)S(1)} %copy-done.5), channel_id=1, source_target_pairs={{0,4},{1,5},{2,6},{3,7},{4,0},{5,1},{6,2},{7,3},{8,12},{9,13},{10,... | collective-permute-start | bytes 589832 | tf_op jit(solution)/shard_map/ppermute | solution.py:266
  36.7 10.1 %collective-permute-start.4 = (bf16[2,128,384]{2,1,0:T(8,128)(2,1)S(1)}, bf16[2,128,384]{2,1,0:T(8,128)(2,1)S(1)}, u32[]{:S(2)}, u32[]{:S(2)}) collective-permute-start(bf16[2,128,384]{2,1,0:T(8,128)(2,1)S(1)} %copy-done.4), channel_id=1, source_target_pairs={{0,2},{1,7},{2,4},{3,1},{4,6},{5,3},{6,0},{7,5},{8,10},{9,15},{10,... | collective-permute-start | bytes 589832 | tf_op jit(solution)/shard_map/ppermute | solution.py:265
  46.9 30.6 %copy-start.1 = (f32[1,1536]{1,0:T(1,128)S(1)}, f32[1,1536]{1,0:T(1,128)}, u32[]{:S(2)}) copy-start(f32[1,1536]{1,0:T(1,128)} %g_ref.1) | copy-start | bytes 18436
  46.9 1.2 %copy-start.2 = (bf16[4,4,128,384]{3,2,1,0:T(8,128)(2,1)}, bf16[4,4,128,384]{3,2,1,0:T(8,128)(2,1)S(1)}, u32[]{:S(2)}) copy-start(bf16[4,4,128,384]{3,2,1,0:T(8,128)(2,1)S(1)} %all-to-all-done.t_hbm) | copy-start | bytes 4718596
  53.0 16.3 %collective-permute-start.7 = (bf16[6,128,384]{2,1,0:T(8,128)(2,1)S(1)}, bf16[6,128,384]{2,1,0:T(8,128)(2,1)S(1)}, u32[]{:S(2)}, u32[]{:S(2)}) collective-permute-start(bf16[6,128,384]{2,1,0:T(8,128)(2,1)S(1)} %get-tuple-element.24), channel_id=1, source_target_pairs={{0,6},{1,3},{2,0},{3,5},{4,2},{5,7},{6,4},{7,1},{8,14},{9,11},{10,... | collective-permute-start | bytes 1769480 | tf_op jit(solution)/shard_map/ppermute | solution.py:286
  55.8 20.8 %collective-permute-start.8 = (bf16[4,2,128,384]{3,2,1,0:T(8,128)(2,1)S(1)}, bf16[4,2,128,384]{3,2,1,0:T(8,128)(2,1)S(1)}, u32[]{:S(2)}, u32[]{:S(2)}) collective-permute-start(bf16[4,2,128,384]{3,2,1,0:T(8,128)(2,1)S(1)} %shard_map.87.early.s_ref), channel_id=1, source_target_pairs={{0,1},{1,0},{2,3},{3,2},{4,5},{5,4},{6,7},{7,6},{8,9},{9,8},{10,11... | collective-permute-start | bytes 2359304 | tf_op jit(solution)/shard_map/ppermute | solution.py:269
  60.2 17.3 %collective-permute-start.6 = (bf16[6,128,384]{2,1,0:T(8,128)(2,1)S(1)}, bf16[6,128,384]{2,1,0:T(8,128)(2,1)S(1)}, u32[]{:S(2)}, u32[]{:S(2)}) collective-permute-start(bf16[6,128,384]{2,1,0:T(8,128)(2,1)S(1)} %get-tuple-element.23), channel_id=1, source_target_pairs={{0,2},{1,7},{2,4},{3,1},{4,6},{5,3},{6,0},{7,5},{8,10},{9,15},{10,... | collective-permute-start | bytes 1769480 | tf_op jit(solution)/shard_map/ppermute | solution.py:285
  69.2 36.9 %collective-permute-start.13 = (bf16[3,128,384]{2,1,0:T(8,128)(2,1)S(1)}, bf16[3,128,384]{2,1,0:T(8,128)(2,1)S(1)}, u32[]{:S(2)}, u32[]{:S(2)}) collective-permute-start(bf16[3,128,384]{2,1,0:T(8,128)(2,1)S(1)} %get-tuple-element.30), channel_id=1, source_target_pairs={{0,4},{1,5},{2,6},{3,7},{4,0},{5,1},{6,2},{7,3},{8,12},{9,13},{10,... | collective-permute-start | bytes 884744 | tf_op jit(solution)/shard_map/ppermute | solution.py:288
  81.9 17.9 %collective-permute-start.9 = (bf16[128,384]{1,0:T(8,128)(2,1)S(1)}, bf16[128,384]{1,0:T(8,128)(2,1)S(1)}, u32[]{:S(2)}, u32[]{:S(2)}) collective-permute-start(bf16[128,384]{1,0:T(8,128)(2,1)S(1)} %get-tuple-element.25), channel_id=1, source_target_pairs={{0,8},{1,9},{2,10},{3,11},{4,12},{5,13},{6,14},{7,15},{8,16},{9,17... | collective-permute-start | bytes 294920 | tf_op jit(solution)/shard_map/ppermute | solution.py:302
  92.2 7.6 %collective-permute-start.10 = (bf16[128,384]{1,0:T(8,128)(2,1)S(1)}, bf16[128,384]{1,0:T(8,128)(2,1)S(1)}, u32[]{:S(2)}, u32[]{:S(2)}) collective-permute-start(bf16[128,384]{1,0:T(8,128)(2,1)S(1)} %get-tuple-element.26), channel_id=1, source_target_pairs={{0,14},{1,11},{2,8},{3,13},{4,10},{5,15},{6,12},{7,9},{8,22},{9,19... | collective-permute-start | bytes 294920 | tf_op jit(solution)/shard_map/ppermute | solution.py:302
  94.1 8.4 %collective-permute-start.11 = (bf16[128,384]{1,0:T(8,128)(2,1)S(1)}, bf16[128,384]{1,0:T(8,128)(2,1)S(1)}, u32[]{:S(2)}, u32[]{:S(2)}) collective-permute-start(bf16[128,384]{1,0:T(8,128)(2,1)S(1)} %get-tuple-element.27), channel_id=1, source_target_pairs={{0,12},{1,13},{2,14},{3,15},{4,8},{5,9},{6,10},{7,11},{8,20},{9,21... | collective-permute-start | bytes 294920 | tf_op jit(solution)/shard_map/ppermute | solution.py:302
  96.0 9.3 %collective-permute-start.12 = (bf16[128,384]{1,0:T(8,128)(2,1)S(1)}, bf16[128,384]{1,0:T(8,128)(2,1)S(1)}, u32[]{:S(2)}, u32[]{:S(2)}) collective-permute-start(bf16[128,384]{1,0:T(8,128)(2,1)S(1)} %get-tuple-element.28), channel_id=1, source_target_pairs={{0,10},{1,15},{2,12},{3,9},{4,14},{5,11},{6,8},{7,13},{8,18},{9,23... | collective-permute-start | bytes 294920 | tf_op jit(solution)/shard_map/ppermute | solution.py:302

commit v8 on v4

--- a/solution.py
+++ b/solution.py
@@ -10,11 +10,14 @@
 D = 1536
 UNIT = 384
 HALF = 192
+PART = 272
 SCALE = HEAD_DIM ** (-0.5)
 BF = jnp.bfloat16
 F32 = jnp.float32
+MARK = jax.ShapeDtypeStruct((8, 128), F32)
 NT = (((1,), (1,)), ((), ()))
 VM = pl.BlockSpec(memory_space=pltpu.VMEM)
+HBM = pl.BlockSpec(memory_space=pltpu.HBM)
 PARAMS = pltpu.CompilerParams(vmem_limit_bytes=16 * 1024 * 1024)
 
 
@@ -60,8 +63,9 @@
     )
 
 
-def norm_body(h_hbm, g_hbm, b_hbm, m_hbm, s_hbm, w_hbm, own, b1, b2, lead, rest, *scratch):
-    h_ref, g_ref, b_ref, m_ref, s_ref, l_sem, r_sem, *sems = scratch
+def norm_body(h_hbm, g_hbm, b_hbm, m_hbm, s_hbm, own, b1, b2, mark, *scratch):
+    mark[...] = jnp.zeros_like(mark)
+    h_ref, g_ref, b_ref, m_ref, s_ref, *sems = scratch
     x, z = where_am_i()
     copies = [
         pltpu.make_async_copy(src, dst, sem)
@@ -69,16 +73,6 @@
             (h_hbm, g_hbm, b_hbm, m_hbm, s_hbm), (h_ref, g_ref, b_ref, m_ref, s_ref), sems
         )
     ]
-    copies.append(
-        pltpu.make_async_copy(
-            w_hbm.at[pl.ds(pl.multiple_of(HALF * z, HALF), UNIT), :], lead, l_sem
-        )
-    )
-    copies.append(
-        pltpu.make_async_copy(
-            w_hbm.at[pl.ds(pl.multiple_of(UNIT * (1 - z), HALF), HALF), :], rest, r_sem
-        )
-    )
     for copy in copies:
         copy.start()
     for copy in copies[:4]:
@@ -102,8 +96,18 @@
         b2[4 + kv] = stale(3, kv)
     b1[6] = stale(2, 0)
     b2[6] = stale(2, 1)
-    copies[5].wait()
-    copies[6].wait()
+
+
+def weight_body(w_hbm, after, far_ref, near_ref, sems):
+    del after
+    copies = [
+        pltpu.make_async_copy(w_hbm.at[:PART], far_ref, sems.at[0]),
+        pltpu.make_async_copy(w_hbm.at[PART:], near_ref, sems.at[1]),
+    ]
+    for copy in copies:
+        copy.start()
+    for copy in copies:
+        copy.wait()
 
 
 def pass_body(t1, t3, from1, from3):
@@ -128,11 +132,15 @@
 
 def project_body(t0, t1, c_ref, d_ref, t3, w_ref, v_ref, u_ref, early, *outs):
     del early
-    front_o, back_o, opp_o, keep_o, both = outs
+    front_o, back_o, opp_o, keep_o, both, other = outs
     _, z = where_am_i()
+    other[:PART] = v_ref[...]
+    other[PART:] = u_ref[...]
     mine = w_ref[pl.ds(pl.multiple_of(UNIT * (1 - z), HALF), HALF), :]
     both[pl.ds(pl.multiple_of(HALF * z, HALF), HALF), :] = mine
-    both[pl.ds(pl.multiple_of(HALF * (1 - z), HALF), HALF), :] = u_ref[...]
+    both[pl.ds(pl.multiple_of(HALF * (1 - z), HALF), HALF), :] = other[
+        pl.ds(pl.multiple_of(UNIT * z, HALF), HALF), :
+    ]
     placed = [[t[g] for g in range(4)] for t in (t0, t1, t3)]
     placed.insert(2, [c_ref[0], c_ref[1], d_ref[0], d_ref[1]])
     tokens = jnp.concatenate([jnp.concatenate(b, axis=1) for b in placed], axis=0)
@@ -143,7 +151,7 @@
 
     front = product(w_ref[pl.ds(pl.multiple_of(HALF * z, HALF), UNIT), :])
     mid = product(both[...])
-    back = product(v_ref[...])
+    back = product(other[pl.ds(pl.multiple_of(HALF * (1 - z), HALF), UNIT), :])
     for j in range(4):
         front_o[j] = front[j]
         back_o[j] = back[j]
@@ -206,8 +214,9 @@
             o_refs[j][:, cols] = (gates[:, cols] * (summed / total)).astype(BF)
 
 
-def fresh_body(k_ref, a_ref, b_ref, p_ref, after, f_ref):
+def fresh_body(k_ref, a_ref, b_ref, p_ref, after, f_ref, mark):
     del after
+    mark[...] = jnp.zeros_like(mark)
     x, z = where_am_i()
     rows = (
         (0, (k_ref.at[4], k_ref.at[0], k_ref.at[5])),
@@ -226,7 +235,8 @@
                 f_ref[0, g // 4 - 1, :, cols] = ref[...]
 
 
-def finish_body(a0, a1, a2, a3, h_ref, o_ref):
+def finish_body(a0, a1, a2, a3, h_ref, after, o_ref):
+    del after
     x, z = where_am_i()
     for j, ref in enumerate((a0, a1, a2, a3)):
         group = ((x + (1 - 2 * z) * j + 4) % 4) ^ 1
@@ -245,11 +255,11 @@
         return jax.ShapeDtypeStruct((count, D), BF)
 
     weight = jnp.swapaxes(w_qkv[0], 0, 1)
-    t0, t3, t1, lead, rest = pl.pallas_call(
+    t0, t3, t1, begun = pl.pallas_call(
         norm_body,
-        out_shape=(blocks(6), blocks(7), blocks(7), rows(UNIT), rows(HALF)),
-        in_specs=[pl.BlockSpec(memory_space=pltpu.HBM)] * 6,
-        out_specs=(VM,) * 5,
+        out_shape=(blocks(6), blocks(7), blocks(7), MARK),
+        in_specs=[HBM] * 5,
+        out_specs=(VM,) * 4,
         scratch_shapes=[
             pltpu.VMEM((1, ROWS, D), BF),
             pltpu.VMEM((1, D), F32),
@@ -257,13 +267,21 @@
             pltpu.VMEM((1, ROWS), jnp.int32),
             pltpu.VMEM((1, 2, ROWS, D), BF),
         ]
-        + [pltpu.SemaphoreType.DMA] * 7,
+        + [pltpu.SemaphoreType.DMA] * 5,
         compiler_params=pltpu.CompilerParams(vmem_limit_bytes=60 * 1024 * 1024),
-    )(hidden, norm_gain, box_vec, box_mask, stale_kv, weight)
-    lead = lax.ppermute(lead, ("dp", "patch"), far_pairs(parts))
+    )(hidden, norm_gain, box_vec, box_mask, stale_kv)
+    far_rows, near_rows = pl.pallas_call(
+        weight_body,
+        out_shape=(rows(PART), rows(UNIT + HALF - PART)),
+        in_specs=[HBM, VM],
+        out_specs=(VM, VM),
+        scratch_shapes=[pltpu.SemaphoreType.DMA((2,))],
+        compiler_params=PARAMS,
+    )(weight, begun)
     t3 = lax.ppermute(t3, "patch", x_pairs(1))
     t1 = lax.ppermute(t1, "patch", x_pairs(3))
-    rest = lax.ppermute(rest, "patch", partner_pairs())
+    near_rows = lax.ppermute(near_rows, "patch", partner_pairs())
+    far_rows = lax.ppermute(far_rows, ("dp", "patch"), far_pairs(parts))
     before = lax.ppermute(hidden, "segment", [(i, (i + 1) % segments) for i in range(segments)])
 
     t2a, t2b = call(pass_body, (blocks(3), blocks(3)), 2)(t1, t3)
@@ -278,8 +296,8 @@
         project_body,
         (blocks(6), blocks(6), blocks(3), blocks(6)),
         9,
-        scratch_shapes=[pltpu.VMEM((UNIT, D), BF)],
-    )(t0, t1, t2a, t2b, t3, weight, lead, rest, before)
+        scratch_shapes=[pltpu.VMEM((UNIT, D), BF), pltpu.VMEM((UNIT + HALF, D), BF)],
+    )(t0, t1, t2a, t2b, t3, weight, far_rows, near_rows, before)
     front = lax.ppermute(front, "patch", x_pairs(1))
     back = lax.ppermute(back, "patch", x_pairs(3))
     opposite, mark = lax.optimization_barrier((opposite, back[0, :16, :128]))
@@ -288,7 +306,7 @@
     out = call(attend_body, (blocks(),) * 4, 11)(
         keep, front, back, t0, t1, t2a, t2b, t3, near, far, gate
     )
-    fresh = call(fresh_body, jax.ShapeDtypeStruct((1, 2, ROWS, D), BF), 5)(
+    fresh, done = call(fresh_body, (jax.ShapeDtypeStruct((1, 2, ROWS, D), BF), MARK), 5)(
         keep, front, back, opposite, mark
     )
 
@@ -300,8 +318,8 @@
             for src, dst in x_pairs(j)
         ]
         came.append(lax.ppermute(out[j], ("segment", "patch"), pairs))
-    passed = call(finish_body, jax.ShapeDtypeStruct((1, ROWS, D), BF), 5)(
-        came[0], came[3], came[2], came[1], before
+    passed = call(finish_body, jax.ShapeDtypeStruct((1, ROWS, D), BF), 6)(
+        came[0], came[3], came[2], came[1], before, done
     )
     return (passed, fresh)
 

time: 99.6 us -> 96.6 us (0.970)
  the two profiles are of different devices: /device:TPU:1 before, /device:TPU:25 now
where the time goes in v8:
time: 96.6 us; the launch traced here: 96 us
  starting transfers between devices  61.3 us (63%)
  waiting for transfers between devices  19.2 us (20%)
  Pallas kernels  12.4 us (13%)
  local copies, waits for them, and re-layouts  2.18 us (2%)
    ppermute x4, starting transfers between devices, local(): came.append(lax.ppermute(out[j], ('segment', 'patch'), pairs))  19.7 us
    ppermute x1, starting transfers between devices, local(): far_rows = lax.ppermute(far_rows, ('dp', 'patch'), far_pairs(parts))  8.79 us
    ppermute x1, waiting for transfers between devices, local(): back = lax.ppermute(back, 'patch', x_pairs(3))  8.18 us
    ppermute x1, waiting for transfers between devices, local(): far_rows = lax.ppermute(far_rows, ('dp', 'patch'), far_pairs(parts))  4.86 us
    ppermute x1, starting transfers between devices, local(): t2a = lax.ppermute(t2a, 'patch', x_pairs(3))  4.85 us
    pallas_call x1, Pallas kernels, local(): call(attend_body, (blocks(),) * 4, 11)  4.45 us
    ppermute x1, starting transfers between devices, local(): t1 = lax.ppermute(t1, 'patch', x_pairs(3))  4.39 us
    ppermute x4, waiting for transfers between devices, local(): came.append(lax.ppermute(out[j], ('segment', 'patch'), pairs))  4.38 us
  transfers between devices with their start and end apart: 16, of which 6 were waited for; matrix products, arithmetic and copies ran while one was open for 0% of the time, Pallas kernels for 9%

profile of v8, /device:TPU:25, one launch (start us, length us, event | category | flops | bytes accessed | tf_op | source)
XLA Modules:
  0.0 96.0 jit_solution(12113808300412546443)
XLA Ops:
  0.6 2.8 %shard_map.86 = (bf16[6,128,384]{2,1,0:T(8,128)(2,1)}, bf16[7,128,384]{2,1,0:T(8,128)(2,1)}, bf16[7,128,384]{2,1,0:T(8,128)(2,1)}, f32[8,128]{1,0:T(8,128)}) custom-call(bf16[1,128,1536]{2,1,0:T(8,128)(2,1)} %h_hbm.1, f32[1,1536]{1,0:T(1,128)} %g_hbm.1, f32[1,1536]{1,0:T(1,128)} %b_hbm.1, s32[1,128]{1,0:T(1,128)} %m_hbm.1, bf16[1,2,128,1536]{3,2,1,0:T(8,128)(2,1)} %s_hbm.1), custom_call_target="tpu_custom_call" | custom-call | tf_op jit(solution)/shard_map/pallas_call | solution.py:258
  3.4 4.4 %collective-permute-start = (bf16[7,128,384]{2,1,0:T(8,128)(2,1)}, bf16[7,128,384]{2,1,0:T(8,128)(2,1)S(1)}, u32[]{:S(2)}, u32[]{:S(2)}) collective-permute-start(bf16[7,128,384]{2,1,0:T(8,128)(2,1)} %get-tuple-element.23), channel_id=1, source_target_pairs={{0,6},{1,3},{2,0},{3,5},{4,2},{5,7},{6,4},{7,1},{8,14},{9,11},{10,... | collective-permute-start | bytes 2064392 | tf_op jit(solution)/shard_map/ppermute | solution.py:282
  7.8 1.9 %collective-permute-start.1 = (bf16[7,128,384]{2,1,0:T(8,128)(2,1)}, bf16[7,128,384]{2,1,0:T(8,128)(2,1)S(1)}, u32[]{:S(2)}, u32[]{:S(2)}) collective-permute-start(bf16[7,128,384]{2,1,0:T(8,128)(2,1)} %get-tuple-element.24), channel_id=1, source_target_pairs={{0,2},{1,7},{2,4},{3,1},{4,6},{5,3},{6,0},{7,5},{8,10},{9,15},{10,... | collective-permute-start | bytes 2064392 | tf_op jit(solution)/shard_map/ppermute | solution.py:281
  9.8 1.5 %copy-done = bf16[1,1536,576]{1,2,0:T(8,128)(2,1)S(1)} copy-done((bf16[1,1536,576]{1,2,0:T(8,128)(2,1)S(1)}, bf16[1,1536,576]{1,2,0:T(8,128)(2,1)}, u32[]{:S(2)}) %copy-start) | copy-done | bytes 1769496
  11.3 0.7 copy-done.4
  11.9 0.4 shard_map.88
  12.3 4.2 %collective-permute-start.5 = (bf16[304,1536]{1,0:T(8,128)(2,1)S(1)}, bf16[304,1536]{1,0:T(8,128)(2,1)S(1)}, u32[]{:S(2)}, u32[]{:S(2)}) collective-permute-start(bf16[304,1536]{1,0:T(8,128)(2,1)S(1)} %get-tuple-element.29), channel_id=1, source_target_pairs={{0,1},{1,0},{2,3},{3,2},{4,5},{5,4},{6,7},{7,6},{8,9},{9,8},{10,11... | collective-permute-start | bytes 2801672 | tf_op jit(solution)/shard_map/ppermute | solution.py:283
  16.5 8.8 %collective-permute-start.4 = (bf16[272,1536]{1,0:T(8,128)(2,1)S(1)}, bf16[272,1536]{1,0:T(8,128)(2,1)S(1)}, u32[]{:S(2)}, u32[]{:S(2)}) collective-permute-start(bf16[272,1536]{1,0:T(8,128)(2,1)S(1)} %get-tuple-element.28), channel_id=1, source_target_pairs={{0,385},{1,128},{2,387},{3,130},{4,389},{5,132},{6,391},{7,134},{1... | collective-permute-start | bytes 2506760 | tf_op jit(solution)/shard_map/ppermute | solution.py:284
  25.3 3.9 %collective-permute-start.6 = (bf16[1,128,1536]{2,1,0:T(8,128)(2,1)S(1)}, bf16[1,128,1536]{2,1,0:T(8,128)(2,1)S(1)}, u32[]{:S(2)}, u32[]{:S(2)}) collective-permute-start(bf16[1,128,1536]{2,1,0:T(8,128)(2,1)S(1)} %copy-done.5), channel_id=1, source_target_pairs={{0,8},{8,16},{16,24},{24,32},{32,40},{40,48},{48,56},{56,64},{64,7... | collective-permute-start | bytes 1179656 | tf_op jit(solution)/shard_map/ppermute | solution.py:285
  29.3 0.1 shard_map.87
  29.3 4.9 %collective-permute-start.2 = (bf16[3,128,384]{2,1,0:T(8,128)(2,1)S(1)}, bf16[3,128,384]{2,1,0:T(8,128)(2,1)S(1)}, u32[]{:S(2)}, u32[]{:S(2)}) collective-permute-start(bf16[3,128,384]{2,1,0:T(8,128)(2,1)S(1)} %get-tuple-element.25), channel_id=1, source_target_pairs={{0,6},{1,3},{2,0},{3,5},{4,2},{5,7},{6,4},{7,1},{8,14},{9,11},{10,... | collective-permute-start | bytes 884744 | tf_op jit(solution)/shard_map/ppermute | solution.py:288
  34.2 1.9 %collective-permute-start.3 = (bf16[3,128,384]{2,1,0:T(8,128)(2,1)S(1)}, bf16[3,128,384]{2,1,0:T(8,128)(2,1)S(1)}, u32[]{:S(2)}, u32[]{:S(2)}) collective-permute-start(bf16[3,128,384]{2,1,0:T(8,128)(2,1)S(1)} %get-tuple-element.26), channel_id=1, source_target_pairs={{0,2},{1,7},{2,4},{3,1},{4,6},{5,3},{6,0},{7,5},{8,10},{9,15},{10,... | collective-permute-start | bytes 884744 | tf_op jit(solution)/shard_map/ppermute | solution.py:289
  36.1 0.1 shard_map.90
  36.2 1.9 %collective-permute-start.9 = (bf16[3,2,128,384]{3,2,1,0:T(8,128)(2,1)S(1)}, bf16[3,2,128,384]{3,2,1,0:T(8,128)(2,1)S(1)}, u32[]{:S(2)}, u32[]{:S(2)}) collective-permute-start(bf16[3,2,128,384]{3,2,1,0:T(8,128)(2,1)S(1)} %shard_map.90), channel_id=1, source_target_pairs={{0,1},{1,0},{2,3},{3,2},{4,5},{5,4},{6,7},{7,6},{8,9},{9,8},{10,11... | collective-permute-start | bytes 1769480 | tf_op jit(solution)/shard_map/ppermute | solution.py:291
  38.1 4.9 %collective-permute-done.4.v_ref = bf16[272,1536]{1,0:T(8,128)(2,1)S(1)} collective-permute-done((bf16[272,1536]{1,0:T(8,128)(2,1)S(1)}, bf16[272,1536]{1,0:T(8,128)(2,1)S(1)}, u32[]{:S(2)}, u32[]{:S(2)}) %collective-permute-start.4) | collective-permute-done | bytes 835616 | tf_op jit(solution)/shard_map/ppermute | solution.py:284
  43.0 1.5 %collective-permute-done.3.d_ref = bf16[3,128,384]{2,1,0:T(8,128)(2,1)S(1)} collective-permute-done((bf16[3,128,384]{2,1,0:T(8,128)(2,1)S(1)}, bf16[3,128,384]{2,1,0:T(8,128)(2,1)S(1)}, u32[]{:S(2)}, u32[]{:S(2)}) %collective-permute-start.3) | collective-permute-done | bytes 294944 | tf_op jit(solution)/shard_map/ppermute | solution.py:289
  44.5 2.7 %shard_map.89 = (bf16[6,128,384]{2,1,0:T(8,128)(2,1)S(1)}, bf16[6,128,384]{2,1,0:T(8,128)(2,1)S(1)}, bf16[3,128,384]{2,1,0:T(8,128)(2,1)S(1)}, bf16[6,128,384]{2,1,0:T(8,128)(2,1)S(1)}) custom-call(bf16[6,128,384]{2,1,0:T(8,128)(2,1)S(1)} %copy-done.2, bf16[7,128,384]{2,1,0:T(8,128)(2,1)S(1)} %collective-permute-done.t1, ...), custom_call_target="tpu_custom_call" | custom-call | tf_op jit(solution)/shard_map/pallas_call | solution.py:295
  47.1 2.8 %collective-permute-start.8 = (bf16[6,128,384]{2,1,0:T(8,128)(2,1)S(1)}, bf16[6,128,384]{2,1,0:T(8,128)(2,1)S(1)}, u32[]{:S(2)}, u32[]{:S(2)}) collective-permute-start(bf16[6,128,384]{2,1,0:T(8,128)(2,1)S(1)} %get-tuple-element.32), channel_id=1, source_target_pairs={{0,6},{1,3},{2,0},{3,5},{4,2},{5,7},{6,4},{7,1},{8,14},{9,11},{10,... | collective-permute-start | bytes 1769480 | tf_op jit(solution)/shard_map/ppermute | solution.py:302
  50.0 2.4 %collective-permute-start.7 = (bf16[6,128,384]{2,1,0:T(8,128)(2,1)S(1)}, bf16[6,128,384]{2,1,0:T(8,128)(2,1)S(1)}, u32[]{:S(2)}, u32[]{:S(2)}) collective-permute-start(bf16[6,128,384]{2,1,0:T(8,128)(2,1)S(1)} %get-tuple-element.31), channel_id=1, source_target_pairs={{0,2},{1,7},{2,4},{3,1},{4,6},{5,3},{6,0},{7,5},{8,10},{9,15},{10,... | collective-permute-start | bytes 1769480 | tf_op jit(solution)/shard_map/ppermute | solution.py:301
  52.4 0.3 collective-permute-done.9.after.pn_ref
  52.7 2.6 %collective-permute-start.10 = (bf16[2,128,384]{2,1,0:T(8,128)(2,1)S(1)}, bf16[2,128,384]{2,1,0:T(8,128)(2,1)S(1)}, u32[]{:S(2)}, u32[]{:S(2)}) collective-permute-start(bf16[2,128,384]{2,1,0:T(8,128)(2,1)S(1)} %shard_map.91), channel_id=1, source_target_pairs={{0,1},{1,0},{2,3},{3,2},{4,5},{5,4},{6,7},{7,6},{8,9},{9,8},{10,11... | collective-permute-start | bytes 589832 | tf_op jit(solution)/shard_map/ppermute | solution.py:293
  55.3 8.2 %collective-permute-done.8.b_ref = bf16[6,128,384]{2,1,0:T(8,128)(2,1)S(1)} collective-permute-done((bf16[6,128,384]{2,1,0:T(8,128)(2,1)S(1)}, bf16[6,128,384]{2,1,0:T(8,128)(2,1)S(1)}, u32[]{:S(2)}, u32[]{:S(2)}) %collective-permute-start.8) | collective-permute-done | bytes 589856 | tf_op jit(solution)/shard_map/ppermute | solution.py:302
  63.5 1.9 %collective-permute-start.15 = (bf16[3,128,384]{2,1,0:T(8,128)(2,1)S(1)}, bf16[3,128,384]{2,1,0:T(8,128)(2,1)S(1)}, u32[]{:S(2)}, u32[]{:S(2)}) collective-permute-start(bf16[3,128,384]{2,1,0:T(8,128)(2,1)S(1)} %get-tuple-element.38), channel_id=1, source_target_pairs={{0,4},{1,5},{2,6},{3,7},{4,0},{5,1},{6,2},{7,3},{8,12},{9,13},{10,... | collective-permute-start | bytes 884744 | tf_op jit(solution)/shard_map/ppermute | solution.py:304
  65.5 4.4 %shard_map.92 = (bf16[128,384]{1,0:T(8,128)(2,1)S(1)}, bf16[128,384]{1,0:T(8,128)(2,1)S(1)}, bf16[128,384]{1,0:T(8,128)(2,1)S(1)}, bf16[128,384]{1,0:T(8,128)(2,1)S(1)}) custom-call(bf16[6,128,384]{2,1,0:T(8,128)(2,1)S(1)} %get-tuple-element.30.m_ref.k_ref, bf16[6,128,384]{2,1,0:T(8,128)(2,1)S(1)} %collective-permute-done.7.a_ref, ...), custom_call_target="tpu_custom_call" | custom-call | tf_op jit(solution)/shard_map/pallas_call | solution.py:306
  69.9 12.1 %collective-permute-start.11 = (bf16[128,384]{1,0:T(8,128)(2,1)S(1)}, bf16[128,384]{1,0:T(8,128)(2,1)S(1)}, u32[]{:S(2)}, u32[]{:S(2)}) collective-permute-start(bf16[128,384]{1,0:T(8,128)(2,1)S(1)} %get-tuple-element.33), channel_id=1, source_target_pairs={{0,8},{1,9},{2,10},{3,11},{4,12},{5,13},{6,14},{7,15},{8,16},{9,17... | collective-permute-start | bytes 294920 | tf_op jit(solution)/shard_map/ppermute | solution.py:320
  82.0 1.9 %collective-permute-start.12 = (bf16[128,384]{1,0:T(8,128)(2,1)S(1)}, bf16[128,384]{1,0:T(8,128)(2,1)S(1)}, u32[]{:S(2)}, u32[]{:S(2)}) collective-permute-start(bf16[128,384]{1,0:T(8,128)(2,1)S(1)} %get-tuple-element.34), channel_id=1, source_target_pairs={{0,14},{1,11},{2,8},{3,13},{4,10},{5,15},{6,12},{7,9},{8,22},{9,19... | collective-permute-start | bytes 294920 | tf_op jit(solution)/shard_map/ppermute | solution.py:320
  83.9 1.9 %collective-permute-start.13 = (bf16[128,384]{1,0:T(8,128)(2,1)S(1)}, bf16[128,384]{1,0:T(8,128)(2,1)S(1)}, u32[]{:S(2)}, u32[]{:S(2)}) collective-permute-start(bf16[128,384]{1,0:T(8,128)(2,1)S(1)} %get-tuple-element.35), channel_id=1, source_target_pairs={{0,12},{1,13},{2,14},{3,15},{4,8},{5,9},{6,10},{7,11},{8,20},{9,21... | collective-permute-start | bytes 294920 | tf_op jit(solution)/shard_map/ppermute | solution.py:320
  85.9 3.8 %collective-permute-start.14 = (bf16[128,384]{1,0:T(8,128)(2,1)S(1)}, bf16[128,384]{1,0:T(8,128)(2,1)S(1)}, u32[]{:S(2)}, u32[]{:S(2)}) collective-permute-start(bf16[128,384]{1,0:T(8,128)(2,1)S(1)} %get-tuple-element.36), channel_id=1, source_target_pairs={{0,10},{1,15},{2,12},{3,9},{4,14},{5,11},{6,8},{7,13},{8,18},{9,23... | collective-permute-start | bytes 294920 | tf_op jit(solution)/shard_map/ppermute | solution.py:320
  89.6 1.1 %shard_map.93 = (bf16[1,2,128,1536]{3,2,1,0:T(8,128)(2,1)}, f32[8,128]{1,0:T(8,128)S(1)}) custom-call(bf16[6,128,384]{2,1,0:T(8,128)(2,1)S(1)} %get-tuple-element.30.m_ref.k_ref, bf16[6,128,384]{2,1,0:T(8,128)(2,1)S(1)} %collective-permute-done.7.a_ref, bf16[6,128,384]{2,1,0:T(8,128)(2,1)S(1)} %collective-permute-done.8.b_ref, ...), custom_call_target="tpu_custom_call" | custom-call | tf_op jit(solution)/shard_map/pallas_call | solution.py:309
  90.7 1.6 %collective-permute-done.13.a2 = bf16[128,384]{1,0:T(8,128)(2,1)S(1)} collective-permute-done((bf16[128,384]{1,0:T(8,128)(2,1)S(1)}, bf16[128,384]{1,0:T(8,128)(2,1)S(1)}, u32[]{:S(2)}, u32[]{:S(2)}) %collective-permute-start.13) | collective-permute-done | bytes 98336 | tf_op jit(solution)/shard_map/ppermute | solution.py:320
  92.3 2.8 %collective-permute-done.14.a3 = bf16[128,384]{1,0:T(8,128)(2,1)S(1)} collective-permute-done((bf16[128,384]{1,0:T(8,128)(2,1)S(1)}, bf16[128,384]{1,0:T(8,128)(2,1)S(1)}, u32[]{:S(2)}, u32[]{:S(2)}) %collective-permute-start.14) | collective-permute-done | bytes 98336 | tf_op jit(solution)/shard_map/ppermute | solution.py:320
  95.1 0.9 shard_map.94
  (22 shorter events, 0.1 us)
Async XLA Ops:
  0.6 24.7 %copy-start.5 = (bf16[1,128,1536]{2,1,0:T(8,128)(2,1)S(1)}, bf16[1,128,1536]{2,1,0:T(8,128)(2,1)}, u32[]{:S(2)}) copy-start(bf16[1,128,1536]{2,1,0:T(8,128)(2,1)} %h_hbm.1) | copy-start | bytes 1179652
  3.4 25.8 %collective-permute-start = (bf16[7,128,384]{2,1,0:T(8,128)(2,1)}, bf16[7,128,384]{2,1,0:T(8,128)(2,1)S(1)}, u32[]{:S(2)}, u32[]{:S(2)}) collective-permute-start(bf16[7,128,384]{2,1,0:T(8,128)(2,1)} %get-tuple-element.23), channel_id=1, source_target_pairs={{0,6},{1,3},{2,0},{3,5},{4,2},{5,7},{6,4},{7,1},{8,14},{9,11},{10,... | collective-permute-start | bytes 2064392 | tf_op jit(solution)/shard_map/ppermute | solution.py:282
  7.8 21.4 %collective-permute-start.1 = (bf16[7,128,384]{2,1,0:T(8,128)(2,1)}, bf16[7,128,384]{2,1,0:T(8,128)(2,1)S(1)}, u32[]{:S(2)}, u32[]{:S(2)}) collective-permute-start(bf16[7,128,384]{2,1,0:T(8,128)(2,1)} %get-tuple-element.24), channel_id=1, source_target_pairs={{0,2},{1,7},{2,4},{3,1},{4,6},{5,3},{6,0},{7,5},{8,10},{9,15},{10,... | collective-permute-start | bytes 2064392 | tf_op jit(solution)/shard_map/ppermute | solution.py:281
  9.8 1.5 %copy-start = (bf16[1,1536,576]{1,2,0:T(8,128)(2,1)S(1)}, bf16[1,1536,576]{1,2,0:T(8,128)(2,1)}, u32[]{:S(2)}) copy-start(bf16[1,1536,576]{1,2,0:T(8,128)(2,1)} %param.8) | copy-start | bytes 5308420
  11.2 0.7 copy-start.4
  11.9 24.2 %copy-start.2 = (bf16[6,128,384]{2,1,0:T(8,128)(2,1)S(1)}, bf16[6,128,384]{2,1,0:T(8,128)(2,1)}, u32[]{:S(2)}) copy-start(bf16[6,128,384]{2,1,0:T(8,128)(2,1)} %get-tuple-element.22.t0) | copy-start | bytes 1769476
  12.3 30.7 %collective-permute-start.5 = (bf16[304,1536]{1,0:T(8,128)(2,1)S(1)}, bf16[304,1536]{1,0:T(8,128)(2,1)S(1)}, u32[]{:S(2)}, u32[]{:S(2)}) collective-permute-start(bf16[304,1536]{1,0:T(8,128)(2,1)S(1)} %get-tuple-element.29), channel_id=1, source_target_pairs={{0,1},{1,0},{2,3},{3,2},{4,5},{5,4},{6,7},{7,6},{8,9},{9,8},{10,11... | collective-permute-start | bytes 2801672 | tf_op jit(solution)/shard_map/ppermute | solution.py:283
  16.5 28.0 %copy-start.1 = (bf16[1,1536,576]{1,2,0:T(8,128)(2,1)S(1)}, bf16[1,1536,576]{1,2,0:T(8,128)(2,1)}, u32[]{:S(2)}) copy-start(bf16[1,1536,576]{1,2,0:T(8,128)(2,1)} %param.8) | copy-start | bytes 5308420
  16.5 26.5 %collective-permute-start.4 = (bf16[272,1536]{1,0:T(8,128)(2,1)S(1)}, bf16[272,1536]{1,0:T(8,128)(2,1)S(1)}, u32[]{:S(2)}, u32[]{:S(2)}) collective-permute-start(bf16[272,1536]{1,0:T(8,128)(2,1)S(1)} %get-tuple-element.28), channel_id=1, source_target_pairs={{0,385},{1,128},{2,387},{3,130},{4,389},{5,132},{6,391},{7,134},{1... | collective-permute-start | bytes 2506760 | tf_op jit(solution)/shard_map/ppermute | solution.py:284
  25.3 10.9 %collective-permute-start.6 = (bf16[1,128,1536]{2,1,0:T(8,128)(2,1)S(1)}, bf16[1,128,1536]{2,1,0:T(8,128)(2,1)S(1)}, u32[]{:S(2)}, u32[]{:S(2)}) collective-permute-start(bf16[1,128,1536]{2,1,0:T(8,128)(2,1)S(1)} %copy-done.5), channel_id=1, source_target_pairs={{0,8},{8,16},{16,24},{24,32},{32,40},{40,48},{48,56},{56,64},{64,7... | collective-permute-start | bytes 1179656 | tf_op jit(solution)/shard_map/ppermute | solution.py:285
  29.3 13.7 %collective-permute-start.2 = (bf16[3,128,384]{2,1,0:T(8,128)(2,1)S(1)}, bf16[3,128,384]{2,1,0:T(8,128)(2,1)S(1)}, u32[]{:S(2)}, u32[]{:S(2)}) collective-permute-start(bf16[3,128,384]{2,1,0:T(8,128)(2,1)S(1)} %get-tuple-element.25), channel_id=1, source_target_pairs={{0,6},{1,3},{2,0},{3,5},{4,2},{5,7},{6,4},{7,1},{8,14},{9,11},{10,... | collective-permute-start | bytes 884744 | tf_op jit(solution)/shard_map/ppermute | solution.py:288
  34.2 10.3 %collective-permute-start.3 = (bf16[3,128,384]{2,1,0:T(8,128)(2,1)S(1)}, bf16[3,128,384]{2,1,0:T(8,128)(2,1)S(1)}, u32[]{:S(2)}, u32[]{:S(2)}) collective-permute-start(bf16[3,128,384]{2,1,0:T(8,128)(2,1)S(1)} %get-tuple-element.26), channel_id=1, source_target_pairs={{0,2},{1,7},{2,4},{3,1},{4,6},{5,3},{6,0},{7,5},{8,10},{9,15},{10,... | collective-permute-start | bytes 884744 | tf_op jit(solution)/shard_map/ppermute | solution.py:289
  36.2 29.3 %copy-start.3 = (f32[1,1536]{1,0:T(1,128)S(1)}, f32[1,1536]{1,0:T(1,128)}, u32[]{:S(2)}) copy-start(f32[1,1536]{1,0:T(1,128)} %g_ref.1) | copy-start | bytes 18436
  36.2 16.5 %collective-permute-start.9 = (bf16[3,2,128,384]{3,2,1,0:T(8,128)(2,1)S(1)}, bf16[3,2,128,384]{3,2,1,0:T(8,128)(2,1)S(1)}, u32[]{:S(2)}, u32[]{:S(2)}) collective-permute-start(bf16[3,2,128,384]{3,2,1,0:T(8,128)(2,1)S(1)} %shard_map.90), channel_id=1, source_target_pairs={{0,1},{1,0},{2,3},{3,2},{4,5},{5,4},{6,7},{7,6},{8,9},{9,8},{10,11... | collective-permute-start | bytes 1769480 | tf_op jit(solution)/shard_map/ppermute | solution.py:291
  47.1 16.4 %collective-permute-start.8 = (bf16[6,128,384]{2,1,0:T(8,128)(2,1)S(1)}, bf16[6,128,384]{2,1,0:T(8,128)(2,1)S(1)}, u32[]{:S(2)}, u32[]{:S(2)}) collective-permute-start(bf16[6,128,384]{2,1,0:T(8,128)(2,1)S(1)} %get-tuple-element.32), channel_id=1, source_target_pairs={{0,6},{1,3},{2,0},{3,5},{4,2},{5,7},{6,4},{7,1},{8,14},{9,11},{10,... | collective-permute-start | bytes 1769480 | tf_op jit(solution)/shard_map/ppermute | solution.py:302
  50.0 15.5 %collective-permute-start.7 = (bf16[6,128,384]{2,1,0:T(8,128)(2,1)S(1)}, bf16[6,128,384]{2,1,0:T(8,128)(2,1)S(1)}, u32[]{:S(2)}, u32[]{:S(2)}) collective-permute-start(bf16[6,128,384]{2,1,0:T(8,128)(2,1)S(1)} %get-tuple-element.31), channel_id=1, source_target_pairs={{0,2},{1,7},{2,4},{3,1},{4,6},{5,3},{6,0},{7,5},{8,10},{9,15},{10,... | collective-permute-start | bytes 1769480 | tf_op jit(solution)/shard_map/ppermute | solution.py:301
  52.7 12.7 %collective-permute-start.10 = (bf16[2,128,384]{2,1,0:T(8,128)(2,1)S(1)}, bf16[2,128,384]{2,1,0:T(8,128)(2,1)S(1)}, u32[]{:S(2)}, u32[]{:S(2)}) collective-permute-start(bf16[2,128,384]{2,1,0:T(8,128)(2,1)S(1)} %shard_map.91), channel_id=1, source_target_pairs={{0,1},{1,0},{2,3},{3,2},{4,5},{5,4},{6,7},{7,6},{8,9},{9,8},{10,11... | collective-permute-start | bytes 589832 | tf_op jit(solution)/shard_map/ppermute | solution.py:293
  63.5 26.1 %collective-permute-start.15 = (bf16[3,128,384]{2,1,0:T(8,128)(2,1)S(1)}, bf16[3,128,384]{2,1,0:T(8,128)(2,1)S(1)}, u32[]{:S(2)}, u32[]{:S(2)}) collective-permute-start(bf16[3,128,384]{2,1,0:T(8,128)(2,1)S(1)} %get-tuple-element.38), channel_id=1, source_target_pairs={{0,4},{1,5},{2,6},{3,7},{4,0},{5,1},{6,2},{7,3},{8,12},{9,13},{10,... | collective-permute-start | bytes 884744 | tf_op jit(solution)/shard_map/ppermute | solution.py:304
  69.9 20.8 %collective-permute-start.11 = (bf16[128,384]{1,0:T(8,128)(2,1)S(1)}, bf16[128,384]{1,0:T(8,128)(2,1)S(1)}, u32[]{:S(2)}, u32[]{:S(2)}) collective-permute-start(bf16[128,384]{1,0:T(8,128)(2,1)S(1)} %get-tuple-element.33), channel_id=1, source_target_pairs={{0,8},{1,9},{2,10},{3,11},{4,12},{5,13},{6,14},{7,15},{8,16},{9,17... | collective-permute-start | bytes 294920 | tf_op jit(solution)/shard_map/ppermute | solution.py:320
  82.0 8.7 %collective-permute-start.12 = (bf16[128,384]{1,0:T(8,128)(2,1)S(1)}, bf16[128,384]{1,0:T(8,128)(2,1)S(1)}, u32[]{:S(2)}, u32[]{:S(2)}) collective-permute-start(bf16[128,384]{1,0:T(8,128)(2,1)S(1)} %get-tuple-element.34), channel_id=1, source_target_pairs={{0,14},{1,11},{2,8},{3,13},{4,10},{5,15},{6,12},{7,9},{8,22},{9,19... | collective-permute-start | bytes 294920 | tf_op jit(solution)/shard_map/ppermute | solution.py:320
  83.9 8.4 %collective-permute-start.13 = (bf16[128,384]{1,0:T(8,128)(2,1)S(1)}, bf16[128,384]{1,0:T(8,128)(2,1)S(1)}, u32[]{:S(2)}, u32[]{:S(2)}) collective-permute-start(bf16[128,384]{1,0:T(8,128)(2,1)S(1)} %get-tuple-element.35), channel_id=1, source_target_pairs={{0,12},{1,13},{2,14},{3,15},{4,8},{5,9},{6,10},{7,11},{8,20},{9,21... | collective-permute-start | bytes 294920 | tf_op jit(solution)/shard_map/ppermute | solution.py:320
  85.9 9.3 %collective-permute-start.14 = (bf16[128,384]{1,0:T(8,128)(2,1)S(1)}, bf16[128,384]{1,0:T(8,128)(2,1)S(1)}, u32[]{:S(2)}, u32[]{:S(2)}) collective-permute-start(bf16[128,384]{1,0:T(8,128)(2,1)S(1)} %get-tuple-element.36), channel_id=1, source_target_pairs={{0,10},{1,15},{2,12},{3,9},{4,14},{5,11},{6,8},{7,13},{8,18},{9,23... | collective-permute-start | bytes 294920 | tf_op jit(solution)/shard_map/ppermute | solution.py:320

commit v9 on v8

--- a/solution.py
+++ b/solution.py
@@ -10,8 +10,8 @@
 D = 1536
 UNIT = 384
 HALF = 192
-PART = 272
-SCALE = HEAD_DIM ** (-0.5)
+PART = 256
+SCALE = HEAD_DIM ** (-0.5) * 1.4426950408889634
 BF = jnp.bfloat16
 F32 = jnp.float32
 MARK = jax.ShapeDtypeStruct((8, 128), F32)
@@ -196,18 +196,24 @@
             + [pf_ref[kv, :, cols]]
             for kv in range(2)
         ]
+        q, k, v = ([part(index, j) for j in range(4)] for index in roled)
+        scores = lax.dot_general(
+            jnp.concatenate(q, axis=0),
+            jnp.concatenate(kept[0], axis=0),
+            NT,
+            preferred_element_type=F32,
+        )
         for j in range(4):
-            q, k, v = (part(index, j) for index in roled)
-            keys = list(kept[0])
+            mine = lax.dot_general(q[j], k[j], NT, preferred_element_type=F32)
+            at = ROWS * j
+            block = scores[at : at + ROWS]
+            parts = [block[:, :at]] if j else []
+            block = jnp.concatenate(parts + [mine, block[:, at + ROWS :]], axis=1) * SCALE
+            top = jnp.max(block, axis=-1, keepdims=True)
+            weights = jnp.exp2(block - top)
+            total = jnp.sum(weights, axis=-1, keepdims=True)
             values = list(kept[1])
-            keys[j] = k
-            values[j] = v
-            scores = lax.dot_general(
-                q, jnp.concatenate(keys, axis=0), NT, preferred_element_type=F32
-            ) * SCALE
-            top = jnp.max(scores, axis=-1, keepdims=True)
-            weights = jnp.exp(scores - top)
-            total = jnp.sum(weights, axis=-1, keepdims=True)
+            values[j] = v[j]
             summed = jnp.dot(
                 weights.astype(BF), jnp.concatenate(values, axis=0), preferred_element_type=F32
             )

time: 96.6 us -> 93.8 us (0.971)
  the two profiles are of different devices: /device:TPU:25 before, /device:TPU:49 now
where the time goes in v9:
time: 93.8 us; the launch traced here: 93.2 us
  starting transfers between devices  54.6 us (58%)
  waiting for transfers between devices  22.7 us (24%)
  Pallas kernels  12.8 us (14%)
  local copies, waits for them, and re-layouts  2.18 us (2%)
    ppermute x4, starting transfers between devices, local(): came.append(lax.ppermute(out[j], ('segment', 'patch'), pairs))  15.7 us
    ppermute x1, starting transfers between devices, local(): far_rows = lax.ppermute(far_rows, ('dp', 'patch'), far_pairs(parts))  8.79 us
    ppermute x1, waiting for transfers between devices, local(): back = lax.ppermute(back, 'patch', x_pairs(3))  8.66 us
    ppermute x4, waiting for transfers between devices, local(): came.append(lax.ppermute(out[j], ('segment', 'patch'), pairs))  6.21 us
    ppermute x1, waiting for transfers between devices, local(): far_rows = lax.ppermute(far_rows, ('dp', 'patch'), far_pairs(parts))  5.92 us
    pallas_call x1, Pallas kernels, local(): call(attend_body, (blocks(),) * 4, 11)  4.87 us
    ppermute x1, starting transfers between devices, local(): t2a = lax.ppermute(t2a, 'patch', x_pairs(3))  4.85 us
    ppermute x1, starting transfers between devices, local(): t1 = lax.ppermute(t1, 'patch', x_pairs(3))  4.39 us
  transfers between devices with their start and end apart: 16, of which 6 were waited for; matrix products, arithmetic and copies ran while one was open for 0% of the time, Pallas kernels for 10%

profile of v9, /device:TPU:49, one launch (start us, length us, event | category | flops | bytes accessed | tf_op | source)
XLA Modules:
  0.0 93.2 jit_solution(400953891387823162)
XLA Ops:
  0.6 2.8 %shard_map.86 = (bf16[6,128,384]{2,1,0:T(8,128)(2,1)}, bf16[7,128,384]{2,1,0:T(8,128)(2,1)}, bf16[7,128,384]{2,1,0:T(8,128)(2,1)}, f32[8,128]{1,0:T(8,128)}) custom-call(bf16[1,128,1536]{2,1,0:T(8,128)(2,1)} %h_hbm.1, f32[1,1536]{1,0:T(1,128)} %g_hbm.1, f32[1,1536]{1,0:T(1,128)} %b_hbm.1, s32[1,128]{1,0:T(1,128)} %m_hbm.1, bf16[1,2,128,1536]{3,2,1,0:T(8,128)(2,1)} %s_hbm.1), custom_call_target="tpu_custom_call" | custom-call | tf_op jit(solution)/shard_map/pallas_call | solution.py:264
  3.4 4.4 %collective-permute-start = (bf16[7,128,384]{2,1,0:T(8,128)(2,1)}, bf16[7,128,384]{2,1,0:T(8,128)(2,1)S(1)}, u32[]{:S(2)}, u32[]{:S(2)}) collective-permute-start(bf16[7,128,384]{2,1,0:T(8,128)(2,1)} %get-tuple-element.23), channel_id=1, source_target_pairs={{0,6},{1,3},{2,0},{3,5},{4,2},{5,7},{6,4},{7,1},{8,14},{9,11},{10,... | collective-permute-start | bytes 2064392 | tf_op jit(solution)/shard_map/ppermute | solution.py:288
  7.8 1.9 %collective-permute-start.1 = (bf16[7,128,384]{2,1,0:T(8,128)(2,1)}, bf16[7,128,384]{2,1,0:T(8,128)(2,1)S(1)}, u32[]{:S(2)}, u32[]{:S(2)}) collective-permute-start(bf16[7,128,384]{2,1,0:T(8,128)(2,1)} %get-tuple-element.24), channel_id=1, source_target_pairs={{0,2},{1,7},{2,4},{3,1},{4,6},{5,3},{6,0},{7,5},{8,10},{9,15},{10,... | collective-permute-start | bytes 2064392 | tf_op jit(solution)/shard_map/ppermute | solution.py:287
  9.8 1.5 %copy-done = bf16[1,1536,576]{1,2,0:T(8,128)(2,1)S(1)} copy-done((bf16[1,1536,576]{1,2,0:T(8,128)(2,1)S(1)}, bf16[1,1536,576]{1,2,0:T(8,128)(2,1)}, u32[]{:S(2)}) %copy-start) | copy-done | bytes 1769496
  11.3 0.7 copy-done.4
  11.9 0.4 shard_map.88
  12.3 4.2 %collective-permute-start.5 = (bf16[320,1536]{1,0:T(8,128)(2,1)S(1)}, bf16[320,1536]{1,0:T(8,128)(2,1)S(1)}, u32[]{:S(2)}, u32[]{:S(2)}) collective-permute-start(bf16[320,1536]{1,0:T(8,128)(2,1)S(1)} %get-tuple-element.29), channel_id=1, source_target_pairs={{0,1},{1,0},{2,3},{3,2},{4,5},{5,4},{6,7},{7,6},{8,9},{9,8},{10,11... | collective-permute-start | bytes 2949128 | tf_op jit(solution)/shard_map/ppermute | solution.py:289
  16.5 8.8 %collective-permute-start.4 = (bf16[256,1536]{1,0:T(8,128)(2,1)S(1)}, bf16[256,1536]{1,0:T(8,128)(2,1)S(1)}, u32[]{:S(2)}, u32[]{:S(2)}) collective-permute-start(bf16[256,1536]{1,0:T(8,128)(2,1)S(1)} %get-tuple-element.28), channel_id=1, source_target_pairs={{0,385},{1,128},{2,387},{3,130},{4,389},{5,132},{6,391},{7,134},{1... | collective-permute-start | bytes 2359304 | tf_op jit(solution)/shard_map/ppermute | solution.py:290
  25.3 1.8 %collective-permute-start.6 = (bf16[1,128,1536]{2,1,0:T(8,128)(2,1)S(1)}, bf16[1,128,1536]{2,1,0:T(8,128)(2,1)S(1)}, u32[]{:S(2)}, u32[]{:S(2)}) collective-permute-start(bf16[1,128,1536]{2,1,0:T(8,128)(2,1)S(1)} %copy-done.5), channel_id=1, source_target_pairs={{0,8},{8,16},{16,24},{24,32},{32,40},{40,48},{48,56},{56,64},{64,7... | collective-permute-start | bytes 1179656 | tf_op jit(solution)/shard_map/ppermute | solution.py:291
  27.2 0.1 shard_map.87
  27.2 4.9 %collective-permute-start.2 = (bf16[3,128,384]{2,1,0:T(8,128)(2,1)S(1)}, bf16[3,128,384]{2,1,0:T(8,128)(2,1)S(1)}, u32[]{:S(2)}, u32[]{:S(2)}) collective-permute-start(bf16[3,128,384]{2,1,0:T(8,128)(2,1)S(1)} %get-tuple-element.25), channel_id=1, source_target_pairs={{0,6},{1,3},{2,0},{3,5},{4,2},{5,7},{6,4},{7,1},{8,14},{9,11},{10,... | collective-permute-start | bytes 884744 | tf_op jit(solution)/shard_map/ppermute | solution.py:294
  32.1 1.9 %collective-permute-start.3 = (bf16[3,128,384]{2,1,0:T(8,128)(2,1)S(1)}, bf16[3,128,384]{2,1,0:T(8,128)(2,1)S(1)}, u32[]{:S(2)}, u32[]{:S(2)}) collective-permute-start(bf16[3,128,384]{2,1,0:T(8,128)(2,1)S(1)} %get-tuple-element.26), channel_id=1, source_target_pairs={{0,2},{1,7},{2,4},{3,1},{4,6},{5,3},{6,0},{7,5},{8,10},{9,15},{10,... | collective-permute-start | bytes 884744 | tf_op jit(solution)/shard_map/ppermute | solution.py:295
  34.0 0.1 shard_map.90
  34.1 1.9 %collective-permute-start.9 = (bf16[3,2,128,384]{3,2,1,0:T(8,128)(2,1)S(1)}, bf16[3,2,128,384]{3,2,1,0:T(8,128)(2,1)S(1)}, u32[]{:S(2)}, u32[]{:S(2)}) collective-permute-start(bf16[3,2,128,384]{3,2,1,0:T(8,128)(2,1)S(1)} %shard_map.90), channel_id=1, source_target_pairs={{0,1},{1,0},{2,3},{3,2},{4,5},{5,4},{6,7},{7,6},{8,9},{9,8},{10,11... | collective-permute-start | bytes 1769480 | tf_op jit(solution)/shard_map/ppermute | solution.py:297
  36.0 5.9 %collective-permute-done.4.v_ref = bf16[256,1536]{1,0:T(8,128)(2,1)S(1)} collective-permute-done((bf16[256,1536]{1,0:T(8,128)(2,1)S(1)}, bf16[256,1536]{1,0:T(8,128)(2,1)S(1)}, u32[]{:S(2)}, u32[]{:S(2)}) %collective-permute-start.4) | collective-permute-done | bytes 786464 | tf_op jit(solution)/shard_map/ppermute | solution.py:290
  41.9 1.8 %collective-permute-done.3.d_ref = bf16[3,128,384]{2,1,0:T(8,128)(2,1)S(1)} collective-permute-done((bf16[3,128,384]{2,1,0:T(8,128)(2,1)S(1)}, bf16[3,128,384]{2,1,0:T(8,128)(2,1)S(1)}, u32[]{:S(2)}, u32[]{:S(2)}) %collective-permute-start.3) | collective-permute-done | bytes 294944 | tf_op jit(solution)/shard_map/ppermute | solution.py:295
  43.8 2.7 %shard_map.89 = (bf16[6,128,384]{2,1,0:T(8,128)(2,1)S(1)}, bf16[6,128,384]{2,1,0:T(8,128)(2,1)S(1)}, bf16[3,128,384]{2,1,0:T(8,128)(2,1)S(1)}, bf16[6,128,384]{2,1,0:T(8,128)(2,1)S(1)}) custom-call(bf16[6,128,384]{2,1,0:T(8,128)(2,1)S(1)} %copy-done.2, bf16[7,128,384]{2,1,0:T(8,128)(2,1)S(1)} %collective-permute-done.t1, ...), custom_call_target="tpu_custom_call" | custom-call | tf_op jit(solution)/shard_map/pallas_call | solution.py:301
  46.5 2.5 %collective-permute-start.8 = (bf16[6,128,384]{2,1,0:T(8,128)(2,1)S(1)}, bf16[6,128,384]{2,1,0:T(8,128)(2,1)S(1)}, u32[]{:S(2)}, u32[]{:S(2)}) collective-permute-start(bf16[6,128,384]{2,1,0:T(8,128)(2,1)S(1)} %get-tuple-element.32), channel_id=1, source_target_pairs={{0,6},{1,3},{2,0},{3,5},{4,2},{5,7},{6,4},{7,1},{8,14},{9,11},{10,... | collective-permute-start | bytes 1769480 | tf_op jit(solution)/shard_map/ppermute | solution.py:308
  48.9 2.8 %collective-permute-start.7 = (bf16[6,128,384]{2,1,0:T(8,128)(2,1)S(1)}, bf16[6,128,384]{2,1,0:T(8,128)(2,1)S(1)}, u32[]{:S(2)}, u32[]{:S(2)}) collective-permute-start(bf16[6,128,384]{2,1,0:T(8,128)(2,1)S(1)} %get-tuple-element.31), channel_id=1, source_target_pairs={{0,2},{1,7},{2,4},{3,1},{4,6},{5,3},{6,0},{7,5},{8,10},{9,15},{10,... | collective-permute-start | bytes 1769480 | tf_op jit(solution)/shard_map/ppermute | solution.py:307
  51.8 1.9 %collective-permute-start.10 = (bf16[2,128,384]{2,1,0:T(8,128)(2,1)S(1)}, bf16[2,128,384]{2,1,0:T(8,128)(2,1)S(1)}, u32[]{:S(2)}, u32[]{:S(2)}) collective-permute-start(bf16[2,128,384]{2,1,0:T(8,128)(2,1)S(1)} %shard_map.91), channel_id=1, source_target_pairs={{0,1},{1,0},{2,3},{3,2},{4,5},{5,4},{6,7},{7,6},{8,9},{9,8},{10,11... | collective-permute-start | bytes 589832 | tf_op jit(solution)/shard_map/ppermute | solution.py:299
  53.7 8.7 %collective-permute-done.8.b_ref = bf16[6,128,384]{2,1,0:T(8,128)(2,1)S(1)} collective-permute-done((bf16[6,128,384]{2,1,0:T(8,128)(2,1)S(1)}, bf16[6,128,384]{2,1,0:T(8,128)(2,1)S(1)}, u32[]{:S(2)}, u32[]{:S(2)}) %collective-permute-start.8) | collective-permute-done | bytes 589856 | tf_op jit(solution)/shard_map/ppermute | solution.py:308
  62.4 1.9 %collective-permute-start.15 = (bf16[3,128,384]{2,1,0:T(8,128)(2,1)S(1)}, bf16[3,128,384]{2,1,0:T(8,128)(2,1)S(1)}, u32[]{:S(2)}, u32[]{:S(2)}) collective-permute-start(bf16[3,128,384]{2,1,0:T(8,128)(2,1)S(1)} %get-tuple-element.38), channel_id=1, source_target_pairs={{0,4},{1,5},{2,6},{3,7},{4,0},{5,1},{6,2},{7,3},{8,12},{9,13},{10,... | collective-permute-start | bytes 884744 | tf_op jit(solution)/shard_map/ppermute | solution.py:310
  64.3 0.1 collective-permute-done.7.a_ref
  64.4 4.9 %shard_map.92 = (bf16[128,384]{1,0:T(8,128)(2,1)S(1)}, bf16[128,384]{1,0:T(8,128)(2,1)S(1)}, bf16[128,384]{1,0:T(8,128)(2,1)S(1)}, bf16[128,384]{1,0:T(8,128)(2,1)S(1)}) custom-call(bf16[6,128,384]{2,1,0:T(8,128)(2,1)S(1)} %get-tuple-element.30.m_ref.k_ref, bf16[6,128,384]{2,1,0:T(8,128)(2,1)S(1)} %collective-permute-done.7.a_ref, ...), custom_call_target="tpu_custom_call" | custom-call | tf_op jit(solution)/shard_map/pallas_call | solution.py:312
  69.3 10.0 %collective-permute-start.11 = (bf16[128,384]{1,0:T(8,128)(2,1)S(1)}, bf16[128,384]{1,0:T(8,128)(2,1)S(1)}, u32[]{:S(2)}, u32[]{:S(2)}) collective-permute-start(bf16[128,384]{1,0:T(8,128)(2,1)S(1)} %get-tuple-element.33), channel_id=1, source_target_pairs={{0,8},{1,9},{2,10},{3,11},{4,12},{5,13},{6,14},{7,15},{8,16},{9,17... | collective-permute-start | bytes 294920 | tf_op jit(solution)/shard_map/ppermute | solution.py:326
  79.3 1.9 %collective-permute-start.12 = (bf16[128,384]{1,0:T(8,128)(2,1)S(1)}, bf16[128,384]{1,0:T(8,128)(2,1)S(1)}, u32[]{:S(2)}, u32[]{:S(2)}) collective-permute-start(bf16[128,384]{1,0:T(8,128)(2,1)S(1)} %get-tuple-element.34), channel_id=1, source_target_pairs={{0,14},{1,11},{2,8},{3,13},{4,10},{5,15},{6,12},{7,9},{8,22},{9,19... | collective-permute-start | bytes 294920 | tf_op jit(solution)/shard_map/ppermute | solution.py:326
  81.2 1.9 %collective-permute-start.13 = (bf16[128,384]{1,0:T(8,128)(2,1)S(1)}, bf16[128,384]{1,0:T(8,128)(2,1)S(1)}, u32[]{:S(2)}, u32[]{:S(2)}) collective-permute-start(bf16[128,384]{1,0:T(8,128)(2,1)S(1)} %get-tuple-element.35), channel_id=1, source_target_pairs={{0,12},{1,13},{2,14},{3,15},{4,8},{5,9},{6,10},{7,11},{8,20},{9,21... | collective-permute-start | bytes 294920 | tf_op jit(solution)/shard_map/ppermute | solution.py:326
  83.1 1.9 %collective-permute-start.14 = (bf16[128,384]{1,0:T(8,128)(2,1)S(1)}, bf16[128,384]{1,0:T(8,128)(2,1)S(1)}, u32[]{:S(2)}, u32[]{:S(2)}) collective-permute-start(bf16[128,384]{1,0:T(8,128)(2,1)S(1)} %get-tuple-element.36), channel_id=1, source_target_pairs={{0,10},{1,15},{2,12},{3,9},{4,14},{5,11},{6,8},{7,13},{8,18},{9,23... | collective-permute-start | bytes 294920 | tf_op jit(solution)/shard_map/ppermute | solution.py:326
  85.1 1.1 %shard_map.93 = (bf16[1,2,128,1536]{3,2,1,0:T(8,128)(2,1)}, f32[8,128]{1,0:T(8,128)S(1)}) custom-call(bf16[6,128,384]{2,1,0:T(8,128)(2,1)S(1)} %get-tuple-element.30.m_ref.k_ref, bf16[6,128,384]{2,1,0:T(8,128)(2,1)S(1)} %collective-permute-done.7.a_ref, bf16[6,128,384]{2,1,0:T(8,128)(2,1)S(1)} %collective-permute-done.8.b_ref, ...), custom_call_target="tpu_custom_call" | custom-call | tf_op jit(solution)/shard_map/pallas_call | solution.py:315
  86.2 3.4 %collective-permute-done.13.a2 = bf16[128,384]{1,0:T(8,128)(2,1)S(1)} collective-permute-done((bf16[128,384]{1,0:T(8,128)(2,1)S(1)}, bf16[128,384]{1,0:T(8,128)(2,1)S(1)}, u32[]{:S(2)}, u32[]{:S(2)}) %collective-permute-start.13) | collective-permute-done | bytes 98336 | tf_op jit(solution)/shard_map/ppermute | solution.py:326
  89.5 2.8 %collective-permute-done.14.a3 = bf16[128,384]{1,0:T(8,128)(2,1)S(1)} collective-permute-done((bf16[128,384]{1,0:T(8,128)(2,1)S(1)}, bf16[128,384]{1,0:T(8,128)(2,1)S(1)}, u32[]{:S(2)}, u32[]{:S(2)}) %collective-permute-start.14) | collective-permute-done | bytes 98336 | tf_op jit(solution)/shard_map/ppermute | solution.py:326
  92.4 0.9 shard_map.94
  (22 shorter events, 0.1 us)
Async XLA Ops:
  0.6 24.7 %copy-start.5 = (bf16[1,128,1536]{2,1,0:T(8,128)(2,1)S(1)}, bf16[1,128,1536]{2,1,0:T(8,128)(2,1)}, u32[]{:S(2)}) copy-start(bf16[1,128,1536]{2,1,0:T(8,128)(2,1)} %h_hbm.1) | copy-start | bytes 1179652
  3.4 23.7 %collective-permute-start = (bf16[7,128,384]{2,1,0:T(8,128)(2,1)}, bf16[7,128,384]{2,1,0:T(8,128)(2,1)S(1)}, u32[]{:S(2)}, u32[]{:S(2)}) collective-permute-start(bf16[7,128,384]{2,1,0:T(8,128)(2,1)} %get-tuple-element.23), channel_id=1, source_target_pairs={{0,6},{1,3},{2,0},{3,5},{4,2},{5,7},{6,4},{7,1},{8,14},{9,11},{10,... | collective-permute-start | bytes 2064392 | tf_op jit(solution)/shard_map/ppermute | solution.py:288
  7.8 19.3 %collective-permute-start.1 = (bf16[7,128,384]{2,1,0:T(8,128)(2,1)}, bf16[7,128,384]{2,1,0:T(8,128)(2,1)S(1)}, u32[]{:S(2)}, u32[]{:S(2)}) collective-permute-start(bf16[7,128,384]{2,1,0:T(8,128)(2,1)} %get-tuple-element.24), channel_id=1, source_target_pairs={{0,2},{1,7},{2,4},{3,1},{4,6},{5,3},{6,0},{7,5},{8,10},{9,15},{10,... | collective-permute-start | bytes 2064392 | tf_op jit(solution)/shard_map/ppermute | solution.py:287
  9.8 1.5 %copy-start = (bf16[1,1536,576]{1,2,0:T(8,128)(2,1)S(1)}, bf16[1,1536,576]{1,2,0:T(8,128)(2,1)}, u32[]{:S(2)}) copy-start(bf16[1,1536,576]{1,2,0:T(8,128)(2,1)} %param.8) | copy-start | bytes 5308420
  11.2 0.7 copy-start.4
  11.9 22.1 %copy-start.2 = (bf16[6,128,384]{2,1,0:T(8,128)(2,1)S(1)}, bf16[6,128,384]{2,1,0:T(8,128)(2,1)}, u32[]{:S(2)}) copy-start(bf16[6,128,384]{2,1,0:T(8,128)(2,1)} %get-tuple-element.22.t0) | copy-start | bytes 1769476
  12.3 31.5 %collective-permute-start.5 = (bf16[320,1536]{1,0:T(8,128)(2,1)S(1)}, bf16[320,1536]{1,0:T(8,128)(2,1)S(1)}, u32[]{:S(2)}, u32[]{:S(2)}) collective-permute-start(bf16[320,1536]{1,0:T(8,128)(2,1)S(1)} %get-tuple-element.29), channel_id=1, source_target_pairs={{0,1},{1,0},{2,3},{3,2},{4,5},{5,4},{6,7},{7,6},{8,9},{9,8},{10,11... | collective-permute-start | bytes 2949128 | tf_op jit(solution)/shard_map/ppermute | solution.py:289
  16.5 27.3 %copy-start.1 = (bf16[1,1536,576]{1,2,0:T(8,128)(2,1)S(1)}, bf16[1,1536,576]{1,2,0:T(8,128)(2,1)}, u32[]{:S(2)}) copy-start(bf16[1,1536,576]{1,2,0:T(8,128)(2,1)} %param.8) | copy-start | bytes 5308420
  16.5 25.4 %collective-permute-start.4 = (bf16[256,1536]{1,0:T(8,128)(2,1)S(1)}, bf16[256,1536]{1,0:T(8,128)(2,1)S(1)}, u32[]{:S(2)}, u32[]{:S(2)}) collective-permute-start(bf16[256,1536]{1,0:T(8,128)(2,1)S(1)} %get-tuple-element.28), channel_id=1, source_target_pairs={{0,385},{1,128},{2,387},{3,130},{4,389},{5,132},{6,391},{7,134},{1... | collective-permute-start | bytes 2359304 | tf_op jit(solution)/shard_map/ppermute | solution.py:290
  25.3 8.7 %collective-permute-start.6 = (bf16[1,128,1536]{2,1,0:T(8,128)(2,1)S(1)}, bf16[1,128,1536]{2,1,0:T(8,128)(2,1)S(1)}, u32[]{:S(2)}, u32[]{:S(2)}) collective-permute-start(bf16[1,128,1536]{2,1,0:T(8,128)(2,1)S(1)} %copy-done.5), channel_id=1, source_target_pairs={{0,8},{8,16},{16,24},{24,32},{32,40},{40,48},{48,56},{56,64},{64,7... | collective-permute-start | bytes 1179656 | tf_op jit(solution)/shard_map/ppermute | solution.py:291
  27.2 14.7 %collective-permute-start.2 = (bf16[3,128,384]{2,1,0:T(8,128)(2,1)S(1)}, bf16[3,128,384]{2,1,0:T(8,128)(2,1)S(1)}, u32[]{:S(2)}, u32[]{:S(2)}) collective-permute-start(bf16[3,128,384]{2,1,0:T(8,128)(2,1)S(1)} %get-tuple-element.25), channel_id=1, source_target_pairs={{0,6},{1,3},{2,0},{3,5},{4,2},{5,7},{6,4},{7,1},{8,14},{9,11},{10,... | collective-permute-start | bytes 884744 | tf_op jit(solution)/shard_map/ppermute | solution.py:294
  32.1 11.7 %collective-permute-start.3 = (bf16[3,128,384]{2,1,0:T(8,128)(2,1)S(1)}, bf16[3,128,384]{2,1,0:T(8,128)(2,1)S(1)}, u32[]{:S(2)}, u32[]{:S(2)}) collective-permute-start(bf16[3,128,384]{2,1,0:T(8,128)(2,1)S(1)} %get-tuple-element.26), channel_id=1, source_target_pairs={{0,2},{1,7},{2,4},{3,1},{4,6},{5,3},{6,0},{7,5},{8,10},{9,15},{10,... | collective-permute-start | bytes 884744 | tf_op jit(solution)/shard_map/ppermute | solution.py:295
  34.1 30.3 %copy-start.3 = (f32[1,1536]{1,0:T(1,128)S(1)}, f32[1,1536]{1,0:T(1,128)}, u32[]{:S(2)}) copy-start(f32[1,1536]{1,0:T(1,128)} %g_ref.1) | copy-start | bytes 18436
  34.1 17.7 %collective-permute-start.9 = (bf16[3,2,128,384]{3,2,1,0:T(8,128)(2,1)S(1)}, bf16[3,2,128,384]{3,2,1,0:T(8,128)(2,1)S(1)}, u32[]{:S(2)}, u32[]{:S(2)}) collective-permute-start(bf16[3,2,128,384]{3,2,1,0:T(8,128)(2,1)S(1)} %shard_map.90), channel_id=1, source_target_pairs={{0,1},{1,0},{2,3},{3,2},{4,5},{5,4},{6,7},{7,6},{8,9},{9,8},{10,11... | collective-permute-start | bytes 1769480 | tf_op jit(solution)/shard_map/ppermute | solution.py:297
  46.5 15.9 %collective-permute-start.8 = (bf16[6,128,384]{2,1,0:T(8,128)(2,1)S(1)}, bf16[6,128,384]{2,1,0:T(8,128)(2,1)S(1)}, u32[]{:S(2)}, u32[]{:S(2)}) collective-permute-start(bf16[6,128,384]{2,1,0:T(8,128)(2,1)S(1)} %get-tuple-element.32), channel_id=1, source_target_pairs={{0,6},{1,3},{2,0},{3,5},{4,2},{5,7},{6,4},{7,1},{8,14},{9,11},{10,... | collective-permute-start | bytes 1769480 | tf_op jit(solution)/shard_map/ppermute | solution.py:308
  48.9 15.5 %collective-permute-start.7 = (bf16[6,128,384]{2,1,0:T(8,128)(2,1)S(1)}, bf16[6,128,384]{2,1,0:T(8,128)(2,1)S(1)}, u32[]{:S(2)}, u32[]{:S(2)}) collective-permute-start(bf16[6,128,384]{2,1,0:T(8,128)(2,1)S(1)} %get-tuple-element.31), channel_id=1, source_target_pairs={{0,2},{1,7},{2,4},{3,1},{4,6},{5,3},{6,0},{7,5},{8,10},{9,15},{10,... | collective-permute-start | bytes 1769480 | tf_op jit(solution)/shard_map/ppermute | solution.py:307
  51.8 12.5 %collective-permute-start.10 = (bf16[2,128,384]{2,1,0:T(8,128)(2,1)S(1)}, bf16[2,128,384]{2,1,0:T(8,128)(2,1)S(1)}, u32[]{:S(2)}, u32[]{:S(2)}) collective-permute-start(bf16[2,128,384]{2,1,0:T(8,128)(2,1)S(1)} %shard_map.91), channel_id=1, source_target_pairs={{0,1},{1,0},{2,3},{3,2},{4,5},{5,4},{6,7},{7,6},{8,9},{9,8},{10,11... | collective-permute-start | bytes 589832 | tf_op jit(solution)/shard_map/ppermute | solution.py:299
  62.4 22.7 %collective-permute-start.15 = (bf16[3,128,384]{2,1,0:T(8,128)(2,1)S(1)}, bf16[3,128,384]{2,1,0:T(8,128)(2,1)S(1)}, u32[]{:S(2)}, u32[]{:S(2)}) collective-permute-start(bf16[3,128,384]{2,1,0:T(8,128)(2,1)S(1)} %get-tuple-element.38), channel_id=1, source_target_pairs={{0,4},{1,5},{2,6},{3,7},{4,0},{5,1},{6,2},{7,3},{8,12},{9,13},{10,... | collective-permute-start | bytes 884744 | tf_op jit(solution)/shard_map/ppermute | solution.py:310
  69.3 16.9 %collective-permute-start.11 = (bf16[128,384]{1,0:T(8,128)(2,1)S(1)}, bf16[128,384]{1,0:T(8,128)(2,1)S(1)}, u32[]{:S(2)}, u32[]{:S(2)}) collective-permute-start(bf16[128,384]{1,0:T(8,128)(2,1)S(1)} %get-tuple-element.33), channel_id=1, source_target_pairs={{0,8},{1,9},{2,10},{3,11},{4,12},{5,13},{6,14},{7,15},{8,16},{9,17... | collective-permute-start | bytes 294920 | tf_op jit(solution)/shard_map/ppermute | solution.py:326
  79.3 6.9 %collective-permute-start.12 = (bf16[128,384]{1,0:T(8,128)(2,1)S(1)}, bf16[128,384]{1,0:T(8,128)(2,1)S(1)}, u32[]{:S(2)}, u32[]{:S(2)}) collective-permute-start(bf16[128,384]{1,0:T(8,128)(2,1)S(1)} %get-tuple-element.34), channel_id=1, source_target_pairs={{0,14},{1,11},{2,8},{3,13},{4,10},{5,15},{6,12},{7,9},{8,22},{9,19... | collective-permute-start | bytes 294920 | tf_op jit(solution)/shard_map/ppermute | solution.py:326
  81.2 8.3 %collective-permute-start.13 = (bf16[128,384]{1,0:T(8,128)(2,1)S(1)}, bf16[128,384]{1,0:T(8,128)(2,1)S(1)}, u32[]{:S(2)}, u32[]{:S(2)}) collective-permute-start(bf16[128,384]{1,0:T(8,128)(2,1)S(1)} %get-tuple-element.35), channel_id=1, source_target_pairs={{0,12},{1,13},{2,14},{3,15},{4,8},{5,9},{6,10},{7,11},{8,20},{9,21... | collective-permute-start | bytes 294920 | tf_op jit(solution)/shard_map/ppermute | solution.py:326
  83.1 9.3 %collective-permute-start.14 = (bf16[128,384]{1,0:T(8,128)(2,1)S(1)}, bf16[128,384]{1,0:T(8,128)(2,1)S(1)}, u32[]{:S(2)}, u32[]{:S(2)}) collective-permute-start(bf16[128,384]{1,0:T(8,128)(2,1)S(1)} %get-tuple-element.36), channel_id=1, source_target_pairs={{0,10},{1,15},{2,12},{3,9},{4,14},{5,11},{6,8},{7,13},{8,18},{9,23... | collective-permute-start | bytes 294920 | tf_op jit(solution)/shard_map/ppermute | solution.py:326

commit v10 on v9

--- a/solution.py
+++ b/solution.py
@@ -180,44 +180,48 @@
     x, z = where_am_i()
     gates = g_ref[:, pl.ds(pl.multiple_of(UNIT * (x ^ 1), UNIT), UNIT)]
     roled = roles(x, z)
-    for head in range(3):
-        cols = slice(HEAD_DIM * head, HEAD_DIM * (head + 1))
-
-        def part(index, j):
-            own = m_ref[j, :, cols]
-            behind = a_ref[(j + 1) % 4, :, cols]
-            ahead = b_ref[(j + 3) % 4, :, cols]
-            return jnp.where(index == 0, own, jnp.where(index == 1, behind, ahead))
-
-        kept = [
-            [t0[4 + kv, :, cols], t1[4 + kv, :, cols]]
-            + [(d_ref, c_ref)[kv][2, :, cols], t3[4 + kv, :, cols]]
-            + [pn_ref[i, kv, :, cols] for i in range(3)]
-            + [pf_ref[kv, :, cols]]
-            for kv in range(2)
-        ]
-        q, k, v = ([part(index, j) for j in range(4)] for index in roled)
-        scores = lax.dot_general(
-            jnp.concatenate(q, axis=0),
-            jnp.concatenate(kept[0], axis=0),
-            NT,
-            preferred_element_type=F32,
+    units = [(head, j) for head in range(3) for j in range(4)]
+
+    def part(index, j, cols):
+        own = m_ref[j, :, cols]
+        behind = a_ref[(j + 1) % 4, :, cols]
+        ahead = b_ref[(j + 3) % 4, :, cols]
+        return jnp.where(index == 0, own, jnp.where(index == 1, behind, ahead))
+
+    def used(kv, j, cols):
+        blocks = [t0[4 + kv, :, cols], t1[4 + kv, :, cols]]
+        blocks += [(d_ref, c_ref)[kv][2, :, cols], t3[4 + kv, :, cols]]
+        blocks += [pn_ref[i, kv, :, cols] for i in range(3)]
+        blocks += [pf_ref[kv, :, cols]]
+        blocks[j] = part(roled[1 + kv], j, cols)
+        return jnp.concatenate(blocks, axis=0)
+
+    def columns(head):
+        return slice(HEAD_DIM * head, HEAD_DIM * (head + 1))
+
+    def score(head, j):
+        cols = columns(head)
+        return lax.dot_general(
+            part(roled[0], j, cols), used(0, j, cols), NT, preferred_element_type=F32
         )
-        for j in range(4):
-            mine = lax.dot_general(q[j], k[j], NT, preferred_element_type=F32)
-            at = ROWS * j
-            block = scores[at : at + ROWS]
-            parts = [block[:, :at]] if j else []
-            block = jnp.concatenate(parts + [mine, block[:, at + ROWS :]], axis=1) * SCALE
-            top = jnp.max(block, axis=-1, keepdims=True)
-            weights = jnp.exp2(block - top)
-            total = jnp.sum(weights, axis=-1, keepdims=True)
-            values = list(kept[1])
-            values[j] = v[j]
-            summed = jnp.dot(
-                weights.astype(BF), jnp.concatenate(values, axis=0), preferred_element_type=F32
-            )
-            o_refs[j][:, cols] = (gates[:, cols] * (summed / total)).astype(BF)
+
+    def finish(head, j, weights, total):
+        cols = columns(head)
+        summed = jnp.dot(weights, used(1, j, cols), preferred_element_type=F32)
+        o_refs[j][:, cols] = (gates[:, cols] * (summed * (1.0 / total))).astype(BF)
+
+    coming = score(*units[0])
+    behind = None
+    for n, unit in enumerate(units):
+        scores = coming * SCALE
+        if n + 1 < len(units):
+            coming = score(*units[n + 1])
+        if behind is not None:
+            finish(*behind)
+        top = jnp.max(scores, axis=-1, keepdims=True)
+        weights = jnp.exp2(scores - top)
+        behind = (*unit, weights.astype(BF), jnp.sum(weights, axis=-1, keepdims=True))
+    finish(*behind)
 
 
 def fresh_body(k_ref, a_ref, b_ref, p_ref, after, f_ref, mark):
@@ -316,14 +320,14 @@
         keep, front, back, opposite, mark
     )
 
-    came = []
-    for j in range(4):
+    came = {}
+    for j in (2, 1, 3, 0):
         pairs = [
             (s * 8 + src, (s + 1) % segments * 8 + dst)
             for s in range(segments)
             for src, dst in x_pairs(j)
         ]
-        came.append(lax.ppermute(out[j], ("segment", "patch"), pairs))
+        came[j] = lax.ppermute(out[j], ("segment", "patch"), pairs)
     passed = call(finish_body, jax.ShapeDtypeStruct((1, ROWS, D), BF), 6)(
         came[0], came[3], came[2], came[1], before, done
     )

time: 93.8 us -> 91.6 us (0.977)
  Pallas kernels: 12.8 us -> 10.6 us
    pallas_call x1, Pallas kernels: 4.87 us -> 2.62 us  [local(): call(attend_body, (blocks(),) * 4, 11)]
  transfers between devices with their start and end apart: 16 -> 16, of which waited for: 6 -> 6; matrix products, arithmetic and copies ran while one was open for 0% -> 0% of each run, Pallas kernels for 10% -> 8%
where the time goes in v10:
time: 91.6 us; the launch traced here: 91 us
  starting transfers between devices  54.6 us (60%)
  waiting for transfers between devices  22.7 us (25%)
  Pallas kernels  10.6 us (12%)
  local copies, waits for them, and re-layouts  2.18 us (2%)
    ppermute x4, starting transfers between devices, local(): came[j] = lax.ppermute(out[j], ('segment', 'patch'), pairs)  15.7 us
    ppermute x1, starting transfers between devices, local(): far_rows = lax.ppermute(far_rows, ('dp', 'patch'), far_pairs(parts))  8.79 us
    ppermute x1, waiting for transfers between devices, local(): back = lax.ppermute(back, 'patch', x_pairs(3))  8.66 us
    ppermute x4, waiting for transfers between devices, local(): came[j] = lax.ppermute(out[j], ('segment', 'patch'), pairs)  6.21 us
    ppermute x1, waiting for transfers between devices, local(): far_rows = lax.ppermute(far_rows, ('dp', 'patch'), far_pairs(parts))  5.92 us
    ppermute x1, starting transfers between devices, local(): t2a = lax.ppermute(t2a, 'patch', x_pairs(3))  4.85 us
    ppermute x1, starting transfers between devices, local(): t1 = lax.ppermute(t1, 'patch', x_pairs(3))  4.39 us
    ppermute x1, starting transfers between devices, local(): near_rows = lax.ppermute(near_rows, 'patch', partner_pairs())  4.19 us
  transfers between devices with their start and end apart: 16, of which 6 were waited for; matrix products, arithmetic and copies ran while one was open for 0% of the time, Pallas kernels for 8%

profile of v10, /device:TPU:49, one launch (start us, length us, event | category | flops | bytes accessed | tf_op | source)
XLA Modules:
  0.0 91.0 jit_solution(13377740345752151165)
XLA Ops:
  0.6 2.8 %shard_map.86 = (bf16[6,128,384]{2,1,0:T(8,128)(2,1)}, bf16[7,128,384]{2,1,0:T(8,128)(2,1)}, bf16[7,128,384]{2,1,0:T(8,128)(2,1)}, f32[8,128]{1,0:T(8,128)}) custom-call(bf16[1,128,1536]{2,1,0:T(8,128)(2,1)} %h_hbm.1, f32[1,1536]{1,0:T(1,128)} %g_hbm.1, f32[1,1536]{1,0:T(1,128)} %b_hbm.1, s32[1,128]{1,0:T(1,128)} %m_hbm.1, bf16[1,2,128,1536]{3,2,1,0:T(8,128)(2,1)} %s_hbm.1), custom_call_target="tpu_custom_call" | custom-call | tf_op jit(solution)/shard_map/pallas_call | solution.py:268
  3.4 4.4 %collective-permute-start = (bf16[7,128,384]{2,1,0:T(8,128)(2,1)}, bf16[7,128,384]{2,1,0:T(8,128)(2,1)S(1)}, u32[]{:S(2)}, u32[]{:S(2)}) collective-permute-start(bf16[7,128,384]{2,1,0:T(8,128)(2,1)} %get-tuple-element.23), channel_id=1, source_target_pairs={{0,6},{1,3},{2,0},{3,5},{4,2},{5,7},{6,4},{7,1},{8,14},{9,11},{10,... | collective-permute-start | bytes 2064392 | tf_op jit(solution)/shard_map/ppermute | solution.py:292
  7.8 1.9 %collective-permute-start.1 = (bf16[7,128,384]{2,1,0:T(8,128)(2,1)}, bf16[7,128,384]{2,1,0:T(8,128)(2,1)S(1)}, u32[]{:S(2)}, u32[]{:S(2)}) collective-permute-start(bf16[7,128,384]{2,1,0:T(8,128)(2,1)} %get-tuple-element.24), channel_id=1, source_target_pairs={{0,2},{1,7},{2,4},{3,1},{4,6},{5,3},{6,0},{7,5},{8,10},{9,15},{10,... | collective-permute-start | bytes 2064392 | tf_op jit(solution)/shard_map/ppermute | solution.py:291
  9.8 1.5 %copy-done = bf16[1,1536,576]{1,2,0:T(8,128)(2,1)S(1)} copy-done((bf16[1,1536,576]{1,2,0:T(8,128)(2,1)S(1)}, bf16[1,1536,576]{1,2,0:T(8,128)(2,1)}, u32[]{:S(2)}) %copy-start) | copy-done | bytes 1769496
  11.3 0.7 copy-done.4
  11.9 0.4 shard_map.88
  12.3 4.2 %collective-permute-start.5 = (bf16[320,1536]{1,0:T(8,128)(2,1)S(1)}, bf16[320,1536]{1,0:T(8,128)(2,1)S(1)}, u32[]{:S(2)}, u32[]{:S(2)}) collective-permute-start(bf16[320,1536]{1,0:T(8,128)(2,1)S(1)} %get-tuple-element.29), channel_id=1, source_target_pairs={{0,1},{1,0},{2,3},{3,2},{4,5},{5,4},{6,7},{7,6},{8,9},{9,8},{10,11... | collective-permute-start | bytes 2949128 | tf_op jit(solution)/shard_map/ppermute | solution.py:293
  16.5 8.8 %collective-permute-start.4 = (bf16[256,1536]{1,0:T(8,128)(2,1)S(1)}, bf16[256,1536]{1,0:T(8,128)(2,1)S(1)}, u32[]{:S(2)}, u32[]{:S(2)}) collective-permute-start(bf16[256,1536]{1,0:T(8,128)(2,1)S(1)} %get-tuple-element.28), channel_id=1, source_target_pairs={{0,385},{1,128},{2,387},{3,130},{4,389},{5,132},{6,391},{7,134},{1... | collective-permute-start | bytes 2359304 | tf_op jit(solution)/shard_map/ppermute | solution.py:294
  25.3 1.8 %collective-permute-start.6 = (bf16[1,128,1536]{2,1,0:T(8,128)(2,1)S(1)}, bf16[1,128,1536]{2,1,0:T(8,128)(2,1)S(1)}, u32[]{:S(2)}, u32[]{:S(2)}) collective-permute-start(bf16[1,128,1536]{2,1,0:T(8,128)(2,1)S(1)} %copy-done.5), channel_id=1, source_target_pairs={{0,8},{8,16},{16,24},{24,32},{32,40},{40,48},{48,56},{56,64},{64,7... | collective-permute-start | bytes 1179656 | tf_op jit(solution)/shard_map/ppermute | solution.py:295
  27.2 0.1 shard_map.87
  27.2 4.9 %collective-permute-start.2 = (bf16[3,128,384]{2,1,0:T(8,128)(2,1)S(1)}, bf16[3,128,384]{2,1,0:T(8,128)(2,1)S(1)}, u32[]{:S(2)}, u32[]{:S(2)}) collective-permute-start(bf16[3,128,384]{2,1,0:T(8,128)(2,1)S(1)} %get-tuple-element.25), channel_id=1, source_target_pairs={{0,6},{1,3},{2,0},{3,5},{4,2},{5,7},{6,4},{7,1},{8,14},{9,11},{10,... | collective-permute-start | bytes 884744 | tf_op jit(solution)/shard_map/ppermute | solution.py:298
  32.1 1.9 %collective-permute-start.3 = (bf16[3,128,384]{2,1,0:T(8,128)(2,1)S(1)}, bf16[3,128,384]{2,1,0:T(8,128)(2,1)S(1)}, u32[]{:S(2)}, u32[]{:S(2)}) collective-permute-start(bf16[3,128,384]{2,1,0:T(8,128)(2,1)S(1)} %get-tuple-element.26), channel_id=1, source_target_pairs={{0,2},{1,7},{2,4},{3,1},{4,6},{5,3},{6,0},{7,5},{8,10},{9,15},{10,... | collective-permute-start | bytes 884744 | tf_op jit(solution)/shard_map/ppermute | solution.py:299
  34.0 0.1 shard_map.90
  34.1 1.9 %collective-permute-start.9 = (bf16[3,2,128,384]{3,2,1,0:T(8,128)(2,1)S(1)}, bf16[3,2,128,384]{3,2,1,0:T(8,128)(2,1)S(1)}, u32[]{:S(2)}, u32[]{:S(2)}) collective-permute-start(bf16[3,2,128,384]{3,2,1,0:T(8,128)(2,1)S(1)} %shard_map.90), channel_id=1, source_target_pairs={{0,1},{1,0},{2,3},{3,2},{4,5},{5,4},{6,7},{7,6},{8,9},{9,8},{10,11... | collective-permute-start | bytes 1769480 | tf_op jit(solution)/shard_map/ppermute | solution.py:301
  36.0 5.9 %collective-permute-done.4.v_ref = bf16[256,1536]{1,0:T(8,128)(2,1)S(1)} collective-permute-done((bf16[256,1536]{1,0:T(8,128)(2,1)S(1)}, bf16[256,1536]{1,0:T(8,128)(2,1)S(1)}, u32[]{:S(2)}, u32[]{:S(2)}) %collective-permute-start.4) | collective-permute-done | bytes 786464 | tf_op jit(solution)/shard_map/ppermute | solution.py:294
  41.9 1.8 %collective-permute-done.3.d_ref = bf16[3,128,384]{2,1,0:T(8,128)(2,1)S(1)} collective-permute-done((bf16[3,128,384]{2,1,0:T(8,128)(2,1)S(1)}, bf16[3,128,384]{2,1,0:T(8,128)(2,1)S(1)}, u32[]{:S(2)}, u32[]{:S(2)}) %collective-permute-start.3) | collective-permute-done | bytes 294944 | tf_op jit(solution)/shard_map/ppermute | solution.py:299
  43.8 2.7 %shard_map.89 = (bf16[6,128,384]{2,1,0:T(8,128)(2,1)S(1)}, bf16[6,128,384]{2,1,0:T(8,128)(2,1)S(1)}, bf16[3,128,384]{2,1,0:T(8,128)(2,1)S(1)}, bf16[6,128,384]{2,1,0:T(8,128)(2,1)S(1)}) custom-call(bf16[6,128,384]{2,1,0:T(8,128)(2,1)S(1)} %copy-done.2, bf16[7,128,384]{2,1,0:T(8,128)(2,1)S(1)} %collective-permute-done.t1, ...), custom_call_target="tpu_custom_call" | custom-call | tf_op jit(solution)/shard_map/pallas_call | solution.py:305
  46.5 2.5 %collective-permute-start.8 = (bf16[6,128,384]{2,1,0:T(8,128)(2,1)S(1)}, bf16[6,128,384]{2,1,0:T(8,128)(2,1)S(1)}, u32[]{:S(2)}, u32[]{:S(2)}) collective-permute-start(bf16[6,128,384]{2,1,0:T(8,128)(2,1)S(1)} %get-tuple-element.32), channel_id=1, source_target_pairs={{0,6},{1,3},{2,0},{3,5},{4,2},{5,7},{6,4},{7,1},{8,14},{9,11},{10,... | collective-permute-start | bytes 1769480 | tf_op jit(solution)/shard_map/ppermute | solution.py:312
  48.9 2.8 %collective-permute-start.7 = (bf16[6,128,384]{2,1,0:T(8,128)(2,1)S(1)}, bf16[6,128,384]{2,1,0:T(8,128)(2,1)S(1)}, u32[]{:S(2)}, u32[]{:S(2)}) collective-permute-start(bf16[6,128,384]{2,1,0:T(8,128)(2,1)S(1)} %get-tuple-element.31), channel_id=1, source_target_pairs={{0,2},{1,7},{2,4},{3,1},{4,6},{5,3},{6,0},{7,5},{8,10},{9,15},{10,... | collective-permute-start | bytes 1769480 | tf_op jit(solution)/shard_map/ppermute | solution.py:311
  51.8 1.9 %collective-permute-start.10 = (bf16[2,128,384]{2,1,0:T(8,128)(2,1)S(1)}, bf16[2,128,384]{2,1,0:T(8,128)(2,1)S(1)}, u32[]{:S(2)}, u32[]{:S(2)}) collective-permute-start(bf16[2,128,384]{2,1,0:T(8,128)(2,1)S(1)} %shard_map.91), channel_id=1, source_target_pairs={{0,1},{1,0},{2,3},{3,2},{4,5},{5,4},{6,7},{7,6},{8,9},{9,8},{10,11... | collective-permute-start | bytes 589832 | tf_op jit(solution)/shard_map/ppermute | solution.py:303
  53.7 8.7 %collective-permute-done.8.b_ref = bf16[6,128,384]{2,1,0:T(8,128)(2,1)S(1)} collective-permute-done((bf16[6,128,384]{2,1,0:T(8,128)(2,1)S(1)}, bf16[6,128,384]{2,1,0:T(8,128)(2,1)S(1)}, u32[]{:S(2)}, u32[]{:S(2)}) %collective-permute-start.8) | collective-permute-done | bytes 589856 | tf_op jit(solution)/shard_map/ppermute | solution.py:312
  62.4 1.9 %collective-permute-start.15 = (bf16[3,128,384]{2,1,0:T(8,128)(2,1)S(1)}, bf16[3,128,384]{2,1,0:T(8,128)(2,1)S(1)}, u32[]{:S(2)}, u32[]{:S(2)}) collective-permute-start(bf16[3,128,384]{2,1,0:T(8,128)(2,1)S(1)} %get-tuple-element.38), channel_id=1, source_target_pairs={{0,4},{1,5},{2,6},{3,7},{4,0},{5,1},{6,2},{7,3},{8,12},{9,13},{10,... | collective-permute-start | bytes 884744 | tf_op jit(solution)/shard_map/ppermute | solution.py:314
  64.3 0.1 collective-permute-done.7.a_ref
  64.4 2.6 %shard_map.92 = (bf16[128,384]{1,0:T(8,128)(2,1)S(1)}, bf16[128,384]{1,0:T(8,128)(2,1)S(1)}, bf16[128,384]{1,0:T(8,128)(2,1)S(1)}, bf16[128,384]{1,0:T(8,128)(2,1)S(1)}) custom-call(bf16[6,128,384]{2,1,0:T(8,128)(2,1)S(1)} %get-tuple-element.30.m_ref.k_ref, bf16[6,128,384]{2,1,0:T(8,128)(2,1)S(1)} %collective-permute-done.7.a_ref, ...), custom_call_target="tpu_custom_call" | custom-call | tf_op jit(solution)/shard_map/pallas_call | solution.py:316
  67.0 10.0 %collective-permute-start.11 = (bf16[128,384]{1,0:T(8,128)(2,1)S(1)}, bf16[128,384]{1,0:T(8,128)(2,1)S(1)}, u32[]{:S(2)}, u32[]{:S(2)}) collective-permute-start(bf16[128,384]{1,0:T(8,128)(2,1)S(1)} %get-tuple-element.33), channel_id=1, source_target_pairs={{0,8},{1,9},{2,10},{3,11},{4,12},{5,13},{6,14},{7,15},{8,16},{9,17... | collective-permute-start | bytes 294920 | tf_op jit(solution)/shard_map/ppermute | solution.py:330
  77.0 1.9 %collective-permute-start.12 = (bf16[128,384]{1,0:T(8,128)(2,1)S(1)}, bf16[128,384]{1,0:T(8,128)(2,1)S(1)}, u32[]{:S(2)}, u32[]{:S(2)}) collective-permute-start(bf16[128,384]{1,0:T(8,128)(2,1)S(1)} %get-tuple-element.34), channel_id=1, source_target_pairs={{0,14},{1,11},{2,8},{3,13},{4,10},{5,15},{6,12},{7,9},{8,22},{9,19... | collective-permute-start | bytes 294920 | tf_op jit(solution)/shard_map/ppermute | solution.py:330
  78.9 1.9 %collective-permute-start.13 = (bf16[128,384]{1,0:T(8,128)(2,1)S(1)}, bf16[128,384]{1,0:T(8,128)(2,1)S(1)}, u32[]{:S(2)}, u32[]{:S(2)}) collective-permute-start(bf16[128,384]{1,0:T(8,128)(2,1)S(1)} %get-tuple-element.35), channel_id=1, source_target_pairs={{0,12},{1,13},{2,14},{3,15},{4,8},{5,9},{6,10},{7,11},{8,20},{9,21... | collective-permute-start | bytes 294920 | tf_op jit(solution)/shard_map/ppermute | solution.py:330
  80.9 1.9 %collective-permute-start.14 = (bf16[128,384]{1,0:T(8,128)(2,1)S(1)}, bf16[128,384]{1,0:T(8,128)(2,1)S(1)}, u32[]{:S(2)}, u32[]{:S(2)}) collective-permute-start(bf16[128,384]{1,0:T(8,128)(2,1)S(1)} %get-tuple-element.36), channel_id=1, source_target_pairs={{0,10},{1,15},{2,12},{3,9},{4,14},{5,11},{6,8},{7,13},{8,18},{9,23... | collective-permute-start | bytes 294920 | tf_op jit(solution)/shard_map/ppermute | solution.py:330
  82.8 1.1 %shard_map.93 = (bf16[1,2,128,1536]{3,2,1,0:T(8,128)(2,1)}, f32[8,128]{1,0:T(8,128)S(1)}) custom-call(bf16[6,128,384]{2,1,0:T(8,128)(2,1)S(1)} %get-tuple-element.30.m_ref.k_ref, bf16[6,128,384]{2,1,0:T(8,128)(2,1)S(1)} %collective-permute-done.7.a_ref, bf16[6,128,384]{2,1,0:T(8,128)(2,1)S(1)} %collective-permute-done.8.b_ref, ...), custom_call_target="tpu_custom_call" | custom-call | tf_op jit(solution)/shard_map/pallas_call | solution.py:319
  83.9 3.4 %collective-permute-done.13.a2 = bf16[128,384]{1,0:T(8,128)(2,1)S(1)} collective-permute-done((bf16[128,384]{1,0:T(8,128)(2,1)S(1)}, bf16[128,384]{1,0:T(8,128)(2,1)S(1)}, u32[]{:S(2)}, u32[]{:S(2)}) %collective-permute-start.13) | collective-permute-done | bytes 98336 | tf_op jit(solution)/shard_map/ppermute | solution.py:330
  87.3 2.8 %collective-permute-done.14.a3 = bf16[128,384]{1,0:T(8,128)(2,1)S(1)} collective-permute-done((bf16[128,384]{1,0:T(8,128)(2,1)S(1)}, bf16[128,384]{1,0:T(8,128)(2,1)S(1)}, u32[]{:S(2)}, u32[]{:S(2)}) %collective-permute-start.14) | collective-permute-done | bytes 98336 | tf_op jit(solution)/shard_map/ppermute | solution.py:330
  90.1 0.9 shard_map.94
  (22 shorter events, 0.1 us)
Async XLA Ops:
  0.6 24.7 %copy-start.5 = (bf16[1,128,1536]{2,1,0:T(8,128)(2,1)S(1)}, bf16[1,128,1536]{2,1,0:T(8,128)(2,1)}, u32[]{:S(2)}) copy-start(bf16[1,128,1536]{2,1,0:T(8,128)(2,1)} %h_hbm.1) | copy-start | bytes 1179652
  3.4 23.7 %collective-permute-start = (bf16[7,128,384]{2,1,0:T(8,128)(2,1)}, bf16[7,128,384]{2,1,0:T(8,128)(2,1)S(1)}, u32[]{:S(2)}, u32[]{:S(2)}) collective-permute-start(bf16[7,128,384]{2,1,0:T(8,128)(2,1)} %get-tuple-element.23), channel_id=1, source_target_pairs={{0,6},{1,3},{2,0},{3,5},{4,2},{5,7},{6,4},{7,1},{8,14},{9,11},{10,... | collective-permute-start | bytes 2064392 | tf_op jit(solution)/shard_map/ppermute | solution.py:292
  7.8 19.3 %collective-permute-start.1 = (bf16[7,128,384]{2,1,0:T(8,128)(2,1)}, bf16[7,128,384]{2,1,0:T(8,128)(2,1)S(1)}, u32[]{:S(2)}, u32[]{:S(2)}) collective-permute-start(bf16[7,128,384]{2,1,0:T(8,128)(2,1)} %get-tuple-element.24), channel_id=1, source_target_pairs={{0,2},{1,7},{2,4},{3,1},{4,6},{5,3},{6,0},{7,5},{8,10},{9,15},{10,... | collective-permute-start | bytes 2064392 | tf_op jit(solution)/shard_map/ppermute | solution.py:291
  9.8 1.5 %copy-start = (bf16[1,1536,576]{1,2,0:T(8,128)(2,1)S(1)}, bf16[1,1536,576]{1,2,0:T(8,128)(2,1)}, u32[]{:S(2)}) copy-start(bf16[1,1536,576]{1,2,0:T(8,128)(2,1)} %param.8) | copy-start | bytes 5308420
  11.2 0.7 copy-start.4
  11.9 22.1 %copy-start.2 = (bf16[6,128,384]{2,1,0:T(8,128)(2,1)S(1)}, bf16[6,128,384]{2,1,0:T(8,128)(2,1)}, u32[]{:S(2)}) copy-start(bf16[6,128,384]{2,1,0:T(8,128)(2,1)} %get-tuple-element.22.t0) | copy-start | bytes 1769476
  12.3 31.5 %collective-permute-start.5 = (bf16[320,1536]{1,0:T(8,128)(2,1)S(1)}, bf16[320,1536]{1,0:T(8,128)(2,1)S(1)}, u32[]{:S(2)}, u32[]{:S(2)}) collective-permute-start(bf16[320,1536]{1,0:T(8,128)(2,1)S(1)} %get-tuple-element.29), channel_id=1, source_target_pairs={{0,1},{1,0},{2,3},{3,2},{4,5},{5,4},{6,7},{7,6},{8,9},{9,8},{10,11... | collective-permute-start | bytes 2949128 | tf_op jit(solution)/shard_map/ppermute | solution.py:293
  16.5 27.3 %copy-start.1 = (bf16[1,1536,576]{1,2,0:T(8,128)(2,1)S(1)}, bf16[1,1536,576]{1,2,0:T(8,128)(2,1)}, u32[]{:S(2)}) copy-start(bf16[1,1536,576]{1,2,0:T(8,128)(2,1)} %param.8) | copy-start | bytes 5308420
  16.5 25.4 %collective-permute-start.4 = (bf16[256,1536]{1,0:T(8,128)(2,1)S(1)}, bf16[256,1536]{1,0:T(8,128)(2,1)S(1)}, u32[]{:S(2)}, u32[]{:S(2)}) collective-permute-start(bf16[256,1536]{1,0:T(8,128)(2,1)S(1)} %get-tuple-element.28), channel_id=1, source_target_pairs={{0,385},{1,128},{2,387},{3,130},{4,389},{5,132},{6,391},{7,134},{1... | collective-permute-start | bytes 2359304 | tf_op jit(solution)/shard_map/ppermute | solution.py:294
  25.3 8.7 %collective-permute-start.6 = (bf16[1,128,1536]{2,1,0:T(8,128)(2,1)S(1)}, bf16[1,128,1536]{2,1,0:T(8,128)(2,1)S(1)}, u32[]{:S(2)}, u32[]{:S(2)}) collective-permute-start(bf16[1,128,1536]{2,1,0:T(8,128)(2,1)S(1)} %copy-done.5), channel_id=1, source_target_pairs={{0,8},{8,16},{16,24},{24,32},{32,40},{40,48},{48,56},{56,64},{64,7... | collective-permute-start | bytes 1179656 | tf_op jit(solution)/shard_map/ppermute | solution.py:295
  27.2 14.7 %collective-permute-start.2 = (bf16[3,128,384]{2,1,0:T(8,128)(2,1)S(1)}, bf16[3,128,384]{2,1,0:T(8,128)(2,1)S(1)}, u32[]{:S(2)}, u32[]{:S(2)}) collective-permute-start(bf16[3,128,384]{2,1,0:T(8,128)(2,1)S(1)} %get-tuple-element.25), channel_id=1, source_target_pairs={{0,6},{1,3},{2,0},{3,5},{4,2},{5,7},{6,4},{7,1},{8,14},{9,11},{10,... | collective-permute-start | bytes 884744 | tf_op jit(solution)/shard_map/ppermute | solution.py:298
  32.1 11.7 %collective-permute-start.3 = (bf16[3,128,384]{2,1,0:T(8,128)(2,1)S(1)}, bf16[3,128,384]{2,1,0:T(8,128)(2,1)S(1)}, u32[]{:S(2)}, u32[]{:S(2)}) collective-permute-start(bf16[3,128,384]{2,1,0:T(8,128)(2,1)S(1)} %get-tuple-element.26), channel_id=1, source_target_pairs={{0,2},{1,7},{2,4},{3,1},{4,6},{5,3},{6,0},{7,5},{8,10},{9,15},{10,... | collective-permute-start | bytes 884744 | tf_op jit(solution)/shard_map/ppermute | solution.py:299
  34.1 30.3 %copy-start.3 = (f32[1,1536]{1,0:T(1,128)S(1)}, f32[1,1536]{1,0:T(1,128)}, u32[]{:S(2)}) copy-start(f32[1,1536]{1,0:T(1,128)} %g_ref.1) | copy-start | bytes 18436
  34.1 17.7 %collective-permute-start.9 = (bf16[3,2,128,384]{3,2,1,0:T(8,128)(2,1)S(1)}, bf16[3,2,128,384]{3,2,1,0:T(8,128)(2,1)S(1)}, u32[]{:S(2)}, u32[]{:S(2)}) collective-permute-start(bf16[3,2,128,384]{3,2,1,0:T(8,128)(2,1)S(1)} %shard_map.90), channel_id=1, source_target_pairs={{0,1},{1,0},{2,3},{3,2},{4,5},{5,4},{6,7},{7,6},{8,9},{9,8},{10,11... | collective-permute-start | bytes 1769480 | tf_op jit(solution)/shard_map/ppermute | solution.py:301
  46.5 15.9 %collective-permute-start.8 = (bf16[6,128,384]{2,1,0:T(8,128)(2,1)S(1)}, bf16[6,128,384]{2,1,0:T(8,128)(2,1)S(1)}, u32[]{:S(2)}, u32[]{:S(2)}) collective-permute-start(bf16[6,128,384]{2,1,0:T(8,128)(2,1)S(1)} %get-tuple-element.32), channel_id=1, source_target_pairs={{0,6},{1,3},{2,0},{3,5},{4,2},{5,7},{6,4},{7,1},{8,14},{9,11},{10,... | collective-permute-start | bytes 1769480 | tf_op jit(solution)/shard_map/ppermute | solution.py:312
  48.9 15.5 %collective-permute-start.7 = (bf16[6,128,384]{2,1,0:T(8,128)(2,1)S(1)}, bf16[6,128,384]{2,1,0:T(8,128)(2,1)S(1)}, u32[]{:S(2)}, u32[]{:S(2)}) collective-permute-start(bf16[6,128,384]{2,1,0:T(8,128)(2,1)S(1)} %get-tuple-element.31), channel_id=1, source_target_pairs={{0,2},{1,7},{2,4},{3,1},{4,6},{5,3},{6,0},{7,5},{8,10},{9,15},{10,... | collective-permute-start | bytes 1769480 | tf_op jit(solution)/shard_map/ppermute | solution.py:311
  51.8 12.5 %collective-permute-start.10 = (bf16[2,128,384]{2,1,0:T(8,128)(2,1)S(1)}, bf16[2,128,384]{2,1,0:T(8,128)(2,1)S(1)}, u32[]{:S(2)}, u32[]{:S(2)}) collective-permute-start(bf16[2,128,384]{2,1,0:T(8,128)(2,1)S(1)} %shard_map.91), channel_id=1, source_target_pairs={{0,1},{1,0},{2,3},{3,2},{4,5},{5,4},{6,7},{7,6},{8,9},{9,8},{10,11... | collective-permute-start | bytes 589832 | tf_op jit(solution)/shard_map/ppermute | solution.py:303
  62.4 20.4 %collective-permute-start.15 = (bf16[3,128,384]{2,1,0:T(8,128)(2,1)S(1)}, bf16[3,128,384]{2,1,0:T(8,128)(2,1)S(1)}, u32[]{:S(2)}, u32[]{:S(2)}) collective-permute-start(bf16[3,128,384]{2,1,0:T(8,128)(2,1)S(1)} %get-tuple-element.38), channel_id=1, source_target_pairs={{0,4},{1,5},{2,6},{3,7},{4,0},{5,1},{6,2},{7,3},{8,12},{9,13},{10,... | collective-permute-start | bytes 884744 | tf_op jit(solution)/shard_map/ppermute | solution.py:314
  67.0 16.9 %collective-permute-start.11 = (bf16[128,384]{1,0:T(8,128)(2,1)S(1)}, bf16[128,384]{1,0:T(8,128)(2,1)S(1)}, u32[]{:S(2)}, u32[]{:S(2)}) collective-permute-start(bf16[128,384]{1,0:T(8,128)(2,1)S(1)} %get-tuple-element.33), channel_id=1, source_target_pairs={{0,8},{1,9},{2,10},{3,11},{4,12},{5,13},{6,14},{7,15},{8,16},{9,17... | collective-permute-start | bytes 294920 | tf_op jit(solution)/shard_map/ppermute | solution.py:330
  77.0 6.9 %collective-permute-start.12 = (bf16[128,384]{1,0:T(8,128)(2,1)S(1)}, bf16[128,384]{1,0:T(8,128)(2,1)S(1)}, u32[]{:S(2)}, u32[]{:S(2)}) collective-permute-start(bf16[128,384]{1,0:T(8,128)(2,1)S(1)} %get-tuple-element.34), channel_id=1, source_target_pairs={{0,14},{1,11},{2,8},{3,13},{4,10},{5,15},{6,12},{7,9},{8,22},{9,19... | collective-permute-start | bytes 294920 | tf_op jit(solution)/shard_map/ppermute | solution.py:330
  78.9 8.3 %collective-permute-start.13 = (bf16[128,384]{1,0:T(8,128)(2,1)S(1)}, bf16[128,384]{1,0:T(8,128)(2,1)S(1)}, u32[]{:S(2)}, u32[]{:S(2)}) collective-permute-start(bf16[128,384]{1,0:T(8,128)(2,1)S(1)} %get-tuple-element.35), channel_id=1, source_target_pairs={{0,12},{1,13},{2,14},{3,15},{4,8},{5,9},{6,10},{7,11},{8,20},{9,21... | collective-permute-start | bytes 294920 | tf_op jit(solution)/shard_map/ppermute | solution.py:330
  80.9 9.3 %collective-permute-start.14 = (bf16[128,384]{1,0:T(8,128)(2,1)S(1)}, bf16[128,384]{1,0:T(8,128)(2,1)S(1)}, u32[]{:S(2)}, u32[]{:S(2)}) collective-permute-start(bf16[128,384]{1,0:T(8,128)(2,1)S(1)} %get-tuple-element.36), channel_id=1, source_target_pairs={{0,10},{1,15},{2,12},{3,9},{4,14},{5,11},{6,8},{7,13},{8,18},{9,23... | collective-permute-start | bytes 294920 | tf_op jit(solution)/shard_map/ppermute | solution.py:330

commit v11 on v10

--- a/solution.py
+++ b/solution.py
@@ -110,13 +110,16 @@
         copy.wait()
 
 
-def pass_body(t1, t3, from1, from3):
-    from1[0] = t1[0]
-    from1[1] = t1[1]
-    from1[2] = t1[6]
-    from3[0] = t3[2]
-    from3[1] = t3[3]
-    from3[2] = t3[6]
+def pass_back_body(t1, o_ref):
+    o_ref[0] = t1[0]
+    o_ref[1] = t1[1]
+    o_ref[2] = t1[6]
+
+
+def pass_on_body(t3, o_ref):
+    o_ref[0] = t3[2]
+    o_ref[1] = t3[3]
+    o_ref[2] = t3[6]
 
 
 def near_body(t0, t1, t3, o_ref):
@@ -294,9 +297,8 @@
     far_rows = lax.ppermute(far_rows, ("dp", "patch"), far_pairs(parts))
     before = lax.ppermute(hidden, "segment", [(i, (i + 1) % segments) for i in range(segments)])
 
-    t2a, t2b = call(pass_body, (blocks(3), blocks(3)), 2)(t1, t3)
-    t2a = lax.ppermute(t2a, "patch", x_pairs(3))
-    t2b = lax.ppermute(t2b, "patch", x_pairs(1))
+    t2a = lax.ppermute(call(pass_back_body, blocks(3), 1)(t1), "patch", x_pairs(3))
+    t2b = lax.ppermute(call(pass_on_body, blocks(3), 1)(t3), "patch", x_pairs(1))
     near = call(near_body, blocks(3, 2), 3)(t0, t1, t3)
     near = lax.ppermute(near, "patch", partner_pairs())
     far = call(far_body, blocks(2), 3)(t2a, t2b, near)

time: 91.6 us -> 91.4 us (level)
  transfers between devices with their start and end apart: 16 -> 16, of which waited for: 6 -> 5; matrix products, arithmetic and copies ran while one was open for 0% -> 0% of each run, Pallas kernels for 8% -> 8%
where the time goes in v11:
time: 91.4 us; the launch traced here: 90.9 us
  starting transfers between devices  54.5 us (60%)
  waiting for transfers between devices  22.7 us (25%)
  Pallas kernels  10.6 us (12%)
  local copies, waits for them, and re-layouts  2.18 us (2%)
    ppermute x4, starting transfers between devices, local(): came[j] = lax.ppermute(out[j], ('segment', 'patch'), pairs)  15.6 us
    ppermute x1, waiting for transfers between devices, local(): back = lax.ppermute(back, 'patch', x_pairs(3))  8.68 us
    ppermute x1, starting transfers between devices, local(): far_rows = lax.ppermute(far_rows, ('dp', 'patch'), far_pairs(parts))  8.66 us
    ppermute x4, waiting for transfers between devices, local(): came[j] = lax.ppermute(out[j], ('segment', 'patch'), pairs)  6.21 us
    ppermute x1, waiting for transfers between devices, local(): far_rows = lax.ppermute(far_rows, ('dp', 'patch'), far_pairs(parts))  5.76 us
    ppermute x1, starting transfers between devices, local(): lax.ppermute(call(pass_back_body, blocks(3), 1)(t1), 'patch', x_pairs(3))  4.98 us
    ppermute x1, starting transfers between devices, local(): t1 = lax.ppermute(t1, 'patch', x_pairs(3))  4.39 us
    ppermute x1, starting transfers between devices, local(): near_rows = lax.ppermute(near_rows, 'patch', partner_pairs())  4.19 us
  transfers between devices with their start and end apart: 16, of which 5 were waited for; matrix products, arithmetic and copies ran while one was open for 0% of the time, Pallas kernels for 8%

profile of v11, /device:TPU:49, one launch (start us, length us, event | category | flops | bytes accessed | tf_op | source)
XLA Modules:
  0.0 90.9 jit_solution(1984893850326521531)
XLA Ops:
  0.6 2.8 %shard_map.86 = (bf16[6,128,384]{2,1,0:T(8,128)(2,1)}, bf16[7,128,384]{2,1,0:T(8,128)(2,1)}, bf16[7,128,384]{2,1,0:T(8,128)(2,1)}, f32[8,128]{1,0:T(8,128)}) custom-call(bf16[1,128,1536]{2,1,0:T(8,128)(2,1)} %h_hbm.1, f32[1,1536]{1,0:T(1,128)} %g_hbm.1, f32[1,1536]{1,0:T(1,128)} %b_hbm.1, s32[1,128]{1,0:T(1,128)} %m_hbm.1, bf16[1,2,128,1536]{3,2,1,0:T(8,128)(2,1)} %s_hbm.1), custom_call_target="tpu_custom_call" | custom-call | tf_op jit(solution)/shard_map/pallas_call | solution.py:271
  3.5 4.4 %collective-permute-start = (bf16[7,128,384]{2,1,0:T(8,128)(2,1)}, bf16[7,128,384]{2,1,0:T(8,128)(2,1)S(1)}, u32[]{:S(2)}, u32[]{:S(2)}) collective-permute-start(bf16[7,128,384]{2,1,0:T(8,128)(2,1)} %get-tuple-element.21), channel_id=1, source_target_pairs={{0,6},{1,3},{2,0},{3,5},{4,2},{5,7},{6,4},{7,1},{8,14},{9,11},{10,... | collective-permute-start | bytes 2064392 | tf_op jit(solution)/shard_map/ppermute | solution.py:295
  7.8 1.9 %collective-permute-start.2 = (bf16[7,128,384]{2,1,0:T(8,128)(2,1)}, bf16[7,128,384]{2,1,0:T(8,128)(2,1)S(1)}, u32[]{:S(2)}, u32[]{:S(2)}) collective-permute-start(bf16[7,128,384]{2,1,0:T(8,128)(2,1)} %get-tuple-element.22), channel_id=1, source_target_pairs={{0,2},{1,7},{2,4},{3,1},{4,6},{5,3},{6,0},{7,5},{8,10},{9,15},{10,... | collective-permute-start | bytes 2064392 | tf_op jit(solution)/shard_map/ppermute | solution.py:294
  9.8 0.0 copy-start
  9.8 1.5 %copy-done = bf16[1,1536,576]{1,2,0:T(8,128)(2,1)S(1)} copy-done((bf16[1,1536,576]{1,2,0:T(8,128)(2,1)S(1)}, bf16[1,1536,576]{1,2,0:T(8,128)(2,1)}, u32[]{:S(2)}) %copy-start) | copy-done | bytes 1769496
  11.3 0.7 copy-done.4
  11.9 0.4 shard_map.89
  12.3 4.2 %collective-permute-start.5 = (bf16[320,1536]{1,0:T(8,128)(2,1)S(1)}, bf16[320,1536]{1,0:T(8,128)(2,1)S(1)}, u32[]{:S(2)}, u32[]{:S(2)}) collective-permute-start(bf16[320,1536]{1,0:T(8,128)(2,1)S(1)} %get-tuple-element.25), channel_id=1, source_target_pairs={{0,1},{1,0},{2,3},{3,2},{4,5},{5,4},{6,7},{7,6},{8,9},{9,8},{10,11... | collective-permute-start | bytes 2949128 | tf_op jit(solution)/shard_map/ppermute | solution.py:296
  16.5 8.7 %collective-permute-start.4 = (bf16[256,1536]{1,0:T(8,128)(2,1)S(1)}, bf16[256,1536]{1,0:T(8,128)(2,1)S(1)}, u32[]{:S(2)}, u32[]{:S(2)}) collective-permute-start(bf16[256,1536]{1,0:T(8,128)(2,1)S(1)} %get-tuple-element.24), channel_id=1, source_target_pairs={{0,385},{1,128},{2,387},{3,130},{4,389},{5,132},{6,391},{7,134},{1... | collective-permute-start | bytes 2359304 | tf_op jit(solution)/shard_map/ppermute | solution.py:297
  25.2 1.8 %collective-permute-start.6 = (bf16[1,128,1536]{2,1,0:T(8,128)(2,1)S(1)}, bf16[1,128,1536]{2,1,0:T(8,128)(2,1)S(1)}, u32[]{:S(2)}, u32[]{:S(2)}) collective-permute-start(bf16[1,128,1536]{2,1,0:T(8,128)(2,1)S(1)} %copy-done.5), channel_id=1, source_target_pairs={{0,8},{8,16},{16,24},{24,32},{32,40},{40,48},{48,56},{56,64},{64,7... | collective-permute-start | bytes 1179656 | tf_op jit(solution)/shard_map/ppermute | solution.py:298
  27.0 0.0 copy-start.1
  27.1 5.0 %collective-permute-start.1 = (bf16[3,128,384]{2,1,0:T(8,128)(2,1)S(1)}, bf16[3,128,384]{2,1,0:T(8,128)(2,1)S(1)}, u32[]{:S(2)}, u32[]{:S(2)}) collective-permute-start(bf16[3,128,384]{2,1,0:T(8,128)(2,1)S(1)} %shard_map.87), channel_id=1, source_target_pairs={{0,6},{1,3},{2,0},{3,5},{4,2},{5,7},{6,4},{7,1},{8,14},{9,11},{10,... | collective-permute-start | bytes 884744 | tf_op jit(solution)/shard_map/ppermute | solution.py:300
  32.1 1.9 %collective-permute-start.3 = (bf16[3,128,384]{2,1,0:T(8,128)(2,1)S(1)}, bf16[3,128,384]{2,1,0:T(8,128)(2,1)S(1)}, u32[]{:S(2)}, u32[]{:S(2)}) collective-permute-start(bf16[3,128,384]{2,1,0:T(8,128)(2,1)S(1)} %shard_map.88), channel_id=1, source_target_pairs={{0,2},{1,7},{2,4},{3,1},{4,6},{5,3},{6,0},{7,5},{8,10},{9,15},{10,... | collective-permute-start | bytes 884744 | tf_op jit(solution)/shard_map/ppermute | solution.py:301
  34.0 0.1 shard_map.91
  34.1 1.9 %collective-permute-start.9 = (bf16[3,2,128,384]{3,2,1,0:T(8,128)(2,1)S(1)}, bf16[3,2,128,384]{3,2,1,0:T(8,128)(2,1)S(1)}, u32[]{:S(2)}, u32[]{:S(2)}) collective-permute-start(bf16[3,2,128,384]{3,2,1,0:T(8,128)(2,1)S(1)} %shard_map.91), channel_id=1, source_target_pairs={{0,1},{1,0},{2,3},{3,2},{4,5},{5,4},{6,7},{7,6},{8,9},{9,8},{10,11... | collective-permute-start | bytes 1769480 | tf_op jit(solution)/shard_map/ppermute | solution.py:303
  36.0 5.8 %collective-permute-done.4.v_ref = bf16[256,1536]{1,0:T(8,128)(2,1)S(1)} collective-permute-done((bf16[256,1536]{1,0:T(8,128)(2,1)S(1)}, bf16[256,1536]{1,0:T(8,128)(2,1)S(1)}, u32[]{:S(2)}, u32[]{:S(2)}) %collective-permute-start.4) | collective-permute-done | bytes 786464 | tf_op jit(solution)/shard_map/ppermute | solution.py:297
  41.8 2.0 %collective-permute-done.3.d_ref = bf16[3,128,384]{2,1,0:T(8,128)(2,1)S(1)} collective-permute-done((bf16[3,128,384]{2,1,0:T(8,128)(2,1)S(1)}, bf16[3,128,384]{2,1,0:T(8,128)(2,1)S(1)}, u32[]{:S(2)}, u32[]{:S(2)}) %collective-permute-start.3) | collective-permute-done | bytes 294944 | tf_op jit(solution)/shard_map/ppermute | solution.py:301
  43.8 2.7 %shard_map.90 = (bf16[6,128,384]{2,1,0:T(8,128)(2,1)S(1)}, bf16[6,128,384]{2,1,0:T(8,128)(2,1)S(1)}, bf16[3,128,384]{2,1,0:T(8,128)(2,1)S(1)}, bf16[6,128,384]{2,1,0:T(8,128)(2,1)S(1)}) custom-call(bf16[6,128,384]{2,1,0:T(8,128)(2,1)S(1)} %copy-done.2, bf16[7,128,384]{2,1,0:T(8,128)(2,1)S(1)} %collective-permute-done.t1, ...), custom_call_target="tpu_custom_call" | custom-call | tf_op jit(solution)/shard_map/pallas_call | solution.py:307
  46.5 2.3 %collective-permute-start.8 = (bf16[6,128,384]{2,1,0:T(8,128)(2,1)S(1)}, bf16[6,128,384]{2,1,0:T(8,128)(2,1)S(1)}, u32[]{:S(2)}, u32[]{:S(2)}) collective-permute-start(bf16[6,128,384]{2,1,0:T(8,128)(2,1)S(1)} %get-tuple-element.28), channel_id=1, source_target_pairs={{0,6},{1,3},{2,0},{3,5},{4,2},{5,7},{6,4},{7,1},{8,14},{9,11},{10,... | collective-permute-start | bytes 1769480 | tf_op jit(solution)/shard_map/ppermute | solution.py:314
  48.8 3.0 %collective-permute-start.7 = (bf16[6,128,384]{2,1,0:T(8,128)(2,1)S(1)}, bf16[6,128,384]{2,1,0:T(8,128)(2,1)S(1)}, u32[]{:S(2)}, u32[]{:S(2)}) collective-permute-start(bf16[6,128,384]{2,1,0:T(8,128)(2,1)S(1)} %get-tuple-element.27), channel_id=1, source_target_pairs={{0,2},{1,7},{2,4},{3,1},{4,6},{5,3},{6,0},{7,5},{8,10},{9,15},{10,... | collective-permute-start | bytes 1769480 | tf_op jit(solution)/shard_map/ppermute | solution.py:313
  51.8 1.9 %collective-permute-start.10 = (bf16[2,128,384]{2,1,0:T(8,128)(2,1)S(1)}, bf16[2,128,384]{2,1,0:T(8,128)(2,1)S(1)}, u32[]{:S(2)}, u32[]{:S(2)}) collective-permute-start(bf16[2,128,384]{2,1,0:T(8,128)(2,1)S(1)} %shard_map.92), channel_id=1, source_target_pairs={{0,1},{1,0},{2,3},{3,2},{4,5},{5,4},{6,7},{7,6},{8,9},{9,8},{10,11... | collective-permute-start | bytes 589832 | tf_op jit(solution)/shard_map/ppermute | solution.py:305
  53.8 8.7 %collective-permute-done.8.b_ref = bf16[6,128,384]{2,1,0:T(8,128)(2,1)S(1)} collective-permute-done((bf16[6,128,384]{2,1,0:T(8,128)(2,1)S(1)}, bf16[6,128,384]{2,1,0:T(8,128)(2,1)S(1)}, u32[]{:S(2)}, u32[]{:S(2)}) %collective-permute-start.8) | collective-permute-done | bytes 589856 | tf_op jit(solution)/shard_map/ppermute | solution.py:314
  62.4 1.9 %collective-permute-start.15 = (bf16[3,128,384]{2,1,0:T(8,128)(2,1)S(1)}, bf16[3,128,384]{2,1,0:T(8,128)(2,1)S(1)}, u32[]{:S(2)}, u32[]{:S(2)}) collective-permute-start(bf16[3,128,384]{2,1,0:T(8,128)(2,1)S(1)} %get-tuple-element.34), channel_id=1, source_target_pairs={{0,4},{1,5},{2,6},{3,7},{4,0},{5,1},{6,2},{7,3},{8,12},{9,13},{10,... | collective-permute-start | bytes 884744 | tf_op jit(solution)/shard_map/ppermute | solution.py:316
  64.4 2.6 %shard_map.93 = (bf16[128,384]{1,0:T(8,128)(2,1)S(1)}, bf16[128,384]{1,0:T(8,128)(2,1)S(1)}, bf16[128,384]{1,0:T(8,128)(2,1)S(1)}, bf16[128,384]{1,0:T(8,128)(2,1)S(1)}) custom-call(bf16[6,128,384]{2,1,0:T(8,128)(2,1)S(1)} %get-tuple-element.26.m_ref.k_ref, bf16[6,128,384]{2,1,0:T(8,128)(2,1)S(1)} %collective-permute-done.7.a_ref, ...), custom_call_target="tpu_custom_call" | custom-call | tf_op jit(solution)/shard_map/pallas_call | solution.py:318
  67.0 9.9 %collective-permute-start.11 = (bf16[128,384]{1,0:T(8,128)(2,1)S(1)}, bf16[128,384]{1,0:T(8,128)(2,1)S(1)}, u32[]{:S(2)}, u32[]{:S(2)}) collective-permute-start(bf16[128,384]{1,0:T(8,128)(2,1)S(1)} %get-tuple-element.29), channel_id=1, source_target_pairs={{0,8},{1,9},{2,10},{3,11},{4,12},{5,13},{6,14},{7,15},{8,16},{9,17... | collective-permute-start | bytes 294920 | tf_op jit(solution)/shard_map/ppermute | solution.py:332
  76.9 1.9 %collective-permute-start.12 = (bf16[128,384]{1,0:T(8,128)(2,1)S(1)}, bf16[128,384]{1,0:T(8,128)(2,1)S(1)}, u32[]{:S(2)}, u32[]{:S(2)}) collective-permute-start(bf16[128,384]{1,0:T(8,128)(2,1)S(1)} %get-tuple-element.30), channel_id=1, source_target_pairs={{0,14},{1,11},{2,8},{3,13},{4,10},{5,15},{6,12},{7,9},{8,22},{9,19... | collective-permute-start | bytes 294920 | tf_op jit(solution)/shard_map/ppermute | solution.py:332
  78.8 1.9 %collective-permute-start.13 = (bf16[128,384]{1,0:T(8,128)(2,1)S(1)}, bf16[128,384]{1,0:T(8,128)(2,1)S(1)}, u32[]{:S(2)}, u32[]{:S(2)}) collective-permute-start(bf16[128,384]{1,0:T(8,128)(2,1)S(1)} %get-tuple-element.31), channel_id=1, source_target_pairs={{0,12},{1,13},{2,14},{3,15},{4,8},{5,9},{6,10},{7,11},{8,20},{9,21... | collective-permute-start | bytes 294920 | tf_op jit(solution)/shard_map/ppermute | solution.py:332
  80.7 1.9 %collective-permute-start.14 = (bf16[128,384]{1,0:T(8,128)(2,1)S(1)}, bf16[128,384]{1,0:T(8,128)(2,1)S(1)}, u32[]{:S(2)}, u32[]{:S(2)}) collective-permute-start(bf16[128,384]{1,0:T(8,128)(2,1)S(1)} %get-tuple-element.32), channel_id=1, source_target_pairs={{0,10},{1,15},{2,12},{3,9},{4,14},{5,11},{6,8},{7,13},{8,18},{9,23... | collective-permute-start | bytes 294920 | tf_op jit(solution)/shard_map/ppermute | solution.py:332
  82.7 1.1 %shard_map.94 = (bf16[1,2,128,1536]{3,2,1,0:T(8,128)(2,1)}, f32[8,128]{1,0:T(8,128)S(1)}) custom-call(bf16[6,128,384]{2,1,0:T(8,128)(2,1)S(1)} %get-tuple-element.26.m_ref.k_ref, bf16[6,128,384]{2,1,0:T(8,128)(2,1)S(1)} %collective-permute-done.7.a_ref, bf16[6,128,384]{2,1,0:T(8,128)(2,1)S(1)} %collective-permute-done.8.b_ref, ...), custom_call_target="tpu_custom_call" | custom-call | tf_op jit(solution)/shard_map/pallas_call | solution.py:321
  83.8 3.4 %collective-permute-done.13.a2 = bf16[128,384]{1,0:T(8,128)(2,1)S(1)} collective-permute-done((bf16[128,384]{1,0:T(8,128)(2,1)S(1)}, bf16[128,384]{1,0:T(8,128)(2,1)S(1)}, u32[]{:S(2)}, u32[]{:S(2)}) %collective-permute-start.13) | collective-permute-done | bytes 98336 | tf_op jit(solution)/shard_map/ppermute | solution.py:332
  87.2 2.8 %collective-permute-done.14.a3 = bf16[128,384]{1,0:T(8,128)(2,1)S(1)} collective-permute-done((bf16[128,384]{1,0:T(8,128)(2,1)S(1)}, bf16[128,384]{1,0:T(8,128)(2,1)S(1)}, u32[]{:S(2)}, u32[]{:S(2)}) %collective-permute-start.14) | collective-permute-done | bytes 98336 | tf_op jit(solution)/shard_map/ppermute | solution.py:332
  90.0 0.9 shard_map.95
  (23 shorter events, 0.1 us)
Async XLA Ops:
  0.6 24.6 %copy-start.5 = (bf16[1,128,1536]{2,1,0:T(8,128)(2,1)S(1)}, bf16[1,128,1536]{2,1,0:T(8,128)(2,1)}, u32[]{:S(2)}) copy-start(bf16[1,128,1536]{2,1,0:T(8,128)(2,1)} %h_hbm.1) | copy-start | bytes 1179652
  3.5 23.6 %collective-permute-start = (bf16[7,128,384]{2,1,0:T(8,128)(2,1)}, bf16[7,128,384]{2,1,0:T(8,128)(2,1)S(1)}, u32[]{:S(2)}, u32[]{:S(2)}) collective-permute-start(bf16[7,128,384]{2,1,0:T(8,128)(2,1)} %get-tuple-element.21), channel_id=1, source_target_pairs={{0,6},{1,3},{2,0},{3,5},{4,2},{5,7},{6,4},{7,1},{8,14},{9,11},{10,... | collective-permute-start | bytes 2064392 | tf_op jit(solution)/shard_map/ppermute | solution.py:295
  7.8 24.2 %collective-permute-start.2 = (bf16[7,128,384]{2,1,0:T(8,128)(2,1)}, bf16[7,128,384]{2,1,0:T(8,128)(2,1)S(1)}, u32[]{:S(2)}, u32[]{:S(2)}) collective-permute-start(bf16[7,128,384]{2,1,0:T(8,128)(2,1)} %get-tuple-element.22), channel_id=1, source_target_pairs={{0,2},{1,7},{2,4},{3,1},{4,6},{5,3},{6,0},{7,5},{8,10},{9,15},{10,... | collective-permute-start | bytes 2064392 | tf_op jit(solution)/shard_map/ppermute | solution.py:294
  9.8 1.5 %copy-start = (bf16[1,1536,576]{1,2,0:T(8,128)(2,1)S(1)}, bf16[1,1536,576]{1,2,0:T(8,128)(2,1)}, u32[]{:S(2)}) copy-start(bf16[1,1536,576]{1,2,0:T(8,128)(2,1)} %param.8) | copy-start | bytes 5308420
  11.3 0.7 copy-start.4
  11.9 22.1 %copy-start.2 = (bf16[6,128,384]{2,1,0:T(8,128)(2,1)S(1)}, bf16[6,128,384]{2,1,0:T(8,128)(2,1)}, u32[]{:S(2)}) copy-start(bf16[6,128,384]{2,1,0:T(8,128)(2,1)} %get-tuple-element.20.t0) | copy-start | bytes 1769476
  12.3 31.5 %collective-permute-start.5 = (bf16[320,1536]{1,0:T(8,128)(2,1)S(1)}, bf16[320,1536]{1,0:T(8,128)(2,1)S(1)}, u32[]{:S(2)}, u32[]{:S(2)}) collective-permute-start(bf16[320,1536]{1,0:T(8,128)(2,1)S(1)} %get-tuple-element.25), channel_id=1, source_target_pairs={{0,1},{1,0},{2,3},{3,2},{4,5},{5,4},{6,7},{7,6},{8,9},{9,8},{10,11... | collective-permute-start | bytes 2949128 | tf_op jit(solution)/shard_map/ppermute | solution.py:296
  16.5 25.3 %collective-permute-start.4 = (bf16[256,1536]{1,0:T(8,128)(2,1)S(1)}, bf16[256,1536]{1,0:T(8,128)(2,1)S(1)}, u32[]{:S(2)}, u32[]{:S(2)}) collective-permute-start(bf16[256,1536]{1,0:T(8,128)(2,1)S(1)} %get-tuple-element.24), channel_id=1, source_target_pairs={{0,385},{1,128},{2,387},{3,130},{4,389},{5,132},{6,391},{7,134},{1... | collective-permute-start | bytes 2359304 | tf_op jit(solution)/shard_map/ppermute | solution.py:297
  25.2 8.9 %collective-permute-start.6 = (bf16[1,128,1536]{2,1,0:T(8,128)(2,1)S(1)}, bf16[1,128,1536]{2,1,0:T(8,128)(2,1)S(1)}, u32[]{:S(2)}, u32[]{:S(2)}) collective-permute-start(bf16[1,128,1536]{2,1,0:T(8,128)(2,1)S(1)} %copy-done.5), channel_id=1, source_target_pairs={{0,8},{8,16},{16,24},{24,32},{32,40},{40,48},{48,56},{56,64},{64,7... | collective-permute-start | bytes 1179656 | tf_op jit(solution)/shard_map/ppermute | solution.py:298
  27.0 16.8 %copy-start.1 = (bf16[1,1536,576]{1,2,0:T(8,128)(2,1)S(1)}, bf16[1,1536,576]{1,2,0:T(8,128)(2,1)}, u32[]{:S(2)}) copy-start(bf16[1,1536,576]{1,2,0:T(8,128)(2,1)} %param.8) | copy-start | bytes 5308420
  27.1 14.8 %collective-permute-start.1 = (bf16[3,128,384]{2,1,0:T(8,128)(2,1)S(1)}, bf16[3,128,384]{2,1,0:T(8,128)(2,1)S(1)}, u32[]{:S(2)}, u32[]{:S(2)}) collective-permute-start(bf16[3,128,384]{2,1,0:T(8,128)(2,1)S(1)} %shard_map.87), channel_id=1, source_target_pairs={{0,6},{1,3},{2,0},{3,5},{4,2},{5,7},{6,4},{7,1},{8,14},{9,11},{10,... | collective-permute-start | bytes 884744 | tf_op jit(solution)/shard_map/ppermute | solution.py:300
  32.1 11.7 %collective-permute-start.3 = (bf16[3,128,384]{2,1,0:T(8,128)(2,1)S(1)}, bf16[3,128,384]{2,1,0:T(8,128)(2,1)S(1)}, u32[]{:S(2)}, u32[]{:S(2)}) collective-permute-start(bf16[3,128,384]{2,1,0:T(8,128)(2,1)S(1)} %shard_map.88), channel_id=1, source_target_pairs={{0,2},{1,7},{2,4},{3,1},{4,6},{5,3},{6,0},{7,5},{8,10},{9,15},{10,... | collective-permute-start | bytes 884744 | tf_op jit(solution)/shard_map/ppermute | solution.py:301
  34.1 30.3 %copy-start.3 = (f32[1,1536]{1,0:T(1,128)S(1)}, f32[1,1536]{1,0:T(1,128)}, u32[]{:S(2)}) copy-start(f32[1,1536]{1,0:T(1,128)} %g_ref.1) | copy-start | bytes 18436
  34.1 17.7 %collective-permute-start.9 = (bf16[3,2,128,384]{3,2,1,0:T(8,128)(2,1)S(1)}, bf16[3,2,128,384]{3,2,1,0:T(8,128)(2,1)S(1)}, u32[]{:S(2)}, u32[]{:S(2)}) collective-permute-start(bf16[3,2,128,384]{3,2,1,0:T(8,128)(2,1)S(1)} %shard_map.91), channel_id=1, source_target_pairs={{0,1},{1,0},{2,3},{3,2},{4,5},{5,4},{6,7},{7,6},{8,9},{9,8},{10,11... | collective-permute-start | bytes 1769480 | tf_op jit(solution)/shard_map/ppermute | solution.py:303
  46.5 15.9 %collective-permute-start.8 = (bf16[6,128,384]{2,1,0:T(8,128)(2,1)S(1)}, bf16[6,128,384]{2,1,0:T(8,128)(2,1)S(1)}, u32[]{:S(2)}, u32[]{:S(2)}) collective-permute-start(bf16[6,128,384]{2,1,0:T(8,128)(2,1)S(1)} %get-tuple-element.28), channel_id=1, source_target_pairs={{0,6},{1,3},{2,0},{3,5},{4,2},{5,7},{6,4},{7,1},{8,14},{9,11},{10,... | collective-permute-start | bytes 1769480 | tf_op jit(solution)/shard_map/ppermute | solution.py:314
  48.8 15.6 %collective-permute-start.7 = (bf16[6,128,384]{2,1,0:T(8,128)(2,1)S(1)}, bf16[6,128,384]{2,1,0:T(8,128)(2,1)S(1)}, u32[]{:S(2)}, u32[]{:S(2)}) collective-permute-start(bf16[6,128,384]{2,1,0:T(8,128)(2,1)S(1)} %get-tuple-element.27), channel_id=1, source_target_pairs={{0,2},{1,7},{2,4},{3,1},{4,6},{5,3},{6,0},{7,5},{8,10},{9,15},{10,... | collective-permute-start | bytes 1769480 | tf_op jit(solution)/shard_map/ppermute | solution.py:313
  51.8 12.5 %collective-permute-start.10 = (bf16[2,128,384]{2,1,0:T(8,128)(2,1)S(1)}, bf16[2,128,384]{2,1,0:T(8,128)(2,1)S(1)}, u32[]{:S(2)}, u32[]{:S(2)}) collective-permute-start(bf16[2,128,384]{2,1,0:T(8,128)(2,1)S(1)} %shard_map.92), channel_id=1, source_target_pairs={{0,1},{1,0},{2,3},{3,2},{4,5},{5,4},{6,7},{7,6},{8,9},{9,8},{10,11... | collective-permute-start | bytes 589832 | tf_op jit(solution)/shard_map/ppermute | solution.py:305
  62.4 20.2 %collective-permute-start.15 = (bf16[3,128,384]{2,1,0:T(8,128)(2,1)S(1)}, bf16[3,128,384]{2,1,0:T(8,128)(2,1)S(1)}, u32[]{:S(2)}, u32[]{:S(2)}) collective-permute-start(bf16[3,128,384]{2,1,0:T(8,128)(2,1)S(1)} %get-tuple-element.34), channel_id=1, source_target_pairs={{0,4},{1,5},{2,6},{3,7},{4,0},{5,1},{6,2},{7,3},{8,12},{9,13},{10,... | collective-permute-start | bytes 884744 | tf_op jit(solution)/shard_map/ppermute | solution.py:316
  67.0 16.8 %collective-permute-start.11 = (bf16[128,384]{1,0:T(8,128)(2,1)S(1)}, bf16[128,384]{1,0:T(8,128)(2,1)S(1)}, u32[]{:S(2)}, u32[]{:S(2)}) collective-permute-start(bf16[128,384]{1,0:T(8,128)(2,1)S(1)} %get-tuple-element.29), channel_id=1, source_target_pairs={{0,8},{1,9},{2,10},{3,11},{4,12},{5,13},{6,14},{7,15},{8,16},{9,17... | collective-permute-start | bytes 294920 | tf_op jit(solution)/shard_map/ppermute | solution.py:332
  76.9 6.9 %collective-permute-start.12 = (bf16[128,384]{1,0:T(8,128)(2,1)S(1)}, bf16[128,384]{1,0:T(8,128)(2,1)S(1)}, u32[]{:S(2)}, u32[]{:S(2)}) collective-permute-start(bf16[128,384]{1,0:T(8,128)(2,1)S(1)} %get-tuple-element.30), channel_id=1, source_target_pairs={{0,14},{1,11},{2,8},{3,13},{4,10},{5,15},{6,12},{7,9},{8,22},{9,19... | collective-permute-start | bytes 294920 | tf_op jit(solution)/shard_map/ppermute | solution.py:332
  78.8 8.3 %collective-permute-start.13 = (bf16[128,384]{1,0:T(8,128)(2,1)S(1)}, bf16[128,384]{1,0:T(8,128)(2,1)S(1)}, u32[]{:S(2)}, u32[]{:S(2)}) collective-permute-start(bf16[128,384]{1,0:T(8,128)(2,1)S(1)} %get-tuple-element.31), channel_id=1, source_target_pairs={{0,12},{1,13},{2,14},{3,15},{4,8},{5,9},{6,10},{7,11},{8,20},{9,21... | collective-permute-start | bytes 294920 | tf_op jit(solution)/shard_map/ppermute | solution.py:332
  80.7 9.3 %collective-permute-start.14 = (bf16[128,384]{1,0:T(8,128)(2,1)S(1)}, bf16[128,384]{1,0:T(8,128)(2,1)S(1)}, u32[]{:S(2)}, u32[]{:S(2)}) collective-permute-start(bf16[128,384]{1,0:T(8,128)(2,1)S(1)} %get-tuple-element.32), channel_id=1, source_target_pairs={{0,10},{1,15},{2,12},{3,9},{4,14},{5,11},{6,8},{7,13},{8,18},{9,23... | collective-permute-start | bytes 294920 | tf_op jit(solution)/shard_map/ppermute | solution.py:332

commit v12 on v11

--- a/solution.py
+++ b/solution.py
@@ -10,7 +10,7 @@
 D = 1536
 UNIT = 384
 HALF = 192
-PART = 256
+PART = 288
 SCALE = HEAD_DIM ** (-0.5) * 1.4426950408889634
 BF = jnp.bfloat16
 F32 = jnp.float32

time: 91.4 us -> 95.3 us (1.043)
  the two profiles are of different devices: /device:TPU:49 before, /device:TPU:25 now
where the time goes in v12:
time: 95.3 us; the launch traced here: 94.8 us
  starting transfers between devices  65.8 us (69%)
  waiting for transfers between devices  15.3 us (16%)
  Pallas kernels  10.6 us (11%)
  local copies, waits for them, and re-layouts  2.18 us (2%)
    ppermute x4, starting transfers between devices, local(): came[j] = lax.ppermute(out[j], ('segment', 'patch'), pairs)  21.7 us
    ppermute x1, starting transfers between devices, local(): far_rows = lax.ppermute(far_rows, ('dp', 'patch'), far_pairs(parts))  10.9 us
    ppermute x1, starting transfers between devices, local(): near = lax.ppermute(near, 'patch', partner_pairs())  4.85 us
    ppermute x1, waiting for transfers between devices, local(): near = lax.ppermute(near, 'patch', partner_pairs())  4.65 us
    ppermute x1, starting transfers between devices, local(): t1 = lax.ppermute(t1, 'patch', x_pairs(3))  4.39 us
    ppermute x4, waiting for transfers between devices, local(): came[j] = lax.ppermute(out[j], ('segment', 'patch'), pairs)  4.38 us
    ppermute x1, starting transfers between devices, local(): lax.ppermute(hidden, 'segment', [(i, (i + 1) % segments) for i in range(s...  3.92 us
    ppermute x1, starting transfers between devices, local(): opposite = lax.ppermute(opposite, 'patch', x_pairs(2))  3.42 us
  transfers between devices with their start and end apart: 16, of which 7 were waited for; matrix products, arithmetic and copies ran while one was open for 0% of the time, Pallas kernels for 7%

profile of v12, /device:TPU:25, one launch (start us, length us, event | category | flops | bytes accessed | tf_op | source)
XLA Modules:
  0.0 94.8 jit_solution(13083026994284054587)
XLA Ops:
  0.6 2.8 %shard_map.86 = (bf16[6,128,384]{2,1,0:T(8,128)(2,1)}, bf16[7,128,384]{2,1,0:T(8,128)(2,1)}, bf16[7,128,384]{2,1,0:T(8,128)(2,1)}, f32[8,128]{1,0:T(8,128)}) custom-call(bf16[1,128,1536]{2,1,0:T(8,128)(2,1)} %h_hbm.1, f32[1,1536]{1,0:T(1,128)} %g_hbm.1, f32[1,1536]{1,0:T(1,128)} %b_hbm.1, s32[1,128]{1,0:T(1,128)} %m_hbm.1, bf16[1,2,128,1536]{3,2,1,0:T(8,128)(2,1)} %s_hbm.1), custom_call_target="tpu_custom_call" | custom-call | tf_op jit(solution)/shard_map/pallas_call | solution.py:271
  3.5 4.4 %collective-permute-start = (bf16[7,128,384]{2,1,0:T(8,128)(2,1)}, bf16[7,128,384]{2,1,0:T(8,128)(2,1)S(1)}, u32[]{:S(2)}, u32[]{:S(2)}) collective-permute-start(bf16[7,128,384]{2,1,0:T(8,128)(2,1)} %get-tuple-element.21), channel_id=1, source_target_pairs={{0,6},{1,3},{2,0},{3,5},{4,2},{5,7},{6,4},{7,1},{8,14},{9,11},{10,... | collective-permute-start | bytes 2064392 | tf_op jit(solution)/shard_map/ppermute | solution.py:295
  7.8 1.9 %collective-permute-start.2 = (bf16[7,128,384]{2,1,0:T(8,128)(2,1)}, bf16[7,128,384]{2,1,0:T(8,128)(2,1)S(1)}, u32[]{:S(2)}, u32[]{:S(2)}) collective-permute-start(bf16[7,128,384]{2,1,0:T(8,128)(2,1)} %get-tuple-element.22), channel_id=1, source_target_pairs={{0,2},{1,7},{2,4},{3,1},{4,6},{5,3},{6,0},{7,5},{8,10},{9,15},{10,... | collective-permute-start | bytes 2064392 | tf_op jit(solution)/shard_map/ppermute | solution.py:294
  9.8 1.5 %copy-done = bf16[1,1536,576]{1,2,0:T(8,128)(2,1)S(1)} copy-done((bf16[1,1536,576]{1,2,0:T(8,128)(2,1)S(1)}, bf16[1,1536,576]{1,2,0:T(8,128)(2,1)}, u32[]{:S(2)}) %copy-start) | copy-done | bytes 1769496
  11.3 0.7 copy-done.4
  11.9 0.4 shard_map.89
  12.3 10.9 %collective-permute-start.4 = (bf16[288,1536]{1,0:T(8,128)(2,1)S(1)}, bf16[288,1536]{1,0:T(8,128)(2,1)S(1)}, u32[]{:S(2)}, u32[]{:S(2)}) collective-permute-start(bf16[288,1536]{1,0:T(8,128)(2,1)S(1)} %get-tuple-element.24), channel_id=1, source_target_pairs={{0,385},{1,128},{2,387},{3,130},{4,389},{5,132},{6,391},{7,134},{1... | collective-permute-start | bytes 2654216 | tf_op jit(solution)/shard_map/ppermute | solution.py:297
  23.2 1.9 %collective-permute-start.5 = (bf16[288,1536]{1,0:T(8,128)(2,1)S(1)}, bf16[288,1536]{1,0:T(8,128)(2,1)S(1)}, u32[]{:S(2)}, u32[]{:S(2)}) collective-permute-start(bf16[288,1536]{1,0:T(8,128)(2,1)S(1)} %get-tuple-element.25), channel_id=1, source_target_pairs={{0,1},{1,0},{2,3},{3,2},{4,5},{5,4},{6,7},{7,6},{8,9},{9,8},{10,11... | collective-permute-start | bytes 2654216 | tf_op jit(solution)/shard_map/ppermute | solution.py:296
  25.1 3.9 %collective-permute-start.6 = (bf16[1,128,1536]{2,1,0:T(8,128)(2,1)S(1)}, bf16[1,128,1536]{2,1,0:T(8,128)(2,1)S(1)}, u32[]{:S(2)}, u32[]{:S(2)}) collective-permute-start(bf16[1,128,1536]{2,1,0:T(8,128)(2,1)S(1)} %copy-done.5), channel_id=1, source_target_pairs={{0,8},{8,16},{16,24},{24,32},{32,40},{40,48},{48,56},{56,64},{64,7... | collective-permute-start | bytes 1179656 | tf_op jit(solution)/shard_map/ppermute | solution.py:298
  29.1 3.3 %collective-permute-start.1 = (bf16[3,128,384]{2,1,0:T(8,128)(2,1)S(1)}, bf16[3,128,384]{2,1,0:T(8,128)(2,1)S(1)}, u32[]{:S(2)}, u32[]{:S(2)}) collective-permute-start(bf16[3,128,384]{2,1,0:T(8,128)(2,1)S(1)} %shard_map.87), channel_id=1, source_target_pairs={{0,6},{1,3},{2,0},{3,5},{4,2},{5,7},{6,4},{7,1},{8,14},{9,11},{10,... | collective-permute-start | bytes 884744 | tf_op jit(solution)/shard_map/ppermute | solution.py:300
  32.5 2.1 %collective-permute-start.3 = (bf16[3,128,384]{2,1,0:T(8,128)(2,1)S(1)}, bf16[3,128,384]{2,1,0:T(8,128)(2,1)S(1)}, u32[]{:S(2)}, u32[]{:S(2)}) collective-permute-start(bf16[3,128,384]{2,1,0:T(8,128)(2,1)S(1)} %shard_map.88), channel_id=1, source_target_pairs={{0,2},{1,7},{2,4},{3,1},{4,6},{5,3},{6,0},{7,5},{8,10},{9,15},{10,... | collective-permute-start | bytes 884744 | tf_op jit(solution)/shard_map/ppermute | solution.py:301
  34.6 0.1 shard_map.91
  34.7 4.9 %collective-permute-start.9 = (bf16[3,2,128,384]{3,2,1,0:T(8,128)(2,1)S(1)}, bf16[3,2,128,384]{3,2,1,0:T(8,128)(2,1)S(1)}, u32[]{:S(2)}, u32[]{:S(2)}) collective-permute-start(bf16[3,2,128,384]{3,2,1,0:T(8,128)(2,1)S(1)} %shard_map.91), channel_id=1, source_target_pairs={{0,1},{1,0},{2,3},{3,2},{4,5},{5,4},{6,7},{7,6},{8,9},{9,8},{10,11... | collective-permute-start | bytes 1769480 | tf_op jit(solution)/shard_map/ppermute | solution.py:303
  39.5 2.4 %collective-permute-done.4.v_ref = bf16[288,1536]{1,0:T(8,128)(2,1)S(1)} collective-permute-done((bf16[288,1536]{1,0:T(8,128)(2,1)S(1)}, bf16[288,1536]{1,0:T(8,128)(2,1)S(1)}, u32[]{:S(2)}, u32[]{:S(2)}) %collective-permute-start.4) | collective-permute-done | bytes 884768 | tf_op jit(solution)/shard_map/ppermute | solution.py:297
  41.9 2.8 %collective-permute-done.5.u_ref = bf16[288,1536]{1,0:T(8,128)(2,1)S(1)} collective-permute-done((bf16[288,1536]{1,0:T(8,128)(2,1)S(1)}, bf16[288,1536]{1,0:T(8,128)(2,1)S(1)}, u32[]{:S(2)}, u32[]{:S(2)}) %collective-permute-start.5) | collective-permute-done | bytes 884768 | tf_op jit(solution)/shard_map/ppermute | solution.py:296
  44.7 2.7 %shard_map.90 = (bf16[6,128,384]{2,1,0:T(8,128)(2,1)S(1)}, bf16[6,128,384]{2,1,0:T(8,128)(2,1)S(1)}, bf16[3,128,384]{2,1,0:T(8,128)(2,1)S(1)}, bf16[6,128,384]{2,1,0:T(8,128)(2,1)S(1)}) custom-call(bf16[6,128,384]{2,1,0:T(8,128)(2,1)S(1)} %copy-done.2, bf16[7,128,384]{2,1,0:T(8,128)(2,1)S(1)} %collective-permute-done.t1, ...), custom_call_target="tpu_custom_call" | custom-call | tf_op jit(solution)/shard_map/pallas_call | solution.py:307
  47.4 3.2 %collective-permute-start.8 = (bf16[6,128,384]{2,1,0:T(8,128)(2,1)S(1)}, bf16[6,128,384]{2,1,0:T(8,128)(2,1)S(1)}, u32[]{:S(2)}, u32[]{:S(2)}) collective-permute-start(bf16[6,128,384]{2,1,0:T(8,128)(2,1)S(1)} %get-tuple-element.28), channel_id=1, source_target_pairs={{0,6},{1,3},{2,0},{3,5},{4,2},{5,7},{6,4},{7,1},{8,14},{9,11},{10,... | collective-permute-start | bytes 1769480 | tf_op jit(solution)/shard_map/ppermute | solution.py:314
  50.6 2.1 %collective-permute-start.7 = (bf16[6,128,384]{2,1,0:T(8,128)(2,1)S(1)}, bf16[6,128,384]{2,1,0:T(8,128)(2,1)S(1)}, u32[]{:S(2)}, u32[]{:S(2)}) collective-permute-start(bf16[6,128,384]{2,1,0:T(8,128)(2,1)S(1)} %get-tuple-element.27), channel_id=1, source_target_pairs={{0,2},{1,7},{2,4},{3,1},{4,6},{5,3},{6,0},{7,5},{8,10},{9,15},{10,... | collective-permute-start | bytes 1769480 | tf_op jit(solution)/shard_map/ppermute | solution.py:313
  52.7 4.7 %collective-permute-done.9.after.pn_ref = bf16[3,2,128,384]{3,2,1,0:T(8,128)(2,1)S(1)} collective-permute-done((bf16[3,2,128,384]{3,2,1,0:T(8,128)(2,1)S(1)}, bf16[3,2,128,384]{3,2,1,0:T(8,128)(2,1)S(1)}, u32[]{:S(2)}, u32[]{:S(2)}) %collective-permute-start.9) | collective-permute-done | bytes 589856 | tf_op jit(solution)/shard_map/ppermute | solution.py:303
  57.4 2.2 %collective-permute-start.10 = (bf16[2,128,384]{2,1,0:T(8,128)(2,1)S(1)}, bf16[2,128,384]{2,1,0:T(8,128)(2,1)S(1)}, u32[]{:S(2)}, u32[]{:S(2)}) collective-permute-start(bf16[2,128,384]{2,1,0:T(8,128)(2,1)S(1)} %shard_map.92), channel_id=1, source_target_pairs={{0,1},{1,0},{2,3},{3,2},{4,5},{5,4},{6,7},{7,6},{8,9},{9,8},{10,11... | collective-permute-start | bytes 589832 | tf_op jit(solution)/shard_map/ppermute | solution.py:305
  59.6 0.1 collective-permute-done.8.b_ref
  59.6 3.4 %collective-permute-start.15 = (bf16[3,128,384]{2,1,0:T(8,128)(2,1)S(1)}, bf16[3,128,384]{2,1,0:T(8,128)(2,1)S(1)}, u32[]{:S(2)}, u32[]{:S(2)}) collective-permute-start(bf16[3,128,384]{2,1,0:T(8,128)(2,1)S(1)} %get-tuple-element.34), channel_id=1, source_target_pairs={{0,4},{1,5},{2,6},{3,7},{4,0},{5,1},{6,2},{7,3},{8,12},{9,13},{10,... | collective-permute-start | bytes 884744 | tf_op jit(solution)/shard_map/ppermute | solution.py:316
  63.1 1.0 %collective-permute-done.10.pf_ref = bf16[2,128,384]{2,1,0:T(8,128)(2,1)S(1)} collective-permute-done((bf16[2,128,384]{2,1,0:T(8,128)(2,1)S(1)}, bf16[2,128,384]{2,1,0:T(8,128)(2,1)S(1)}, u32[]{:S(2)}, u32[]{:S(2)}) %collective-permute-start.10) | collective-permute-done | bytes 196640 | tf_op jit(solution)/shard_map/ppermute | solution.py:305
  64.1 2.6 %shard_map.93 = (bf16[128,384]{1,0:T(8,128)(2,1)S(1)}, bf16[128,384]{1,0:T(8,128)(2,1)S(1)}, bf16[128,384]{1,0:T(8,128)(2,1)S(1)}, bf16[128,384]{1,0:T(8,128)(2,1)S(1)}) custom-call(bf16[6,128,384]{2,1,0:T(8,128)(2,1)S(1)} %get-tuple-element.26.m_ref.k_ref, bf16[6,128,384]{2,1,0:T(8,128)(2,1)S(1)} %collective-permute-done.7.a_ref, ...), custom_call_target="tpu_custom_call" | custom-call | tf_op jit(solution)/shard_map/pallas_call | solution.py:318
  66.7 14.1 %collective-permute-start.11 = (bf16[128,384]{1,0:T(8,128)(2,1)S(1)}, bf16[128,384]{1,0:T(8,128)(2,1)S(1)}, u32[]{:S(2)}, u32[]{:S(2)}) collective-permute-start(bf16[128,384]{1,0:T(8,128)(2,1)S(1)} %get-tuple-element.29), channel_id=1, source_target_pairs={{0,8},{1,9},{2,10},{3,11},{4,12},{5,13},{6,14},{7,15},{8,16},{9,17... | collective-permute-start | bytes 294920 | tf_op jit(solution)/shard_map/ppermute | solution.py:332
  80.8 1.9 %collective-permute-start.12 = (bf16[128,384]{1,0:T(8,128)(2,1)S(1)}, bf16[128,384]{1,0:T(8,128)(2,1)S(1)}, u32[]{:S(2)}, u32[]{:S(2)}) collective-permute-start(bf16[128,384]{1,0:T(8,128)(2,1)S(1)} %get-tuple-element.30), channel_id=1, source_target_pairs={{0,14},{1,11},{2,8},{3,13},{4,10},{5,15},{6,12},{7,9},{8,22},{9,19... | collective-permute-start | bytes 294920 | tf_op jit(solution)/shard_map/ppermute | solution.py:332
  82.7 1.9 %collective-permute-start.13 = (bf16[128,384]{1,0:T(8,128)(2,1)S(1)}, bf16[128,384]{1,0:T(8,128)(2,1)S(1)}, u32[]{:S(2)}, u32[]{:S(2)}) collective-permute-start(bf16[128,384]{1,0:T(8,128)(2,1)S(1)} %get-tuple-element.31), channel_id=1, source_target_pairs={{0,12},{1,13},{2,14},{3,15},{4,8},{5,9},{6,10},{7,11},{8,20},{9,21... | collective-permute-start | bytes 294920 | tf_op jit(solution)/shard_map/ppermute | solution.py:332
  84.6 3.8 %collective-permute-start.14 = (bf16[128,384]{1,0:T(8,128)(2,1)S(1)}, bf16[128,384]{1,0:T(8,128)(2,1)S(1)}, u32[]{:S(2)}, u32[]{:S(2)}) collective-permute-start(bf16[128,384]{1,0:T(8,128)(2,1)S(1)} %get-tuple-element.32), channel_id=1, source_target_pairs={{0,10},{1,15},{2,12},{3,9},{4,14},{5,11},{6,8},{7,13},{8,18},{9,23... | collective-permute-start | bytes 294920 | tf_op jit(solution)/shard_map/ppermute | solution.py:332
  88.4 1.1 %shard_map.94 = (bf16[1,2,128,1536]{3,2,1,0:T(8,128)(2,1)}, f32[8,128]{1,0:T(8,128)S(1)}) custom-call(bf16[6,128,384]{2,1,0:T(8,128)(2,1)S(1)} %get-tuple-element.26.m_ref.k_ref, bf16[6,128,384]{2,1,0:T(8,128)(2,1)S(1)} %collective-permute-done.7.a_ref, bf16[6,128,384]{2,1,0:T(8,128)(2,1)S(1)} %collective-permute-done.8.b_ref, ...), custom_call_target="tpu_custom_call" | custom-call | tf_op jit(solution)/shard_map/pallas_call | solution.py:321
  89.5 1.6 %collective-permute-done.13.a2 = bf16[128,384]{1,0:T(8,128)(2,1)S(1)} collective-permute-done((bf16[128,384]{1,0:T(8,128)(2,1)S(1)}, bf16[128,384]{1,0:T(8,128)(2,1)S(1)}, u32[]{:S(2)}, u32[]{:S(2)}) %collective-permute-start.13) | collective-permute-done | bytes 98336 | tf_op jit(solution)/shard_map/ppermute | solution.py:332
  91.1 2.8 %collective-permute-done.14.a3 = bf16[128,384]{1,0:T(8,128)(2,1)S(1)} collective-permute-done((bf16[128,384]{1,0:T(8,128)(2,1)S(1)}, bf16[128,384]{1,0:T(8,128)(2,1)S(1)}, u32[]{:S(2)}, u32[]{:S(2)}) %collective-permute-start.14) | collective-permute-done | bytes 98336 | tf_op jit(solution)/shard_map/ppermute | solution.py:332
  93.9 0.9 shard_map.95
  (23 shorter events, 0.1 us)
Async XLA Ops:
  0.6 24.5 %copy-start.5 = (bf16[1,128,1536]{2,1,0:T(8,128)(2,1)S(1)}, bf16[1,128,1536]{2,1,0:T(8,128)(2,1)}, u32[]{:S(2)}) copy-start(bf16[1,128,1536]{2,1,0:T(8,128)(2,1)} %h_hbm.1) | copy-start | bytes 1179652
  3.5 25.6 %collective-permute-start = (bf16[7,128,384]{2,1,0:T(8,128)(2,1)}, bf16[7,128,384]{2,1,0:T(8,128)(2,1)S(1)}, u32[]{:S(2)}, u32[]{:S(2)}) collective-permute-start(bf16[7,128,384]{2,1,0:T(8,128)(2,1)} %get-tuple-element.21), channel_id=1, source_target_pairs={{0,6},{1,3},{2,0},{3,5},{4,2},{5,7},{6,4},{7,1},{8,14},{9,11},{10,... | collective-permute-start | bytes 2064392 | tf_op jit(solution)/shard_map/ppermute | solution.py:295
  7.8 24.6 %collective-permute-start.2 = (bf16[7,128,384]{2,1,0:T(8,128)(2,1)}, bf16[7,128,384]{2,1,0:T(8,128)(2,1)S(1)}, u32[]{:S(2)}, u32[]{:S(2)}) collective-permute-start(bf16[7,128,384]{2,1,0:T(8,128)(2,1)} %get-tuple-element.22), channel_id=1, source_target_pairs={{0,2},{1,7},{2,4},{3,1},{4,6},{5,3},{6,0},{7,5},{8,10},{9,15},{10,... | collective-permute-start | bytes 2064392 | tf_op jit(solution)/shard_map/ppermute | solution.py:294
  9.8 1.5 %copy-start = (bf16[1,1536,576]{1,2,0:T(8,128)(2,1)S(1)}, bf16[1,1536,576]{1,2,0:T(8,128)(2,1)}, u32[]{:S(2)}) copy-start(bf16[1,1536,576]{1,2,0:T(8,128)(2,1)} %param.8) | copy-start | bytes 5308420
  11.3 0.7 copy-start.4
  11.9 22.6 %copy-start.2 = (bf16[6,128,384]{2,1,0:T(8,128)(2,1)S(1)}, bf16[6,128,384]{2,1,0:T(8,128)(2,1)}, u32[]{:S(2)}) copy-start(bf16[6,128,384]{2,1,0:T(8,128)(2,1)} %get-tuple-element.20.t0) | copy-start | bytes 1769476
  12.3 29.6 %collective-permute-start.4 = (bf16[288,1536]{1,0:T(8,128)(2,1)S(1)}, bf16[288,1536]{1,0:T(8,128)(2,1)S(1)}, u32[]{:S(2)}, u32[]{:S(2)}) collective-permute-start(bf16[288,1536]{1,0:T(8,128)(2,1)S(1)} %get-tuple-element.24), channel_id=1, source_target_pairs={{0,385},{1,128},{2,387},{3,130},{4,389},{5,132},{6,391},{7,134},{1... | collective-permute-start | bytes 2654216 | tf_op jit(solution)/shard_map/ppermute | solution.py:297
  23.2 21.5 %collective-permute-start.5 = (bf16[288,1536]{1,0:T(8,128)(2,1)S(1)}, bf16[288,1536]{1,0:T(8,128)(2,1)S(1)}, u32[]{:S(2)}, u32[]{:S(2)}) collective-permute-start(bf16[288,1536]{1,0:T(8,128)(2,1)S(1)} %get-tuple-element.25), channel_id=1, source_target_pairs={{0,1},{1,0},{2,3},{3,2},{4,5},{5,4},{6,7},{7,6},{8,9},{9,8},{10,11... | collective-permute-start | bytes 2654216 | tf_op jit(solution)/shard_map/ppermute | solution.py:296
  25.1 9.5 %collective-permute-start.6 = (bf16[1,128,1536]{2,1,0:T(8,128)(2,1)S(1)}, bf16[1,128,1536]{2,1,0:T(8,128)(2,1)S(1)}, u32[]{:S(2)}, u32[]{:S(2)}) collective-permute-start(bf16[1,128,1536]{2,1,0:T(8,128)(2,1)S(1)} %copy-done.5), channel_id=1, source_target_pairs={{0,8},{8,16},{16,24},{24,32},{32,40},{40,48},{48,56},{56,64},{64,7... | collective-permute-start | bytes 1179656 | tf_op jit(solution)/shard_map/ppermute | solution.py:298
  29.1 15.6 %copy-start.1 = (bf16[1,1536,576]{1,2,0:T(8,128)(2,1)S(1)}, bf16[1,1536,576]{1,2,0:T(8,128)(2,1)}, u32[]{:S(2)}) copy-start(bf16[1,1536,576]{1,2,0:T(8,128)(2,1)} %param.8) | copy-start | bytes 5308420
  29.1 15.6 %collective-permute-start.1 = (bf16[3,128,384]{2,1,0:T(8,128)(2,1)S(1)}, bf16[3,128,384]{2,1,0:T(8,128)(2,1)S(1)}, u32[]{:S(2)}, u32[]{:S(2)}) collective-permute-start(bf16[3,128,384]{2,1,0:T(8,128)(2,1)S(1)} %shard_map.87), channel_id=1, source_target_pairs={{0,6},{1,3},{2,0},{3,5},{4,2},{5,7},{6,4},{7,1},{8,14},{9,11},{10,... | collective-permute-start | bytes 884744 | tf_op jit(solution)/shard_map/ppermute | solution.py:300
  32.5 12.3 %collective-permute-start.3 = (bf16[3,128,384]{2,1,0:T(8,128)(2,1)S(1)}, bf16[3,128,384]{2,1,0:T(8,128)(2,1)S(1)}, u32[]{:S(2)}, u32[]{:S(2)}) collective-permute-start(bf16[3,128,384]{2,1,0:T(8,128)(2,1)S(1)} %shard_map.88), channel_id=1, source_target_pairs={{0,2},{1,7},{2,4},{3,1},{4,6},{5,3},{6,0},{7,5},{8,10},{9,15},{10,... | collective-permute-start | bytes 884744 | tf_op jit(solution)/shard_map/ppermute | solution.py:301
  34.6 29.4 %copy-start.3 = (f32[1,1536]{1,0:T(1,128)S(1)}, f32[1,1536]{1,0:T(1,128)}, u32[]{:S(2)}) copy-start(f32[1,1536]{1,0:T(1,128)} %g_ref.1) | copy-start | bytes 18436
  34.7 22.7 %collective-permute-start.9 = (bf16[3,2,128,384]{3,2,1,0:T(8,128)(2,1)S(1)}, bf16[3,2,128,384]{3,2,1,0:T(8,128)(2,1)S(1)}, u32[]{:S(2)}, u32[]{:S(2)}) collective-permute-start(bf16[3,2,128,384]{3,2,1,0:T(8,128)(2,1)S(1)} %shard_map.91), channel_id=1, source_target_pairs={{0,1},{1,0},{2,3},{3,2},{4,5},{5,4},{6,7},{7,6},{8,9},{9,8},{10,11... | collective-permute-start | bytes 1769480 | tf_op jit(solution)/shard_map/ppermute | solution.py:303
  47.4 12.2 %collective-permute-start.8 = (bf16[6,128,384]{2,1,0:T(8,128)(2,1)S(1)}, bf16[6,128,384]{2,1,0:T(8,128)(2,1)S(1)}, u32[]{:S(2)}, u32[]{:S(2)}) collective-permute-start(bf16[6,128,384]{2,1,0:T(8,128)(2,1)S(1)} %get-tuple-element.28), channel_id=1, source_target_pairs={{0,6},{1,3},{2,0},{3,5},{4,2},{5,7},{6,4},{7,1},{8,14},{9,11},{10,... | collective-permute-start | bytes 1769480 | tf_op jit(solution)/shard_map/ppermute | solution.py:314
  50.6 13.5 %collective-permute-start.7 = (bf16[6,128,384]{2,1,0:T(8,128)(2,1)S(1)}, bf16[6,128,384]{2,1,0:T(8,128)(2,1)S(1)}, u32[]{:S(2)}, u32[]{:S(2)}) collective-permute-start(bf16[6,128,384]{2,1,0:T(8,128)(2,1)S(1)} %get-tuple-element.27), channel_id=1, source_target_pairs={{0,2},{1,7},{2,4},{3,1},{4,6},{5,3},{6,0},{7,5},{8,10},{9,15},{10,... | collective-permute-start | bytes 1769480 | tf_op jit(solution)/shard_map/ppermute | solution.py:313
  57.4 6.7 %collective-permute-start.10 = (bf16[2,128,384]{2,1,0:T(8,128)(2,1)S(1)}, bf16[2,128,384]{2,1,0:T(8,128)(2,1)S(1)}, u32[]{:S(2)}, u32[]{:S(2)}) collective-permute-start(bf16[2,128,384]{2,1,0:T(8,128)(2,1)S(1)} %shard_map.92), channel_id=1, source_target_pairs={{0,1},{1,0},{2,3},{3,2},{4,5},{5,4},{6,7},{7,6},{8,9},{9,8},{10,11... | collective-permute-start | bytes 589832 | tf_op jit(solution)/shard_map/ppermute | solution.py:305
  59.6 28.8 %collective-permute-start.15 = (bf16[3,128,384]{2,1,0:T(8,128)(2,1)S(1)}, bf16[3,128,384]{2,1,0:T(8,128)(2,1)S(1)}, u32[]{:S(2)}, u32[]{:S(2)}) collective-permute-start(bf16[3,128,384]{2,1,0:T(8,128)(2,1)S(1)} %get-tuple-element.34), channel_id=1, source_target_pairs={{0,4},{1,5},{2,6},{3,7},{4,0},{5,1},{6,2},{7,3},{8,12},{9,13},{10,... | collective-permute-start | bytes 884744 | tf_op jit(solution)/shard_map/ppermute | solution.py:316
  66.7 22.8 %collective-permute-start.11 = (bf16[128,384]{1,0:T(8,128)(2,1)S(1)}, bf16[128,384]{1,0:T(8,128)(2,1)S(1)}, u32[]{:S(2)}, u32[]{:S(2)}) collective-permute-start(bf16[128,384]{1,0:T(8,128)(2,1)S(1)} %get-tuple-element.29), channel_id=1, source_target_pairs={{0,8},{1,9},{2,10},{3,11},{4,12},{5,13},{6,14},{7,15},{8,16},{9,17... | collective-permute-start | bytes 294920 | tf_op jit(solution)/shard_map/ppermute | solution.py:332
  80.8 8.7 %collective-permute-start.12 = (bf16[128,384]{1,0:T(8,128)(2,1)S(1)}, bf16[128,384]{1,0:T(8,128)(2,1)S(1)}, u32[]{:S(2)}, u32[]{:S(2)}) collective-permute-start(bf16[128,384]{1,0:T(8,128)(2,1)S(1)} %get-tuple-element.30), channel_id=1, source_target_pairs={{0,14},{1,11},{2,8},{3,13},{4,10},{5,15},{6,12},{7,9},{8,22},{9,19... | collective-permute-start | bytes 294920 | tf_op jit(solution)/shard_map/ppermute | solution.py:332
  82.7 8.4 %collective-permute-start.13 = (bf16[128,384]{1,0:T(8,128)(2,1)S(1)}, bf16[128,384]{1,0:T(8,128)(2,1)S(1)}, u32[]{:S(2)}, u32[]{:S(2)}) collective-permute-start(bf16[128,384]{1,0:T(8,128)(2,1)S(1)} %get-tuple-element.31), channel_id=1, source_target_pairs={{0,12},{1,13},{2,14},{3,15},{4,8},{5,9},{6,10},{7,11},{8,20},{9,21... | collective-permute-start | bytes 294920 | tf_op jit(solution)/shard_map/ppermute | solution.py:332
  84.6 9.3 %collective-permute-start.14 = (bf16[128,384]{1,0:T(8,128)(2,1)S(1)}, bf16[128,384]{1,0:T(8,128)(2,1)S(1)}, u32[]{:S(2)}, u32[]{:S(2)}) collective-permute-start(bf16[128,384]{1,0:T(8,128)(2,1)S(1)} %get-tuple-element.32), channel_id=1, source_target_pairs={{0,10},{1,15},{2,12},{3,9},{4,14},{5,11},{6,8},{7,13},{8,18},{9,23... | collective-permute-start | bytes 294920 | tf_op jit(solution)/shard_map/ppermute | solution.py:332

commit v13 on v11

--- a/solution.py
+++ b/solution.py
@@ -133,8 +133,7 @@
     o_ref[1] = c_ref[2]
 
 
-def project_body(t0, t1, c_ref, d_ref, t3, w_ref, v_ref, u_ref, early, *outs):
-    del early
+def project_body(t0, t1, c_ref, d_ref, t3, w_ref, v_ref, u_ref, *outs):
     front_o, back_o, opp_o, keep_o, both, other = outs
     _, z = where_am_i()
     other[:PART] = v_ref[...]
@@ -179,8 +178,11 @@
     return q, k, v
 
 
-def attend_body(m_ref, a_ref, b_ref, t0, t1, c_ref, d_ref, t3, pn_ref, pf_ref, g_ref, *o_refs):
+def attend_body(m_ref, a_ref, b_ref, t0, t1, c_ref, d_ref, t3, pn_ref, pf_ref, g_ref, h_ref, *o_refs):
     x, z = where_am_i()
+    for g in range(4):
+        o_refs[0][1 + g] = h_ref[0, :, UNIT * g : UNIT * (g + 1)]
+    o_refs = (o_refs[0].at[0], *o_refs[1:])
     gates = g_ref[:, pl.ds(pl.multiple_of(UNIT * (x ^ 1), UNIT), UNIT)]
     roled = roles(x, z)
     units = [(head, j) for head in range(3) for j in range(4)]
@@ -248,13 +250,13 @@
                 f_ref[0, g // 4 - 1, :, cols] = ref[...]
 
 
-def finish_body(a0, a1, a2, a3, h_ref, after, o_ref):
+def finish_body(a0, a1, a2, a3, after, o_ref):
     del after
     x, z = where_am_i()
-    for j, ref in enumerate((a0, a1, a2, a3)):
+    for j, ref in enumerate((a0.at[0], a1, a2, a3)):
         group = ((x + (1 - 2 * z) * j + 4) % 4) ^ 1
         cols = pl.ds(pl.multiple_of(UNIT * group, UNIT), UNIT)
-        o_ref[0, :, cols] = (h_ref[0, :, cols].astype(F32) + ref[...].astype(F32)).astype(BF)
+        o_ref[0, :, cols] = (a0[1 + group].astype(F32) + ref[...].astype(F32)).astype(BF)
 
 
 def local(hidden, w_qkv, norm_gain, box_vec, gate, box_mask, stale_kv):
@@ -295,8 +297,6 @@
     t1 = lax.ppermute(t1, "patch", x_pairs(3))
     near_rows = lax.ppermute(near_rows, "patch", partner_pairs())
     far_rows = lax.ppermute(far_rows, ("dp", "patch"), far_pairs(parts))
-    before = lax.ppermute(hidden, "segment", [(i, (i + 1) % segments) for i in range(segments)])
-
     t2a = lax.ppermute(call(pass_back_body, blocks(3), 1)(t1), "patch", x_pairs(3))
     t2b = lax.ppermute(call(pass_on_body, blocks(3), 1)(t3), "patch", x_pairs(1))
     near = call(near_body, blocks(3, 2), 3)(t0, t1, t3)
@@ -307,31 +307,31 @@
     front, back, opposite, keep = call(
         project_body,
         (blocks(6), blocks(6), blocks(3), blocks(6)),
-        9,
+        8,
         scratch_shapes=[pltpu.VMEM((UNIT, D), BF), pltpu.VMEM((UNIT + HALF, D), BF)],
-    )(t0, t1, t2a, t2b, t3, weight, far_rows, near_rows, before)
+    )(t0, t1, t2a, t2b, t3, weight, far_rows, near_rows)
     front = lax.ppermute(front, "patch", x_pairs(1))
     back = lax.ppermute(back, "patch", x_pairs(3))
     opposite, mark = lax.optimization_barrier((opposite, back[0, :16, :128]))
     opposite = lax.ppermute(opposite, "patch", x_pairs(2))
 
-    out = call(attend_body, (blocks(),) * 4, 11)(
-        keep, front, back, t0, t1, t2a, t2b, t3, near, far, gate
+    out = call(attend_body, (blocks(5),) + (blocks(),) * 3, 12)(
+        keep, front, back, t0, t1, t2a, t2b, t3, near, far, gate, hidden
     )
     fresh, done = call(fresh_body, (jax.ShapeDtypeStruct((1, 2, ROWS, D), BF), MARK), 5)(
         keep, front, back, opposite, mark
     )
 
     came = {}
-    for j in (2, 1, 3, 0):
+    for j in (0, 2, 1, 3):
         pairs = [
             (s * 8 + src, (s + 1) % segments * 8 + dst)
             for s in range(segments)
             for src, dst in x_pairs(j)
         ]
         came[j] = lax.ppermute(out[j], ("segment", "patch"), pairs)
-    passed = call(finish_body, jax.ShapeDtypeStruct((1, ROWS, D), BF), 6)(
-        came[0], came[3], came[2], came[1], before, done
+    passed = call(finish_body, jax.ShapeDtypeStruct((1, ROWS, D), BF), 5)(
+        came[0], came[3], came[2], came[1], done
     )
     return (passed, fresh)
 

time: 91.4 us -> 91.8 us (level)
  the two profiles are of different devices: /device:TPU:49 before, /device:TPU:1 now
where the time goes in v13:
time: 91.8 us; the launch traced here: 91.2 us
  starting transfers between devices  56.1 us (61%)
  waiting for transfers between devices  21.4 us (23%)
  Pallas kernels  10.7 us (12%)
  local copies, waits for them, and re-layouts  2.18 us (2%)
    ppermute x4, starting transfers between devices, local(): came[j] = lax.ppermute(out[j], ('segment', 'patch'), pairs)  14 us
    ppermute x1, starting transfers between devices, local(): far_rows = lax.ppermute(far_rows, ('dp', 'patch'), far_pairs(parts))  8.66 us
    ppermute x1, waiting for transfers between devices, local(): far_rows = lax.ppermute(far_rows, ('dp', 'patch'), far_pairs(parts))  7.72 us
    ppermute x1, starting transfers between devices, local(): t1 = lax.ppermute(t1, 'patch', x_pairs(3))  5.22 us
    ppermute x4, waiting for transfers between devices, local(): came[j] = lax.ppermute(out[j], ('segment', 'patch'), pairs)  5.15 us
    ppermute x1, starting transfers between devices, local(): opposite = lax.ppermute(opposite, 'patch', x_pairs(2))  4.97 us
    ppermute x1, waiting for transfers between devices, local(): far = lax.ppermute(far, 'patch', partner_pairs())  4.78 us
    ppermute x1, starting transfers between devices, local(): lax.ppermute(call(pass_back_body, blocks(3), 1)(t1), 'patch', x_pairs(3))  4.7 us
  transfers between devices with their start and end apart: 15, of which 6 were waited for; matrix products, arithmetic and copies ran while one was open for 0% of the time, Pallas kernels for 5%

profile of v13, /device:TPU:1, one launch (start us, length us, event | category | flops | bytes accessed | tf_op | source)
XLA Modules:
  0.0 91.2 jit_solution(5934031444472437748)
XLA Ops:
  0.6 2.7 %shard_map.86 = (bf16[6,128,384]{2,1,0:T(8,128)(2,1)}, bf16[7,128,384]{2,1,0:T(8,128)(2,1)}, bf16[7,128,384]{2,1,0:T(8,128)(2,1)}, f32[8,128]{1,0:T(8,128)}) custom-call(bf16[1,128,1536]{2,1,0:T(8,128)(2,1)} %h_ref.1, f32[1,1536]{1,0:T(1,128)} %g_hbm.1, f32[1,1536]{1,0:T(1,128)} %b_hbm.1, s32[1,128]{1,0:T(1,128)} %m_hbm.1, bf16[1,2,128,1536]{3,2,1,0:T(8,128)(2,1)} %s_hbm.1), custom_call_target="tpu_custom_call" | custom-call | tf_op jit(solution)/shard_map/pallas_call | solution.py:273
  3.4 5.2 %collective-permute-start = (bf16[7,128,384]{2,1,0:T(8,128)(2,1)}, bf16[7,128,384]{2,1,0:T(8,128)(2,1)S(1)}, u32[]{:S(2)}, u32[]{:S(2)}) collective-permute-start(bf16[7,128,384]{2,1,0:T(8,128)(2,1)} %get-tuple-element.21), channel_id=1, source_target_pairs={{0,6},{1,3},{2,0},{3,5},{4,2},{5,7},{6,4},{7,1},{8,14},{9,11},{10,... | collective-permute-start | bytes 2064392 | tf_op jit(solution)/shard_map/ppermute | solution.py:297
  8.6 1.9 %collective-permute-start.2 = (bf16[7,128,384]{2,1,0:T(8,128)(2,1)}, bf16[7,128,384]{2,1,0:T(8,128)(2,1)S(1)}, u32[]{:S(2)}, u32[]{:S(2)}) collective-permute-start(bf16[7,128,384]{2,1,0:T(8,128)(2,1)} %get-tuple-element.22), channel_id=1, source_target_pairs={{0,2},{1,7},{2,4},{3,1},{4,6},{5,3},{6,0},{7,5},{8,10},{9,15},{10,... | collective-permute-start | bytes 2064392 | tf_op jit(solution)/shard_map/ppermute | solution.py:296
  10.5 1.5 %copy-done = bf16[1,1536,576]{1,2,0:T(8,128)(2,1)S(1)} copy-done((bf16[1,1536,576]{1,2,0:T(8,128)(2,1)S(1)}, bf16[1,1536,576]{1,2,0:T(8,128)(2,1)}, u32[]{:S(2)}) %copy-start) | copy-done | bytes 1769496
  12.0 0.7 copy-done.5
  12.7 0.4 shard_map.89
  13.1 4.2 %collective-permute-start.5 = (bf16[320,1536]{1,0:T(8,128)(2,1)S(1)}, bf16[320,1536]{1,0:T(8,128)(2,1)S(1)}, u32[]{:S(2)}, u32[]{:S(2)}) collective-permute-start(bf16[320,1536]{1,0:T(8,128)(2,1)S(1)} %get-tuple-element.25), channel_id=1, source_target_pairs={{0,1},{1,0},{2,3},{3,2},{4,5},{5,4},{6,7},{7,6},{8,9},{9,8},{10,11... | collective-permute-start | bytes 2949128 | tf_op jit(solution)/shard_map/ppermute | solution.py:298
  17.3 8.7 %collective-permute-start.4 = (bf16[256,1536]{1,0:T(8,128)(2,1)S(1)}, bf16[256,1536]{1,0:T(8,128)(2,1)S(1)}, u32[]{:S(2)}, u32[]{:S(2)}) collective-permute-start(bf16[256,1536]{1,0:T(8,128)(2,1)S(1)} %get-tuple-element.24), channel_id=1, source_target_pairs={{0,385},{1,128},{2,387},{3,130},{4,389},{5,132},{6,391},{7,134},{1... | collective-permute-start | bytes 2359304 | tf_op jit(solution)/shard_map/ppermute | solution.py:299
  26.0 0.0 copy-start.1
  26.0 4.7 %collective-permute-start.1 = (bf16[3,128,384]{2,1,0:T(8,128)(2,1)S(1)}, bf16[3,128,384]{2,1,0:T(8,128)(2,1)S(1)}, u32[]{:S(2)}, u32[]{:S(2)}) collective-permute-start(bf16[3,128,384]{2,1,0:T(8,128)(2,1)S(1)} %shard_map.87), channel_id=1, source_target_pairs={{0,6},{1,3},{2,0},{3,5},{4,2},{5,7},{6,4},{7,1},{8,14},{9,11},{10,... | collective-permute-start | bytes 884744 | tf_op jit(solution)/shard_map/ppermute | solution.py:300
  30.8 1.9 %collective-permute-start.3 = (bf16[3,128,384]{2,1,0:T(8,128)(2,1)S(1)}, bf16[3,128,384]{2,1,0:T(8,128)(2,1)S(1)}, u32[]{:S(2)}, u32[]{:S(2)}) collective-permute-start(bf16[3,128,384]{2,1,0:T(8,128)(2,1)S(1)} %shard_map.88), channel_id=1, source_target_pairs={{0,2},{1,7},{2,4},{3,1},{4,6},{5,3},{6,0},{7,5},{8,10},{9,15},{10,... | collective-permute-start | bytes 884744 | tf_op jit(solution)/shard_map/ppermute | solution.py:301
  32.7 0.1 shard_map.91
  32.8 0.0 copy-start.4
  32.8 2.1 %collective-permute-start.8 = (bf16[3,2,128,384]{3,2,1,0:T(8,128)(2,1)S(1)}, bf16[3,2,128,384]{3,2,1,0:T(8,128)(2,1)S(1)}, u32[]{:S(2)}, u32[]{:S(2)}) collective-permute-start(bf16[3,2,128,384]{3,2,1,0:T(8,128)(2,1)S(1)} %shard_map.91), channel_id=1, source_target_pairs={{0,1},{1,0},{2,3},{3,2},{4,5},{5,4},{6,7},{7,6},{8,9},{9,8},{10,11... | collective-permute-start | bytes 1769480 | tf_op jit(solution)/shard_map/ppermute | solution.py:303
  34.9 7.7 %collective-permute-done.4.v_ref = bf16[256,1536]{1,0:T(8,128)(2,1)S(1)} collective-permute-done((bf16[256,1536]{1,0:T(8,128)(2,1)S(1)}, bf16[256,1536]{1,0:T(8,128)(2,1)S(1)}, u32[]{:S(2)}, u32[]{:S(2)}) %collective-permute-start.4) | collective-permute-done | bytes 786464 | tf_op jit(solution)/shard_map/ppermute | solution.py:299
  42.6 2.7 %shard_map.90 = (bf16[6,128,384]{2,1,0:T(8,128)(2,1)S(1)}, bf16[6,128,384]{2,1,0:T(8,128)(2,1)S(1)}, bf16[3,128,384]{2,1,0:T(8,128)(2,1)S(1)}, bf16[6,128,384]{2,1,0:T(8,128)(2,1)S(1)}) custom-call(bf16[6,128,384]{2,1,0:T(8,128)(2,1)S(1)} %copy-done.2, bf16[7,128,384]{2,1,0:T(8,128)(2,1)S(1)} %collective-permute-done.t1, ...), custom_call_target="tpu_custom_call" | custom-call | tf_op jit(solution)/shard_map/pallas_call | solution.py:307
  45.3 1.9 %collective-permute-start.6 = (bf16[6,128,384]{2,1,0:T(8,128)(2,1)S(1)}, bf16[6,128,384]{2,1,0:T(8,128)(2,1)S(1)}, u32[]{:S(2)}, u32[]{:S(2)}) collective-permute-start(bf16[6,128,384]{2,1,0:T(8,128)(2,1)S(1)} %get-tuple-element.27), channel_id=1, source_target_pairs={{0,2},{1,7},{2,4},{3,1},{4,6},{5,3},{6,0},{7,5},{8,10},{9,15},{10,... | collective-permute-start | bytes 1769480 | tf_op jit(solution)/shard_map/ppermute | solution.py:313
  47.2 4.6 %collective-permute-start.7 = (bf16[6,128,384]{2,1,0:T(8,128)(2,1)S(1)}, bf16[6,128,384]{2,1,0:T(8,128)(2,1)S(1)}, u32[]{:S(2)}, u32[]{:S(2)}) collective-permute-start(bf16[6,128,384]{2,1,0:T(8,128)(2,1)S(1)} %get-tuple-element.28), channel_id=1, source_target_pairs={{0,6},{1,3},{2,0},{3,5},{4,2},{5,7},{6,4},{7,1},{8,14},{9,11},{10,... | collective-permute-start | bytes 1769480 | tf_op jit(solution)/shard_map/ppermute | solution.py:314
  51.8 1.9 %collective-permute-start.9 = (bf16[2,128,384]{2,1,0:T(8,128)(2,1)S(1)}, bf16[2,128,384]{2,1,0:T(8,128)(2,1)S(1)}, u32[]{:S(2)}, u32[]{:S(2)}) collective-permute-start(bf16[2,128,384]{2,1,0:T(8,128)(2,1)S(1)} %shard_map.92), channel_id=1, source_target_pairs={{0,1},{1,0},{2,3},{3,2},{4,5},{5,4},{6,7},{7,6},{8,9},{9,8},{10,11... | collective-permute-start | bytes 589832 | tf_op jit(solution)/shard_map/ppermute | solution.py:305
  53.7 4.8 %collective-permute-done.9.pf_ref = bf16[2,128,384]{2,1,0:T(8,128)(2,1)S(1)} collective-permute-done((bf16[2,128,384]{2,1,0:T(8,128)(2,1)S(1)}, bf16[2,128,384]{2,1,0:T(8,128)(2,1)S(1)}, u32[]{:S(2)}, u32[]{:S(2)}) %collective-permute-start.9) | collective-permute-done | bytes 196640 | tf_op jit(solution)/shard_map/ppermute | solution.py:305
  58.5 2.8 %collective-permute-done.6.a_ref = bf16[6,128,384]{2,1,0:T(8,128)(2,1)S(1)} collective-permute-done((bf16[6,128,384]{2,1,0:T(8,128)(2,1)S(1)}, bf16[6,128,384]{2,1,0:T(8,128)(2,1)S(1)}, u32[]{:S(2)}, u32[]{:S(2)}) %collective-permute-start.6) | collective-permute-done | bytes 589856 | tf_op jit(solution)/shard_map/ppermute | solution.py:313
  61.3 0.9 collective-permute-done.7.b_ref
  62.2 2.8 %shard_map.93 = (bf16[5,128,384]{2,1,0:T(8,128)(2,1)S(1)}, bf16[128,384]{1,0:T(8,128)(2,1)S(1)}, bf16[128,384]{1,0:T(8,128)(2,1)S(1)}, bf16[128,384]{1,0:T(8,128)(2,1)S(1)}) custom-call(bf16[6,128,384]{2,1,0:T(8,128)(2,1)S(1)} %get-tuple-element.26.m_ref.k_ref, bf16[6,128,384]{2,1,0:T(8,128)(2,1)S(1)} %collective-permute-done.6.a_ref, ...), custom_call_target="tpu_custom_call" | custom-call | tf_op jit(solution)/shard_map/pallas_call | solution.py:318
  65.0 4.3 %collective-permute-start.10 = (bf16[5,128,384]{2,1,0:T(8,128)(2,1)S(1)}, bf16[5,128,384]{2,1,0:T(8,128)(2,1)S(1)}, u32[]{:S(2)}, u32[]{:S(2)}) collective-permute-start(bf16[5,128,384]{2,1,0:T(8,128)(2,1)S(1)} %get-tuple-element.29), channel_id=1, source_target_pairs={{0,8},{1,9},{2,10},{3,11},{4,12},{5,13},{6,14},{7,15},{8,16},{9,17... | collective-permute-start | bytes 1474568 | tf_op jit(solution)/shard_map/ppermute | solution.py:332
  69.3 5.0 %collective-permute-start.14 = (bf16[3,128,384]{2,1,0:T(8,128)(2,1)S(1)}, bf16[3,128,384]{2,1,0:T(8,128)(2,1)S(1)}, u32[]{:S(2)}, u32[]{:S(2)}) collective-permute-start(bf16[3,128,384]{2,1,0:T(8,128)(2,1)S(1)} %get-tuple-element.34), channel_id=1, source_target_pairs={{0,4},{1,5},{2,6},{3,7},{4,0},{5,1},{6,2},{7,3},{8,12},{9,13},{10,... | collective-permute-start | bytes 884744 | tf_op jit(solution)/shard_map/ppermute | solution.py:316
  74.3 2.6 %collective-permute-start.11 = (bf16[128,384]{1,0:T(8,128)(2,1)S(1)}, bf16[128,384]{1,0:T(8,128)(2,1)S(1)}, u32[]{:S(2)}, u32[]{:S(2)}) collective-permute-start(bf16[128,384]{1,0:T(8,128)(2,1)S(1)} %get-tuple-element.30), channel_id=1, source_target_pairs={{0,14},{1,11},{2,8},{3,13},{4,10},{5,15},{6,12},{7,9},{8,22},{9,19... | collective-permute-start | bytes 294920 | tf_op jit(solution)/shard_map/ppermute | solution.py:332
  76.9 5.3 %collective-permute-start.12 = (bf16[128,384]{1,0:T(8,128)(2,1)S(1)}, bf16[128,384]{1,0:T(8,128)(2,1)S(1)}, u32[]{:S(2)}, u32[]{:S(2)}) collective-permute-start(bf16[128,384]{1,0:T(8,128)(2,1)S(1)} %get-tuple-element.31), channel_id=1, source_target_pairs={{0,12},{1,13},{2,14},{3,15},{4,8},{5,9},{6,10},{7,11},{8,20},{9,21... | collective-permute-start | bytes 294920 | tf_op jit(solution)/shard_map/ppermute | solution.py:332
  82.1 1.9 %collective-permute-start.13 = (bf16[128,384]{1,0:T(8,128)(2,1)S(1)}, bf16[128,384]{1,0:T(8,128)(2,1)S(1)}, u32[]{:S(2)}, u32[]{:S(2)}) collective-permute-start(bf16[128,384]{1,0:T(8,128)(2,1)S(1)} %get-tuple-element.32), channel_id=1, source_target_pairs={{0,10},{1,15},{2,12},{3,9},{4,14},{5,11},{6,8},{7,13},{8,18},{9,23... | collective-permute-start | bytes 294920 | tf_op jit(solution)/shard_map/ppermute | solution.py:332
  84.1 1.1 %shard_map.94 = (bf16[1,2,128,1536]{3,2,1,0:T(8,128)(2,1)}, f32[8,128]{1,0:T(8,128)S(1)}) custom-call(bf16[6,128,384]{2,1,0:T(8,128)(2,1)S(1)} %get-tuple-element.26.m_ref.k_ref, bf16[6,128,384]{2,1,0:T(8,128)(2,1)S(1)} %collective-permute-done.6.a_ref, bf16[6,128,384]{2,1,0:T(8,128)(2,1)S(1)} %collective-permute-done.7.b_ref, ...), custom_call_target="tpu_custom_call" | custom-call | tf_op jit(solution)/shard_map/pallas_call | solution.py:321
  85.2 0.1 collective-permute-done.11.a1
  85.3 5.1 %collective-permute-done.13.a3 = bf16[128,384]{1,0:T(8,128)(2,1)S(1)} collective-permute-done((bf16[128,384]{1,0:T(8,128)(2,1)S(1)}, bf16[128,384]{1,0:T(8,128)(2,1)S(1)}, u32[]{:S(2)}, u32[]{:S(2)}) %collective-permute-start.13) | collective-permute-done | bytes 98336 | tf_op jit(solution)/shard_map/ppermute | solution.py:332
  90.3 0.9 shard_map.95
  (21 shorter events, 0.1 us)
Async XLA Ops:
  3.4 22.6 %collective-permute-start = (bf16[7,128,384]{2,1,0:T(8,128)(2,1)}, bf16[7,128,384]{2,1,0:T(8,128)(2,1)S(1)}, u32[]{:S(2)}, u32[]{:S(2)}) collective-permute-start(bf16[7,128,384]{2,1,0:T(8,128)(2,1)} %get-tuple-element.21), channel_id=1, source_target_pairs={{0,6},{1,3},{2,0},{3,5},{4,2},{5,7},{6,4},{7,1},{8,14},{9,11},{10,... | collective-permute-start | bytes 2064392 | tf_op jit(solution)/shard_map/ppermute | solution.py:297
  8.6 22.1 %collective-permute-start.2 = (bf16[7,128,384]{2,1,0:T(8,128)(2,1)}, bf16[7,128,384]{2,1,0:T(8,128)(2,1)S(1)}, u32[]{:S(2)}, u32[]{:S(2)}) collective-permute-start(bf16[7,128,384]{2,1,0:T(8,128)(2,1)} %get-tuple-element.22), channel_id=1, source_target_pairs={{0,2},{1,7},{2,4},{3,1},{4,6},{5,3},{6,0},{7,5},{8,10},{9,15},{10,... | collective-permute-start | bytes 2064392 | tf_op jit(solution)/shard_map/ppermute | solution.py:296
  10.5 1.5 %copy-start = (bf16[1,1536,576]{1,2,0:T(8,128)(2,1)S(1)}, bf16[1,1536,576]{1,2,0:T(8,128)(2,1)}, u32[]{:S(2)}) copy-start(bf16[1,1536,576]{1,2,0:T(8,128)(2,1)} %param.8) | copy-start | bytes 5308420
  12.0 0.7 copy-start.5
  12.7 20.0 %copy-start.2 = (bf16[6,128,384]{2,1,0:T(8,128)(2,1)S(1)}, bf16[6,128,384]{2,1,0:T(8,128)(2,1)}, u32[]{:S(2)}) copy-start(bf16[6,128,384]{2,1,0:T(8,128)(2,1)} %get-tuple-element.20.t0) | copy-start | bytes 1769476
  13.1 29.5 %collective-permute-start.5 = (bf16[320,1536]{1,0:T(8,128)(2,1)S(1)}, bf16[320,1536]{1,0:T(8,128)(2,1)S(1)}, u32[]{:S(2)}, u32[]{:S(2)}) collective-permute-start(bf16[320,1536]{1,0:T(8,128)(2,1)S(1)} %get-tuple-element.25), channel_id=1, source_target_pairs={{0,1},{1,0},{2,3},{3,2},{4,5},{5,4},{6,7},{7,6},{8,9},{9,8},{10,11... | collective-permute-start | bytes 2949128 | tf_op jit(solution)/shard_map/ppermute | solution.py:298
  17.3 25.3 %collective-permute-start.4 = (bf16[256,1536]{1,0:T(8,128)(2,1)S(1)}, bf16[256,1536]{1,0:T(8,128)(2,1)S(1)}, u32[]{:S(2)}, u32[]{:S(2)}) collective-permute-start(bf16[256,1536]{1,0:T(8,128)(2,1)S(1)} %get-tuple-element.24), channel_id=1, source_target_pairs={{0,385},{1,128},{2,387},{3,130},{4,389},{5,132},{6,391},{7,134},{1... | collective-permute-start | bytes 2359304 | tf_op jit(solution)/shard_map/ppermute | solution.py:299
  26.0 16.6 %copy-start.1 = (bf16[1,1536,576]{1,2,0:T(8,128)(2,1)S(1)}, bf16[1,1536,576]{1,2,0:T(8,128)(2,1)}, u32[]{:S(2)}) copy-start(bf16[1,1536,576]{1,2,0:T(8,128)(2,1)} %param.8) | copy-start | bytes 5308420
  26.0 16.6 %collective-permute-start.1 = (bf16[3,128,384]{2,1,0:T(8,128)(2,1)S(1)}, bf16[3,128,384]{2,1,0:T(8,128)(2,1)S(1)}, u32[]{:S(2)}, u32[]{:S(2)}) collective-permute-start(bf16[3,128,384]{2,1,0:T(8,128)(2,1)S(1)} %shard_map.87), channel_id=1, source_target_pairs={{0,6},{1,3},{2,0},{3,5},{4,2},{5,7},{6,4},{7,1},{8,14},{9,11},{10,... | collective-permute-start | bytes 884744 | tf_op jit(solution)/shard_map/ppermute | solution.py:300
  30.8 11.8 %collective-permute-start.3 = (bf16[3,128,384]{2,1,0:T(8,128)(2,1)S(1)}, bf16[3,128,384]{2,1,0:T(8,128)(2,1)S(1)}, u32[]{:S(2)}, u32[]{:S(2)}) collective-permute-start(bf16[3,128,384]{2,1,0:T(8,128)(2,1)S(1)} %shard_map.88), channel_id=1, source_target_pairs={{0,2},{1,7},{2,4},{3,1},{4,6},{5,3},{6,0},{7,5},{8,10},{9,15},{10,... | collective-permute-start | bytes 884744 | tf_op jit(solution)/shard_map/ppermute | solution.py:301
  32.8 29.5 %copy-start.3 = (bf16[1,128,1536]{2,1,0:T(8,128)(2,1)S(1)}, bf16[1,128,1536]{2,1,0:T(8,128)(2,1)}, u32[]{:S(2)}) copy-start(bf16[1,128,1536]{2,1,0:T(8,128)(2,1)} %h_ref.1) | copy-start | bytes 1179652
  32.8 29.4 %copy-start.4 = (f32[1,1536]{1,0:T(1,128)S(1)}, f32[1,1536]{1,0:T(1,128)}, u32[]{:S(2)}) copy-start(f32[1,1536]{1,0:T(1,128)} %g_ref.1) | copy-start | bytes 18436
  32.8 19.0 %collective-permute-start.8 = (bf16[3,2,128,384]{3,2,1,0:T(8,128)(2,1)S(1)}, bf16[3,2,128,384]{3,2,1,0:T(8,128)(2,1)S(1)}, u32[]{:S(2)}, u32[]{:S(2)}) collective-permute-start(bf16[3,2,128,384]{3,2,1,0:T(8,128)(2,1)S(1)} %shard_map.91), channel_id=1, source_target_pairs={{0,1},{1,0},{2,3},{3,2},{4,5},{5,4},{6,7},{7,6},{8,9},{9,8},{10,11... | collective-permute-start | bytes 1769480 | tf_op jit(solution)/shard_map/ppermute | solution.py:303
  45.3 16.1 %collective-permute-start.6 = (bf16[6,128,384]{2,1,0:T(8,128)(2,1)S(1)}, bf16[6,128,384]{2,1,0:T(8,128)(2,1)S(1)}, u32[]{:S(2)}, u32[]{:S(2)}) collective-permute-start(bf16[6,128,384]{2,1,0:T(8,128)(2,1)S(1)} %get-tuple-element.27), channel_id=1, source_target_pairs={{0,2},{1,7},{2,4},{3,1},{4,6},{5,3},{6,0},{7,5},{8,10},{9,15},{10,... | collective-permute-start | bytes 1769480 | tf_op jit(solution)/shard_map/ppermute | solution.py:313
  47.2 15.0 %collective-permute-start.7 = (bf16[6,128,384]{2,1,0:T(8,128)(2,1)S(1)}, bf16[6,128,384]{2,1,0:T(8,128)(2,1)S(1)}, u32[]{:S(2)}, u32[]{:S(2)}) collective-permute-start(bf16[6,128,384]{2,1,0:T(8,128)(2,1)S(1)} %get-tuple-element.28), channel_id=1, source_target_pairs={{0,6},{1,3},{2,0},{3,5},{4,2},{5,7},{6,4},{7,1},{8,14},{9,11},{10,... | collective-permute-start | bytes 1769480 | tf_op jit(solution)/shard_map/ppermute | solution.py:314
  51.8 6.7 %collective-permute-start.9 = (bf16[2,128,384]{2,1,0:T(8,128)(2,1)S(1)}, bf16[2,128,384]{2,1,0:T(8,128)(2,1)S(1)}, u32[]{:S(2)}, u32[]{:S(2)}) collective-permute-start(bf16[2,128,384]{2,1,0:T(8,128)(2,1)S(1)} %shard_map.92), channel_id=1, source_target_pairs={{0,1},{1,0},{2,3},{3,2},{4,5},{5,4},{6,7},{7,6},{8,9},{9,8},{10,11... | collective-permute-start | bytes 589832 | tf_op jit(solution)/shard_map/ppermute | solution.py:305
  65.0 25.3 %collective-permute-start.10 = (bf16[5,128,384]{2,1,0:T(8,128)(2,1)S(1)}, bf16[5,128,384]{2,1,0:T(8,128)(2,1)S(1)}, u32[]{:S(2)}, u32[]{:S(2)}) collective-permute-start(bf16[5,128,384]{2,1,0:T(8,128)(2,1)S(1)} %get-tuple-element.29), channel_id=1, source_target_pairs={{0,8},{1,9},{2,10},{3,11},{4,12},{5,13},{6,14},{7,15},{8,16},{9,17... | collective-permute-start | bytes 1474568 | tf_op jit(solution)/shard_map/ppermute | solution.py:332
  69.3 14.7 %collective-permute-start.14 = (bf16[3,128,384]{2,1,0:T(8,128)(2,1)S(1)}, bf16[3,128,384]{2,1,0:T(8,128)(2,1)S(1)}, u32[]{:S(2)}, u32[]{:S(2)}) collective-permute-start(bf16[3,128,384]{2,1,0:T(8,128)(2,1)S(1)} %get-tuple-element.34), channel_id=1, source_target_pairs={{0,4},{1,5},{2,6},{3,7},{4,0},{5,1},{6,2},{7,3},{8,12},{9,13},{10,... | collective-permute-start | bytes 884744 | tf_op jit(solution)/shard_map/ppermute | solution.py:316
  74.3 11.0 %collective-permute-start.11 = (bf16[128,384]{1,0:T(8,128)(2,1)S(1)}, bf16[128,384]{1,0:T(8,128)(2,1)S(1)}, u32[]{:S(2)}, u32[]{:S(2)}) collective-permute-start(bf16[128,384]{1,0:T(8,128)(2,1)S(1)} %get-tuple-element.30), channel_id=1, source_target_pairs={{0,14},{1,11},{2,8},{3,13},{4,10},{5,15},{6,12},{7,9},{8,22},{9,19... | collective-permute-start | bytes 294920 | tf_op jit(solution)/shard_map/ppermute | solution.py:332
  76.9 8.4 %collective-permute-start.12 = (bf16[128,384]{1,0:T(8,128)(2,1)S(1)}, bf16[128,384]{1,0:T(8,128)(2,1)S(1)}, u32[]{:S(2)}, u32[]{:S(2)}) collective-permute-start(bf16[128,384]{1,0:T(8,128)(2,1)S(1)} %get-tuple-element.31), channel_id=1, source_target_pairs={{0,12},{1,13},{2,14},{3,15},{4,8},{5,9},{6,10},{7,11},{8,20},{9,21... | collective-permute-start | bytes 294920 | tf_op jit(solution)/shard_map/ppermute | solution.py:332
  82.1 8.2 %collective-permute-start.13 = (bf16[128,384]{1,0:T(8,128)(2,1)S(1)}, bf16[128,384]{1,0:T(8,128)(2,1)S(1)}, u32[]{:S(2)}, u32[]{:S(2)}) collective-permute-start(bf16[128,384]{1,0:T(8,128)(2,1)S(1)} %get-tuple-element.32), channel_id=1, source_target_pairs={{0,10},{1,15},{2,12},{3,9},{4,14},{5,11},{6,8},{7,13},{8,18},{9,23... | collective-permute-start | bytes 294920 | tf_op jit(solution)/shard_map/ppermute | solution.py:332

commit v14 on v13

--- a/solution.py
+++ b/solution.py
@@ -329,7 +329,10 @@
             for s in range(segments)
             for src, dst in x_pairs(j)
         ]
-        came[j] = lax.ppermute(out[j], ("segment", "patch"), pairs)
+        piece = out[j]
+        if j == 0:
+            piece, done = lax.optimization_barrier((piece, done))
+        came[j] = lax.ppermute(piece, ("segment", "patch"), pairs)
     passed = call(finish_body, jax.ShapeDtypeStruct((1, ROWS, D), BF), 5)(
         came[0], came[3], came[2], came[1], done
     )

time: 91.8 us -> 98.7 us (1.075)
  waiting for transfers between devices: 21.4 us -> 27.7 us
    ppermute x1, waiting for transfers between devices: 0.9 us -> 6.64 us  [local(): back = lax.ppermute(back, 'patch', x_pairs(3))]
    ppermute x1, waiting for transfers between devices: 2.8 us -> 0.01 us  [local(): front = lax.ppermute(front, 'patch', x_pairs(1))]
    ppermute x1, waiting for transfers between devices: 7.72 us -> 10 us  [local(): far_rows = lax.ppermute(far_rows, ('dp', 'patch'), far_pairs(parts))]
    ppermute x4, starting transfers between devices: 14 us -> 16 us  [local(): came[j] = lax.ppermute(piece, ('segment', 'patch'), pairs)]
    ppermute x4, waiting for transfers between devices: 5.15 us -> 6.27 us  [local(): came[j] = lax.ppermute(piece, ('segment', 'patch'), pairs)]
    ppermute x1, starting transfers between devices: 4.97 us -> 3.98 us  [local(): opposite = lax.ppermute(opposite, 'patch', x_pairs(2))]
  transfers between devices with their start and end apart: 15 -> 15, of which waited for: 6 -> 5; matrix products, arithmetic and copies ran while one was open for 0% -> 0% of each run, Pallas kernels for 5% -> 3%
where the time goes in v14:
time: 98.7 us; the launch traced here: 98.1 us
  starting transfers between devices  56.8 us (58%)
  waiting for transfers between devices  27.7 us (28%)
  Pallas kernels  10.6 us (11%)
  local copies, waits for them, and re-layouts  2.18 us (2%)
    ppermute x4, starting transfers between devices, local(): came[j] = lax.ppermute(piece, ('segment', 'patch'), pairs)  16 us
    ppermute x1, waiting for transfers between devices, local(): far_rows = lax.ppermute(far_rows, ('dp', 'patch'), far_pairs(parts))  10 us
    ppermute x1, starting transfers between devices, local(): far_rows = lax.ppermute(far_rows, ('dp', 'patch'), far_pairs(parts))  8.66 us
    ppermute x1, waiting for transfers between devices, local(): back = lax.ppermute(back, 'patch', x_pairs(3))  6.64 us
    ppermute x4, waiting for transfers between devices, local(): came[j] = lax.ppermute(piece, ('segment', 'patch'), pairs)  6.27 us
    ppermute x1, starting transfers between devices, local(): t1 = lax.ppermute(t1, 'patch', x_pairs(3))  5.22 us
    ppermute x1, waiting for transfers between devices, local(): far = lax.ppermute(far, 'patch', partner_pairs())  4.74 us
    ppermute x1, starting transfers between devices, local(): lax.ppermute(call(pass_back_body, blocks(3), 1)(t1), 'patch', x_pairs(3))  4.57 us
  transfers between devices with their start and end apart: 15, of which 5 were waited for; matrix products, arithmetic and copies ran while one was open for 0% of the time, Pallas kernels for 3%

profile of v14, /device:TPU:1, one launch (start us, length us, event | category | flops | bytes accessed | tf_op | source)
XLA Modules:
  0.0 98.1 jit_solution(17508257846960359664)
XLA Ops:
  0.6 2.7 %shard_map.86 = (bf16[6,128,384]{2,1,0:T(8,128)(2,1)}, bf16[7,128,384]{2,1,0:T(8,128)(2,1)}, bf16[7,128,384]{2,1,0:T(8,128)(2,1)}, f32[8,128]{1,0:T(8,128)}) custom-call(bf16[1,128,1536]{2,1,0:T(8,128)(2,1)} %h_ref.1, f32[1,1536]{1,0:T(1,128)} %g_hbm.1, f32[1,1536]{1,0:T(1,128)} %b_hbm.1, s32[1,128]{1,0:T(1,128)} %m_hbm.1, bf16[1,2,128,1536]{3,2,1,0:T(8,128)(2,1)} %s_hbm.1), custom_call_target="tpu_custom_call" | custom-call | tf_op jit(solution)/shard_map/pallas_call | solution.py:273
  3.4 5.2 %collective-permute-start = (bf16[7,128,384]{2,1,0:T(8,128)(2,1)}, bf16[7,128,384]{2,1,0:T(8,128)(2,1)S(1)}, u32[]{:S(2)}, u32[]{:S(2)}) collective-permute-start(bf16[7,128,384]{2,1,0:T(8,128)(2,1)} %get-tuple-element.23), channel_id=1, source_target_pairs={{0,6},{1,3},{2,0},{3,5},{4,2},{5,7},{6,4},{7,1},{8,14},{9,11},{10,... | collective-permute-start | bytes 2064392 | tf_op jit(solution)/shard_map/ppermute | solution.py:297
  8.6 1.9 %collective-permute-start.2 = (bf16[7,128,384]{2,1,0:T(8,128)(2,1)}, bf16[7,128,384]{2,1,0:T(8,128)(2,1)S(1)}, u32[]{:S(2)}, u32[]{:S(2)}) collective-permute-start(bf16[7,128,384]{2,1,0:T(8,128)(2,1)} %get-tuple-element.24), channel_id=1, source_target_pairs={{0,2},{1,7},{2,4},{3,1},{4,6},{5,3},{6,0},{7,5},{8,10},{9,15},{10,... | collective-permute-start | bytes 2064392 | tf_op jit(solution)/shard_map/ppermute | solution.py:296
  10.5 0.0 copy-start
  10.5 1.5 %copy-done = bf16[1,1536,576]{1,2,0:T(8,128)(2,1)S(1)} copy-done((bf16[1,1536,576]{1,2,0:T(8,128)(2,1)S(1)}, bf16[1,1536,576]{1,2,0:T(8,128)(2,1)}, u32[]{:S(2)}) %copy-start) | copy-done | bytes 1769496
  12.0 0.7 copy-done.5
  12.7 0.4 shard_map.89
  13.1 4.3 %collective-permute-start.5 = (bf16[320,1536]{1,0:T(8,128)(2,1)S(1)}, bf16[320,1536]{1,0:T(8,128)(2,1)S(1)}, u32[]{:S(2)}, u32[]{:S(2)}) collective-permute-start(bf16[320,1536]{1,0:T(8,128)(2,1)S(1)} %get-tuple-element.27), channel_id=1, source_target_pairs={{0,1},{1,0},{2,3},{3,2},{4,5},{5,4},{6,7},{7,6},{8,9},{9,8},{10,11... | collective-permute-start | bytes 2949128 | tf_op jit(solution)/shard_map/ppermute | solution.py:298
  17.4 8.7 %collective-permute-start.4 = (bf16[256,1536]{1,0:T(8,128)(2,1)S(1)}, bf16[256,1536]{1,0:T(8,128)(2,1)S(1)}, u32[]{:S(2)}, u32[]{:S(2)}) collective-permute-start(bf16[256,1536]{1,0:T(8,128)(2,1)S(1)} %get-tuple-element.26), channel_id=1, source_target_pairs={{0,385},{1,128},{2,387},{3,130},{4,389},{5,132},{6,391},{7,134},{1... | collective-permute-start | bytes 2359304 | tf_op jit(solution)/shard_map/ppermute | solution.py:299
  26.1 4.6 %collective-permute-start.1 = (bf16[3,128,384]{2,1,0:T(8,128)(2,1)S(1)}, bf16[3,128,384]{2,1,0:T(8,128)(2,1)S(1)}, u32[]{:S(2)}, u32[]{:S(2)}) collective-permute-start(bf16[3,128,384]{2,1,0:T(8,128)(2,1)S(1)} %shard_map.87), channel_id=1, source_target_pairs={{0,6},{1,3},{2,0},{3,5},{4,2},{5,7},{6,4},{7,1},{8,14},{9,11},{10,... | collective-permute-start | bytes 884744 | tf_op jit(solution)/shard_map/ppermute | solution.py:300
  30.8 1.9 %collective-permute-start.3 = (bf16[3,128,384]{2,1,0:T(8,128)(2,1)S(1)}, bf16[3,128,384]{2,1,0:T(8,128)(2,1)S(1)}, u32[]{:S(2)}, u32[]{:S(2)}) collective-permute-start(bf16[3,128,384]{2,1,0:T(8,128)(2,1)S(1)} %shard_map.88), channel_id=1, source_target_pairs={{0,2},{1,7},{2,4},{3,1},{4,6},{5,3},{6,0},{7,5},{8,10},{9,15},{10,... | collective-permute-start | bytes 884744 | tf_op jit(solution)/shard_map/ppermute | solution.py:301
  32.7 10.0 %collective-permute-done.4.v_ref = bf16[256,1536]{1,0:T(8,128)(2,1)S(1)} collective-permute-done((bf16[256,1536]{1,0:T(8,128)(2,1)S(1)}, bf16[256,1536]{1,0:T(8,128)(2,1)S(1)}, u32[]{:S(2)}, u32[]{:S(2)}) %collective-permute-start.4) | collective-permute-done | bytes 786464 | tf_op jit(solution)/shard_map/ppermute | solution.py:299
  42.7 2.7 %shard_map.90 = (bf16[6,128,384]{2,1,0:T(8,128)(2,1)S(1)}, bf16[6,128,384]{2,1,0:T(8,128)(2,1)S(1)}, bf16[3,128,384]{2,1,0:T(8,128)(2,1)S(1)}, bf16[6,128,384]{2,1,0:T(8,128)(2,1)S(1)}) custom-call(bf16[6,128,384]{2,1,0:T(8,128)(2,1)S(1)} %copy-done.2, bf16[7,128,384]{2,1,0:T(8,128)(2,1)S(1)} %collective-permute-done.t1, ...), custom_call_target="tpu_custom_call" | custom-call | tf_op jit(solution)/shard_map/pallas_call | solution.py:307
  45.4 0.0 copy-start.3
  45.4 0.0 copy-start.4
  45.4 4.4 %collective-permute-start.7 = (bf16[6,128,384]{2,1,0:T(8,128)(2,1)S(1)}, bf16[6,128,384]{2,1,0:T(8,128)(2,1)S(1)}, u32[]{:S(2)}, u32[]{:S(2)}) collective-permute-start(bf16[6,128,384]{2,1,0:T(8,128)(2,1)S(1)} %get-tuple-element.30), channel_id=1, source_target_pairs={{0,6},{1,3},{2,0},{3,5},{4,2},{5,7},{6,4},{7,1},{8,14},{9,11},{10,... | collective-permute-start | bytes 1769480 | tf_op jit(solution)/shard_map/ppermute | solution.py:314
  49.9 0.1 shard_map.91
  49.9 1.9 %collective-permute-start.8 = (bf16[3,2,128,384]{3,2,1,0:T(8,128)(2,1)S(1)}, bf16[3,2,128,384]{3,2,1,0:T(8,128)(2,1)S(1)}, u32[]{:S(2)}, u32[]{:S(2)}) collective-permute-start(bf16[3,2,128,384]{3,2,1,0:T(8,128)(2,1)S(1)} %shard_map.91), channel_id=1, source_target_pairs={{0,1},{1,0},{2,3},{3,2},{4,5},{5,4},{6,7},{7,6},{8,9},{9,8},{10,11... | collective-permute-start | bytes 1769480 | tf_op jit(solution)/shard_map/ppermute | solution.py:303
  51.8 1.9 %collective-permute-start.6 = (bf16[6,128,384]{2,1,0:T(8,128)(2,1)S(1)}, bf16[6,128,384]{2,1,0:T(8,128)(2,1)S(1)}, u32[]{:S(2)}, u32[]{:S(2)}) collective-permute-start(bf16[6,128,384]{2,1,0:T(8,128)(2,1)S(1)} %get-tuple-element.29), channel_id=1, source_target_pairs={{0,2},{1,7},{2,4},{3,1},{4,6},{5,3},{6,0},{7,5},{8,10},{9,15},{10,... | collective-permute-start | bytes 1769480 | tf_op jit(solution)/shard_map/ppermute | solution.py:313
  53.8 6.6 %collective-permute-done.7.b_ref = bf16[6,128,384]{2,1,0:T(8,128)(2,1)S(1)} collective-permute-done((bf16[6,128,384]{2,1,0:T(8,128)(2,1)S(1)}, bf16[6,128,384]{2,1,0:T(8,128)(2,1)S(1)}, u32[]{:S(2)}, u32[]{:S(2)}) %collective-permute-start.7) | collective-permute-done | bytes 589856 | tf_op jit(solution)/shard_map/ppermute | solution.py:314
  60.4 4.0 %collective-permute-start.10 = (bf16[3,128,384]{2,1,0:T(8,128)(2,1)S(1)}, bf16[3,128,384]{2,1,0:T(8,128)(2,1)S(1)}, u32[]{:S(2)}, u32[]{:S(2)}) collective-permute-start(bf16[3,128,384]{2,1,0:T(8,128)(2,1)S(1)} %get-tuple-element.33), channel_id=1, source_target_pairs={{0,4},{1,5},{2,6},{3,7},{4,0},{5,1},{6,2},{7,3},{8,12},{9,13},{10,... | collective-permute-start | bytes 884744 | tf_op jit(solution)/shard_map/ppermute | solution.py:316
  64.4 2.0 %collective-permute-start.9 = (bf16[2,128,384]{2,1,0:T(8,128)(2,1)S(1)}, bf16[2,128,384]{2,1,0:T(8,128)(2,1)S(1)}, u32[]{:S(2)}, u32[]{:S(2)}) collective-permute-start(bf16[2,128,384]{2,1,0:T(8,128)(2,1)S(1)} %shard_map.92), channel_id=1, source_target_pairs={{0,1},{1,0},{2,3},{3,2},{4,5},{5,4},{6,7},{7,6},{8,9},{9,8},{10,11... | collective-permute-start | bytes 589832 | tf_op jit(solution)/shard_map/ppermute | solution.py:305
  66.4 4.7 %collective-permute-done.9.pf_ref = bf16[2,128,384]{2,1,0:T(8,128)(2,1)S(1)} collective-permute-done((bf16[2,128,384]{2,1,0:T(8,128)(2,1)S(1)}, bf16[2,128,384]{2,1,0:T(8,128)(2,1)S(1)}, u32[]{:S(2)}, u32[]{:S(2)}) %collective-permute-start.9) | collective-permute-done | bytes 196640 | tf_op jit(solution)/shard_map/ppermute | solution.py:305
  71.2 2.7 %shard_map.93 = (bf16[5,128,384]{2,1,0:T(8,128)(2,1)S(1)}, bf16[128,384]{1,0:T(8,128)(2,1)S(1)}, bf16[128,384]{1,0:T(8,128)(2,1)S(1)}, bf16[128,384]{1,0:T(8,128)(2,1)S(1)}) custom-call(bf16[6,128,384]{2,1,0:T(8,128)(2,1)S(1)} %get-tuple-element.28.m_ref.k_ref, bf16[6,128,384]{2,1,0:T(8,128)(2,1)S(1)} %collective-permute-done.6.a_ref, ...), custom_call_target="tpu_custom_call" | custom-call | tf_op jit(solution)/shard_map/pallas_call | solution.py:318
  73.9 1.1 %shard_map.94 = (bf16[1,2,128,1536]{3,2,1,0:T(8,128)(2,1)}, f32[8,128]{1,0:T(8,128)S(1)}) custom-call(bf16[6,128,384]{2,1,0:T(8,128)(2,1)S(1)} %get-tuple-element.28.m_ref.k_ref, bf16[6,128,384]{2,1,0:T(8,128)(2,1)S(1)} %collective-permute-done.6.a_ref, bf16[6,128,384]{2,1,0:T(8,128)(2,1)S(1)} %collective-permute-done.7.b_ref, ...), custom_call_target="tpu_custom_call" | custom-call | tf_op jit(solution)/shard_map/pallas_call | solution.py:321
  75.0 7.0 %collective-permute-start.11 = (bf16[5,128,384]{2,1,0:T(8,128)(2,1)S(1)}, bf16[5,128,384]{2,1,0:T(8,128)(2,1)S(1)}, u32[]{:S(2)}, u32[]{:S(2)}) collective-permute-start(bf16[5,128,384]{2,1,0:T(8,128)(2,1)S(1)} %get-tuple-element.36), channel_id=1, source_target_pairs={{0,8},{1,9},{2,10},{3,11},{4,12},{5,13},{6,14},{7,15},{8,16},{9,17... | collective-permute-start | bytes 1474568 | tf_op jit(solution)/shard_map/ppermute | solution.py:335
  82.0 1.9 %collective-permute-start.12 = (bf16[128,384]{1,0:T(8,128)(2,1)S(1)}, bf16[128,384]{1,0:T(8,128)(2,1)S(1)}, u32[]{:S(2)}, u32[]{:S(2)}) collective-permute-start(bf16[128,384]{1,0:T(8,128)(2,1)S(1)} %get-tuple-element.37), channel_id=1, source_target_pairs={{0,14},{1,11},{2,8},{3,13},{4,10},{5,15},{6,12},{7,9},{8,22},{9,19... | collective-permute-start | bytes 294920 | tf_op jit(solution)/shard_map/ppermute | solution.py:335
  83.9 5.1 %collective-permute-start.13 = (bf16[128,384]{1,0:T(8,128)(2,1)S(1)}, bf16[128,384]{1,0:T(8,128)(2,1)S(1)}, u32[]{:S(2)}, u32[]{:S(2)}) collective-permute-start(bf16[128,384]{1,0:T(8,128)(2,1)S(1)} %get-tuple-element.38), channel_id=1, source_target_pairs={{0,12},{1,13},{2,14},{3,15},{4,8},{5,9},{6,10},{7,11},{8,20},{9,21... | collective-permute-start | bytes 294920 | tf_op jit(solution)/shard_map/ppermute | solution.py:335
  89.0 1.9 %collective-permute-start.14 = (bf16[128,384]{1,0:T(8,128)(2,1)S(1)}, bf16[128,384]{1,0:T(8,128)(2,1)S(1)}, u32[]{:S(2)}, u32[]{:S(2)}) collective-permute-start(bf16[128,384]{1,0:T(8,128)(2,1)S(1)} %get-tuple-element.39), channel_id=1, source_target_pairs={{0,10},{1,15},{2,12},{3,9},{4,14},{5,11},{6,8},{7,13},{8,18},{9,23... | collective-permute-start | bytes 294920 | tf_op jit(solution)/shard_map/ppermute | solution.py:335
  91.0 0.4 collective-permute-done.13.a2
  91.3 5.9 %collective-permute-done.14.a3 = bf16[128,384]{1,0:T(8,128)(2,1)S(1)} collective-permute-done((bf16[128,384]{1,0:T(8,128)(2,1)S(1)}, bf16[128,384]{1,0:T(8,128)(2,1)S(1)}, u32[]{:S(2)}, u32[]{:S(2)}) %collective-permute-start.14) | collective-permute-done | bytes 98336 | tf_op jit(solution)/shard_map/ppermute | solution.py:335
  97.2 0.9 shard_map.95
  (21 shorter events, 0.1 us)
Async XLA Ops:
  3.4 22.7 %collective-permute-start = (bf16[7,128,384]{2,1,0:T(8,128)(2,1)}, bf16[7,128,384]{2,1,0:T(8,128)(2,1)S(1)}, u32[]{:S(2)}, u32[]{:S(2)}) collective-permute-start(bf16[7,128,384]{2,1,0:T(8,128)(2,1)} %get-tuple-element.23), channel_id=1, source_target_pairs={{0,6},{1,3},{2,0},{3,5},{4,2},{5,7},{6,4},{7,1},{8,14},{9,11},{10,... | collective-permute-start | bytes 2064392 | tf_op jit(solution)/shard_map/ppermute | solution.py:297
  8.6 22.1 %collective-permute-start.2 = (bf16[7,128,384]{2,1,0:T(8,128)(2,1)}, bf16[7,128,384]{2,1,0:T(8,128)(2,1)S(1)}, u32[]{:S(2)}, u32[]{:S(2)}) collective-permute-start(bf16[7,128,384]{2,1,0:T(8,128)(2,1)} %get-tuple-element.24), channel_id=1, source_target_pairs={{0,2},{1,7},{2,4},{3,1},{4,6},{5,3},{6,0},{7,5},{8,10},{9,15},{10,... | collective-permute-start | bytes 2064392 | tf_op jit(solution)/shard_map/ppermute | solution.py:296
  10.5 1.5 %copy-start = (bf16[1,1536,576]{1,2,0:T(8,128)(2,1)S(1)}, bf16[1,1536,576]{1,2,0:T(8,128)(2,1)}, u32[]{:S(2)}) copy-start(bf16[1,1536,576]{1,2,0:T(8,128)(2,1)} %param.8) | copy-start | bytes 5308420
  12.0 0.7 copy-start.5
  12.7 30.0 %copy-start.1 = (bf16[1,1536,576]{1,2,0:T(8,128)(2,1)S(1)}, bf16[1,1536,576]{1,2,0:T(8,128)(2,1)}, u32[]{:S(2)}) copy-start(bf16[1,1536,576]{1,2,0:T(8,128)(2,1)} %param.8) | copy-start | bytes 5308420
  12.7 30.0 %copy-start.2 = (bf16[6,128,384]{2,1,0:T(8,128)(2,1)S(1)}, bf16[6,128,384]{2,1,0:T(8,128)(2,1)}, u32[]{:S(2)}) copy-start(bf16[6,128,384]{2,1,0:T(8,128)(2,1)} %get-tuple-element.22.t0) | copy-start | bytes 1769476
  13.1 29.6 %collective-permute-start.5 = (bf16[320,1536]{1,0:T(8,128)(2,1)S(1)}, bf16[320,1536]{1,0:T(8,128)(2,1)S(1)}, u32[]{:S(2)}, u32[]{:S(2)}) collective-permute-start(bf16[320,1536]{1,0:T(8,128)(2,1)S(1)} %get-tuple-element.27), channel_id=1, source_target_pairs={{0,1},{1,0},{2,3},{3,2},{4,5},{5,4},{6,7},{7,6},{8,9},{9,8},{10,11... | collective-permute-start | bytes 2949128 | tf_op jit(solution)/shard_map/ppermute | solution.py:298
  17.4 25.3 %collective-permute-start.4 = (bf16[256,1536]{1,0:T(8,128)(2,1)S(1)}, bf16[256,1536]{1,0:T(8,128)(2,1)S(1)}, u32[]{:S(2)}, u32[]{:S(2)}) collective-permute-start(bf16[256,1536]{1,0:T(8,128)(2,1)S(1)} %get-tuple-element.26), channel_id=1, source_target_pairs={{0,385},{1,128},{2,387},{3,130},{4,389},{5,132},{6,391},{7,134},{1... | collective-permute-start | bytes 2359304 | tf_op jit(solution)/shard_map/ppermute | solution.py:299
  26.1 16.6 %collective-permute-start.1 = (bf16[3,128,384]{2,1,0:T(8,128)(2,1)S(1)}, bf16[3,128,384]{2,1,0:T(8,128)(2,1)S(1)}, u32[]{:S(2)}, u32[]{:S(2)}) collective-permute-start(bf16[3,128,384]{2,1,0:T(8,128)(2,1)S(1)} %shard_map.87), channel_id=1, source_target_pairs={{0,6},{1,3},{2,0},{3,5},{4,2},{5,7},{6,4},{7,1},{8,14},{9,11},{10,... | collective-permute-start | bytes 884744 | tf_op jit(solution)/shard_map/ppermute | solution.py:300
  30.8 11.9 %collective-permute-start.3 = (bf16[3,128,384]{2,1,0:T(8,128)(2,1)S(1)}, bf16[3,128,384]{2,1,0:T(8,128)(2,1)S(1)}, u32[]{:S(2)}, u32[]{:S(2)}) collective-permute-start(bf16[3,128,384]{2,1,0:T(8,128)(2,1)S(1)} %shard_map.88), channel_id=1, source_target_pairs={{0,2},{1,7},{2,4},{3,1},{4,6},{5,3},{6,0},{7,5},{8,10},{9,15},{10,... | collective-permute-start | bytes 884744 | tf_op jit(solution)/shard_map/ppermute | solution.py:301
  45.4 25.7 %copy-start.3 = (bf16[1,128,1536]{2,1,0:T(8,128)(2,1)S(1)}, bf16[1,128,1536]{2,1,0:T(8,128)(2,1)}, u32[]{:S(2)}) copy-start(bf16[1,128,1536]{2,1,0:T(8,128)(2,1)} %h_ref.1) | copy-start | bytes 1179652
  45.4 25.7 %copy-start.4 = (f32[1,1536]{1,0:T(1,128)S(1)}, f32[1,1536]{1,0:T(1,128)}, u32[]{:S(2)}) copy-start(f32[1,1536]{1,0:T(1,128)} %g_ref.1) | copy-start | bytes 18436
  45.4 15.0 %collective-permute-start.7 = (bf16[6,128,384]{2,1,0:T(8,128)(2,1)S(1)}, bf16[6,128,384]{2,1,0:T(8,128)(2,1)S(1)}, u32[]{:S(2)}, u32[]{:S(2)}) collective-permute-start(bf16[6,128,384]{2,1,0:T(8,128)(2,1)S(1)} %get-tuple-element.30), channel_id=1, source_target_pairs={{0,6},{1,3},{2,0},{3,5},{4,2},{5,7},{6,4},{7,1},{8,14},{9,11},{10,... | collective-permute-start | bytes 1769480 | tf_op jit(solution)/shard_map/ppermute | solution.py:314
  49.9 14.5 %collective-permute-start.8 = (bf16[3,2,128,384]{3,2,1,0:T(8,128)(2,1)S(1)}, bf16[3,2,128,384]{3,2,1,0:T(8,128)(2,1)S(1)}, u32[]{:S(2)}, u32[]{:S(2)}) collective-permute-start(bf16[3,2,128,384]{3,2,1,0:T(8,128)(2,1)S(1)} %shard_map.91), channel_id=1, source_target_pairs={{0,1},{1,0},{2,3},{3,2},{4,5},{5,4},{6,7},{7,6},{8,9},{9,8},{10,11... | collective-permute-start | bytes 1769480 | tf_op jit(solution)/shard_map/ppermute | solution.py:303
  51.8 19.3 %collective-permute-start.6 = (bf16[6,128,384]{2,1,0:T(8,128)(2,1)S(1)}, bf16[6,128,384]{2,1,0:T(8,128)(2,1)S(1)}, u32[]{:S(2)}, u32[]{:S(2)}) collective-permute-start(bf16[6,128,384]{2,1,0:T(8,128)(2,1)S(1)} %get-tuple-element.29), channel_id=1, source_target_pairs={{0,2},{1,7},{2,4},{3,1},{4,6},{5,3},{6,0},{7,5},{8,10},{9,15},{10,... | collective-permute-start | bytes 1769480 | tf_op jit(solution)/shard_map/ppermute | solution.py:313
  60.4 13.4 %collective-permute-start.10 = (bf16[3,128,384]{2,1,0:T(8,128)(2,1)S(1)}, bf16[3,128,384]{2,1,0:T(8,128)(2,1)S(1)}, u32[]{:S(2)}, u32[]{:S(2)}) collective-permute-start(bf16[3,128,384]{2,1,0:T(8,128)(2,1)S(1)} %get-tuple-element.33), channel_id=1, source_target_pairs={{0,4},{1,5},{2,6},{3,7},{4,0},{5,1},{6,2},{7,3},{8,12},{9,13},{10,... | collective-permute-start | bytes 884744 | tf_op jit(solution)/shard_map/ppermute | solution.py:316
  64.4 6.7 %collective-permute-start.9 = (bf16[2,128,384]{2,1,0:T(8,128)(2,1)S(1)}, bf16[2,128,384]{2,1,0:T(8,128)(2,1)S(1)}, u32[]{:S(2)}, u32[]{:S(2)}) collective-permute-start(bf16[2,128,384]{2,1,0:T(8,128)(2,1)S(1)} %shard_map.92), channel_id=1, source_target_pairs={{0,1},{1,0},{2,3},{3,2},{4,5},{5,4},{6,7},{7,6},{8,9},{9,8},{10,11... | collective-permute-start | bytes 589832 | tf_op jit(solution)/shard_map/ppermute | solution.py:305
  75.0 22.3 %collective-permute-start.11 = (bf16[5,128,384]{2,1,0:T(8,128)(2,1)S(1)}, bf16[5,128,384]{2,1,0:T(8,128)(2,1)S(1)}, u32[]{:S(2)}, u32[]{:S(2)}) collective-permute-start(bf16[5,128,384]{2,1,0:T(8,128)(2,1)S(1)} %get-tuple-element.36), channel_id=1, source_target_pairs={{0,8},{1,9},{2,10},{3,11},{4,12},{5,13},{6,14},{7,15},{8,16},{9,17... | collective-permute-start | bytes 1474568 | tf_op jit(solution)/shard_map/ppermute | solution.py:335
  82.0 9.0 %collective-permute-start.12 = (bf16[128,384]{1,0:T(8,128)(2,1)S(1)}, bf16[128,384]{1,0:T(8,128)(2,1)S(1)}, u32[]{:S(2)}, u32[]{:S(2)}) collective-permute-start(bf16[128,384]{1,0:T(8,128)(2,1)S(1)} %get-tuple-element.37), channel_id=1, source_target_pairs={{0,14},{1,11},{2,8},{3,13},{4,10},{5,15},{6,12},{7,9},{8,22},{9,19... | collective-permute-start | bytes 294920 | tf_op jit(solution)/shard_map/ppermute | solution.py:335
  83.9 7.4 %collective-permute-start.13 = (bf16[128,384]{1,0:T(8,128)(2,1)S(1)}, bf16[128,384]{1,0:T(8,128)(2,1)S(1)}, u32[]{:S(2)}, u32[]{:S(2)}) collective-permute-start(bf16[128,384]{1,0:T(8,128)(2,1)S(1)} %get-tuple-element.38), channel_id=1, source_target_pairs={{0,12},{1,13},{2,14},{3,15},{4,8},{5,9},{6,10},{7,11},{8,20},{9,21... | collective-permute-start | bytes 294920 | tf_op jit(solution)/shard_map/ppermute | solution.py:335
  89.0 8.2 %collective-permute-start.14 = (bf16[128,384]{1,0:T(8,128)(2,1)S(1)}, bf16[128,384]{1,0:T(8,128)(2,1)S(1)}, u32[]{:S(2)}, u32[]{:S(2)}) collective-permute-start(bf16[128,384]{1,0:T(8,128)(2,1)S(1)} %get-tuple-element.39), channel_id=1, source_target_pairs={{0,10},{1,15},{2,12},{3,9},{4,14},{5,11},{6,8},{7,13},{8,18},{9,23... | collective-permute-start | bytes 294920 | tf_op jit(solution)/shard_map/ppermute | solution.py:335

commit v15 on v12

--- a/solution.py
+++ b/solution.py
@@ -10,7 +10,7 @@
 D = 1536
 UNIT = 384
 HALF = 192
-PART = 288
+PART = 272
 SCALE = HEAD_DIM ** (-0.5) * 1.4426950408889634
 BF = jnp.bfloat16
 F32 = jnp.float32

time: 95.3 us -> 92.5 us (0.971)
  the two profiles are of different devices: /device:TPU:25 before, /device:TPU:49 now
where the time goes in v15:
time: 92.5 us; the launch traced here: 91.9 us
  starting transfers between devices  54.8 us (59%)
  waiting for transfers between devices  23.4 us (25%)
  Pallas kernels  10.6 us (11%)
  local copies, waits for them, and re-layouts  2.18 us (2%)
    ppermute x4, starting transfers between devices, local(): came[j] = lax.ppermute(out[j], ('segment', 'patch'), pairs)  15.7 us
    ppermute x1, starting transfers between devices, local(): far_rows = lax.ppermute(far_rows, ('dp', 'patch'), far_pairs(parts))  8.66 us
    ppermute x1, waiting for transfers between devices, local(): back = lax.ppermute(back, 'patch', x_pairs(3))  8.52 us
    ppermute x1, waiting for transfers between devices, local(): far_rows = lax.ppermute(far_rows, ('dp', 'patch'), far_pairs(parts))  6.81 us
    ppermute x4, waiting for transfers between devices, local(): came[j] = lax.ppermute(out[j], ('segment', 'patch'), pairs)  6.21 us
    ppermute x1, starting transfers between devices, local(): lax.ppermute(call(pass_back_body, blocks(3), 1)(t1), 'patch', x_pairs(3))  4.98 us
    ppermute x1, starting transfers between devices, local(): t1 = lax.ppermute(t1, 'patch', x_pairs(3))  4.39 us
    ppermute x1, starting transfers between devices, local(): near_rows = lax.ppermute(near_rows, 'patch', partner_pairs())  4.19 us
  transfers between devices with their start and end apart: 16, of which 6 were waited for; matrix products, arithmetic and copies ran while one was open for 0% of the time, Pallas kernels for 7%

profile of v15, /device:TPU:49, one launch (start us, length us, event | category | flops | bytes accessed | tf_op | source)
XLA Modules:
  0.0 91.9 jit_solution(13911068256847408169)
XLA Ops:
  0.6 2.8 %shard_map.86 = (bf16[6,128,384]{2,1,0:T(8,128)(2,1)}, bf16[7,128,384]{2,1,0:T(8,128)(2,1)}, bf16[7,128,384]{2,1,0:T(8,128)(2,1)}, f32[8,128]{1,0:T(8,128)}) custom-call(bf16[1,128,1536]{2,1,0:T(8,128)(2,1)} %h_hbm.1, f32[1,1536]{1,0:T(1,128)} %g_hbm.1, f32[1,1536]{1,0:T(1,128)} %b_hbm.1, s32[1,128]{1,0:T(1,128)} %m_hbm.1, bf16[1,2,128,1536]{3,2,1,0:T(8,128)(2,1)} %s_hbm.1), custom_call_target="tpu_custom_call" | custom-call | tf_op jit(solution)/shard_map/pallas_call | solution.py:271
  3.5 4.4 %collective-permute-start = (bf16[7,128,384]{2,1,0:T(8,128)(2,1)}, bf16[7,128,384]{2,1,0:T(8,128)(2,1)S(1)}, u32[]{:S(2)}, u32[]{:S(2)}) collective-permute-start(bf16[7,128,384]{2,1,0:T(8,128)(2,1)} %get-tuple-element.21), channel_id=1, source_target_pairs={{0,6},{1,3},{2,0},{3,5},{4,2},{5,7},{6,4},{7,1},{8,14},{9,11},{10,... | collective-permute-start | bytes 2064392 | tf_op jit(solution)/shard_map/ppermute | solution.py:295
  7.8 1.9 %collective-permute-start.2 = (bf16[7,128,384]{2,1,0:T(8,128)(2,1)}, bf16[7,128,384]{2,1,0:T(8,128)(2,1)S(1)}, u32[]{:S(2)}, u32[]{:S(2)}) collective-permute-start(bf16[7,128,384]{2,1,0:T(8,128)(2,1)} %get-tuple-element.22), channel_id=1, source_target_pairs={{0,2},{1,7},{2,4},{3,1},{4,6},{5,3},{6,0},{7,5},{8,10},{9,15},{10,... | collective-permute-start | bytes 2064392 | tf_op jit(solution)/shard_map/ppermute | solution.py:294
  9.8 0.0 copy-start
  9.8 1.5 %copy-done = bf16[1,1536,576]{1,2,0:T(8,128)(2,1)S(1)} copy-done((bf16[1,1536,576]{1,2,0:T(8,128)(2,1)S(1)}, bf16[1,1536,576]{1,2,0:T(8,128)(2,1)}, u32[]{:S(2)}) %copy-start) | copy-done | bytes 1769496
  11.3 0.7 copy-done.4
  11.9 0.4 shard_map.89
  12.3 4.2 %collective-permute-start.5 = (bf16[304,1536]{1,0:T(8,128)(2,1)S(1)}, bf16[304,1536]{1,0:T(8,128)(2,1)S(1)}, u32[]{:S(2)}, u32[]{:S(2)}) collective-permute-start(bf16[304,1536]{1,0:T(8,128)(2,1)S(1)} %get-tuple-element.25), channel_id=1, source_target_pairs={{0,1},{1,0},{2,3},{3,2},{4,5},{5,4},{6,7},{7,6},{8,9},{9,8},{10,11... | collective-permute-start | bytes 2801672 | tf_op jit(solution)/shard_map/ppermute | solution.py:296
  16.5 8.7 %collective-permute-start.4 = (bf16[272,1536]{1,0:T(8,128)(2,1)S(1)}, bf16[272,1536]{1,0:T(8,128)(2,1)S(1)}, u32[]{:S(2)}, u32[]{:S(2)}) collective-permute-start(bf16[272,1536]{1,0:T(8,128)(2,1)S(1)} %get-tuple-element.24), channel_id=1, source_target_pairs={{0,385},{1,128},{2,387},{3,130},{4,389},{5,132},{6,391},{7,134},{1... | collective-permute-start | bytes 2506760 | tf_op jit(solution)/shard_map/ppermute | solution.py:297
  25.2 1.8 %collective-permute-start.6 = (bf16[1,128,1536]{2,1,0:T(8,128)(2,1)S(1)}, bf16[1,128,1536]{2,1,0:T(8,128)(2,1)S(1)}, u32[]{:S(2)}, u32[]{:S(2)}) collective-permute-start(bf16[1,128,1536]{2,1,0:T(8,128)(2,1)S(1)} %copy-done.5), channel_id=1, source_target_pairs={{0,8},{8,16},{16,24},{24,32},{32,40},{40,48},{48,56},{56,64},{64,7... | collective-permute-start | bytes 1179656 | tf_op jit(solution)/shard_map/ppermute | solution.py:298
  27.1 5.0 %collective-permute-start.1 = (bf16[3,128,384]{2,1,0:T(8,128)(2,1)S(1)}, bf16[3,128,384]{2,1,0:T(8,128)(2,1)S(1)}, u32[]{:S(2)}, u32[]{:S(2)}) collective-permute-start(bf16[3,128,384]{2,1,0:T(8,128)(2,1)S(1)} %shard_map.87), channel_id=1, source_target_pairs={{0,6},{1,3},{2,0},{3,5},{4,2},{5,7},{6,4},{7,1},{8,14},{9,11},{10,... | collective-permute-start | bytes 884744 | tf_op jit(solution)/shard_map/ppermute | solution.py:300
  32.1 1.9 %collective-permute-start.3 = (bf16[3,128,384]{2,1,0:T(8,128)(2,1)S(1)}, bf16[3,128,384]{2,1,0:T(8,128)(2,1)S(1)}, u32[]{:S(2)}, u32[]{:S(2)}) collective-permute-start(bf16[3,128,384]{2,1,0:T(8,128)(2,1)S(1)} %shard_map.88), channel_id=1, source_target_pairs={{0,2},{1,7},{2,4},{3,1},{4,6},{5,3},{6,0},{7,5},{8,10},{9,15},{10,... | collective-permute-start | bytes 884744 | tf_op jit(solution)/shard_map/ppermute | solution.py:301
  34.0 0.1 shard_map.91
  34.1 1.9 %collective-permute-start.9 = (bf16[3,2,128,384]{3,2,1,0:T(8,128)(2,1)S(1)}, bf16[3,2,128,384]{3,2,1,0:T(8,128)(2,1)S(1)}, u32[]{:S(2)}, u32[]{:S(2)}) collective-permute-start(bf16[3,2,128,384]{3,2,1,0:T(8,128)(2,1)S(1)} %shard_map.91), channel_id=1, source_target_pairs={{0,1},{1,0},{2,3},{3,2},{4,5},{5,4},{6,7},{7,6},{8,9},{9,8},{10,11... | collective-permute-start | bytes 1769480 | tf_op jit(solution)/shard_map/ppermute | solution.py:303
  36.0 6.8 %collective-permute-done.4.v_ref = bf16[272,1536]{1,0:T(8,128)(2,1)S(1)} collective-permute-done((bf16[272,1536]{1,0:T(8,128)(2,1)S(1)}, bf16[272,1536]{1,0:T(8,128)(2,1)S(1)}, u32[]{:S(2)}, u32[]{:S(2)}) %collective-permute-start.4) | collective-permute-done | bytes 835616 | tf_op jit(solution)/shard_map/ppermute | solution.py:297
  42.9 1.0 %collective-permute-done.3.d_ref = bf16[3,128,384]{2,1,0:T(8,128)(2,1)S(1)} collective-permute-done((bf16[3,128,384]{2,1,0:T(8,128)(2,1)S(1)}, bf16[3,128,384]{2,1,0:T(8,128)(2,1)S(1)}, u32[]{:S(2)}, u32[]{:S(2)}) %collective-permute-start.3) | collective-permute-done | bytes 294944 | tf_op jit(solution)/shard_map/ppermute | solution.py:301
  43.8 2.7 %shard_map.90 = (bf16[6,128,384]{2,1,0:T(8,128)(2,1)S(1)}, bf16[6,128,384]{2,1,0:T(8,128)(2,1)S(1)}, bf16[3,128,384]{2,1,0:T(8,128)(2,1)S(1)}, bf16[6,128,384]{2,1,0:T(8,128)(2,1)S(1)}) custom-call(bf16[6,128,384]{2,1,0:T(8,128)(2,1)S(1)} %copy-done.2, bf16[7,128,384]{2,1,0:T(8,128)(2,1)S(1)} %collective-permute-done.t1, ...), custom_call_target="tpu_custom_call" | custom-call | tf_op jit(solution)/shard_map/pallas_call | solution.py:307
  46.5 3.4 %collective-permute-start.8 = (bf16[6,128,384]{2,1,0:T(8,128)(2,1)S(1)}, bf16[6,128,384]{2,1,0:T(8,128)(2,1)S(1)}, u32[]{:S(2)}, u32[]{:S(2)}) collective-permute-start(bf16[6,128,384]{2,1,0:T(8,128)(2,1)S(1)} %get-tuple-element.28), channel_id=1, source_target_pairs={{0,6},{1,3},{2,0},{3,5},{4,2},{5,7},{6,4},{7,1},{8,14},{9,11},{10,... | collective-permute-start | bytes 1769480 | tf_op jit(solution)/shard_map/ppermute | solution.py:314
  49.8 1.9 %collective-permute-start.7 = (bf16[6,128,384]{2,1,0:T(8,128)(2,1)S(1)}, bf16[6,128,384]{2,1,0:T(8,128)(2,1)S(1)}, u32[]{:S(2)}, u32[]{:S(2)}) collective-permute-start(bf16[6,128,384]{2,1,0:T(8,128)(2,1)S(1)} %get-tuple-element.27), channel_id=1, source_target_pairs={{0,2},{1,7},{2,4},{3,1},{4,6},{5,3},{6,0},{7,5},{8,10},{9,15},{10,... | collective-permute-start | bytes 1769480 | tf_op jit(solution)/shard_map/ppermute | solution.py:313
  51.8 1.9 %collective-permute-start.10 = (bf16[2,128,384]{2,1,0:T(8,128)(2,1)S(1)}, bf16[2,128,384]{2,1,0:T(8,128)(2,1)S(1)}, u32[]{:S(2)}, u32[]{:S(2)}) collective-permute-start(bf16[2,128,384]{2,1,0:T(8,128)(2,1)S(1)} %shard_map.92), channel_id=1, source_target_pairs={{0,1},{1,0},{2,3},{3,2},{4,5},{5,4},{6,7},{7,6},{8,9},{9,8},{10,11... | collective-permute-start | bytes 589832 | tf_op jit(solution)/shard_map/ppermute | solution.py:305
  53.8 8.5 %collective-permute-done.8.b_ref = bf16[6,128,384]{2,1,0:T(8,128)(2,1)S(1)} collective-permute-done((bf16[6,128,384]{2,1,0:T(8,128)(2,1)S(1)}, bf16[6,128,384]{2,1,0:T(8,128)(2,1)S(1)}, u32[]{:S(2)}, u32[]{:S(2)}) %collective-permute-start.8) | collective-permute-done | bytes 589856 | tf_op jit(solution)/shard_map/ppermute | solution.py:314
  62.3 2.1 %collective-permute-start.15 = (bf16[3,128,384]{2,1,0:T(8,128)(2,1)S(1)}, bf16[3,128,384]{2,1,0:T(8,128)(2,1)S(1)}, u32[]{:S(2)}, u32[]{:S(2)}) collective-permute-start(bf16[3,128,384]{2,1,0:T(8,128)(2,1)S(1)} %get-tuple-element.34), channel_id=1, source_target_pairs={{0,4},{1,5},{2,6},{3,7},{4,0},{5,1},{6,2},{7,3},{8,12},{9,13},{10,... | collective-permute-start | bytes 884744 | tf_op jit(solution)/shard_map/ppermute | solution.py:316
  64.4 0.9 %collective-permute-done.7.a_ref = bf16[6,128,384]{2,1,0:T(8,128)(2,1)S(1)} collective-permute-done((bf16[6,128,384]{2,1,0:T(8,128)(2,1)S(1)}, bf16[6,128,384]{2,1,0:T(8,128)(2,1)S(1)}, u32[]{:S(2)}, u32[]{:S(2)}) %collective-permute-start.7) | collective-permute-done | bytes 589856 | tf_op jit(solution)/shard_map/ppermute | solution.py:313
  65.3 2.6 %shard_map.93 = (bf16[128,384]{1,0:T(8,128)(2,1)S(1)}, bf16[128,384]{1,0:T(8,128)(2,1)S(1)}, bf16[128,384]{1,0:T(8,128)(2,1)S(1)}, bf16[128,384]{1,0:T(8,128)(2,1)S(1)}) custom-call(bf16[6,128,384]{2,1,0:T(8,128)(2,1)S(1)} %get-tuple-element.26.m_ref.k_ref, bf16[6,128,384]{2,1,0:T(8,128)(2,1)S(1)} %collective-permute-done.7.a_ref, ...), custom_call_target="tpu_custom_call" | custom-call | tf_op jit(solution)/shard_map/pallas_call | solution.py:318
  68.0 10.0 %collective-permute-start.11 = (bf16[128,384]{1,0:T(8,128)(2,1)S(1)}, bf16[128,384]{1,0:T(8,128)(2,1)S(1)}, u32[]{:S(2)}, u32[]{:S(2)}) collective-permute-start(bf16[128,384]{1,0:T(8,128)(2,1)S(1)} %get-tuple-element.29), channel_id=1, source_target_pairs={{0,8},{1,9},{2,10},{3,11},{4,12},{5,13},{6,14},{7,15},{8,16},{9,17... | collective-permute-start | bytes 294920 | tf_op jit(solution)/shard_map/ppermute | solution.py:332
  77.9 1.9 %collective-permute-start.12 = (bf16[128,384]{1,0:T(8,128)(2,1)S(1)}, bf16[128,384]{1,0:T(8,128)(2,1)S(1)}, u32[]{:S(2)}, u32[]{:S(2)}) collective-permute-start(bf16[128,384]{1,0:T(8,128)(2,1)S(1)} %get-tuple-element.30), channel_id=1, source_target_pairs={{0,14},{1,11},{2,8},{3,13},{4,10},{5,15},{6,12},{7,9},{8,22},{9,19... | collective-permute-start | bytes 294920 | tf_op jit(solution)/shard_map/ppermute | solution.py:332
  79.9 1.9 %collective-permute-start.13 = (bf16[128,384]{1,0:T(8,128)(2,1)S(1)}, bf16[128,384]{1,0:T(8,128)(2,1)S(1)}, u32[]{:S(2)}, u32[]{:S(2)}) collective-permute-start(bf16[128,384]{1,0:T(8,128)(2,1)S(1)} %get-tuple-element.31), channel_id=1, source_target_pairs={{0,12},{1,13},{2,14},{3,15},{4,8},{5,9},{6,10},{7,11},{8,20},{9,21... | collective-permute-start | bytes 294920 | tf_op jit(solution)/shard_map/ppermute | solution.py:332
  81.8 1.9 %collective-permute-start.14 = (bf16[128,384]{1,0:T(8,128)(2,1)S(1)}, bf16[128,384]{1,0:T(8,128)(2,1)S(1)}, u32[]{:S(2)}, u32[]{:S(2)}) collective-permute-start(bf16[128,384]{1,0:T(8,128)(2,1)S(1)} %get-tuple-element.32), channel_id=1, source_target_pairs={{0,10},{1,15},{2,12},{3,9},{4,14},{5,11},{6,8},{7,13},{8,18},{9,23... | collective-permute-start | bytes 294920 | tf_op jit(solution)/shard_map/ppermute | solution.py:332
  83.7 1.1 %shard_map.94 = (bf16[1,2,128,1536]{3,2,1,0:T(8,128)(2,1)}, f32[8,128]{1,0:T(8,128)S(1)}) custom-call(bf16[6,128,384]{2,1,0:T(8,128)(2,1)S(1)} %get-tuple-element.26.m_ref.k_ref, bf16[6,128,384]{2,1,0:T(8,128)(2,1)S(1)} %collective-permute-done.7.a_ref, bf16[6,128,384]{2,1,0:T(8,128)(2,1)S(1)} %collective-permute-done.8.b_ref, ...), custom_call_target="tpu_custom_call" | custom-call | tf_op jit(solution)/shard_map/pallas_call | solution.py:321
  84.8 3.4 %collective-permute-done.13.a2 = bf16[128,384]{1,0:T(8,128)(2,1)S(1)} collective-permute-done((bf16[128,384]{1,0:T(8,128)(2,1)S(1)}, bf16[128,384]{1,0:T(8,128)(2,1)S(1)}, u32[]{:S(2)}, u32[]{:S(2)}) %collective-permute-start.13) | collective-permute-done | bytes 98336 | tf_op jit(solution)/shard_map/ppermute | solution.py:332
  88.2 2.8 %collective-permute-done.14.a3 = bf16[128,384]{1,0:T(8,128)(2,1)S(1)} collective-permute-done((bf16[128,384]{1,0:T(8,128)(2,1)S(1)}, bf16[128,384]{1,0:T(8,128)(2,1)S(1)}, u32[]{:S(2)}, u32[]{:S(2)}) %collective-permute-start.14) | collective-permute-done | bytes 98336 | tf_op jit(solution)/shard_map/ppermute | solution.py:332
  91.1 0.9 shard_map.95
  (23 shorter events, 0.1 us)
Async XLA Ops:
  0.6 24.6 %copy-start.5 = (bf16[1,128,1536]{2,1,0:T(8,128)(2,1)S(1)}, bf16[1,128,1536]{2,1,0:T(8,128)(2,1)}, u32[]{:S(2)}) copy-start(bf16[1,128,1536]{2,1,0:T(8,128)(2,1)} %h_hbm.1) | copy-start | bytes 1179652
  3.5 23.6 %collective-permute-start = (bf16[7,128,384]{2,1,0:T(8,128)(2,1)}, bf16[7,128,384]{2,1,0:T(8,128)(2,1)S(1)}, u32[]{:S(2)}, u32[]{:S(2)}) collective-permute-start(bf16[7,128,384]{2,1,0:T(8,128)(2,1)} %get-tuple-element.21), channel_id=1, source_target_pairs={{0,6},{1,3},{2,0},{3,5},{4,2},{5,7},{6,4},{7,1},{8,14},{9,11},{10,... | collective-permute-start | bytes 2064392 | tf_op jit(solution)/shard_map/ppermute | solution.py:295
  7.8 24.2 %collective-permute-start.2 = (bf16[7,128,384]{2,1,0:T(8,128)(2,1)}, bf16[7,128,384]{2,1,0:T(8,128)(2,1)S(1)}, u32[]{:S(2)}, u32[]{:S(2)}) collective-permute-start(bf16[7,128,384]{2,1,0:T(8,128)(2,1)} %get-tuple-element.22), channel_id=1, source_target_pairs={{0,2},{1,7},{2,4},{3,1},{4,6},{5,3},{6,0},{7,5},{8,10},{9,15},{10,... | collective-permute-start | bytes 2064392 | tf_op jit(solution)/shard_map/ppermute | solution.py:294
  9.8 1.5 %copy-start = (bf16[1,1536,576]{1,2,0:T(8,128)(2,1)S(1)}, bf16[1,1536,576]{1,2,0:T(8,128)(2,1)}, u32[]{:S(2)}) copy-start(bf16[1,1536,576]{1,2,0:T(8,128)(2,1)} %param.8) | copy-start | bytes 5308420
  11.3 0.7 copy-start.4
  11.9 22.1 %copy-start.2 = (bf16[6,128,384]{2,1,0:T(8,128)(2,1)S(1)}, bf16[6,128,384]{2,1,0:T(8,128)(2,1)}, u32[]{:S(2)}) copy-start(bf16[6,128,384]{2,1,0:T(8,128)(2,1)} %get-tuple-element.20.t0) | copy-start | bytes 1769476
  12.3 30.5 %collective-permute-start.5 = (bf16[304,1536]{1,0:T(8,128)(2,1)S(1)}, bf16[304,1536]{1,0:T(8,128)(2,1)S(1)}, u32[]{:S(2)}, u32[]{:S(2)}) collective-permute-start(bf16[304,1536]{1,0:T(8,128)(2,1)S(1)} %get-tuple-element.25), channel_id=1, source_target_pairs={{0,1},{1,0},{2,3},{3,2},{4,5},{5,4},{6,7},{7,6},{8,9},{9,8},{10,11... | collective-permute-start | bytes 2801672 | tf_op jit(solution)/shard_map/ppermute | solution.py:296
  16.5 26.3 %collective-permute-start.4 = (bf16[272,1536]{1,0:T(8,128)(2,1)S(1)}, bf16[272,1536]{1,0:T(8,128)(2,1)S(1)}, u32[]{:S(2)}, u32[]{:S(2)}) collective-permute-start(bf16[272,1536]{1,0:T(8,128)(2,1)S(1)} %get-tuple-element.24), channel_id=1, source_target_pairs={{0,385},{1,128},{2,387},{3,130},{4,389},{5,132},{6,391},{7,134},{1... | collective-permute-start | bytes 2506760 | tf_op jit(solution)/shard_map/ppermute | solution.py:297
  25.2 8.9 %collective-permute-start.6 = (bf16[1,128,1536]{2,1,0:T(8,128)(2,1)S(1)}, bf16[1,128,1536]{2,1,0:T(8,128)(2,1)S(1)}, u32[]{:S(2)}, u32[]{:S(2)}) collective-permute-start(bf16[1,128,1536]{2,1,0:T(8,128)(2,1)S(1)} %copy-done.5), channel_id=1, source_target_pairs={{0,8},{8,16},{16,24},{24,32},{32,40},{40,48},{48,56},{56,64},{64,7... | collective-permute-start | bytes 1179656 | tf_op jit(solution)/shard_map/ppermute | solution.py:298
  27.0 16.8 %copy-start.1 = (bf16[1,1536,576]{1,2,0:T(8,128)(2,1)S(1)}, bf16[1,1536,576]{1,2,0:T(8,128)(2,1)}, u32[]{:S(2)}) copy-start(bf16[1,1536,576]{1,2,0:T(8,128)(2,1)} %param.8) | copy-start | bytes 5308420
  27.1 15.8 %collective-permute-start.1 = (bf16[3,128,384]{2,1,0:T(8,128)(2,1)S(1)}, bf16[3,128,384]{2,1,0:T(8,128)(2,1)S(1)}, u32[]{:S(2)}, u32[]{:S(2)}) collective-permute-start(bf16[3,128,384]{2,1,0:T(8,128)(2,1)S(1)} %shard_map.87), channel_id=1, source_target_pairs={{0,6},{1,3},{2,0},{3,5},{4,2},{5,7},{6,4},{7,1},{8,14},{9,11},{10,... | collective-permute-start | bytes 884744 | tf_op jit(solution)/shard_map/ppermute | solution.py:300
  32.1 11.7 %collective-permute-start.3 = (bf16[3,128,384]{2,1,0:T(8,128)(2,1)S(1)}, bf16[3,128,384]{2,1,0:T(8,128)(2,1)S(1)}, u32[]{:S(2)}, u32[]{:S(2)}) collective-permute-start(bf16[3,128,384]{2,1,0:T(8,128)(2,1)S(1)} %shard_map.88), channel_id=1, source_target_pairs={{0,2},{1,7},{2,4},{3,1},{4,6},{5,3},{6,0},{7,5},{8,10},{9,15},{10,... | collective-permute-start | bytes 884744 | tf_op jit(solution)/shard_map/ppermute | solution.py:301
  34.1 31.2 %copy-start.3 = (f32[1,1536]{1,0:T(1,128)S(1)}, f32[1,1536]{1,0:T(1,128)}, u32[]{:S(2)}) copy-start(f32[1,1536]{1,0:T(1,128)} %g_ref.1) | copy-start | bytes 18436
  34.1 17.7 %collective-permute-start.9 = (bf16[3,2,128,384]{3,2,1,0:T(8,128)(2,1)S(1)}, bf16[3,2,128,384]{3,2,1,0:T(8,128)(2,1)S(1)}, u32[]{:S(2)}, u32[]{:S(2)}) collective-permute-start(bf16[3,2,128,384]{3,2,1,0:T(8,128)(2,1)S(1)} %shard_map.91), channel_id=1, source_target_pairs={{0,1},{1,0},{2,3},{3,2},{4,5},{5,4},{6,7},{7,6},{8,9},{9,8},{10,11... | collective-permute-start | bytes 1769480 | tf_op jit(solution)/shard_map/ppermute | solution.py:303
  46.5 15.8 %collective-permute-start.8 = (bf16[6,128,384]{2,1,0:T(8,128)(2,1)S(1)}, bf16[6,128,384]{2,1,0:T(8,128)(2,1)S(1)}, u32[]{:S(2)}, u32[]{:S(2)}) collective-permute-start(bf16[6,128,384]{2,1,0:T(8,128)(2,1)S(1)} %get-tuple-element.28), channel_id=1, source_target_pairs={{0,6},{1,3},{2,0},{3,5},{4,2},{5,7},{6,4},{7,1},{8,14},{9,11},{10,... | collective-permute-start | bytes 1769480 | tf_op jit(solution)/shard_map/ppermute | solution.py:314
  49.8 15.5 %collective-permute-start.7 = (bf16[6,128,384]{2,1,0:T(8,128)(2,1)S(1)}, bf16[6,128,384]{2,1,0:T(8,128)(2,1)S(1)}, u32[]{:S(2)}, u32[]{:S(2)}) collective-permute-start(bf16[6,128,384]{2,1,0:T(8,128)(2,1)S(1)} %get-tuple-element.27), channel_id=1, source_target_pairs={{0,2},{1,7},{2,4},{3,1},{4,6},{5,3},{6,0},{7,5},{8,10},{9,15},{10,... | collective-permute-start | bytes 1769480 | tf_op jit(solution)/shard_map/ppermute | solution.py:313
  51.8 12.6 %collective-permute-start.10 = (bf16[2,128,384]{2,1,0:T(8,128)(2,1)S(1)}, bf16[2,128,384]{2,1,0:T(8,128)(2,1)S(1)}, u32[]{:S(2)}, u32[]{:S(2)}) collective-permute-start(bf16[2,128,384]{2,1,0:T(8,128)(2,1)S(1)} %shard_map.92), channel_id=1, source_target_pairs={{0,1},{1,0},{2,3},{3,2},{4,5},{5,4},{6,7},{7,6},{8,9},{9,8},{10,11... | collective-permute-start | bytes 589832 | tf_op jit(solution)/shard_map/ppermute | solution.py:305
  62.3 21.4 %collective-permute-start.15 = (bf16[3,128,384]{2,1,0:T(8,128)(2,1)S(1)}, bf16[3,128,384]{2,1,0:T(8,128)(2,1)S(1)}, u32[]{:S(2)}, u32[]{:S(2)}) collective-permute-start(bf16[3,128,384]{2,1,0:T(8,128)(2,1)S(1)} %get-tuple-element.34), channel_id=1, source_target_pairs={{0,4},{1,5},{2,6},{3,7},{4,0},{5,1},{6,2},{7,3},{8,12},{9,13},{10,... | collective-permute-start | bytes 884744 | tf_op jit(solution)/shard_map/ppermute | solution.py:316
  68.0 16.9 %collective-permute-start.11 = (bf16[128,384]{1,0:T(8,128)(2,1)S(1)}, bf16[128,384]{1,0:T(8,128)(2,1)S(1)}, u32[]{:S(2)}, u32[]{:S(2)}) collective-permute-start(bf16[128,384]{1,0:T(8,128)(2,1)S(1)} %get-tuple-element.29), channel_id=1, source_target_pairs={{0,8},{1,9},{2,10},{3,11},{4,12},{5,13},{6,14},{7,15},{8,16},{9,17... | collective-permute-start | bytes 294920 | tf_op jit(solution)/shard_map/ppermute | solution.py:332
  77.9 6.9 %collective-permute-start.12 = (bf16[128,384]{1,0:T(8,128)(2,1)S(1)}, bf16[128,384]{1,0:T(8,128)(2,1)S(1)}, u32[]{:S(2)}, u32[]{:S(2)}) collective-permute-start(bf16[128,384]{1,0:T(8,128)(2,1)S(1)} %get-tuple-element.30), channel_id=1, source_target_pairs={{0,14},{1,11},{2,8},{3,13},{4,10},{5,15},{6,12},{7,9},{8,22},{9,19... | collective-permute-start | bytes 294920 | tf_op jit(solution)/shard_map/ppermute | solution.py:332
  79.9 8.3 %collective-permute-start.13 = (bf16[128,384]{1,0:T(8,128)(2,1)S(1)}, bf16[128,384]{1,0:T(8,128)(2,1)S(1)}, u32[]{:S(2)}, u32[]{:S(2)}) collective-permute-start(bf16[128,384]{1,0:T(8,128)(2,1)S(1)} %get-tuple-element.31), channel_id=1, source_target_pairs={{0,12},{1,13},{2,14},{3,15},{4,8},{5,9},{6,10},{7,11},{8,20},{9,21... | collective-permute-start | bytes 294920 | tf_op jit(solution)/shard_map/ppermute | solution.py:332
  81.8 9.3 %collective-permute-start.14 = (bf16[128,384]{1,0:T(8,128)(2,1)S(1)}, bf16[128,384]{1,0:T(8,128)(2,1)S(1)}, u32[]{:S(2)}, u32[]{:S(2)}) collective-permute-start(bf16[128,384]{1,0:T(8,128)(2,1)S(1)} %get-tuple-element.32), channel_id=1, source_target_pairs={{0,10},{1,15},{2,12},{3,9},{4,14},{5,11},{6,8},{7,13},{8,18},{9,23... | collective-permute-start | bytes 294920 | tf_op jit(solution)/shard_map/ppermute | solution.py:332
